TPU v7x, 256 devices: a whole 4x4x8 slice. The times are simulated.
256 devices in a mesh: rows: 32 (over y, z), protos: 8 (over x, core).
Axes of the slice: x: 4, y: 4, z: 8, core: 2. Of those that a mesh axis runs over, the one named last changes fastest.
Arguments:
- teacher_patches: bfloat16 [128, 256, 256], P('rows'), may hold values from -7 to 7
- student_patches: bfloat16 [128, 256, 256], P('rows'), may hold values from -0.0625 to 0.0625
- mask_order: int32 [128, 256], P('rows'), may hold values from 0 to 255, each once within a row
- teacher_protos: bfloat16 [65536, 256], P('protos'), may hold values from -1 to 1
- student_protos: bfloat16 [65536, 256], P('protos'), may hold values from -0.0234375 to 0.0234375
Outputs:
- grad_student: float32 [128, 128, 256], P('rows')
- grad_protos: float32 [65536, 256], P(('protos', 'rows'))
Inputs may be any that keep to these rules, and one draw needn't show every extreme that they name: `mask_order`: each row is an order of the 256 patch positions of its image, each once; its first 128 entries are the masked patches.
All inputs are finite; a program needn't handle non-finite values.
Results may differ from a plain program's by a relative error of at most 0.007.
The roundings to bfloat16 on the way count: a program that leaves them out, or rounds other values in their place, can miss the bound.
Values sent between devices are 32-bit elements; how exact they have to be, the bound alone decides.
No kernel may reach another device: no remote copies, remote signals or barrier semaphores. Data moves between devices by JAX's collectives and lax.ppermute only.
A program may use at most 128 MiB of HBM per device.

v0:
```python
import jax
import jax.numpy as jnp
from jax import lax
from jax.sharding import PartitionSpec as P

D = 256
MASKED = 128
ITERS = 3


teacher_temp = 0.07
student_temp = 0.1
epsilon = 1e-06


def unit_rows(values):
    length = jnp.sqrt(jnp.sum(values * values, axis=-1, keepdims=True) + epsilon)
    return (values / length, length)


def column_scale(energy, row_scale):
    return 1.0 / lax.psum(jnp.sum(energy * row_scale[:, None], axis=0), "rows")


def row_totals(row_part):
    return lax.psum(row_part, "protos")


def on_device(teacher_patches, student_patches, mask_order, teacher_protos, student_protos):
    chosen = mask_order[:, :MASKED]
    image_count = teacher_patches.shape[0]
    teacher_sel = (
        jnp.take_along_axis(teacher_patches, chosen[:, :, None], axis=1)
        .reshape(-1, D)
        .astype(jnp.float32)
    )
    student_sel = (
        jnp.take_along_axis(student_patches, chosen[:, :, None], axis=1)
        .reshape(-1, D)
        .astype(jnp.float32)
    )
    teacher_unit, teacher_length = unit_rows(teacher_sel)
    student_unit, student_length = unit_rows(student_sel)
    teacher_dir, teacher_plen = unit_rows(teacher_protos.astype(jnp.float32))
    student_dir, proto_length = unit_rows(student_protos.astype(jnp.float32))
    teacher_cast = teacher_unit.astype(jnp.bfloat16)
    student_cast = student_unit.astype(jnp.bfloat16)
    teacher_wcast = teacher_dir.astype(jnp.bfloat16)
    student_wcast = student_dir.astype(jnp.bfloat16)
    token_count = teacher_cast.shape[0]
    energy = jnp.exp(
        jnp.dot(teacher_cast, teacher_wcast.T, preferred_element_type=jnp.float32) / teacher_temp
    )
    student_exp = jnp.exp(
        jnp.dot(student_cast, student_wcast.T, preferred_element_type=jnp.float32) / student_temp
    )
    norm_part = jnp.sum(student_exp, axis=1)
    row_scale = jnp.ones((token_count,), jnp.float32)
    col_scale = None
    normalizer = None
    for sweep in range(ITERS):
        col_scale = column_scale(energy, row_scale)
        row_part = jnp.sum(energy * col_scale[None, :], axis=1)
        row_scale = 1.0 / row_totals(row_part)
    normalizer = lax.psum(norm_part, "protos")
    targets = energy * row_scale[:, None] * col_scale[None, :]
    logit_grad = ((student_exp / normalizer[:, None] - targets) / student_temp).astype(jnp.bfloat16)
    feature_grad = lax.psum(
        jnp.dot(logit_grad, student_wcast, preferred_element_type=jnp.float32), "protos"
    )
    result = (
        feature_grad - student_unit * jnp.sum(student_unit * feature_grad, axis=-1, keepdims=True)
    ) / student_length
    grad_student = result.reshape(image_count, MASKED, D)
    share_protos = logit_grad.shape[1] // lax.axis_size("rows")
    proto_share = lax.psum_scatter(
        lax.dot_general(
            logit_grad, student_cast, (((0,), (0,)), ((), ())), preferred_element_type=jnp.float32
        ),
        "rows",
        scatter_dimension=0,
        tiled=True,
    )
    first_proto = lax.axis_index("rows") * share_protos
    dir_piece = lax.dynamic_slice_in_dim(student_dir, first_proto, share_protos, 0)
    plen_piece = lax.dynamic_slice_in_dim(proto_length, first_proto, share_protos, 0)
    grad_protos = (
        proto_share - dir_piece * jnp.sum(dir_piece * proto_share, axis=-1, keepdims=True)
    ) / plen_piece
    return (grad_student, grad_protos)


def solution(mesh):
    return jax.shard_map(
        on_device,
        mesh=mesh,
        in_specs=(
            P("rows", None, None),
            P("rows", None, None),
            P("rows", None),
            P("protos", None),
            P("protos", None),
        ),
        out_specs=(P("rows", None, None), P(("protos", "rows"), None)),
        check_vma=False,
    )
```

profile of v0, /device:TPU:1, one launch (start us, length us, event | category | flops | bytes accessed | tf_op | source)
XLA Modules:
  0.0 794.1 jit_solution(10483050453688421116)
XLA Ops:
  9.5 3.2 gather_fusion
  12.7 7.0 gather_fusion.1
  20.2 3.3 fusion.2
  23.8 9.4 %fusion.14 = (f32[8192]{0:T(1024)S(1)}, f32[512,8192]{1,0:T(8,128)}) fusion(bf16[512,256]{1,0:T(8,128)(2,1)S(1)} %get-tuple-element.13, bf16[8192,256]{1,0:T(8,128)(2,1)} %param.10, f32[8192]{0:T(1024)S(1)} %add_sqrt_fusion), kind=kOutput, calls=%fused_computation.50 | convolution fusion | flops 2162155520 | bytes 21299200 | tf_op jit(solution)/shard_map/dot_general | solution.py:52
  33.2 118.9 %psum.57 = f32[8192]{0:T(1024)S(1)} all-reduce(f32[8192]{0:T(1024)S(1)} %get-tuple-element.9), channel_id=1, replica_groups=mesh['rows'=32,'protos'=8] {'rows'}, use_global_device_ids=true, to_apply=%region_7.0 | all-reduce | flops 8192 | bytes 65536 | tf_op jit(solution)/shard_map/psum | solution.py:22
  152.1 7.3 multiply_reduce_fusion.4
  159.4 40.3 %psum.58 = f32[512]{0:T(512)S(1)} all-reduce(f32[512]{0:T(512)S(1)} %multiply_reduce_fusion.4), channel_id=1, replica_groups=mesh['rows'=32,'protos'=8] {'protos'}, use_global_device_ids=true, to_apply=%region_9.0 | all-reduce | flops 512 | bytes 4096 | tf_op jit(solution)/shard_map/psum | solution.py:26
  199.7 8.3 %multiply_reduce_fusion.3 = f32[8192]{0:T(1024)S(1)} fusion(f32[512,8192]{1,0:T(8,128)} %get-tuple-element.10, f32[512]{0:T(512)S(1)} %broadcast_divide_fusion.5), kind=kLoop, calls=%fused_computation.6 | loop fusion | flops 8380416 | bytes 16812032 | tf_op jit(solution)/shard_map/reduce_sum | solution.py:22
  208.0 109.9 %psum.59 = f32[8192]{0:T(1024)S(1)} all-reduce(f32[8192]{0:T(1024)S(1)} %multiply_reduce_fusion.3), channel_id=1, replica_groups=mesh['rows'=32,'protos'=8] {'rows'}, use_global_device_ids=true, to_apply=%region_11.0 | all-reduce | flops 8192 | bytes 65536 | tf_op jit(solution)/shard_map/psum | solution.py:22
  317.9 7.3 multiply_reduce_fusion.2
  325.2 40.4 %psum.60 = f32[512]{0:T(512)S(1)} all-reduce(f32[512]{0:T(512)S(1)} %multiply_reduce_fusion.2), channel_id=1, replica_groups=mesh['rows'=32,'protos'=8] {'protos'}, use_global_device_ids=true, to_apply=%region_13.0 | all-reduce | flops 512 | bytes 4096 | tf_op jit(solution)/shard_map/psum | solution.py:26
  365.6 8.3 %multiply_reduce_fusion.1 = f32[8192]{0:T(1024)S(1)} fusion(f32[512,8192]{1,0:T(8,128)} %get-tuple-element.10, f32[512]{0:T(512)S(1)} %broadcast_divide_fusion.4), kind=kLoop, calls=%fused_computation.4 | loop fusion | flops 8380416 | bytes 16812032 | tf_op jit(solution)/shard_map/reduce_sum | solution.py:22
  373.9 109.9 %psum.61 = f32[8192]{0:T(1024)S(1)} all-reduce(f32[8192]{0:T(1024)S(1)} %multiply_reduce_fusion.1), channel_id=1, replica_groups=mesh['rows'=32,'protos'=8] {'rows'}, use_global_device_ids=true, to_apply=%region_15.0 | all-reduce | flops 8192 | bytes 65536 | tf_op jit(solution)/shard_map/psum | solution.py:22
  483.8 7.4 multiply_reduce_fusion
  492.4 7.1 fusion
  499.5 40.2 %all-reduce = (f32[512]{0:T(512)S(1)}, f32[512]{0:T(512)S(1)}) all-reduce(f32[512]{0:T(512)S(1)} %multiply_reduce_fusion, f32[512]{0:T(512)S(1)} %get-tuple-element.11), channel_id=1, replica_groups=mesh['rows'=32,'protos'=8] {'protos'}, use_global_device_ids=true, to_apply=%region_17.0 | all-reduce | flops 1024 | bytes 8192 | tf_op jit(solution)/shard_map/psum | solution.py:26
  539.7 12.3 %multiply_convert_fusion = bf16[512,8192]{1,0:T(8,128)(2,1)S(1)} fusion(f32[512,8192]{1,0:T(8,128)} %get-tuple-element.10, f32[512,8192]{1,0:T(8,128)} %get-tuple-element.12, f32[512]{0:T(512)S(1)} %broadcast_divide_fusion.3, f32[8192]{0:T(1024)S(1)} %broadcast_divide_fusion, f32[512]{0:T(512)S(1)} %get-tuple-element.6), kind=kLoop, calls=%fused_computation.2 | loop fusion | flops 29360128 | bytes 41979904 | tf_op jit(solution)/shard_map/convert_element_type | solution.py:67
  552.0 3.2 copy-done.2
  555.2 3.4 fusion.6
  558.9 9.0 %fusion.11 = f32[8192,256]{1,0:T(8,128)} fusion(bf16[512,8192]{1,0:T(8,128)(2,1)} %copy-done.2, f32[512,256]{1,0:T(8,128)S(1)} %get-tuple-element.14), kind=kOutput, calls=%fused_computation.34 | convolution fusion | flops 2147614720 | bytes 17301504 | tf_op jit(solution)/shard_map/dot_general | solution.py:77
  568.1 5.6 convert_divide_fusion.1
  573.6 40.4 %all-reduce.3.cloned.1.call-done = f32[512,256]{1,0:T(8,128)} async-done(((f32[512,256]{1,0:T(8,128)}), f32[512,256]{1,0:T(8,128)}) %all-reduce.3.cloned.1.call-update) | async-done | bytes 524304 | tf_op jit(solution)/shard_map/psum | solution.py:68
  615.2 2.0 subtract_divide_fusion
  617.3 166.3 %reduce-scatter.2.cloned.1.call-done = f32[256,256]{1,0:T(8,128)} async-done(((f32[8192,256]{1,0:T(8,128)}), f32[256,256]{1,0:T(8,128)}) %reduce-scatter.2.cloned.1.call-update) | async-done | bytes 262160 | tf_op jit(solution)/shard_map/reduce_scatter | solution.py:76
  (37 shorter events, 8.1 us)
Async XLA Ops:
  8.0 1.5 copy-start
  8.0 606.0 %all-reduce.3.cloned.1.call-start = ((), (), s32[]{:S(2)}) async-start(), calls=%async_computation.1 | async-start | bytes 1048576 | tf_op jit(solution)/shard_map/psum | solution.py:68
  23.8 535.1 %copy-start.5 = (f32[512,256]{1,0:T(8,128)}, f32[512,256]{1,0:T(8,128)S(1)}, u32[]{:S(2)}) copy-start(f32[512,256]{1,0:T(8,128)S(1)} %get-tuple-element.14) | copy-start | bytes 1572868
  483.8 7.4 copy-start.3
  539.7 15.5 %copy-start.4 = (bf16[8192,256]{1,0:T(8,128)(2,1)S(1)}, bf16[8192,256]{1,0:T(8,128)(2,1)}, u32[]{:S(2)}) copy-start(bf16[8192,256]{1,0:T(8,128)(2,1)} %param.11) | copy-start | bytes 12582916
  552.0 3.2 copy-start.2
  558.6 225.0 %reduce-scatter.2.cloned.1.call-start = ((), (), s32[]{:S(2)}) async-start(), calls=%async_computation.2 | async-start | bytes 8650752 | tf_op jit(solution)/shard_map/reduce_scatter | solution.py:76
  568.0 46.0 %copy-start.6 = (f32[512,256]{1,0:T(8,128)S(1)}, f32[512,256]{1,0:T(8,128)}, u32[]{:S(2)}) copy-start(f32[512,256]{1,0:T(8,128)} %copy-done.5) | copy-start | bytes 1572868
  568.0 218.6 %copy-start.1 = (bf16[4,256,256]{2,1,0:T(8,128)(2,1)S(1)}, bf16[4,256,256]{2,1,0:T(8,128)(2,1)}, u32[]{:S(2)}) copy-start(bf16[4,256,256]{2,1,0:T(8,128)(2,1)} %param.8) | copy-start | bytes 1572868
Sparse Core Ops, SparseCore 0:
  558.7 55.2 all-reduce.2
Sparse Core Ops, SparseCore 1:
  568.1 215.5 reduce-scatter.1
where the time goes:
time: 798 us; the launch traced here: 794 us
  blocking collectives  460 us (58%)
  waiting for transfers between devices  207 us (26%)
  other arithmetic  69.4 us (9%)
  matrix products  28.9 us (4%)
  between operations  15.7 us (2%)
  local copies, waits for them, and re-layouts  13.5 us (2%)
    psum x3, blocking collectives, column_scale(): return 1.0 / lax.psum(jnp.sum(energy * row_scale[:, None], axis=0), 'rows')  339 us
    reduce_scatter x1, waiting for transfers between devices, on_device(): lax.psum_scatter(lax.dot_general(logit_grad, student_cast, (((0,), (0,)),...  166 us
    psum x3, blocking collectives, row_totals(): return lax.psum(row_part, 'protos')  121 us
    psum x1, waiting for transfers between devices, on_device(): lax.psum(jnp.dot(logit_grad, student_wcast, preferred_element_type=jnp.fl...  40.4 us
    reduce_sum x3, other arithmetic, on_device(): row_part = jnp.sum(energy * col_scale[None, :], axis=1)  22 us
    reduce_sum x2, other arithmetic, column_scale(): return 1.0 / lax.psum(jnp.sum(energy * row_scale[:, None], axis=0), 'rows')  16.6 us
  transfers between devices with their start and end apart: 2, of which 2 were waited for; matrix products, arithmetic and copies ran while one was open for 2% of the time, Pallas kernels for 0%

commit v1 on v0

v1 whole, which is shorter than its diff:
```python
import math

import jax
import jax.numpy as jnp
from jax import lax
from jax.experimental import pallas as pl
from jax.experimental.pallas import tpu as pltpu
from jax.sharding import Mesh, PartitionSpec as P

D = 256
MASKED = 128
ITERS = 3
LANES = 128

teacher_temp = 0.07
student_temp = 0.1
epsilon = 1e-06

teacher_power = math.log2(math.e) / teacher_temp
student_power = math.log2(math.e) / student_temp

ROWS = ("y", "z")
PROTOS = ("x", "core")

f32 = jnp.float32
bf16 = jnp.bfloat16


def params(mib):
    return pltpu.CompilerParams(vmem_limit_bytes=mib * 2**20)


def spread(value, axes):
    return lax.all_to_all(value, axes, 0, 0, tiled=True)


def work(flops, moved, powers=0):
    return pl.CostEstimate(flops=int(flops), bytes_accessed=int(moved), transcendentals=int(powers))


def in_hbm(value):
    return pltpu.with_memory_space_constraint(value, pltpu.HBM)


def nt_dot(a, b):
    return lax.dot_general(a, b, (((1,), (1,)), ((), ())), preferred_element_type=f32)


def unit_rows(values):
    length = jnp.sqrt(jnp.sum(values * values, axis=-1, keepdims=True) + epsilon)
    return (values / length, length)


def directions(values):
    values = values.astype(f32)
    return (values * lax.rsqrt(jnp.sum(values * values, axis=-1, keepdims=True) + epsilon)).astype(bf16)


def to_column(row):
    return jnp.broadcast_to(row, (LANES, LANES)).T


def fill_columns(rows, tile_ref):
    for k in range(rows.shape[0]):
        tile_ref[k * LANES : (k + 1) * LANES, :] = to_column(rows[k : k + 1, :])


def lane_totals(tile):
    parts = [
        jnp.sum(tile[k * LANES : (k + 1) * LANES, :].T, axis=0, keepdims=True)
        for k in range(tile.shape[0] // LANES)
    ]
    return jnp.concatenate(parts, axis=0)


def select_body(place_ref, teacher_ref, student_ref, order_ref, units_ref, length_ref, mine_ref):
    images, patches, _ = teacher_ref.shape
    for image in range(images):
        chosen = order_ref[image : image + 1, :MASKED]
        place = lax.broadcasted_iota(jnp.int32, (patches, MASKED), 0)
        onehot = jnp.where(place == chosen, 1.0, 0.0).astype(bf16)

        def pick(ref):
            return lax.dot_general(
                onehot, ref[image], (((0,), (0,)), ((), ())), preferred_element_type=f32
            )

        rows = slice(image * MASKED, (image + 1) * MASKED)
        teacher = unit_rows(pick(teacher_ref))[0]
        student, length_ref[rows, :] = unit_rows(pick(student_ref))
        units_ref[rows, :D] = teacher
        units_ref[rows, D:] = student
        mine_ref[rows, :] = jnp.where(place_ref[3] == 0, teacher, student)


def select_tokens(place, teacher_patches, student_patches, mask_order):
    tokens = teacher_patches.shape[0] * MASKED
    return pl.pallas_call(
        select_body,
        in_specs=[pl.BlockSpec(memory_space=pltpu.SMEM)]
        + [pl.BlockSpec(memory_space=pltpu.VMEM)] * 3,
        out_specs=[pl.BlockSpec(memory_space=pltpu.VMEM)] * 3,
        out_shape=[
            pltpu.HBM((tokens, 2 * D), f32),
            pltpu.HBM((tokens, 1), f32),
            pltpu.HBM((tokens, D), f32),
        ],
        compiler_params=params(8),
        name="select",
    )(place, in_hbm(teacher_patches), in_hbm(student_patches), in_hbm(mask_order))


def lane_rows(row):
    parts = [row[:, j * LANES : (j + 1) * LANES] for j in range(row.shape[1] // LANES)]
    return jnp.concatenate(parts, axis=0)


def chunks(tokens):
    return [slice(c, c + LANES) for c in range(0, tokens, LANES)]


FETCHES = 8
WIDE = 256


def fetch(protos_ref, buffer_ref, sems, i):
    size = buffer_ref.shape[0] // FETCHES
    rows = pl.ds(pl.multiple_of(i * size, size), size)
    return pltpu.make_async_copy(protos_ref.at[rows, :], buffer_ref.at[rows, :], sems.at[i])


def fetch_all(units_ref, column, unit_ref, protos_ref, buffer_ref, sems):
    units = pltpu.make_async_copy(
        units_ref.at[:, pl.ds(column, D)], unit_ref, sems.at[FETCHES]
    )
    units.start()
    for i in range(FETCHES):
        fetch(protos_ref, buffer_ref, sems, i).start()
    units.wait()


def energy_body(units_ref, protos_ref, energy_ref, sums_ref, unit_ref, cast_ref, buffer_ref, sems):
    size = buffer_ref.shape[0] // FETCHES
    tiles = size // LANES
    fetch_all(units_ref, 0, unit_ref, protos_ref, buffer_ref, sems)
    cast_ref[...] = unit_ref[...].astype(bf16)

    def step(i, carry):
        fetch(protos_ref, buffer_ref, sems, i).wait()
        totals = []

        def logits_of(part):
            rows = pl.ds(pl.multiple_of(i * size + part * WIDE, WIDE), WIDE)
            return nt_dot(cast_ref[...], directions(buffer_ref[rows, :]))

        parts = size // WIDE
        logits = logits_of(0)
        for part in range(parts):
            following = logits_of(part + 1) if part + 1 < parts else None
            energy = jnp.exp2(logits * teacher_power)
            logits = following
            totals.append(lane_rows(jnp.sum(energy, axis=0, keepdims=True)))
            for j in range(WIDE // LANES):
                tile = i * tiles + part * (WIDE // LANES) + j
                energy_ref[tile] = energy[:, j * LANES : (j + 1) * LANES].astype(bf16)
        sums_ref[pl.ds(pl.multiple_of(i * tiles, tiles), tiles), :] = jnp.concatenate(totals, axis=0)
        return carry

    lax.fori_loop(0, FETCHES, step, 0)


def fixed(*shape):
    return pl.BlockSpec(shape, lambda i: (0,) * len(shape))


def left(tokens):
    return pl.BlockSpec((tokens, D), lambda *i: (0, 0))


def right(tokens):
    return pl.BlockSpec((tokens, D), lambda *i: (0, 1))


def energy_of(units, protos):
    tokens, count = units.shape[0], protos.shape[0]
    tiles = count // LANES
    whole = pl.BlockSpec(memory_space=pltpu.VMEM)
    return pl.pallas_call(
        energy_body,
        in_specs=[pl.BlockSpec(memory_space=pl.ANY)] * 2,
        out_specs=[whole] * 2,
        out_shape=[
            pltpu.VMEM((tiles, tokens, LANES), bf16),
            jax.ShapeDtypeStruct((tiles, LANES), f32),
        ],
        scratch_shapes=[
            pltpu.VMEM((tokens, D), f32),
            pltpu.VMEM((tokens, D), bf16),
            pltpu.VMEM((count, D), bf16),
            pltpu.SemaphoreType.DMA((FETCHES + 1,)),
        ],
        compiler_params=params(16),
        cost_estimate=work(4 * tokens * count * D, 8 * 2**20, tokens * count),
        name="energy",
    )(in_hbm(units), in_hbm(protos))


def student_body(units_ref, protos_ref, sums_ref, unit_ref, cast_ref, total_ref, buffer_ref, sems):
    size = buffer_ref.shape[0] // FETCHES
    fetch_all(units_ref, D, unit_ref, protos_ref, buffer_ref, sems)
    cast_ref[...] = unit_ref[...].astype(bf16)
    total_ref[...] = jnp.zeros_like(total_ref)

    def step(i, carry):
        fetch(protos_ref, buffer_ref, sems, i).wait()
        total = total_ref[...]

        def logits_of(part):
            rows = pl.ds(pl.multiple_of(i * size + part * WIDE, WIDE), WIDE)
            return nt_dot(cast_ref[...], directions(buffer_ref[rows, :]))

        parts = size // WIDE
        logits = logits_of(0)
        for part in range(parts):
            following = logits_of(part + 1) if part + 1 < parts else None
            values = jnp.exp2(logits * student_power)
            logits = following
            for j in range(WIDE // LANES):
                total = total + values[:, j * LANES : (j + 1) * LANES]
        total_ref[...] = total
        return carry

    lax.fori_loop(0, FETCHES, step, 0)
    sums_ref[...] = lane_totals(total_ref[...])


def student_sums(units, protos):
    tokens, count = units.shape[0], protos.shape[0]
    return pl.pallas_call(
        student_body,
        in_specs=[pl.BlockSpec(memory_space=pl.ANY)] * 2,
        out_specs=pl.BlockSpec(memory_space=pltpu.VMEM),
        out_shape=jax.ShapeDtypeStruct((tokens // LANES, LANES), f32),
        scratch_shapes=[
            pltpu.VMEM((tokens, D), f32),
            pltpu.VMEM((tokens, D), bf16),
            pltpu.VMEM((tokens, LANES), f32),
            pltpu.VMEM((count, D), bf16),
            pltpu.SemaphoreType.DMA((FETCHES + 1,)),
        ],
        compiler_params=params(16),
        cost_estimate=work(4 * tokens * count * D, 8 * 2**20, tokens * count),
        name="student",
    )(in_hbm(units), in_hbm(protos))


def right(tokens):
    return pl.BlockSpec((tokens, D), lambda *i: (0, 1))


def row_body(energy_ref, pieces_ref, scale_ref, sums_ref):
    tiles, tokens, _ = energy_ref.shape
    scale_ref[...] = 1.0 / jnp.sum(pieces_ref[...], axis=0)
    for k, rows in enumerate(chunks(tokens)):

        def step(j, total):
            return total + energy_ref[j, rows, :].astype(f32) * scale_ref[pl.ds(j, 1), :]

        total = lax.fori_loop(0, tiles, step, jnp.zeros((LANES, LANES), f32), unroll=8)
        totals = lane_totals(total)
        for copy in range(sums_ref.shape[0]):
            sums_ref[copy, k : k + 1, :] = totals


def row_sums(energy, pieces, copies):
    tiles, tokens, _ = energy.shape
    whole = pl.BlockSpec(memory_space=pltpu.VMEM)
    return pl.pallas_call(
        row_body,
        in_specs=[whole] * 2,
        out_specs=[whole] * 2,
        out_shape=[
            jax.ShapeDtypeStruct((tiles, LANES), f32),
            jax.ShapeDtypeStruct((copies, tokens // LANES, LANES), f32),
        ],
        compiler_params=params(12),
        cost_estimate=work(2 * energy.size, 0),
        name="row_sums",
    )(energy, pieces)


def column_body(energy_ref, pieces_ref, sums_ref, tile_ref):
    tiles = energy_ref.shape[0]
    fill_columns(1.0 / jnp.sum(pieces_ref[...], axis=0), tile_ref)

    def step(j, carry):
        total = jnp.sum(energy_ref[j].astype(f32) * tile_ref[...], axis=0, keepdims=True)
        sums_ref[pl.ds(j, 1), :] = total
        return carry

    lax.fori_loop(0, tiles, step, 0, unroll=4)


def column_sums(energy, pieces):
    tiles, tokens, _ = energy.shape
    whole = pl.BlockSpec(memory_space=pltpu.VMEM)
    return pl.pallas_call(
        column_body,
        in_specs=[whole] * 2,
        out_specs=whole,
        out_shape=jax.ShapeDtypeStruct((tiles, LANES), f32),
        scratch_shapes=[pltpu.VMEM((tokens, LANES), f32)],
        compiler_params=params(12),
        cost_estimate=work(2 * energy.size, 0),
        name="column_sums",
    )(energy, pieces)


LEFT_PLACE = [4, 5, 6, 7, 3, 2, 1, 0]
RIGHT_PLACE = [4, 0, 1, 2, 3, 7, 6, 5]


def collect(send, keep, offset):
    n = lax.axis_size("z")
    way = [1 if (z + offset) % 2 else -1 for z in range(n)]
    got = lax.ppermute(send, "z", [(z, (z - way[z]) % n) for z in range(n)])
    return [keep[k] + got[k] for k in range(4)]


def deliver(parts, offset):
    n = lax.axis_size("z")
    way = [1 if (z + offset) % 2 else -1 for z in range(n)]
    return [parts[0]] + [
        lax.ppermute(parts[k], "z", [(z, (z + way[z] * k) % n) for z in range(n)]) for k in (1, 2, 3)
    ]


def cast_body(place_ref, units_ref, *refs):
    *got_refs, out_ref = refs
    tokens = units_ref.shape[0]
    half = len(got_refs) // 2
    out_ref[:tokens, :] = units_ref[...].astype(bf16)
    for core in range(2):

        @pl.when(place_ref[3] == core)
        def _(core=core):
            for i in range(half):
                rows = slice((i + 1) * tokens, (i + 2) * tokens)
                mine, other = slice(core * D, (core + 1) * D), slice((1 - core) * D, (2 - core) * D)
                out_ref[rows, mine] = got_refs[i][...].astype(bf16)
                out_ref[rows, other] = got_refs[half + i][...].astype(bf16)


def cast_units(place, units, got, other):
    tokens, width = units.shape
    whole = pl.BlockSpec(memory_space=pltpu.VMEM)
    return pl.pallas_call(
        cast_body,
        in_specs=[pl.BlockSpec(memory_space=pltpu.SMEM)] + [whole] * (1 + len(got) + len(other)),
        out_specs=whole,
        out_shape=pltpu.HBM((tokens * (1 + len(got)), width), bf16),
        compiler_params=params(12),
        cost_estimate=work(0, 24 * units.size),
        name="cast",
    )(place, in_hbm(units), *got, *other)


def proto_body(
    table_ref,
    units_ref,
    pieces_ref,
    tw_first_ref,
    tw_second_ref,
    sw_first_ref,
    sw_second_ref,
    first_scale_ref,
    second_scale_ref,
    send_left_ref,
    send_right_ref,
    keep_left_ref,
    keep_right_ref,
    r_ref,
    n_ref,
    total_ref,
):
    groups, _, double, _ = pieces_ref.shape
    rows = double // 2
    step = pl.program_id(0)

    @pl.when(step == 0)
    def _():
        for group in range(groups):
            inverse = (1.0 / student_temp) / jnp.sum(pieces_ref[table_ref[3, group]], axis=0)
            for k in range(rows):
                lanes = slice((group * rows + k) * LANES, (group * rows + k + 1) * LANES)
                r_ref[:, lanes] = inverse[k : k + 1, :]
                n_ref[:, lanes] = inverse[rows + k : rows + k + 1, :]

    both = lambda first, second: jnp.concatenate([first, second], axis=0)
    tw = both(directions(tw_first_ref[...]), directions(tw_second_ref[...]))
    sw = both(directions(sw_first_ref[...]), directions(sw_second_ref[...]))
    scale = both(first_scale_ref[0], second_scale_ref[0])
    columns = [to_column(scale[k : k + 1, :]) for k in range(scale.shape[0])]
    col_scale = jnp.concatenate(columns, axis=0)[:, 0:1]

    def logits_of(part):
        return nt_dot(tw, units_ref[part, :D]), nt_dot(sw, units_ref[part, D:])

    parts = [slice(c, c + WIDE) for c in range(0, units_ref.shape[0], WIDE)]
    logits = logits_of(parts[0])
    for i, part in enumerate(parts):
        following = logits_of(parts[i + 1]) if i + 1 < len(parts) else None
        targets = jnp.exp2(logits[0] * teacher_power) * (r_ref[:, part] * col_scale)
        probs = jnp.exp2(logits[1] * student_power) * n_ref[:, part]
        added = jnp.dot(
            (probs - targets).astype(bf16), units_ref[part, D:], preferred_element_type=f32
        )
        total_ref[...] = added if i == 0 else total_ref[...] + added
        logits = following

    block = tw_first_ref.shape[0]
    for which in range(2):
        rows_here = slice(which * block, (which + 1) * block)
        for row, columns_here, sent_ref, kept_ref in (
            (1, slice(0, D // 2), send_left_ref, keep_left_ref),
            (2, slice(D // 2, D), send_right_ref, keep_right_ref),
        ):
            place = table_ref[row, 2 * step + which]

            @pl.when(place < 4)
            def _():
                sent_ref[jnp.minimum(place, 3)] = total_ref[rows_here, columns_here]

            @pl.when(place >= 4)
            def _():
                kept_ref[jnp.maximum(place - 4, 0)] = total_ref[rows_here, columns_here]


def proto_gradient(y, z, units_all, pieces, teacher_protos, student_protos, scale, share):
    tokens = units_all.shape[0]
    block = 256
    blocks = share // block
    way = jnp.where(z % 2 == 1, 1, -1)
    source = y * blocks + (z + way * jnp.arange(blocks) + blocks) % blocks
    owners = (y - jnp.arange(blocks) + blocks) % pieces.shape[0]
    table = jnp.stack([source, jnp.array(LEFT_PLACE), jnp.array(RIGHT_PLACE), owners])
    table = table.astype(jnp.int32)
    whole = lambda *shape: pl.BlockSpec(shape, lambda i, p: (0,) * len(shape))
    first = pl.BlockSpec((block, D), lambda i, p: (p[0, 2 * i], 0))
    second = pl.BlockSpec((block, D), lambda i, p: (p[0, 2 * i + 1], 0))
    direct = pl.BlockSpec(memory_space=pltpu.VMEM)
    scale = scale.reshape(-1, block // LANES, LANES)
    return pl.pallas_call(
        proto_body,
        grid_spec=pltpu.PrefetchScalarGridSpec(
            num_scalar_prefetch=1,
            grid=(blocks // 2,),
            in_specs=[
                whole(tokens, 2 * D),
                whole(*pieces.shape),
                first,
                second,
                first,
                second,
                pl.BlockSpec((1, block // LANES, LANES), lambda i, p: (p[0, 2 * i], 0, 0)),
                pl.BlockSpec((1, block // LANES, LANES), lambda i, p: (p[0, 2 * i + 1], 0, 0)),
            ],
            out_specs=[direct] * 4,
            scratch_shapes=[
                pltpu.VMEM((1, tokens), f32),
                pltpu.VMEM((1, tokens), f32),
                pltpu.VMEM((2 * block, D), f32),
            ],
        ),
        out_shape=[pltpu.VMEM((blocks // 2, block, D // 2), f32)] * 4,
        compiler_params=params(24),
        cost_estimate=work(8 * tokens * share * D, 8 * 2**20, 2 * tokens * share),
        name="proto_gradient",
    )(
        table,
        in_hbm(units_all),
        pieces,
        in_hbm(teacher_protos),
        in_hbm(teacher_protos),
        in_hbm(student_protos),
        in_hbm(student_protos),
        scale,
        scale,
    )


def feature_body(
    place_ref, energy_ref, student_ref, pieces_ref, sw_ref, scale_ref, out_ref, s_ref, r_ref, n_ref, total_ref
):
    step = pl.program_id(0)

    @pl.when(step == 0)
    def _():
        s_ref[...] = student_ref[...].astype(bf16)
        inverse = (1.0 / student_temp) / jnp.sum(pieces_ref[0], axis=0)
        rows = inverse.shape[0] // 2
        fill_columns(inverse[:rows], r_ref)
        fill_columns(inverse[rows:], n_ref)
        total_ref[...] = jnp.zeros_like(total_ref)

    weights = directions(sw_ref[...])
    part_of = lambda part: weights[part * WIDE : (part + 1) * WIDE, :]
    parts = weights.shape[0] // WIDE
    logits = nt_dot(s_ref[...], part_of(0))
    grads = []
    for part in range(parts):
        following = nt_dot(s_ref[...], part_of(part + 1)) if part + 1 < parts else None
        for j in range(WIDE // LANES):
            tile = part * (WIDE // LANES) + j
            probs = jnp.exp2(logits[:, j * LANES : (j + 1) * LANES] * student_power) * n_ref[...]
            targets = energy_ref[tile].astype(f32) * r_ref[...] * scale_ref[tile : tile + 1, :]
            grads.append((probs - targets).astype(bf16))
        logits = following
    logit_grad = jnp.concatenate(grads, axis=1)
    total_ref[...] += jnp.dot(logit_grad, weights, preferred_element_type=f32)

    @pl.when(step == pl.num_programs(0) - 1)
    def _():
        out_ref[...] = total_ref[...].reshape(out_ref.shape)


def feature_gradient(place, energy, units, pieces, protos, scale, copies):
    tiles, tokens, _ = energy.shape
    block = 1024
    steps = block // LANES
    whole = lambda *shape: pl.BlockSpec(shape, lambda i, p: (0,) * len(shape))
    return pl.pallas_call(
        feature_body,
        grid_spec=pltpu.PrefetchScalarGridSpec(
            num_scalar_prefetch=1,
            grid=(tiles // steps,),
            in_specs=[
                pl.BlockSpec((steps, tokens, LANES), lambda i, p: (i, 0, 0)),
                right(tokens),
                pl.BlockSpec((1,) + pieces.shape[1:], lambda i, p: (p[0], 0, 0, 0)),
                pl.BlockSpec((block, D), lambda i, p: (i, 0)),
                pl.BlockSpec((steps, LANES), lambda i, p: (i, 0)),
            ],
            out_specs=whole(copies, tokens // copies, D),
            scratch_shapes=[
                pltpu.VMEM((tokens, D), bf16),
                pltpu.VMEM((tokens, LANES), f32),
                pltpu.VMEM((tokens, LANES), f32),
                pltpu.VMEM((tokens, D), f32),
            ],
        ),
        out_shape=jax.ShapeDtypeStruct((copies, tokens // copies, D), f32),
        compiler_params=params(32),
        cost_estimate=work(8 * energy.size * D, 16 * 2**20, energy.size),
        name="feature_gradient",
    )(place, in_hbm(energy), in_hbm(units), pieces, in_hbm(protos), scale)


def project(total, unit, length):
    return (total - unit * jnp.sum(unit * total, axis=-1, keepdims=True)) / length


def student_end_body(place_ref, pieces_ref, unit_ref, length_ref, out_ref):
    result = project(jnp.sum(pieces_ref[...], axis=0), unit_ref[...], length_ref[...])
    for copy in range(out_ref.shape[0]):
        out_ref[copy] = result


def student_end(place, pieces, units, length):
    copies, rows, _ = pieces.shape
    return pl.pallas_call(
        student_end_body,
        grid_spec=pltpu.PrefetchScalarGridSpec(
            num_scalar_prefetch=1,
            grid=(1,),
            in_specs=[
                pl.BlockSpec(pieces.shape, lambda i, p: (0, 0, 0)),
                pl.BlockSpec((rows, D), lambda i, p: (p[2], 1)),
                pl.BlockSpec((rows, 1), lambda i, p: (p[2], 0)),
            ],
            out_specs=pl.BlockSpec(pieces.shape, lambda i, p: (0, 0, 0)),
        ),
        out_shape=jax.ShapeDtypeStruct(pieces.shape, f32),
        compiler_params=params(8),
        name="student_end",
    )(place, pieces, in_hbm(units), in_hbm(length))


def proto_end_body(place_ref, *refs):
    piece_refs, (protos_ref, out_ref) = refs[:-2], refs[-2:]
    unit, length = unit_rows(protos_ref[...].astype(f32))
    half = len(piece_refs) // 2
    sums = []
    for group in (piece_refs[:half], piece_refs[half:]):
        total = group[0][...]
        for ref in group[1:]:
            total = total + ref[...]
        sums.append(total)
    out_ref[...] = project(jnp.concatenate(sums, axis=1), unit, length)


def proto_end(place, pieces, protos):
    rows, width = pieces[0].shape
    return pl.pallas_call(
        proto_end_body,
        grid_spec=pltpu.PrefetchScalarGridSpec(
            num_scalar_prefetch=1,
            grid=(1,),
            in_specs=[pl.BlockSpec((rows, width), lambda i, p: (0, 0))] * len(pieces)
            + [pl.BlockSpec((rows, D), lambda i, p: (p[1], 0))],
            out_specs=pl.BlockSpec((rows, D), lambda i, p: (0, 0)),
        ),
        out_shape=jax.ShapeDtypeStruct((rows, D), f32),
        compiler_params=params(8),
        name="proto_end",
    )(place, *pieces, in_hbm(protos))


def direct_sum(value, axis):
    n = lax.axis_size(axis)
    total = value
    for step in range(1, n):
        total = total + lax.ppermute(value, axis, [(i, (i + step) % n) for i in range(n)])
    return total


def on_device(teacher_patches, student_patches, mask_order, teacher_protos, student_protos):
    y_size, z_size = lax.axis_size("y"), lax.axis_size("z")
    proto_size = lax.axis_size("x") * lax.axis_size("core")
    y, z = lax.axis_index("y"), lax.axis_index("z")
    core = lax.axis_index("core")
    place = jnp.stack([y, y * z_size + z, lax.axis_index(PROTOS), core]).astype(jnp.int32)

    units, student_length, mine = select_tokens(
        place, teacher_patches, student_patches, mask_order
    )
    from_y = lambda value, step: lax.ppermute(
        value, "y", [(i, (i + step) % y_size) for i in range(y_size)]
    )
    from_core = lambda value: lax.ppermute(value, "core", [(0, 1), (1, 0)])

    energy, sums = energy_of(units, teacher_protos)
    norm_part = student_sums(units, student_protos)
    for sweep in range(ITERS):
        last = sweep == ITERS - 1
        if sweep > 0:
            sums = column_sums(energy, pieces)
        sums = direct_sum(sums, "y")
        if sweep == 0:
            sums, mine = lax.optimization_barrier((sums, mine))
            got_first, got_third = from_y(mine, 1), from_y(mine, 3)
        elif sweep == 1:
            sums, mine, got_first, got_third = lax.optimization_barrier(
                (sums, mine, got_first, got_third)
            )
            got_second = from_y(mine, 2)
            other_first, other_third = from_core(got_first), from_core(got_third)
        else:
            sums, got_second = lax.optimization_barrier((sums, got_second))
            other_second = from_core(got_second)
        sums = spread(jnp.broadcast_to(sums, (z_size,) + sums.shape), "z")
        col_scale, row_part = row_sums(energy, sums, 1 if last else proto_size)
        if not last:
            pieces = spread(row_part, PROTOS)
        if sweep == 0:
            pieces, got_first, got_third = lax.optimization_barrier((pieces, got_first, got_third))
        elif sweep == 1:
            pieces, got_second, other_first, other_third = lax.optimization_barrier(
                (pieces, got_second, other_first, other_third)
            )
    row_part, other_second = lax.optimization_barrier((row_part, other_second))
    units_cast = cast_units(
        place, units, [got_first, got_second, got_third], [other_first, other_second, other_third]
    )
    both = jnp.concatenate([row_part[0], norm_part], axis=0)
    peers = y_size * proto_size
    both = jnp.broadcast_to(both, (peers,) + both.shape)
    pieces = spread(both, ("y",) + PROTOS).reshape((y_size, proto_size) + both.shape[1:])

    share = teacher_protos.shape[0] // y_size
    send_left, send_right, keep_left, keep_right = proto_gradient(
        y, z, units_cast, pieces, teacher_protos, student_protos, col_scale, share
    )
    keep_left, col_scale = lax.optimization_barrier((keep_left, col_scale))
    left = collect(send_left, keep_left, 0)
    right_half = collect(send_right, keep_right, 1)
    feature_part = feature_gradient(
        place, energy, units, pieces, student_protos, col_scale, proto_size
    )
    feature_part, left, right_half = lax.optimization_barrier((feature_part, left, right_half))
    left, right_half = deliver(left, 0), deliver(right_half, 1)
    feature_pieces = spread(feature_part, PROTOS)
    feature_pieces, left, right_half = lax.optimization_barrier((feature_pieces, left, right_half))
    result = spread(student_end(place, feature_pieces, units, student_length), PROTOS)
    grad_protos = proto_end(place, left + right_half, student_protos)
    return (result.reshape(-1, MASKED, D), grad_protos)


def solution(mesh):
    fine = Mesh(mesh.devices.reshape(4, 8, 4, 2), ("y", "z", "x", "core"))
    return jax.shard_map(
        on_device,
        mesh=fine,
        in_specs=(
            P(ROWS, None, None),
            P(ROWS, None, None),
            P(ROWS, None),
            P(PROTOS, None),
            P(PROTOS, None),
        ),
        out_specs=(P(ROWS, None, None), P(PROTOS + ROWS, None)),
        check_vma=False,
    )
```

time: 798 us -> 210 us (0.26)
  blocking collectives: 460 us -> 52.4 us
  waiting for transfers between devices: 207 us -> 43.1 us
  other arithmetic: 69.4 us -> 0.26 us
  Pallas kernels: 0 us -> 60.3 us
  starting transfers between devices: 0.3 us -> 46.5 us
  matrix products: 28.9 us -> 0 us
  between operations: 15.7 us -> 0.85 us
    psum x6 -> x0, blocking collectives: 460 us -> none  [the longest x3 339 us: column_scale(): return 1.0 / lax.psum(jnp.sum(energy * row_scale[:, None], axis=0), 'rows')]
    reduce_scatter x1 -> x0, waiting for transfers between devices: 166 us -> none  [on_device(): lax.psum_scatter(lax.dot_general(logit_grad, student_cast, (((0,), (0,)),...]
    pallas_call x0 -> x13, Pallas kernels: none -> 60.3 us  [the longest x1 12.4 us: proto_gradient(): pl.pallas_call(proto_body, grid_spec=pltpu.PrefetchScalarGridSpec(num_sca...]
    all_to_all x0 -> x4, blocking collectives: none -> 52.4 us  [spread(): return lax.all_to_all(value, axes, 0, 0, tiled=True)]
    reduce_sum x10 -> x0, other arithmetic: 45.8 us -> none  [the longest x3 22 us: on_device(): row_part = jnp.sum(energy * col_scale[None, :], axis=1)]
    psum x1 -> x0, waiting for transfers between devices: 40.4 us -> none  [on_device(): lax.psum(jnp.dot(logit_grad, student_wcast, preferred_element_type=jnp.fl...]
    ppermute x0 -> x23, starting transfers between devices: none -> 29.1 us  [the longest x9 12.5 us: direct_sum(): lax.ppermute(value, axis, [(i, (i + step) % n) for i in range(n)])]
    dot_general x4 -> x0, matrix products: 28.9 us -> none  [the longest x1 9.36 us: on_device(): jnp.dot(teacher_cast, teacher_wcast.T, preferred_element_type=jnp.float32)]
  transfers between devices with their start and end apart: 2 -> 27, of which waited for: 2 -> 17; matrix products, arithmetic and copies ran while one was open for 2% -> 0% of each run, Pallas kernels for 0% -> 15%
where the time goes in v1:
time: 210 us; the launch traced here: 209 us
  Pallas kernels  60.3 us (29%)
  blocking collectives  52.4 us (25%)
  starting transfers between devices  46.5 us (22%)
  waiting for transfers between devices  43.1 us (21%)
  local copies, waits for them, and re-layouts  5.61 us (3%)
    all_to_all x4, blocking collectives, spread(): return lax.all_to_all(value, axes, 0, 0, tiled=True)  52.4 us
    all_to_all x4, waiting for transfers between devices, spread(): return lax.all_to_all(value, axes, 0, 0, tiled=True)  18.1 us
    all_to_all x4, starting transfers between devices, spread(): return lax.all_to_all(value, axes, 0, 0, tiled=True)  17.4 us
    ppermute x6, waiting for transfers between devices, deliver(): lax.ppermute(parts[k], 'z', [(z, (z + way[z] * k) % n) for z in range(n)])  15.9 us
    ppermute x9, starting transfers between devices, direct_sum(): lax.ppermute(value, axis, [(i, (i + step) % n) for i in range(n)])  12.5 us
    pallas_call x1, Pallas kernels, proto_gradient(): pl.pallas_call(proto_body, grid_spec=pltpu.PrefetchScalarGridSpec(num_sca...  12.4 us
    pallas_call x1, Pallas kernels, feature_gradient(): pl.pallas_call(feature_body, grid_spec=pltpu.PrefetchScalarGridSpec(num_s...  12.3 us
    ppermute x6, starting transfers between devices, deliver(): lax.ppermute(parts[k], 'z', [(z, (z + way[z] * k) % n) for z in range(n)])  7.58 us
  transfers between devices with their start and end apart: 27, of which 17 were waited for; matrix products, arithmetic and copies ran while one was open for 0% of the time, Pallas kernels for 15%

profile of v1, /device:TPU:1, one launch (start us, length us, event | category | flops | bytes accessed | tf_op | source)
XLA Modules:
  0.0 208.9 jit_solution(10689477988155347719)
XLA Ops:
  0.7 3.0 %select.31 = (f32[512,512]{1,0:T(8,128)}, f32[512,1]{1,0:T(8,128)}, f32[512,256]{1,0:T(8,128)}) custom-call(s32[4]{0:T(128)S(1)} %pad_add_fusion.1.place_ref, bf16[4,256,256]{2,1,0:T(8,128)(2,1)} %teacher_ref.1, bf16[4,256,256]{2,1,0:T(8,128)(2,1)} %student_ref.1, s32[4,256]{1,0:T(4,128)} %order_ref.1), custom_call_target="tpu_custom_call" | custom-call | tf_op jit(solution)/shard_map/select/pallas_call | solution.py:98
  3.7 6.1 %energy.1 = (bf16[64,512,128]{2,1,0:T(8,128)(2,1)S(1)}, f32[64,128]{1,0:T(8,128)S(1)}) custom-call(f32[512,512]{1,0:T(8,128)} %get-tuple-element.52.units_ref.student_ref.unit_ref, bf16[8192,256]{1,0:T(8,128)(2,1)} %tw_second_ref.1), custom_call_target="tpu_custom_call" | custom-call | flops 4294967296 | bytes 8388608 | tf_op jit(solution)/shard_map/energy/pallas_call | solution.py:188
  20.5 17.4 %all_to_all.40.pieces_ref = f32[8,64,128]{2,1,0:T(8,128)S(1)} all-to-all(f32[8,64,128]{2,1,0:T(8,128)S(1)} %broadcast_in_dim.12), channel_id=1, replica_groups=mesh['y'=4,'z'=8,'x'=4,'core'=2] {'z'}, dimensions={0} | all-to-all | bytes 524288 | tf_op jit(solution)/shard_map/all_to_all | solution.py:34
  40.5 12.8 %all_to_all.41.pieces_ref = f32[8,4,128]{2,1,0:T(4,128)S(1)} all-to-all(f32[8,4,128]{2,1,0:T(4,128)S(1)} %get-tuple-element.57), channel_id=1, replica_groups=mesh['y'=4,'z'=8,'x'=4,'core'=2] {'x','core'}, dimensions={0} | all-to-all | bytes 32768 | tf_op jit(solution)/shard_map/all_to_all | solution.py:34
  53.3 2.7 %column_sums.2 = f32[64,128]{1,0:T(8,128)S(1)} custom-call(bf16[64,512,128]{2,1,0:T(8,128)(2,1)S(1)} %get-tuple-element.53.energy_ref, f32[8,4,128]{2,1,0:T(4,128)S(1)} %all_to_all.41.pieces_ref), custom_call_target="tpu_custom_call" | custom-call | flops 8388608 | tf_op jit(solution)/shard_map/column_sums/pallas_call | solution.py:307
  65.3 14.8 %all_to_all.42.pieces_ref = f32[8,64,128]{2,1,0:T(8,128)S(1)} all-to-all(f32[8,64,128]{2,1,0:T(8,128)S(1)} %broadcast_in_dim.13), channel_id=1, replica_groups=mesh['y'=4,'z'=8,'x'=4,'core'=2] {'z'}, dimensions={0} | all-to-all | bytes 524288 | tf_op jit(solution)/shard_map/all_to_all | solution.py:34
  82.7 7.4 %all_to_all.43.pieces_ref = f32[8,4,128]{2,1,0:T(4,128)S(1)} all-to-all(f32[8,4,128]{2,1,0:T(4,128)S(1)} %get-tuple-element.63), channel_id=1, replica_groups=mesh['y'=4,'z'=8,'x'=4,'core'=2] {'x','core'}, dimensions={0} | all-to-all | bytes 32768 | tf_op jit(solution)/shard_map/all_to_all | solution.py:34
  90.2 2.7 %column_sums.3 = f32[64,128]{1,0:T(8,128)S(1)} custom-call(bf16[64,512,128]{2,1,0:T(8,128)(2,1)S(1)} %get-tuple-element.53.energy_ref, f32[8,4,128]{2,1,0:T(4,128)S(1)} %all_to_all.43.pieces_ref), custom_call_target="tpu_custom_call" | custom-call | flops 8388608 | tf_op jit(solution)/shard_map/column_sums/pallas_call | solution.py:307
  102.3 3.4 %all-to-all-start.4 = ((f32[8,64,128]{2,1,0:T(8,128)}), f32[8,64,128]{2,1,0:T(8,128)S(1)}, u32[]{:S(2)}, u32[]{:S(2)}) async-start(f32[8,64,128]{2,1,0:T(8,128)} %broadcast_in_dim.14), calls=%async_computation.4 | async-start | bytes 524288 | tf_op jit(solution)/shard_map/all_to_all | solution.py:34
  105.8 6.1 %student.1 = f32[4,128]{1,0:T(4,128)S(1)} custom-call(f32[512,512]{1,0:T(8,128)} %get-tuple-element.52.units_ref.student_ref.unit_ref, bf16[8192,256]{1,0:T(8,128)(2,1)} %refs_8_.1), custom_call_target="tpu_custom_call" | custom-call | flops 4294967296 | bytes 8388608 | tf_op jit(solution)/shard_map/student/pallas_call | solution.py:239
  111.9 6.2 %all-to-all-done.4.pieces_ref = f32[8,64,128]{2,1,0:T(8,128)S(1)} async-done(((f32[8,64,128]{2,1,0:T(8,128)}), f32[8,64,128]{2,1,0:T(8,128)S(1)}, u32[]{:S(2)}, u32[]{:S(2)}) %all-to-all-start.4) | async-done | bytes 262176 | tf_op jit(solution)/shard_map/all_to_all | solution.py:34
  118.1 3.4 %copy-done.1 = bf16[64,512,128]{2,1,0:T(8,128)(2,1)S(1)} copy-done((bf16[64,512,128]{2,1,0:T(8,128)(2,1)S(1)}, bf16[64,512,128]{2,1,0:T(8,128)(2,1)}, u32[]{:S(2)}) %copy-start.1) | copy-done | bytes 8388632
  124.3 4.4 %all-to-all-start.5 = ((f32[32,8,128]{2,1,0:T(8,128)}), f32[32,8,128]{2,1,0:T(8,128)S(1)}, u32[]{:S(2)}, u32[]{:S(2)}) async-start(f32[32,8,128]{2,1,0:T(8,128)} %broadcast_in_dim.15), calls=%async_computation.5 | async-start | bytes 262144 | tf_op jit(solution)/shard_map/all_to_all | solution.py:34
  128.8 2.8 %cast.1.units_ref = bf16[2048,512]{1,0:T(8,128)(2,1)} custom-call(s32[4]{0:T(128)S(1)} %pad_add_fusion.1.place_ref, f32[512,512]{1,0:T(8,128)} %get-tuple-element.52.units_ref.student_ref.unit_ref, f32[512,256]{1,0:T(8,128)S(1)} %collective-permute-done.3.refs_0_, f32[512,256]{1,0:T(8,128)S(1)} %collective-permute-done.8.refs_1_, ...), custom_call_target="tpu_custom_call" | custom-call | bytes 6291456 | tf_op jit(solution)/shard_map/cast/pallas_call | solution.py:357
  131.6 4.8 %all-to-all-done.5 = f32[32,8,128]{2,1,0:T(8,128)S(1)} async-done(((f32[32,8,128]{2,1,0:T(8,128)}), f32[32,8,128]{2,1,0:T(8,128)S(1)}, u32[]{:S(2)}, u32[]{:S(2)}) %all-to-all-start.5) | async-done | bytes 131104 | tf_op jit(solution)/shard_map/all_to_all | solution.py:34
  136.4 12.4 %proto_gradient.1 = (f32[4,256,128]{2,1,0:T(8,128)S(1)}, f32[4,256,128]{2,1,0:T(8,128)S(1)}, f32[4,256,128]{2,1,0:T(8,128)S(1)}, f32[4,256,128]{2,1,0:T(8,128)S(1)}) custom-call(s32[4,8]{1,0:T(4,128)S(1)} %pad_add_fusion.table_ref, bf16[2048,512]{1,0:T(8,128)(2,1)} %cast.1.units_ref, f32[4,8,8,128]{3,2,1,0:T(8,128)S(1)} %bitcast.24, ...), custom_call_target="tpu_custom_call" | custom-call | flops 8589934592 | bytes 8388608 | tf_op jit(solution)/shard_map/proto_gradient/pallas_call | solution.py:453
  149.2 12.3 %feature_gradient.1 = f32[8,64,256]{2,1,0:T(8,128)} custom-call(s32[4]{0:T(128)S(1)} %pad_add_fusion.1.place_ref, bf16[64,512,128]{2,1,0:T(8,128)(2,1)} %copy-done, f32[512,512]{1,0:T(8,128)} %get-tuple-element.52.units_ref.student_ref.unit_ref, f32[4,8,8,128]{3,2,1,0:T(8,128)S(1)} %bitcast.25, bf16[8192,256]{1,0:T(8,128)(2,1)} %refs_8_.1, ...), custom_call_target="tpu_custom_call" | custom-call | flops 8589934592 | bytes 16777216 | tf_op jit(solution)/shard_map/feature_gradient/pallas_call | solution.py:532
  163.3 4.6 %all-to-all-start.6 = ((f32[8,64,256]{2,1,0:T(8,128)}), f32[8,64,256]{2,1,0:T(8,128)S(1)}, u32[]{:S(2)}, u32[]{:S(2)}) async-start(f32[8,64,256]{2,1,0:T(8,128)} %feature_gradient.1), calls=%async_computation.6 | async-start | bytes 1048576 | tf_op jit(solution)/shard_map/all_to_all | solution.py:34
  169.5 3.2 %collective-permute-start.19 = (f32[256,128]{1,0:T(8,128)S(1)}, f32[256,128]{1,0:T(8,128)S(1)}, u32[]{:S(2)}, u32[]{:S(2)}) collective-permute-start(f32[256,128]{1,0:T(8,128)S(1)} %get-tuple-element.87), channel_id=1, source_target_pairs={{0,40},{8,32},{16,56},{24,48},{32,8},{40,0},{48,24},{56,16},{1,41}... | collective-permute-start | bytes 393224 | tf_op jit(solution)/shard_map/ppermute | solution.py:334
  176.2 4.7 %collective-permute-done.19.refs_3_ = f32[256,128]{1,0:T(8,128)S(1)} collective-permute-done((f32[256,128]{1,0:T(8,128)S(1)}, f32[256,128]{1,0:T(8,128)S(1)}, u32[]{:S(2)}, u32[]{:S(2)}) %collective-permute-start.19) | collective-permute-done | bytes 131104 | tf_op jit(solution)/shard_map/ppermute | solution.py:334
  181.3 4.5 %collective-permute-done.21.refs_6_ = f32[256,128]{1,0:T(8,128)S(1)} collective-permute-done((f32[256,128]{1,0:T(8,128)S(1)}, f32[256,128]{1,0:T(8,128)S(1)}, u32[]{:S(2)}, u32[]{:S(2)}) %collective-permute-start.21) | collective-permute-done | bytes 131104 | tf_op jit(solution)/shard_map/ppermute | solution.py:334
  185.7 5.7 %collective-permute-done.22.refs_7_ = f32[256,128]{1,0:T(8,128)S(1)} collective-permute-done((f32[256,128]{1,0:T(8,128)S(1)}, f32[256,128]{1,0:T(8,128)S(1)}, u32[]{:S(2)}, u32[]{:S(2)}) %collective-permute-start.22) | collective-permute-done | bytes 131104 | tf_op jit(solution)/shard_map/ppermute | solution.py:334
  193.8 4.9 %all-to-all-start.7 = ((f32[8,64,256]{2,1,0:T(8,128)}), f32[8,64,256]{2,1,0:T(8,128)S(1)}, u32[]{:S(2)}, u32[]{:S(2)}) async-start(f32[8,64,256]{2,1,0:T(8,128)} %student_end.1), calls=%async_computation.7 | async-start | bytes 1048576 | tf_op jit(solution)/shard_map/all_to_all | solution.py:34
  201.1 7.1 %all-to-all-done.7 = f32[8,64,256]{2,1,0:T(8,128)S(1)} async-done(((f32[8,64,256]{2,1,0:T(8,128)}), f32[8,64,256]{2,1,0:T(8,128)S(1)}, u32[]{:S(2)}, u32[]{:S(2)}) %all-to-all-start.7) | async-done | bytes 524320 | tf_op jit(solution)/shard_map/all_to_all | solution.py:34
  (71 shorter events, 50.8 us)
Async XLA Ops:
  9.8 5.9 %collective-permute-start = (f32[64,128]{1,0:T(8,128)S(1)}, f32[64,128]{1,0:T(8,128)S(1)}, u32[]{:S(2)}, u32[]{:S(2)}) collective-permute-start(f32[64,128]{1,0:T(8,128)S(1)} %get-tuple-element.54), channel_id=1, source_target_pairs={{0,64},{64,128},{128,192},{192,0},{1,65},{65,129},{129,193},{193,1... | collective-permute-start | bytes 98312 | tf_op jit(solution)/shard_map/ppermute | solution.py:623
  12.0 4.3 %collective-permute-start.1 = (f32[64,128]{1,0:T(8,128)S(1)}, f32[64,128]{1,0:T(8,128)S(1)}, u32[]{:S(2)}, u32[]{:S(2)}) collective-permute-start(f32[64,128]{1,0:T(8,128)S(1)} %get-tuple-element.54), channel_id=1, source_target_pairs={{0,128},{64,192},{128,0},{192,64},{1,129},{65,193},{129,1},{193,65... | collective-permute-start | bytes 98312 | tf_op jit(solution)/shard_map/ppermute | solution.py:623
  17.7 35.6 %collective-permute-start.3 = (f32[512,256]{1,0:T(8,128)S(1)}, f32[512,256]{1,0:T(8,128)S(1)}, u32[]{:S(2)}, u32[]{:S(2)}) collective-permute-start(f32[512,256]{1,0:T(8,128)S(1)} %copy-done.4), channel_id=1, source_target_pairs={{0,64},{64,128},{128,192},{192,0},{1,65},{65,129},{129,193},{193,1... | collective-permute-start | bytes 1572872 | tf_op jit(solution)/shard_map/ppermute | solution.py:637
  17.8 35.5 %collective-permute-start.4 = (f32[512,256]{1,0:T(8,128)S(1)}, f32[512,256]{1,0:T(8,128)S(1)}, u32[]{:S(2)}, u32[]{:S(2)}) collective-permute-start(f32[512,256]{1,0:T(8,128)S(1)} %copy-done.4), channel_id=1, source_target_pairs={{0,192},{64,0},{128,64},{192,128},{1,193},{65,1},{129,65},{193,129... | collective-permute-start | bytes 1572872 | tf_op jit(solution)/shard_map/ppermute | solution.py:637
  56.0 4.1 %collective-permute-start.5 = (f32[64,128]{1,0:T(8,128)S(1)}, f32[64,128]{1,0:T(8,128)S(1)}, u32[]{:S(2)}, u32[]{:S(2)}) collective-permute-start(f32[64,128]{1,0:T(8,128)S(1)} %column_sums.2), channel_id=1, source_target_pairs={{0,64},{64,128},{128,192},{192,0},{1,65},{65,129},{129,193},{193,1... | collective-permute-start | bytes 98312 | tf_op jit(solution)/shard_map/ppermute | solution.py:623
  56.1 4.4 %collective-permute-start.6 = (f32[64,128]{1,0:T(8,128)S(1)}, f32[64,128]{1,0:T(8,128)S(1)}, u32[]{:S(2)}, u32[]{:S(2)}) collective-permute-start(f32[64,128]{1,0:T(8,128)S(1)} %column_sums.2), channel_id=1, source_target_pairs={{0,128},{64,192},{128,0},{192,64},{1,129},{65,193},{129,1},{193,65... | collective-permute-start | bytes 98312 | tf_op jit(solution)/shard_map/ppermute | solution.py:623
  61.4 28.7 %collective-permute-start.10 = (f32[512,256]{1,0:T(8,128)S(1)}, f32[512,256]{1,0:T(8,128)S(1)}, u32[]{:S(2)}, u32[]{:S(2)}) collective-permute-start(f32[512,256]{1,0:T(8,128)S(1)} %collective-permute-done.4.refs_2_), channel_id=1, source_target_pairs={{0,1},{1,0},{2,3},{3,2},{4,5},{5,4},{6,7},{7,6},{8,9},{9,8},{10,11... | collective-permute-start | bytes 1572872 | tf_op jit(solution)/shard_map/ppermute | solution.py:640
  63.6 26.5 %collective-permute-start.8 = (f32[512,256]{1,0:T(8,128)S(1)}, f32[512,256]{1,0:T(8,128)S(1)}, u32[]{:S(2)}, u32[]{:S(2)}) collective-permute-start(f32[512,256]{1,0:T(8,128)S(1)} %copy-done.4), channel_id=1, source_target_pairs={{0,128},{64,192},{128,0},{192,64},{1,129},{65,193},{129,1},{193,65... | collective-permute-start | bytes 1572872 | tf_op jit(solution)/shard_map/ppermute | solution.py:637
  64.9 25.3 %collective-permute-start.9 = (f32[512,256]{1,0:T(8,128)S(1)}, f32[512,256]{1,0:T(8,128)S(1)}, u32[]{:S(2)}, u32[]{:S(2)}) collective-permute-start(f32[512,256]{1,0:T(8,128)S(1)} %collective-permute-done.3.refs_0_), channel_id=1, source_target_pairs={{0,1},{1,0},{2,3},{3,2},{4,5},{5,4},{6,7},{7,6},{8,9},{9,8},{10,11... | collective-permute-start | bytes 1572872 | tf_op jit(solution)/shard_map/ppermute | solution.py:640
  92.9 4.1 %collective-permute-start.11 = (f32[64,128]{1,0:T(8,128)S(1)}, f32[64,128]{1,0:T(8,128)S(1)}, u32[]{:S(2)}, u32[]{:S(2)}) collective-permute-start(f32[64,128]{1,0:T(8,128)S(1)} %column_sums.3), channel_id=1, source_target_pairs={{0,64},{64,128},{128,192},{192,0},{1,65},{65,129},{129,193},{193,1... | collective-permute-start | bytes 98312 | tf_op jit(solution)/shard_map/ppermute | solution.py:623
  94.2 4.3 %collective-permute-start.12 = (f32[64,128]{1,0:T(8,128)S(1)}, f32[64,128]{1,0:T(8,128)S(1)}, u32[]{:S(2)}, u32[]{:S(2)}) collective-permute-start(f32[64,128]{1,0:T(8,128)S(1)} %column_sums.3), channel_id=1, source_target_pairs={{0,128},{64,192},{128,0},{192,64},{1,129},{65,193},{129,1},{193,65... | collective-permute-start | bytes 98312 | tf_op jit(solution)/shard_map/ppermute | solution.py:623
  99.6 24.0 %collective-permute-start.14 = (f32[512,256]{1,0:T(8,128)S(1)}, f32[512,256]{1,0:T(8,128)S(1)}, u32[]{:S(2)}, u32[]{:S(2)}) collective-permute-start(f32[512,256]{1,0:T(8,128)S(1)} %collective-permute-done.8.refs_1_), channel_id=1, source_target_pairs={{0,1},{1,0},{2,3},{3,2},{4,5},{5,4},{6,7},{7,6},{8,9},{9,8},{10,11... | collective-permute-start | bytes 1572872 | tf_op jit(solution)/shard_map/ppermute | solution.py:640
  102.3 15.7 %all-to-all-start.4 = ((f32[8,64,128]{2,1,0:T(8,128)}), f32[8,64,128]{2,1,0:T(8,128)S(1)}, u32[]{:S(2)}, u32[]{:S(2)}) async-start(f32[8,64,128]{2,1,0:T(8,128)} %broadcast_in_dim.14), calls=%async_computation.4 | async-start | bytes 524288 | tf_op jit(solution)/shard_map/all_to_all | solution.py:34
  124.3 12.1 %all-to-all-start.5 = ((f32[32,8,128]{2,1,0:T(8,128)}), f32[32,8,128]{2,1,0:T(8,128)S(1)}, u32[]{:S(2)}, u32[]{:S(2)}) async-start(f32[32,8,128]{2,1,0:T(8,128)} %broadcast_in_dim.15), calls=%async_computation.5 | async-start | bytes 262144 | tf_op jit(solution)/shard_map/all_to_all | solution.py:34
  148.8 14.4 %collective-permute-start.16 = (f32[4,256,128]{2,1,0:T(8,128)S(1)}, f32[4,256,128]{2,1,0:T(8,128)S(1)}, u32[]{:S(2)}, u32[]{:S(2)}) collective-permute-start(f32[4,256,128]{2,1,0:T(8,128)S(1)} %get-tuple-element.82), channel_id=1, source_target_pairs={{0,56},{8,16},{16,8},{24,32},{32,24},{40,48},{48,40},{56,0},{1,57}... | collective-permute-start | bytes 1572872 | tf_op jit(solution)/shard_map/ppermute | solution.py:326
  148.9 14.4 %collective-permute-start.15 = (f32[4,256,128]{2,1,0:T(8,128)S(1)}, f32[4,256,128]{2,1,0:T(8,128)S(1)}, u32[]{:S(2)}, u32[]{:S(2)}) collective-permute-start(f32[4,256,128]{2,1,0:T(8,128)S(1)} %get-tuple-element.80), channel_id=1, source_target_pairs={{0,8},{8,0},{16,24},{24,16},{32,40},{40,32},{48,56},{56,48},{1,9},... | collective-permute-start | bytes 1572872 | tf_op jit(solution)/shard_map/ppermute | solution.py:326
  163.3 28.2 %all-to-all-start.6 = ((f32[8,64,256]{2,1,0:T(8,128)}), f32[8,64,256]{2,1,0:T(8,128)S(1)}, u32[]{:S(2)}, u32[]{:S(2)}) async-start(f32[8,64,256]{2,1,0:T(8,128)} %feature_gradient.1), calls=%async_computation.6 | async-start | bytes 1048576 | tf_op jit(solution)/shard_map/all_to_all | solution.py:34
  167.9 6.1 %collective-permute-start.17 = (f32[256,128]{1,0:T(8,128)S(1)}, f32[256,128]{1,0:T(8,128)S(1)}, u32[]{:S(2)}, u32[]{:S(2)}) collective-permute-start(f32[256,128]{1,0:T(8,128)S(1)} %get-tuple-element.85), channel_id=1, source_target_pairs={{0,56},{8,16},{16,8},{24,32},{32,24},{40,48},{48,40},{56,0},{1,57}... | collective-permute-start | bytes 393224 | tf_op jit(solution)/shard_map/ppermute | solution.py:334
  169.3 6.9 %collective-permute-start.18 = (f32[256,128]{1,0:T(8,128)S(1)}, f32[256,128]{1,0:T(8,128)S(1)}, u32[]{:S(2)}, u32[]{:S(2)}) collective-permute-start(f32[256,128]{1,0:T(8,128)S(1)} %get-tuple-element.86), channel_id=1, source_target_pairs={{0,48},{8,24},{16,0},{24,40},{32,16},{40,56},{48,32},{56,8},{1,49}... | collective-permute-start | bytes 393224 | tf_op jit(solution)/shard_map/ppermute | solution.py:334
  169.5 11.4 %collective-permute-start.19 = (f32[256,128]{1,0:T(8,128)S(1)}, f32[256,128]{1,0:T(8,128)S(1)}, u32[]{:S(2)}, u32[]{:S(2)}) collective-permute-start(f32[256,128]{1,0:T(8,128)S(1)} %get-tuple-element.87), channel_id=1, source_target_pairs={{0,40},{8,32},{16,56},{24,48},{32,8},{40,0},{48,24},{56,16},{1,41}... | collective-permute-start | bytes 393224 | tf_op jit(solution)/shard_map/ppermute | solution.py:334
  172.7 8.6 %collective-permute-start.20 = (f32[256,128]{1,0:T(8,128)S(1)}, f32[256,128]{1,0:T(8,128)S(1)}, u32[]{:S(2)}, u32[]{:S(2)}) collective-permute-start(f32[256,128]{1,0:T(8,128)S(1)} %get-tuple-element.89), channel_id=1, source_target_pairs={{0,8},{8,0},{16,24},{24,16},{32,40},{40,32},{48,56},{56,48},{1,9},... | collective-permute-start | bytes 393224 | tf_op jit(solution)/shard_map/ppermute | solution.py:334
  172.7 13.0 %collective-permute-start.21 = (f32[256,128]{1,0:T(8,128)S(1)}, f32[256,128]{1,0:T(8,128)S(1)}, u32[]{:S(2)}, u32[]{:S(2)}) collective-permute-start(f32[256,128]{1,0:T(8,128)S(1)} %get-tuple-element.90), channel_id=1, source_target_pairs={{0,16},{8,56},{16,32},{24,8},{32,48},{40,24},{48,0},{56,40},{1,17}... | collective-permute-start | bytes 393224 | tf_op jit(solution)/shard_map/ppermute | solution.py:334
  174.0 17.4 %collective-permute-start.22 = (f32[256,128]{1,0:T(8,128)S(1)}, f32[256,128]{1,0:T(8,128)S(1)}, u32[]{:S(2)}, u32[]{:S(2)}) collective-permute-start(f32[256,128]{1,0:T(8,128)S(1)} %get-tuple-element.91), channel_id=1, source_target_pairs={{0,24},{8,48},{16,40},{24,0},{32,56},{40,16},{48,8},{56,32},{1,25}... | collective-permute-start | bytes 393224 | tf_op jit(solution)/shard_map/ppermute | solution.py:334
  193.8 14.4 %all-to-all-start.7 = ((f32[8,64,256]{2,1,0:T(8,128)}), f32[8,64,256]{2,1,0:T(8,128)S(1)}, u32[]{:S(2)}, u32[]{:S(2)}) async-start(f32[8,64,256]{2,1,0:T(8,128)} %student_end.1), calls=%async_computation.7 | async-start | bytes 1048576 | tf_op jit(solution)/shard_map/all_to_all | solution.py:34
  (8 other events, 121.8 us)

commit v2 on v1

--- a/solution.py
+++ b/solution.py
@@ -324,15 +324,22 @@
     n = lax.axis_size("z")
     way = [1 if (z + offset) % 2 else -1 for z in range(n)]
     got = lax.ppermute(send, "z", [(z, (z - way[z]) % n) for z in range(n)])
-    return [keep[k] + got[k] for k in range(4)]
-
-
-def deliver(parts, offset):
+    return keep[0] + got[0], keep[1] + got[1], keep[2:] + got[2:]
+
+
+def pass_on(sums, offset):
     n = lax.axis_size("z")
     way = [1 if (z + offset) % 2 else -1 for z in range(n)]
-    return [parts[0]] + [
-        lax.ppermute(parts[k], "z", [(z, (z + way[z] * k) % n) for z in range(n)]) for k in (1, 2, 3)
-    ]
+    own, following, far = sums
+    got = lax.ppermute(far, "z", [(z, (z + 2 * way[z]) % n) for z in range(n)])
+    return own + got[0], following + got[1]
+
+
+def deliver(sums, offset):
+    n = lax.axis_size("z")
+    way = [1 if (z + offset) % 2 else -1 for z in range(n)]
+    own, following = sums
+    return [own, lax.ppermute(following, "z", [(z, (z + way[z]) % n) for z in range(n)])]
 
 
 def cast_body(place_ref, units_ref, *refs):
@@ -688,9 +695,10 @@
         place, energy, units, pieces, student_protos, col_scale, proto_size
     )
     feature_part, left, right_half = lax.optimization_barrier((feature_part, left, right_half))
-    left, right_half = deliver(left, 0), deliver(right_half, 1)
+    left, right_half = pass_on(left, 0), pass_on(right_half, 1)
     feature_pieces = spread(feature_part, PROTOS)
     feature_pieces, left, right_half = lax.optimization_barrier((feature_pieces, left, right_half))
+    left, right_half = deliver(left, 0), deliver(right_half, 1)
     result = spread(student_end(place, feature_pieces, units, student_length), PROTOS)
     grad_protos = proto_end(place, left + right_half, student_protos)
     return (result.reshape(-1, MASKED, D), grad_protos)

time: 210 us -> 199 us (0.948)
  waiting for transfers between devices: 43.1 us -> 35.2 us
  starting transfers between devices: 46.5 us -> 43.9 us
    ppermute x6 -> x4, waiting for transfers between devices: 15.9 us -> 9.97 us  [the longest x2 5.23 us: pass_on(): got = lax.ppermute(far, 'z', [(z, (z + 2 * way[z]) % n) for z in range(n)])]
    ppermute x6 -> x4, starting transfers between devices: 7.58 us -> 5.03 us  [the longest x2 3.65 us: pass_on(): got = lax.ppermute(far, 'z', [(z, (z + 2 * way[z]) % n) for z in range(n)])]
  transfers between devices with their start and end apart: 27 -> 25, of which waited for: 17 -> 16; matrix products, arithmetic and copies ran while one was open for 0% -> 0% of each run, Pallas kernels for 15% -> 16%
where the time goes in v2:
time: 199 us
  Pallas kernels  60.3 us (30%)
  blocking collectives  52.4 us (26%)
  starting transfers between devices  43.9 us (22%)
  waiting for transfers between devices  35.2 us (18%)
  local copies, waits for them, and re-layouts  5.61 us (3%)
    all_to_all x4, blocking collectives, spread(): return lax.all_to_all(value, axes, 0, 0, tiled=True)  52.4 us
    all_to_all x4, starting transfers between devices, spread(): return lax.all_to_all(value, axes, 0, 0, tiled=True)  17.3 us
    all_to_all x4, waiting for transfers between devices, spread(): return lax.all_to_all(value, axes, 0, 0, tiled=True)  16.1 us
    ppermute x9, starting transfers between devices, direct_sum(): lax.ppermute(value, axis, [(i, (i + step) % n) for i in range(n)])  12.5 us
    pallas_call x1, Pallas kernels, proto_gradient(): pl.pallas_call(proto_body, grid_spec=pltpu.PrefetchScalarGridSpec(num_sca...  12.4 us
    pallas_call x1, Pallas kernels, feature_gradient(): pl.pallas_call(feature_body, grid_spec=pltpu.PrefetchScalarGridSpec(num_s...  12.3 us
    ppermute x9, waiting for transfers between devices, direct_sum(): lax.ppermute(value, axis, [(i, (i + step) % n) for i in range(n)])  7.45 us
    pallas_call x3, Pallas kernels, row_sums(): pl.pallas_call(row_body, in_specs=[whole] * 2, out_specs=[whole] * 2, out...  7.45 us
  transfers between devices with their start and end apart: 25, of which 16 were waited for; matrix products, arithmetic and copies ran while one was open for 0% of the time, Pallas kernels for 16%

profile of v2, /device:TPU:1, one launch (start us, length us, event | category | flops | bytes accessed | tf_op | source)
XLA Modules:
  0.0 198.6 jit_solution(5519865324159866594)
XLA Ops:
  0.7 3.0 %select.31 = (f32[512,512]{1,0:T(8,128)}, f32[512,1]{1,0:T(8,128)}, f32[512,256]{1,0:T(8,128)}) custom-call(s32[4]{0:T(128)S(1)} %pad_add_fusion.1.place_ref, bf16[4,256,256]{2,1,0:T(8,128)(2,1)} %teacher_ref.1, bf16[4,256,256]{2,1,0:T(8,128)(2,1)} %student_ref.1, s32[4,256]{1,0:T(4,128)} %order_ref.1), custom_call_target="tpu_custom_call" | custom-call | tf_op jit(solution)/shard_map/select/pallas_call | solution.py:98
  3.7 6.1 %energy.1 = (bf16[64,512,128]{2,1,0:T(8,128)(2,1)S(1)}, f32[64,128]{1,0:T(8,128)S(1)}) custom-call(f32[512,512]{1,0:T(8,128)} %get-tuple-element.46.units_ref.student_ref.unit_ref, bf16[8192,256]{1,0:T(8,128)(2,1)} %tw_second_ref.1), custom_call_target="tpu_custom_call" | custom-call | flops 4294967296 | bytes 8388608 | tf_op jit(solution)/shard_map/energy/pallas_call | solution.py:188
  17.8 2.7 %collective-permute-start.4 = (f32[512,256]{1,0:T(8,128)S(1)}, f32[512,256]{1,0:T(8,128)S(1)}, u32[]{:S(2)}, u32[]{:S(2)}) collective-permute-start(f32[512,256]{1,0:T(8,128)S(1)} %copy-done.4), channel_id=1, source_target_pairs={{0,192},{64,0},{128,64},{192,128},{1,193},{65,1},{129,65},{193,129... | collective-permute-start | bytes 1572872 | tf_op jit(solution)/shard_map/ppermute | solution.py:644
  20.5 17.4 %all_to_all.40.pieces_ref = f32[8,64,128]{2,1,0:T(8,128)S(1)} all-to-all(f32[8,64,128]{2,1,0:T(8,128)S(1)} %broadcast_in_dim.12), channel_id=1, replica_groups=mesh['y'=4,'z'=8,'x'=4,'core'=2] {'z'}, dimensions={0} | all-to-all | bytes 524288 | tf_op jit(solution)/shard_map/all_to_all | solution.py:34
  40.5 12.8 %all_to_all.41.pieces_ref = f32[8,4,128]{2,1,0:T(4,128)S(1)} all-to-all(f32[8,4,128]{2,1,0:T(4,128)S(1)} %get-tuple-element.51), channel_id=1, replica_groups=mesh['y'=4,'z'=8,'x'=4,'core'=2] {'x','core'}, dimensions={0} | all-to-all | bytes 32768 | tf_op jit(solution)/shard_map/all_to_all | solution.py:34
  53.3 2.7 %column_sums.2 = f32[64,128]{1,0:T(8,128)S(1)} custom-call(bf16[64,512,128]{2,1,0:T(8,128)(2,1)S(1)} %get-tuple-element.47.energy_ref, f32[8,4,128]{2,1,0:T(4,128)S(1)} %all_to_all.41.pieces_ref), custom_call_target="tpu_custom_call" | custom-call | flops 8388608 | tf_op jit(solution)/shard_map/column_sums/pallas_call | solution.py:307
  65.3 14.8 %all_to_all.42.pieces_ref = f32[8,64,128]{2,1,0:T(8,128)S(1)} all-to-all(f32[8,64,128]{2,1,0:T(8,128)S(1)} %broadcast_in_dim.13), channel_id=1, replica_groups=mesh['y'=4,'z'=8,'x'=4,'core'=2] {'z'}, dimensions={0} | all-to-all | bytes 524288 | tf_op jit(solution)/shard_map/all_to_all | solution.py:34
  82.7 7.4 %all_to_all.43.pieces_ref = f32[8,4,128]{2,1,0:T(4,128)S(1)} all-to-all(f32[8,4,128]{2,1,0:T(4,128)S(1)} %get-tuple-element.57), channel_id=1, replica_groups=mesh['y'=4,'z'=8,'x'=4,'core'=2] {'x','core'}, dimensions={0} | all-to-all | bytes 32768 | tf_op jit(solution)/shard_map/all_to_all | solution.py:34
  90.2 2.7 %column_sums.3 = f32[64,128]{1,0:T(8,128)S(1)} custom-call(bf16[64,512,128]{2,1,0:T(8,128)(2,1)S(1)} %get-tuple-element.47.energy_ref, f32[8,4,128]{2,1,0:T(4,128)S(1)} %all_to_all.43.pieces_ref), custom_call_target="tpu_custom_call" | custom-call | flops 8388608 | tf_op jit(solution)/shard_map/column_sums/pallas_call | solution.py:307
  102.3 3.4 %all-to-all-start.4 = ((f32[8,64,128]{2,1,0:T(8,128)}), f32[8,64,128]{2,1,0:T(8,128)S(1)}, u32[]{:S(2)}, u32[]{:S(2)}) async-start(f32[8,64,128]{2,1,0:T(8,128)} %broadcast_in_dim.14), calls=%async_computation.4 | async-start | bytes 524288 | tf_op jit(solution)/shard_map/all_to_all | solution.py:34
  105.8 6.1 %student.1 = f32[4,128]{1,0:T(4,128)S(1)} custom-call(f32[512,512]{1,0:T(8,128)} %get-tuple-element.46.units_ref.student_ref.unit_ref, bf16[8192,256]{1,0:T(8,128)(2,1)} %refs_4_.1), custom_call_target="tpu_custom_call" | custom-call | flops 4294967296 | bytes 8388608 | tf_op jit(solution)/shard_map/student/pallas_call | solution.py:239
  111.9 6.2 %all-to-all-done.4.pieces_ref = f32[8,64,128]{2,1,0:T(8,128)S(1)} async-done(((f32[8,64,128]{2,1,0:T(8,128)}), f32[8,64,128]{2,1,0:T(8,128)S(1)}, u32[]{:S(2)}, u32[]{:S(2)}) %all-to-all-start.4) | async-done | bytes 262176 | tf_op jit(solution)/shard_map/all_to_all | solution.py:34
  118.1 3.4 %copy-done.1 = bf16[64,512,128]{2,1,0:T(8,128)(2,1)S(1)} copy-done((bf16[64,512,128]{2,1,0:T(8,128)(2,1)S(1)}, bf16[64,512,128]{2,1,0:T(8,128)(2,1)}, u32[]{:S(2)}) %copy-start.1) | copy-done | bytes 8388632
  124.3 4.4 %all-to-all-start.5 = ((f32[32,8,128]{2,1,0:T(8,128)}), f32[32,8,128]{2,1,0:T(8,128)S(1)}, u32[]{:S(2)}, u32[]{:S(2)}) async-start(f32[32,8,128]{2,1,0:T(8,128)} %broadcast_in_dim.15), calls=%async_computation.5 | async-start | bytes 262144 | tf_op jit(solution)/shard_map/all_to_all | solution.py:34
  128.8 2.8 %cast.1.units_ref = bf16[2048,512]{1,0:T(8,128)(2,1)} custom-call(s32[4]{0:T(128)S(1)} %pad_add_fusion.1.place_ref, f32[512,512]{1,0:T(8,128)} %get-tuple-element.46.units_ref.student_ref.unit_ref, f32[512,256]{1,0:T(8,128)S(1)} %collective-permute-done.3.refs_0_, f32[512,256]{1,0:T(8,128)S(1)} %collective-permute-done.8.refs_1_, ...), custom_call_target="tpu_custom_call" | custom-call | bytes 6291456 | tf_op jit(solution)/shard_map/cast/pallas_call | solution.py:364
  131.6 4.8 %all-to-all-done.5 = f32[32,8,128]{2,1,0:T(8,128)S(1)} async-done(((f32[32,8,128]{2,1,0:T(8,128)}), f32[32,8,128]{2,1,0:T(8,128)S(1)}, u32[]{:S(2)}, u32[]{:S(2)}) %all-to-all-start.5) | async-done | bytes 131104 | tf_op jit(solution)/shard_map/all_to_all | solution.py:34
  136.4 12.4 %proto_gradient.1 = (f32[4,256,128]{2,1,0:T(8,128)S(1)}, f32[4,256,128]{2,1,0:T(8,128)S(1)}, f32[4,256,128]{2,1,0:T(8,128)S(1)}, f32[4,256,128]{2,1,0:T(8,128)S(1)}) custom-call(s32[4,8]{1,0:T(4,128)S(1)} %pad_add_fusion.table_ref, bf16[2048,512]{1,0:T(8,128)(2,1)} %cast.1.units_ref, f32[4,8,8,128]{3,2,1,0:T(8,128)S(1)} %bitcast.32, ...), custom_call_target="tpu_custom_call" | custom-call | flops 8589934592 | bytes 8388608 | tf_op jit(solution)/shard_map/proto_gradient/pallas_call | solution.py:460
  149.2 12.3 %feature_gradient.1 = f32[8,64,256]{2,1,0:T(8,128)} custom-call(s32[4]{0:T(128)S(1)} %pad_add_fusion.1.place_ref, bf16[64,512,128]{2,1,0:T(8,128)(2,1)} %copy-done, f32[512,512]{1,0:T(8,128)} %get-tuple-element.46.units_ref.student_ref.unit_ref, f32[4,8,8,128]{3,2,1,0:T(8,128)S(1)} %bitcast.33, bf16[8192,256]{1,0:T(8,128)(2,1)} %refs_4_.1, ...), custom_call_target="tpu_custom_call" | custom-call | flops 8589934592 | bytes 16777216 | tf_op jit(solution)/shard_map/feature_gradient/pallas_call | solution.py:539
  163.4 3.6 %collective-permute-start.17 = (f32[2,256,128]{2,1,0:T(8,128)S(1)}, f32[2,256,128]{2,1,0:T(8,128)S(1)}, u32[]{:S(2)}, u32[]{:S(2)}) collective-permute-start(f32[2,256,128]{2,1,0:T(8,128)S(1)} %slice_add_fusion.1), channel_id=1, source_target_pairs={{0,48},{8,24},{16,0},{24,40},{32,16},{40,56},{48,32},{56,8},{1,49}... | collective-permute-start | bytes 786440 | tf_op jit(solution)/shard_map/ppermute | solution.py:334
  167.0 5.2 %all-to-all-start.6 = ((f32[8,64,256]{2,1,0:T(8,128)}), f32[8,64,256]{2,1,0:T(8,128)S(1)}, u32[]{:S(2)}, u32[]{:S(2)}) async-start(f32[8,64,256]{2,1,0:T(8,128)} %feature_gradient.1), calls=%async_computation.6 | async-start | bytes 1048576 | tf_op jit(solution)/shard_map/all_to_all | solution.py:34
  173.0 4.4 %collective-permute-done.17 = f32[2,256,128]{2,1,0:T(8,128)S(1)} collective-permute-done((f32[2,256,128]{2,1,0:T(8,128)S(1)}, f32[2,256,128]{2,1,0:T(8,128)S(1)}, u32[]{:S(2)}, u32[]{:S(2)}) %collective-permute-start.17) | collective-permute-done | bytes 262176 | tf_op jit(solution)/shard_map/ppermute | solution.py:334
  177.5 4.2 %all-to-all-done.6.pieces_ref = f32[8,64,256]{2,1,0:T(8,128)S(1)} async-done(((f32[8,64,256]{2,1,0:T(8,128)}), f32[8,64,256]{2,1,0:T(8,128)S(1)}, u32[]{:S(2)}, u32[]{:S(2)}) %all-to-all-start.6) | async-done | bytes 524320 | tf_op jit(solution)/shard_map/all_to_all | solution.py:34
  184.0 4.3 %all-to-all-start.7 = ((f32[8,64,256]{2,1,0:T(8,128)}), f32[8,64,256]{2,1,0:T(8,128)S(1)}, u32[]{:S(2)}, u32[]{:S(2)}) async-start(f32[8,64,256]{2,1,0:T(8,128)} %student_end.1), calls=%async_computation.7 | async-start | bytes 1048576 | tf_op jit(solution)/shard_map/all_to_all | solution.py:34
  189.6 4.7 %collective-permute-done.19.refs_1_ = f32[256,128]{1,0:T(8,128)S(1)} collective-permute-done((f32[256,128]{1,0:T(8,128)S(1)}, f32[256,128]{1,0:T(8,128)S(1)}, u32[]{:S(2)}, u32[]{:S(2)}) %collective-permute-start.19) | collective-permute-done | bytes 131104 | tf_op jit(solution)/shard_map/ppermute | solution.py:342
  (71 shorter events, 46.0 us)
Async XLA Ops:
  9.8 5.9 %collective-permute-start = (f32[64,128]{1,0:T(8,128)S(1)}, f32[64,128]{1,0:T(8,128)S(1)}, u32[]{:S(2)}, u32[]{:S(2)}) collective-permute-start(f32[64,128]{1,0:T(8,128)S(1)} %get-tuple-element.48), channel_id=1, source_target_pairs={{0,64},{64,128},{128,192},{192,0},{1,65},{65,129},{129,193},{193,1... | collective-permute-start | bytes 98312 | tf_op jit(solution)/shard_map/ppermute | solution.py:630
  12.0 4.3 %collective-permute-start.1 = (f32[64,128]{1,0:T(8,128)S(1)}, f32[64,128]{1,0:T(8,128)S(1)}, u32[]{:S(2)}, u32[]{:S(2)}) collective-permute-start(f32[64,128]{1,0:T(8,128)S(1)} %get-tuple-element.48), channel_id=1, source_target_pairs={{0,128},{64,192},{128,0},{192,64},{1,129},{65,193},{129,1},{193,65... | collective-permute-start | bytes 98312 | tf_op jit(solution)/shard_map/ppermute | solution.py:630
  14.6 3.1 %collective-permute-start.2 = (f32[64,128]{1,0:T(8,128)S(1)}, f32[64,128]{1,0:T(8,128)S(1)}, u32[]{:S(2)}, u32[]{:S(2)}) collective-permute-start(f32[64,128]{1,0:T(8,128)S(1)} %get-tuple-element.48), channel_id=1, source_target_pairs={{0,192},{64,0},{128,64},{192,128},{1,193},{65,1},{129,65},{193,129... | collective-permute-start | bytes 98312 | tf_op jit(solution)/shard_map/ppermute | solution.py:630
  17.7 35.6 %collective-permute-start.3 = (f32[512,256]{1,0:T(8,128)S(1)}, f32[512,256]{1,0:T(8,128)S(1)}, u32[]{:S(2)}, u32[]{:S(2)}) collective-permute-start(f32[512,256]{1,0:T(8,128)S(1)} %copy-done.4), channel_id=1, source_target_pairs={{0,64},{64,128},{128,192},{192,0},{1,65},{65,129},{129,193},{193,1... | collective-permute-start | bytes 1572872 | tf_op jit(solution)/shard_map/ppermute | solution.py:644
  17.8 35.5 %collective-permute-start.4 = (f32[512,256]{1,0:T(8,128)S(1)}, f32[512,256]{1,0:T(8,128)S(1)}, u32[]{:S(2)}, u32[]{:S(2)}) collective-permute-start(f32[512,256]{1,0:T(8,128)S(1)} %copy-done.4), channel_id=1, source_target_pairs={{0,192},{64,0},{128,64},{192,128},{1,193},{65,1},{129,65},{193,129... | collective-permute-start | bytes 1572872 | tf_op jit(solution)/shard_map/ppermute | solution.py:644
  56.0 4.1 %collective-permute-start.5 = (f32[64,128]{1,0:T(8,128)S(1)}, f32[64,128]{1,0:T(8,128)S(1)}, u32[]{:S(2)}, u32[]{:S(2)}) collective-permute-start(f32[64,128]{1,0:T(8,128)S(1)} %column_sums.2), channel_id=1, source_target_pairs={{0,64},{64,128},{128,192},{192,0},{1,65},{65,129},{129,193},{193,1... | collective-permute-start | bytes 98312 | tf_op jit(solution)/shard_map/ppermute | solution.py:630
  56.1 4.4 %collective-permute-start.6 = (f32[64,128]{1,0:T(8,128)S(1)}, f32[64,128]{1,0:T(8,128)S(1)}, u32[]{:S(2)}, u32[]{:S(2)}) collective-permute-start(f32[64,128]{1,0:T(8,128)S(1)} %column_sums.2), channel_id=1, source_target_pairs={{0,128},{64,192},{128,0},{192,64},{1,129},{65,193},{129,1},{193,65... | collective-permute-start | bytes 98312 | tf_op jit(solution)/shard_map/ppermute | solution.py:630
  61.4 28.7 %collective-permute-start.10 = (f32[512,256]{1,0:T(8,128)S(1)}, f32[512,256]{1,0:T(8,128)S(1)}, u32[]{:S(2)}, u32[]{:S(2)}) collective-permute-start(f32[512,256]{1,0:T(8,128)S(1)} %collective-permute-done.4.refs_2_), channel_id=1, source_target_pairs={{0,1},{1,0},{2,3},{3,2},{4,5},{5,4},{6,7},{7,6},{8,9},{9,8},{10,11... | collective-permute-start | bytes 1572872 | tf_op jit(solution)/shard_map/ppermute | solution.py:647
  63.6 26.5 %collective-permute-start.8 = (f32[512,256]{1,0:T(8,128)S(1)}, f32[512,256]{1,0:T(8,128)S(1)}, u32[]{:S(2)}, u32[]{:S(2)}) collective-permute-start(f32[512,256]{1,0:T(8,128)S(1)} %copy-done.4), channel_id=1, source_target_pairs={{0,128},{64,192},{128,0},{192,64},{1,129},{65,193},{129,1},{193,65... | collective-permute-start | bytes 1572872 | tf_op jit(solution)/shard_map/ppermute | solution.py:644
  64.9 25.3 %collective-permute-start.9 = (f32[512,256]{1,0:T(8,128)S(1)}, f32[512,256]{1,0:T(8,128)S(1)}, u32[]{:S(2)}, u32[]{:S(2)}) collective-permute-start(f32[512,256]{1,0:T(8,128)S(1)} %collective-permute-done.3.refs_0_), channel_id=1, source_target_pairs={{0,1},{1,0},{2,3},{3,2},{4,5},{5,4},{6,7},{7,6},{8,9},{9,8},{10,11... | collective-permute-start | bytes 1572872 | tf_op jit(solution)/shard_map/ppermute | solution.py:647
  92.9 4.1 %collective-permute-start.11 = (f32[64,128]{1,0:T(8,128)S(1)}, f32[64,128]{1,0:T(8,128)S(1)}, u32[]{:S(2)}, u32[]{:S(2)}) collective-permute-start(f32[64,128]{1,0:T(8,128)S(1)} %column_sums.3), channel_id=1, source_target_pairs={{0,64},{64,128},{128,192},{192,0},{1,65},{65,129},{129,193},{193,1... | collective-permute-start | bytes 98312 | tf_op jit(solution)/shard_map/ppermute | solution.py:630
  94.2 4.3 %collective-permute-start.12 = (f32[64,128]{1,0:T(8,128)S(1)}, f32[64,128]{1,0:T(8,128)S(1)}, u32[]{:S(2)}, u32[]{:S(2)}) collective-permute-start(f32[64,128]{1,0:T(8,128)S(1)} %column_sums.3), channel_id=1, source_target_pairs={{0,128},{64,192},{128,0},{192,64},{1,129},{65,193},{129,1},{193,65... | collective-permute-start | bytes 98312 | tf_op jit(solution)/shard_map/ppermute | solution.py:630
  96.3 3.3 %collective-permute-start.13 = (f32[64,128]{1,0:T(8,128)S(1)}, f32[64,128]{1,0:T(8,128)S(1)}, u32[]{:S(2)}, u32[]{:S(2)}) collective-permute-start(f32[64,128]{1,0:T(8,128)S(1)} %column_sums.3), channel_id=1, source_target_pairs={{0,192},{64,0},{128,64},{192,128},{1,193},{65,1},{129,65},{193,129... | collective-permute-start | bytes 98312 | tf_op jit(solution)/shard_map/ppermute | solution.py:630
  99.6 24.0 %collective-permute-start.14 = (f32[512,256]{1,0:T(8,128)S(1)}, f32[512,256]{1,0:T(8,128)S(1)}, u32[]{:S(2)}, u32[]{:S(2)}) collective-permute-start(f32[512,256]{1,0:T(8,128)S(1)} %collective-permute-done.8.refs_1_), channel_id=1, source_target_pairs={{0,1},{1,0},{2,3},{3,2},{4,5},{5,4},{6,7},{7,6},{8,9},{9,8},{10,11... | collective-permute-start | bytes 1572872 | tf_op jit(solution)/shard_map/ppermute | solution.py:647
  102.3 15.7 %all-to-all-start.4 = ((f32[8,64,128]{2,1,0:T(8,128)}), f32[8,64,128]{2,1,0:T(8,128)S(1)}, u32[]{:S(2)}, u32[]{:S(2)}) async-start(f32[8,64,128]{2,1,0:T(8,128)} %broadcast_in_dim.14), calls=%async_computation.4 | async-start | bytes 524288 | tf_op jit(solution)/shard_map/all_to_all | solution.py:34
  124.3 12.1 %all-to-all-start.5 = ((f32[32,8,128]{2,1,0:T(8,128)}), f32[32,8,128]{2,1,0:T(8,128)S(1)}, u32[]{:S(2)}, u32[]{:S(2)}) async-start(f32[32,8,128]{2,1,0:T(8,128)} %broadcast_in_dim.15), calls=%async_computation.5 | async-start | bytes 262144 | tf_op jit(solution)/shard_map/all_to_all | solution.py:34
  148.8 14.4 %collective-permute-start.16 = (f32[4,256,128]{2,1,0:T(8,128)S(1)}, f32[4,256,128]{2,1,0:T(8,128)S(1)}, u32[]{:S(2)}, u32[]{:S(2)}) collective-permute-start(f32[4,256,128]{2,1,0:T(8,128)S(1)} %get-tuple-element.76), channel_id=1, source_target_pairs={{0,56},{8,16},{16,8},{24,32},{32,24},{40,48},{48,40},{56,0},{1,57}... | collective-permute-start | bytes 1572872 | tf_op jit(solution)/shard_map/ppermute | solution.py:326
  148.9 14.4 %collective-permute-start.15 = (f32[4,256,128]{2,1,0:T(8,128)S(1)}, f32[4,256,128]{2,1,0:T(8,128)S(1)}, u32[]{:S(2)}, u32[]{:S(2)}) collective-permute-start(f32[4,256,128]{2,1,0:T(8,128)S(1)} %get-tuple-element.74), channel_id=1, source_target_pairs={{0,8},{8,0},{16,24},{24,16},{32,40},{40,32},{48,56},{56,48},{1,9},... | collective-permute-start | bytes 1572872 | tf_op jit(solution)/shard_map/ppermute | solution.py:326
  163.3 9.7 %collective-permute-start.18 = (f32[2,256,128]{2,1,0:T(8,128)S(1)}, f32[2,256,128]{2,1,0:T(8,128)S(1)}, u32[]{:S(2)}, u32[]{:S(2)}) collective-permute-start(f32[2,256,128]{2,1,0:T(8,128)S(1)} %slice_add_fusion), channel_id=1, source_target_pairs={{0,16},{8,56},{16,32},{24,8},{32,48},{40,24},{48,0},{56,40},{1,17}... | collective-permute-start | bytes 786440 | tf_op jit(solution)/shard_map/ppermute | solution.py:334
  163.4 14.0 %collective-permute-start.17 = (f32[2,256,128]{2,1,0:T(8,128)S(1)}, f32[2,256,128]{2,1,0:T(8,128)S(1)}, u32[]{:S(2)}, u32[]{:S(2)}) collective-permute-start(f32[2,256,128]{2,1,0:T(8,128)S(1)} %slice_add_fusion.1), channel_id=1, source_target_pairs={{0,48},{8,24},{16,0},{24,40},{32,16},{40,56},{48,32},{56,8},{1,49}... | collective-permute-start | bytes 786440 | tf_op jit(solution)/shard_map/ppermute | solution.py:334
  167.0 14.7 %all-to-all-start.6 = ((f32[8,64,256]{2,1,0:T(8,128)}), f32[8,64,256]{2,1,0:T(8,128)S(1)}, u32[]{:S(2)}, u32[]{:S(2)}) async-start(f32[8,64,256]{2,1,0:T(8,128)} %feature_gradient.1), calls=%async_computation.6 | async-start | bytes 1048576 | tf_op jit(solution)/shard_map/all_to_all | solution.py:34
  184.0 13.8 %all-to-all-start.7 = ((f32[8,64,256]{2,1,0:T(8,128)}), f32[8,64,256]{2,1,0:T(8,128)S(1)}, u32[]{:S(2)}, u32[]{:S(2)}) async-start(f32[8,64,256]{2,1,0:T(8,128)} %student_end.1), calls=%async_computation.7 | async-start | bytes 1048576 | tf_op jit(solution)/shard_map/all_to_all | solution.py:34
  188.3 6.1 %collective-permute-start.19 = (f32[256,128]{1,0:T(8,128)S(1)}, f32[256,128]{1,0:T(8,128)S(1)}, u32[]{:S(2)}, u32[]{:S(2)}) collective-permute-start(f32[256,128]{1,0:T(8,128)S(1)} %get-tuple-element.87), channel_id=1, source_target_pairs={{0,56},{8,16},{16,8},{24,32},{32,24},{40,48},{48,40},{56,0},{1,57}... | collective-permute-start | bytes 393224 | tf_op jit(solution)/shard_map/ppermute | solution.py:342
  189.6 4.7 %collective-permute-start.20 = (f32[256,128]{1,0:T(8,128)S(1)}, f32[256,128]{1,0:T(8,128)S(1)}, u32[]{:S(2)}, u32[]{:S(2)}) collective-permute-start(f32[256,128]{1,0:T(8,128)S(1)} %get-tuple-element.89), channel_id=1, source_target_pairs={{0,8},{8,0},{16,24},{24,16},{32,40},{40,32},{48,56},{56,48},{1,9},... | collective-permute-start | bytes 393224 | tf_op jit(solution)/shard_map/ppermute | solution.py:342
  (6 other events, 115.5 us)

commit v3 on v2

v3 whole, which is shorter than its diff:
```python
import math

import jax
import jax.numpy as jnp
from jax import lax
from jax.experimental import pallas as pl
from jax.experimental.pallas import tpu as pltpu
from jax.sharding import Mesh, PartitionSpec as P

D = 256
MASKED = 128
ITERS = 3
LANES = 128

teacher_temp = 0.07
student_temp = 0.1
epsilon = 1e-06

teacher_power = math.log2(math.e) / teacher_temp
student_power = math.log2(math.e) / student_temp

ROWS = ("y", "z")
PROTOS = ("x", "core")

f32 = jnp.float32
bf16 = jnp.bfloat16


def params(mib):
    return pltpu.CompilerParams(vmem_limit_bytes=mib * 2**20)


def spread(value, axes):
    return lax.all_to_all(value, axes, 0, 0, tiled=True)


def work(flops, moved, powers=0):
    return pl.CostEstimate(flops=int(flops), bytes_accessed=int(moved), transcendentals=int(powers))


def in_hbm(value):
    return pltpu.with_memory_space_constraint(value, pltpu.HBM)


def nt_dot(a, b):
    return lax.dot_general(a, b, (((1,), (1,)), ((), ())), preferred_element_type=f32)


def unit_rows(values):
    length = jnp.sqrt(jnp.sum(values * values, axis=-1, keepdims=True) + epsilon)
    return (values / length, length)


def directions(values):
    values = values.astype(f32)
    return (values * lax.rsqrt(jnp.sum(values * values, axis=-1, keepdims=True) + epsilon)).astype(bf16)


def to_column(row):
    return jnp.broadcast_to(row, (LANES, LANES)).T


def fill_columns(rows, tile_ref):
    for k in range(rows.shape[0]):
        tile_ref[k * LANES : (k + 1) * LANES, :] = to_column(rows[k : k + 1, :])


def lane_totals(tile):
    parts = [
        jnp.sum(tile[k * LANES : (k + 1) * LANES, :].T, axis=0, keepdims=True)
        for k in range(tile.shape[0] // LANES)
    ]
    return jnp.concatenate(parts, axis=0)


def select_body(place_ref, teacher_ref, student_ref, order_ref, units_ref, length_ref, mine_ref):
    images, patches, _ = teacher_ref.shape
    for image in range(images):
        chosen = order_ref[image : image + 1, :MASKED]
        place = lax.broadcasted_iota(jnp.int32, (patches, MASKED), 0)
        onehot = jnp.where(place == chosen, 1.0, 0.0).astype(bf16)

        def pick(ref):
            return lax.dot_general(
                onehot, ref[image], (((0,), (0,)), ((), ())), preferred_element_type=f32
            )

        rows = slice(image * MASKED, (image + 1) * MASKED)
        teacher = unit_rows(pick(teacher_ref))[0]
        student, length_ref[rows, :] = unit_rows(pick(student_ref))
        units_ref[rows, :D] = teacher
        units_ref[rows, D:] = student
        mine_ref[rows, :] = jnp.where(place_ref[3] == 0, teacher, student)


def select_tokens(place, teacher_patches, student_patches, mask_order):
    tokens = teacher_patches.shape[0] * MASKED
    return pl.pallas_call(
        select_body,
        in_specs=[pl.BlockSpec(memory_space=pltpu.SMEM)]
        + [pl.BlockSpec(memory_space=pltpu.VMEM)] * 3,
        out_specs=[pl.BlockSpec(memory_space=pltpu.VMEM)] * 3,
        out_shape=[
            pltpu.HBM((tokens, 2 * D), f32),
            pltpu.HBM((tokens, 1), f32),
            pltpu.HBM((tokens, D), f32),
        ],
        compiler_params=params(8),
        name="select",
    )(place, in_hbm(teacher_patches), in_hbm(student_patches), in_hbm(mask_order))


def lane_rows(row):
    parts = [row[:, j * LANES : (j + 1) * LANES] for j in range(row.shape[1] // LANES)]
    return jnp.concatenate(parts, axis=0)


def chunks(tokens):
    return [slice(c, c + LANES) for c in range(0, tokens, LANES)]


FETCHES = 8
WIDE = 256


def fetch(protos_ref, buffer_ref, sems, i):
    size = buffer_ref.shape[0] // FETCHES
    rows = pl.ds(pl.multiple_of(i * size, size), size)
    return pltpu.make_async_copy(protos_ref.at[rows, :], buffer_ref.at[rows, :], sems.at[i])


def fetch_all(units_ref, column, unit_ref, protos_ref, buffer_ref, sems):
    units = pltpu.make_async_copy(
        units_ref.at[:, pl.ds(column, D)], unit_ref, sems.at[FETCHES]
    )
    units.start()
    for i in range(FETCHES):
        fetch(protos_ref, buffer_ref, sems, i).start()
    units.wait()


def energy_body(
    place_ref, units_ref, *refs
):
    piece_refs, (protos_ref, energy_ref, sums_ref, cast_ref, weights_ref, total_ref) = refs[:8], refs[8:]
    own = units_ref.shape[0]
    tokens = cast_ref.shape[0]

    def rows_of(slot, start, size):
        return pl.ds(pl.multiple_of(place_ref[4 + slot] * own + start, size), size)

    cast_ref[rows_of(0, 0, own), :] = units_ref[...].astype(bf16)
    places = [(1, 0, own), (3, 0, own), (2, 0, own // 2), (2, own // 2, own // 2)]
    for core in range(2):

        @pl.when(place_ref[3] == core)
        def _(core=core):
            for i, ref in enumerate(piece_refs):
                kind = core if i < 4 else 1 - core
                cast_ref[rows_of(*places[i % 4]), kind * D : (kind + 1) * D] = ref[...].astype(bf16)

    weights_ref[...] = directions(protos_ref[...])
    total_ref[...] = jnp.zeros_like(total_ref)
    size = 512
    parts = [slice(c, c + size) for c in range(0, weights_ref.shape[0], size)]

    def step(i, carry):
        chunk = cast_ref[pl.ds(pl.multiple_of(i * WIDE, WIDE), WIDE), :][:, :D]
        logits = nt_dot(weights_ref[parts[0], :], chunk)
        for k, part in enumerate(parts):
            following = nt_dot(weights_ref[parts[k + 1], :], chunk) if k + 1 < len(parts) else None
            energy = jnp.exp2(logits * teacher_power)
            total = total_ref[part, :]
            for j in range(WIDE // LANES):
                tile = energy[:, j * LANES : (j + 1) * LANES]
                energy_ref[i * (WIDE // LANES) + j, part, :] = tile.astype(bf16)
                total = total + tile
            total_ref[part, :] = total
            logits = following
        return carry

    lax.fori_loop(0, tokens // WIDE, step, 0)
    totals = lane_totals(total_ref[...])
    for copy in range(sums_ref.shape[0]):
        sums_ref[copy] = totals


def fixed(*shape):
    return pl.BlockSpec(shape, lambda i: (0,) * len(shape))


def left(tokens):
    return pl.BlockSpec((tokens, D), lambda *i: (0, 0))


def right(tokens):
    return pl.BlockSpec((tokens, D), lambda *i: (0, 1))


def energy_of(place, units, pieces, protos, share, copies):
    own = units.shape[0]
    tokens = own * 4
    direct = pl.BlockSpec(memory_space=pltpu.VMEM)
    return pl.pallas_call(
        energy_body,
        grid_spec=pltpu.PrefetchScalarGridSpec(
            num_scalar_prefetch=1,
            grid=(1,),
            in_specs=[pl.BlockSpec(units.shape, lambda i, p: (0, 0))]
            + [pl.BlockSpec(piece.shape, lambda i, p: (0, 0)) for piece in pieces]
            + [pl.BlockSpec((share, D), lambda i, p: (p[0], 0))],
            out_specs=[
                direct,
                pl.BlockSpec((copies, share // LANES, LANES), lambda i, p: (0, 0, 0)),
                pl.BlockSpec((tokens, 2 * D), lambda i, p: (0, 0)),
            ],
            scratch_shapes=[pltpu.VMEM((share, D), bf16), pltpu.VMEM((share, LANES), f32)],
        ),
        out_shape=[
            pltpu.VMEM((tokens // LANES, share, LANES), bf16),
            jax.ShapeDtypeStruct((copies, share // LANES, LANES), f32),
            pltpu.HBM((tokens, 2 * D), bf16),
        ],
        compiler_params=params(24),
        cost_estimate=work(4 * tokens * share * D, 8 * 2**20, tokens * share),
        name="energy",
    )(place, in_hbm(units), *pieces, in_hbm(protos))


def student_body(units_ref, protos_ref, sums_ref, unit_ref, cast_ref, total_ref, buffer_ref, sems):
    size = buffer_ref.shape[0] // FETCHES
    fetch_all(units_ref, D, unit_ref, protos_ref, buffer_ref, sems)
    cast_ref[...] = unit_ref[...].astype(bf16)
    total_ref[...] = jnp.zeros_like(total_ref)

    def step(i, carry):
        fetch(protos_ref, buffer_ref, sems, i).wait()
        total = total_ref[...]

        def logits_of(part):
            rows = pl.ds(pl.multiple_of(i * size + part * WIDE, WIDE), WIDE)
            return nt_dot(cast_ref[...], directions(buffer_ref[rows, :]))

        parts = size // WIDE
        logits = logits_of(0)
        for part in range(parts):
            following = logits_of(part + 1) if part + 1 < parts else None
            values = jnp.exp2(logits * student_power)
            logits = following
            for j in range(WIDE // LANES):
                total = total + values[:, j * LANES : (j + 1) * LANES]
        total_ref[...] = total
        return carry

    lax.fori_loop(0, FETCHES, step, 0)
    sums_ref[...] = lane_totals(total_ref[...])


def student_sums(units, protos):
    tokens, count = units.shape[0], protos.shape[0]
    return pl.pallas_call(
        student_body,
        in_specs=[pl.BlockSpec(memory_space=pl.ANY)] * 2,
        out_specs=pl.BlockSpec(memory_space=pltpu.VMEM),
        out_shape=jax.ShapeDtypeStruct((tokens // LANES, LANES), f32),
        scratch_shapes=[
            pltpu.VMEM((tokens, D), f32),
            pltpu.VMEM((tokens, D), bf16),
            pltpu.VMEM((tokens, LANES), f32),
            pltpu.VMEM((count, D), bf16),
            pltpu.SemaphoreType.DMA((FETCHES + 1,)),
        ],
        compiler_params=params(16),
        cost_estimate=work(4 * tokens * count * D, 8 * 2**20, tokens * count),
        name="student",
    )(in_hbm(units), in_hbm(protos))


def right(tokens):
    return pl.BlockSpec((tokens, D), lambda *i: (0, 1))


def row_body(energy_ref, pieces_ref, *refs):
    norm_refs, (scale_ref, sums_ref, tile_ref) = refs[:-3], refs[-3:]
    scale_ref[...] = 1.0 / jnp.sum(pieces_ref[...], axis=0)
    fill_columns(scale_ref[...], tile_ref)
    tiles, protos, _ = energy_ref.shape
    size = 512
    totals = []
    for j in range(tiles):
        total = jnp.zeros((1, LANES), f32)
        for start in range(0, protos, size):
            part = slice(start, start + size)
            energy = energy_ref[j, part, :].astype(f32)
            total = total + jnp.sum(energy * tile_ref[part, :], axis=0, keepdims=True)
        totals.append(total)
    for ref in norm_refs:
        totals += [ref[...], jnp.zeros_like(ref)]
    totals = jnp.concatenate(totals, axis=0)
    for copy in range(sums_ref.shape[0]):
        sums_ref[copy] = totals


def row_sums(energy, pieces, copies, norm_part=()):
    tiles, protos, _ = energy.shape
    whole = pl.BlockSpec(memory_space=pltpu.VMEM)
    rows = tiles + 2 * sum(part.shape[0] for part in norm_part)
    return pl.pallas_call(
        row_body,
        in_specs=[whole] * (2 + len(norm_part)),
        out_specs=[whole] * 2,
        out_shape=[
            jax.ShapeDtypeStruct((protos // LANES, LANES), f32),
            jax.ShapeDtypeStruct((copies, rows, LANES), f32),
        ],
        scratch_shapes=[pltpu.VMEM((protos, LANES), f32)],
        compiler_params=params(12),
        cost_estimate=work(2 * energy.size, 0),
        name="row_sums",
    )(energy, pieces, *norm_part)


def column_body(energy_ref, pieces_ref, sums_ref, scale_ref):
    tiles, protos, _ = energy_ref.shape
    scale_ref[...] = 1.0 / jnp.sum(pieces_ref[...], axis=0)

    def step(k, carry):
        rows = pl.ds(pl.multiple_of(k * LANES, LANES), LANES)
        total = jnp.zeros((LANES, LANES), f32)
        for j in range(tiles):
            total = total + energy_ref[j, rows, :].astype(f32) * scale_ref[j : j + 1, :]
        sums_ref[0, pl.ds(k, 1), :] = lane_totals(total)
        return carry

    lax.fori_loop(0, protos // LANES, step, 0, unroll=4)
    for copy in range(1, sums_ref.shape[0]):
        sums_ref[copy] = sums_ref[0]


def column_sums(energy, pieces, copies):
    tiles, protos, _ = energy.shape
    whole = pl.BlockSpec(memory_space=pltpu.VMEM)
    return pl.pallas_call(
        column_body,
        in_specs=[whole] * 2,
        out_specs=whole,
        out_shape=jax.ShapeDtypeStruct((copies, protos // LANES, LANES), f32),
        scratch_shapes=[pltpu.VMEM((tiles, LANES), f32)],
        compiler_params=params(12),
        cost_estimate=work(2 * energy.size, 0),
        name="column_sums",
    )(energy, pieces)


LEFT_PLACE = [4, 5, 6, 7, 3, 2, 1, 0]
RIGHT_PLACE = [4, 0, 1, 2, 3, 7, 6, 5]


def collect(send, keep, offset):
    n = lax.axis_size("z")
    way = [1 if (z + offset) % 2 else -1 for z in range(n)]
    got = lax.ppermute(send, "z", [(z, (z - way[z]) % n) for z in range(n)])
    return keep[0] + got[0], keep[1] + got[1], keep[2:] + got[2:]


def pass_on(sums, offset):
    n = lax.axis_size("z")
    way = [1 if (z + offset) % 2 else -1 for z in range(n)]
    own, following, far = sums
    got = lax.ppermute(far, "z", [(z, (z + 2 * way[z]) % n) for z in range(n)])
    return own + got[0], following + got[1]


def deliver(sums, offset):
    n = lax.axis_size("z")
    way = [1 if (z + offset) % 2 else -1 for z in range(n)]
    own, following = sums
    return [own, lax.ppermute(following, "z", [(z, (z + way[z]) % n) for z in range(n)])]


def gradient_body(
    table_ref,
    units_ref,
    energy_ref,
    pieces_ref,
    sw_first_ref,
    sw_second_ref,
    scale_ref,
    send_left_ref,
    send_right_ref,
    keep_left_ref,
    keep_right_ref,
    feature_ref,
    r_ref,
    n_ref,
    total_ref,
):
    step = pl.program_id(0)
    tiles = energy_ref.shape[0]
    groups = pieces_ref.shape[0]
    own = tiles // groups

    @pl.when(step == 0)
    def _():
        scale = (1.0 / student_temp) / jnp.sum(pieces_ref[:, :, :tiles, :], axis=(0, 1))
        for k in range(tiles):
            r_ref[:, k * LANES : (k + 1) * LANES] = scale[k : k + 1, :]
        for group in range(groups):
            total = jnp.sum(pieces_ref[group, :, tiles : tiles + own, :], axis=0)
            inverse = (1.0 / student_temp) / total
            for k in range(own):
                lanes = slice((group * own + k) * LANES, (group * own + k + 1) * LANES)
                n_ref[:, lanes] = inverse[k : k + 1, :]
        feature_ref[...] = jnp.zeros_like(feature_ref)

    both = lambda first, second: jnp.concatenate([first, second], axis=0)
    block = sw_first_ref.shape[0]
    sw = both(directions(sw_first_ref[...]), directions(sw_second_ref[...]))
    local = [table_ref[3, 2 * step], table_ref[3, 2 * step + 1]]
    here = [pl.ds(pl.multiple_of(place * block, block), block) for place in local]
    columns = []
    for place in local:
        for k in range(block // LANES):
            row = scale_ref[pl.ds(place * (block // LANES) + k, 1), :]
            columns.append(to_column(row))
    col_scale = jnp.concatenate(columns, axis=0)

    def logits_of(part):
        return nt_dot(sw, units_ref[part, D:])

    parts = [slice(c, c + WIDE) for c in range(0, units_ref.shape[0], WIDE)]
    logits = logits_of(parts[0])
    for i, part in enumerate(parts):
        following = logits_of(parts[i + 1]) if i + 1 < len(parts) else None
        grads = []
        for j in range(WIDE // LANES):
            tile = i * (WIDE // LANES) + j
            lanes = slice(tile * LANES, (tile + 1) * LANES)
            energy = both(energy_ref[tile, here[0], :], energy_ref[tile, here[1], :]).astype(f32)
            probs = jnp.exp2(logits[:, j * LANES : (j + 1) * LANES] * student_power) * n_ref[:, lanes]
            grads.append((probs - energy * r_ref[:, lanes] * col_scale).astype(bf16))
        logit_grad = jnp.concatenate(grads, axis=1)
        added = jnp.dot(logit_grad, units_ref[part, D:], preferred_element_type=f32)
        total_ref[...] = added if i == 0 else total_ref[...] + added
        feature_ref[part, :] += lax.dot_general(
            logit_grad, sw, (((0,), (0,)), ((), ())), preferred_element_type=f32
        )
        logits = following

    for which in range(2):
        rows_here = slice(which * block, (which + 1) * block)
        for row, columns_here, sent_ref, kept_ref in (
            (1, slice(0, D // 2), send_left_ref, keep_left_ref),
            (2, slice(D // 2, D), send_right_ref, keep_right_ref),
        ):
            place = table_ref[row, 2 * step + which]

            @pl.when(place < 4)
            def _():
                sent_ref[jnp.minimum(place, 3)] = total_ref[rows_here, columns_here]

            @pl.when(place >= 4)
            def _():
                kept_ref[jnp.maximum(place - 4, 0)] = total_ref[rows_here, columns_here]


def gradients(y, z, units_all, energy, pieces, student_protos, scale):
    tiles, share, _ = energy.shape
    tokens = units_all.shape[0]
    block = 256
    blocks = share // block
    way = jnp.where(z % 2 == 1, 1, -1)
    local = (z + way * jnp.arange(blocks) + blocks) % blocks
    table = jnp.stack(
        [y * blocks + local, jnp.array(LEFT_PLACE), jnp.array(RIGHT_PLACE), local]
    ).astype(jnp.int32)
    whole = lambda *shape: pl.BlockSpec(shape, lambda i, p: (0,) * len(shape))
    first = pl.BlockSpec((block, D), lambda i, p: (p[0, 2 * i], 0))
    second = pl.BlockSpec((block, D), lambda i, p: (p[0, 2 * i + 1], 0))
    direct = pl.BlockSpec(memory_space=pltpu.VMEM)
    half = pltpu.VMEM((blocks // 2, block, D // 2), f32)
    return pl.pallas_call(
        gradient_body,
        grid_spec=pltpu.PrefetchScalarGridSpec(
            num_scalar_prefetch=1,
            grid=(blocks // 2,),
            in_specs=[
                whole(tokens, 2 * D),
                direct,
                whole(*pieces.shape),
                first,
                second,
                whole(*scale.shape),
            ],
            out_specs=[direct] * 5,
            scratch_shapes=[
                pltpu.VMEM((1, tokens), f32),
                pltpu.VMEM((1, tokens), f32),
                pltpu.VMEM((2 * block, D), f32),
            ],
        ),
        out_shape=[half, half, half, half, pltpu.VMEM((tokens, D), f32)],
        compiler_params=params(24),
        cost_estimate=work(8 * tokens * share * D, 8 * 2**20, tokens * share),
        name="gradients",
    )(
        table,
        in_hbm(units_all),
        energy,
        pieces,
        in_hbm(student_protos),
        in_hbm(student_protos),
        scale,
    )


def project(total, unit, length):
    return (total - unit * jnp.sum(unit * total, axis=-1, keepdims=True)) / length


def student_end_body(place_ref, pieces_ref, unit_ref, length_ref, out_ref):
    result = project(jnp.sum(pieces_ref[...], axis=0), unit_ref[...], length_ref[...])
    for copy in range(out_ref.shape[0]):
        out_ref[copy] = result


def student_end(place, pieces, units, length, copies):
    _, rows, _ = pieces.shape
    return pl.pallas_call(
        student_end_body,
        grid_spec=pltpu.PrefetchScalarGridSpec(
            num_scalar_prefetch=1,
            grid=(1,),
            in_specs=[
                pl.BlockSpec(pieces.shape, lambda i, p: (0, 0, 0)),
                pl.BlockSpec((rows, D), lambda i, p: (p[2], 1)),
                pl.BlockSpec((rows, 1), lambda i, p: (p[2], 0)),
            ],
            out_specs=pl.BlockSpec((copies, rows, D), lambda i, p: (0, 0, 0)),
        ),
        out_shape=jax.ShapeDtypeStruct((copies, rows, D), f32),
        compiler_params=params(8),
        name="student_end",
    )(place, pieces, in_hbm(units), in_hbm(length))


def proto_end_body(place_ref, *refs):
    piece_refs, (protos_ref, out_ref) = refs[:-2], refs[-2:]
    unit, length = unit_rows(protos_ref[...].astype(f32))
    half = len(piece_refs) // 2
    sums = []
    for group in (piece_refs[:half], piece_refs[half:]):
        total = group[0][...]
        for ref in group[1:]:
            total = total + ref[...]
        sums.append(total)
    out_ref[...] = project(jnp.concatenate(sums, axis=1), unit, length)


def proto_end(place, pieces, protos):
    rows, width = pieces[0].shape
    return pl.pallas_call(
        proto_end_body,
        grid_spec=pltpu.PrefetchScalarGridSpec(
            num_scalar_prefetch=1,
            grid=(1,),
            in_specs=[pl.BlockSpec((rows, width), lambda i, p: (0, 0))] * len(pieces)
            + [pl.BlockSpec((rows, D), lambda i, p: (p[1], 0))],
            out_specs=pl.BlockSpec((rows, D), lambda i, p: (0, 0)),
        ),
        out_shape=jax.ShapeDtypeStruct((rows, D), f32),
        compiler_params=params(8),
        name="proto_end",
    )(place, *pieces, in_hbm(protos))


def on_device(teacher_patches, student_patches, mask_order, teacher_protos, student_protos):
    y_size, z_size = lax.axis_size("y"), lax.axis_size("z")
    proto_size = lax.axis_size("x") * lax.axis_size("core")
    y, z = lax.axis_index("y"), lax.axis_index("z")
    others = [(y - step + y_size) % y_size for step in range(y_size)]
    place = [y, y * z_size + z, lax.axis_index(PROTOS), lax.axis_index("core")] + others
    place = jnp.stack(place).astype(jnp.int32)
    share = teacher_protos.shape[0] // y_size

    units, student_length, mine = select_tokens(
        place, teacher_patches, student_patches, mask_order
    )
    from_y = lambda value, step: lax.ppermute(
        value, "y", [(i, (i + step) % y_size) for i in range(y_size)]
    )
    from_core = lambda value: lax.ppermute(value, "core", [(0, 1), (1, 0)])
    half = mine.shape[0] // 2
    first, third = from_y(mine, 1), from_y(mine, 3)
    got = [first, third, from_y(first[:half], 1), from_y(third[half:], 3)]
    got = got + [from_core(piece) for piece in got]
    norm_part = student_sums(units, student_protos)
    norm_part, got = lax.optimization_barrier((norm_part, got))

    rows = ("y",) + PROTOS
    peers = y_size * proto_size
    energy, sums, units_all = energy_of(place, units, got, teacher_protos, share, z_size)
    for sweep in range(ITERS):
        if sweep > 0:
            sums = column_sums(energy, pieces, z_size)
        norms = (norm_part,) if sweep == ITERS - 1 else ()
        col_scale, row_part = row_sums(energy, spread(sums, "z"), peers, norms)
        pieces = spread(row_part, rows)
    pieces = pieces.reshape((y_size, proto_size) + pieces.shape[1:])

    send_left, send_right, keep_left, keep_right, feature_part = gradients(
        y, z, units_all, energy, pieces, student_protos, col_scale
    )
    left = pass_on(collect(send_left, keep_left, 0), 0)
    right_half = pass_on(collect(send_right, keep_right, 1), 1)
    feature_pieces = spread(feature_part.reshape(peers, -1, D), rows)
    feature_pieces, left, right_half = lax.optimization_barrier((feature_pieces, left, right_half))
    left, right_half = deliver(left, 0), deliver(right_half, 1)
    result = student_end(place, feature_pieces, units, student_length, proto_size)
    result = spread(result, PROTOS)
    grad_protos = proto_end(place, left + right_half, student_protos)
    return (result.reshape(-1, MASKED, D), grad_protos)


def solution(mesh):
    fine = Mesh(mesh.devices.reshape(4, 8, 4, 2), ("y", "z", "x", "core"))
    return jax.shard_map(
        on_device,
        mesh=fine,
        in_specs=(
            P(ROWS, None, None),
            P(ROWS, None, None),
            P(ROWS, None),
            P(PROTOS, None),
            P(PROTOS, None),
        ),
        out_specs=(P(ROWS, None, None), P(PROTOS + ROWS, None)),
        check_vma=False,
    )
```

time: 199 us -> 204 us (1.025)
  waiting for transfers between devices: 35.2 us -> 54.4 us
  Pallas kernels: 60.3 us -> 44.4 us
  starting transfers between devices: 43.9 us -> 33.4 us
  blocking collectives: 52.4 us -> 62.6 us
    pallas_call x7 -> x5, Pallas kernels: 41 us -> 26.2 us  [the longest x1 11.6 us: gradients(): pl.pallas_call(gradient_body, grid_spec=pltpu.PrefetchScalarGridSpec(num_...]
    ppermute x3 -> x4, waiting for transfers between devices: 0.01 us -> 13.6 us  [on_device(): lax.ppermute(value, 'y', [(i, (i + step) % y_size) for i in range(y_size)])]
    ppermute x9 -> x0, starting transfers between devices: 12.5 us -> none  [direct_sum(): lax.ppermute(value, axis, [(i, (i + step) % n) for i in range(n)])]
    ppermute x2, waiting for transfers between devices: 1.64 us -> 13.8 us  [collect(): got = lax.ppermute(send, 'z', [(z, (z - way[z]) % n) for z in range(n)])]
    all_to_all x4 -> x5, blocking collectives: 52.4 us -> 62.6 us  [spread(): return lax.all_to_all(value, axes, 0, 0, tiled=True)]
    ppermute x9 -> x0, waiting for transfers between devices: 7.45 us -> none  [direct_sum(): lax.ppermute(value, axis, [(i, (i + step) % n) for i in range(n)])]
    ppermute x2, waiting for transfers between devices: 5.23 us -> 11.9 us  [pass_on(): got = lax.ppermute(far, 'z', [(z, (z + 2 * way[z]) % n) for z in range(n)])]
    all_to_all x4 -> x3, waiting for transfers between devices: 16.1 us -> 10.3 us  [spread(): return lax.all_to_all(value, axes, 0, 0, tiled=True)]
  transfers between devices with their start and end apart: 25 -> 17, of which waited for: 16 -> 11; matrix products, arithmetic and copies ran while one was open for 0% -> 0% of each run, Pallas kernels for 16% -> 4%
where the time goes in v3:
time: 204 us; the launch traced here: 203 us
  blocking collectives  62.6 us (31%)
  waiting for transfers between devices  54.4 us (27%)
  Pallas kernels  44.4 us (22%)
  starting transfers between devices  33.4 us (16%)
  local copies, waits for them, and re-layouts  7.25 us (4%)
    all_to_all x5, blocking collectives, spread(): return lax.all_to_all(value, axes, 0, 0, tiled=True)  62.6 us
    all_to_all x3, starting transfers between devices, spread(): return lax.all_to_all(value, axes, 0, 0, tiled=True)  14.7 us
    ppermute x2, waiting for transfers between devices, collect(): got = lax.ppermute(send, 'z', [(z, (z - way[z]) % n) for z in range(n)])  13.8 us
    ppermute x4, waiting for transfers between devices, on_device(): lax.ppermute(value, 'y', [(i, (i + step) % y_size) for i in range(y_size)])  13.6 us
    ppermute x2, waiting for transfers between devices, pass_on(): got = lax.ppermute(far, 'z', [(z, (z + 2 * way[z]) % n) for z in range(n)])  11.9 us
    pallas_call x1, Pallas kernels, gradients(): pl.pallas_call(gradient_body, grid_spec=pltpu.PrefetchScalarGridSpec(num_...  11.6 us
    all_to_all x3, waiting for transfers between devices, spread(): return lax.all_to_all(value, axes, 0, 0, tiled=True)  10.3 us
    pallas_call x1, Pallas kernels, energy_of(): pl.pallas_call(energy_body, grid_spec=pltpu.PrefetchScalarGridSpec(num_sc...  7.45 us
  transfers between devices with their start and end apart: 17, of which 11 were waited for; matrix products, arithmetic and copies ran while one was open for 0% of the time, Pallas kernels for 4%

profile of v3, /device:TPU:1, one launch (start us, length us, event | category | flops | bytes accessed | tf_op | source)
XLA Modules:
  0.0 203.2 jit_solution(8895613873605463246)
XLA Ops:
  0.8 3.0 %select.31 = (f32[512,512]{1,0:T(8,128)}, f32[512,1]{1,0:T(8,128)}, f32[512,256]{1,0:T(8,128)}) custom-call(s32[8]{0:T(128)S(1)} %stack.46.place_ref, bf16[4,256,256]{2,1,0:T(8,128)(2,1)} %teacher_ref.1, bf16[4,256,256]{2,1,0:T(8,128)(2,1)} %student_ref.1, s32[4,256]{1,0:T(4,128)} %order_ref.1), custom_call_target="tpu_custom_call" | custom-call | tf_op jit(solution)/shard_map/select/pallas_call | solution.py:98
  3.8 3.6 %collective-permute-start.1 = (f32[512,256]{1,0:T(8,128)}, f32[512,256]{1,0:T(8,128)S(1)}, u32[]{:S(2)}, u32[]{:S(2)}) collective-permute-start(f32[512,256]{1,0:T(8,128)} %get-tuple-element.32), channel_id=1, source_target_pairs={{0,192},{64,0},{128,64},{192,128},{1,193},{65,1},{129,65},{193,129... | collective-permute-start | bytes 1572872 | tf_op jit(solution)/shard_map/ppermute | solution.py:589
  7.3 10.9 %collective-permute-done.1.refs_1_ = f32[512,256]{1,0:T(8,128)S(1)} collective-permute-done((f32[512,256]{1,0:T(8,128)}, f32[512,256]{1,0:T(8,128)S(1)}, u32[]{:S(2)}, u32[]{:S(2)}) %collective-permute-start.1) | collective-permute-done | bytes 524320 | tf_op jit(solution)/shard_map/ppermute | solution.py:589
  18.2 3.4 %collective-permute-start.3 = (f32[256,256]{1,0:T(8,128)S(1)}, f32[256,256]{1,0:T(8,128)S(1)}, u32[]{:S(2)}, u32[]{:S(2)}) collective-permute-start(f32[256,256]{1,0:T(8,128)S(1)} %slice.73), channel_id=1, source_target_pairs={{0,192},{64,0},{128,64},{192,128},{1,193},{65,1},{129,65},{193,129... | collective-permute-start | bytes 786440 | tf_op jit(solution)/shard_map/ppermute | solution.py:589
  25.7 2.5 %collective-permute-start.7 = (f32[256,256]{1,0:T(8,128)S(1)}, f32[256,256]{1,0:T(8,128)S(1)}, u32[]{:S(2)}, u32[]{:S(2)}) collective-permute-start(f32[256,256]{1,0:T(8,128)S(1)} %collective-permute-done.3.refs_3_), channel_id=1, source_target_pairs={{0,1},{1,0},{2,3},{3,2},{4,5},{5,4},{6,7},{7,6},{8,9},{9,8},{10,11... | collective-permute-start | bytes 786440 | tf_op jit(solution)/shard_map/ppermute | solution.py:592
  28.9 2.8 %collective-permute-start.6 = (f32[256,256]{1,0:T(8,128)S(1)}, f32[256,256]{1,0:T(8,128)S(1)}, u32[]{:S(2)}, u32[]{:S(2)}) collective-permute-start(f32[256,256]{1,0:T(8,128)S(1)} %collective-permute-done.2.refs_2_), channel_id=1, source_target_pairs={{0,1},{1,0},{2,3},{3,2},{4,5},{5,4},{6,7},{7,6},{8,9},{9,8},{10,11... | collective-permute-start | bytes 786440 | tf_op jit(solution)/shard_map/ppermute | solution.py:592
  31.7 6.1 %student.1.refs_0_ = f32[4,128]{1,0:T(4,128)S(1)} custom-call(f32[512,512]{1,0:T(8,128)} %get-tuple-element.31.units_ref.unit_ref, bf16[8192,256]{1,0:T(8,128)(2,1)} %refs_4_.1), custom_call_target="tpu_custom_call" | custom-call | flops 4294967296 | bytes 8388608 | tf_op jit(solution)/shard_map/student/pallas_call | solution.py:261
  37.8 7.5 %energy.1 = (bf16[16,2048,128]{2,1,0:T(8,128)(2,1)S(1)}, f32[8,16,128]{2,1,0:T(8,128)S(1)}, bf16[2048,512]{1,0:T(8,128)(2,1)}) custom-call(s32[8]{0:T(128)S(1)} %stack.46.place_ref, f32[512,512]{1,0:T(8,128)} %get-tuple-element.31.units_ref.unit_ref, f32[512,256]{1,0:T(8,128)S(1)} %collective-permute-done.refs_0_, ...), custom_call_target="tpu_custom_call" | custom-call | flops 4294967296 | bytes 8388608 | tf_op jit(solution)/shard_map/energy/pallas_call | solution.py:204
  45.3 15.1 %all_to_all.40.pieces_ref = f32[8,16,128]{2,1,0:T(8,128)S(1)} all-to-all(f32[8,16,128]{2,1,0:T(8,128)S(1)} %get-tuple-element.43), channel_id=1, replica_groups=mesh['y'=4,'z'=8,'x'=4,'core'=2] {'z'}, dimensions={0} | all-to-all | bytes 131072 | tf_op jit(solution)/shard_map/all_to_all | solution.py:34
  62.5 14.8 %all_to_all.41.pieces_ref = f32[32,16,128]{2,1,0:T(8,128)S(1)} all-to-all(f32[32,16,128]{2,1,0:T(8,128)S(1)} %get-tuple-element.44), channel_id=1, replica_groups=mesh['y'=4,'z'=8,'x'=4,'core'=2] {'y','x','core'}, dimensions={0} | all-to-all | bytes 524288 | tf_op jit(solution)/shard_map/all_to_all | solution.py:34
  79.5 9.5 %all_to_all.42.pieces_ref = f32[8,16,128]{2,1,0:T(8,128)S(1)} all-to-all(f32[8,16,128]{2,1,0:T(8,128)S(1)} %column_sums.2), channel_id=1, replica_groups=mesh['y'=4,'z'=8,'x'=4,'core'=2] {'z'}, dimensions={0} | all-to-all | bytes 131072 | tf_op jit(solution)/shard_map/all_to_all | solution.py:34
  91.2 13.7 %all_to_all.43.pieces_ref = f32[32,16,128]{2,1,0:T(8,128)S(1)} all-to-all(f32[32,16,128]{2,1,0:T(8,128)S(1)} %get-tuple-element.45), channel_id=1, replica_groups=mesh['y'=4,'z'=8,'x'=4,'core'=2] {'y','x','core'}, dimensions={0} | all-to-all | bytes 524288 | tf_op jit(solution)/shard_map/all_to_all | solution.py:34
  107.1 9.5 %all_to_all.44.pieces_ref = f32[8,16,128]{2,1,0:T(8,128)S(1)} all-to-all(f32[8,16,128]{2,1,0:T(8,128)S(1)} %column_sums.3), channel_id=1, replica_groups=mesh['y'=4,'z'=8,'x'=4,'core'=2] {'z'}, dimensions={0} | all-to-all | bytes 131072 | tf_op jit(solution)/shard_map/all_to_all | solution.py:34
  116.6 2.9 %row_sums.5 = (f32[16,128]{1,0:T(8,128)S(1)}, f32[32,24,128]{2,1,0:T(8,128)}) custom-call(bf16[16,2048,128]{2,1,0:T(8,128)(2,1)S(1)} %get-tuple-element.42.energy_ref, f32[8,16,128]{2,1,0:T(8,128)S(1)} %all_to_all.44.pieces_ref, f32[4,128]{1,0:T(4,128)S(1)} %student.1.refs_0_), custom_call_target="tpu_custom_call" | custom-call | flops 8388608 | tf_op jit(solution)/shard_map/row_sums/pallas_call | solution.py:308
  119.5 5.1 %all-to-all-start.5 = ((f32[32,24,128]{2,1,0:T(8,128)}), f32[32,24,128]{2,1,0:T(8,128)S(1)}, u32[]{:S(2)}, u32[]{:S(2)}) async-start(f32[32,24,128]{2,1,0:T(8,128)} %get-tuple-element.47), calls=%async_computation.5 | async-start | bytes 786432 | tf_op jit(solution)/shard_map/all_to_all | solution.py:34
  124.6 10.2 %all-to-all-done.5 = f32[32,24,128]{2,1,0:T(8,128)S(1)} async-done(((f32[32,24,128]{2,1,0:T(8,128)}), f32[32,24,128]{2,1,0:T(8,128)S(1)}, u32[]{:S(2)}, u32[]{:S(2)}) %all-to-all-start.5) | async-done | bytes 393248 | tf_op jit(solution)/shard_map/all_to_all | solution.py:34
  134.8 3.4 %copy-done.1 = bf16[16,2048,128]{2,1,0:T(8,128)(2,1)S(1)} copy-done((bf16[16,2048,128]{2,1,0:T(8,128)(2,1)S(1)}, bf16[16,2048,128]{2,1,0:T(8,128)(2,1)}, u32[]{:S(2)}) %copy-start.1) | copy-done | bytes 8388632
  138.2 11.6 %gradients.1 = (f32[4,256,128]{2,1,0:T(8,128)S(1)}, f32[4,256,128]{2,1,0:T(8,128)S(1)}, f32[4,256,128]{2,1,0:T(8,128)S(1)}, f32[4,256,128]{2,1,0:T(8,128)S(1)}, f32[2048,256]{1,0:T(8,128)S(1)}) custom-call(s32[4,8]{1,0:T(4,128)S(1)} %pad_add_fusion.table_ref, bf16[2048,512]{1,0:T(8,128)(2,1)} %get-tuple-element.41.units_ref, ...), custom_call_target="tpu_custom_call" | custom-call | flops 8589934592 | bytes 8388608 | tf_op jit(solution)/shard_map/gradients/pallas_call | solution.py:482
  152.8 4.0 %all-to-all-start.6 = ((f32[32,64,256]{2,1,0:T(8,128)}), f32[32,64,256]{2,1,0:T(8,128)S(1)}, u32[]{:S(2)}, u32[]{:S(2)}) async-start(f32[32,64,256]{2,1,0:T(8,128)} %bitcast.19), calls=%async_computation.6 | async-start | bytes 4194304 | tf_op jit(solution)/shard_map/all_to_all | solution.py:34
  157.3 13.0 %collective-permute-done.8 = f32[4,256,128]{2,1,0:T(8,128)S(1)} collective-permute-done((f32[4,256,128]{2,1,0:T(8,128)}, f32[4,256,128]{2,1,0:T(8,128)S(1)}, u32[]{:S(2)}, u32[]{:S(2)}) %collective-permute-start.8) | collective-permute-done | bytes 524320 | tf_op jit(solution)/shard_map/ppermute | solution.py:362
  172.9 5.5 %collective-permute-done.9 = f32[2,256,128]{2,1,0:T(8,128)S(1)} collective-permute-done((f32[2,256,128]{2,1,0:T(8,128)S(1)}, f32[2,256,128]{2,1,0:T(8,128)S(1)}, u32[]{:S(2)}, u32[]{:S(2)}) %collective-permute-start.9) | collective-permute-done | bytes 262176 | tf_op jit(solution)/shard_map/ppermute | solution.py:370
  178.4 6.4 %collective-permute-done.11 = f32[2,256,128]{2,1,0:T(8,128)S(1)} collective-permute-done((f32[2,256,128]{2,1,0:T(8,128)S(1)}, f32[2,256,128]{2,1,0:T(8,128)S(1)}, u32[]{:S(2)}, u32[]{:S(2)}) %collective-permute-start.11) | collective-permute-done | bytes 262176 | tf_op jit(solution)/shard_map/ppermute | solution.py:370
  187.3 5.6 %all-to-all-start.7 = ((f32[8,64,256]{2,1,0:T(8,128)}), f32[8,64,256]{2,1,0:T(8,128)S(1)}, u32[]{:S(2)}, u32[]{:S(2)}) async-start(f32[8,64,256]{2,1,0:T(8,128)} %student_end.1), calls=%async_computation.7 | async-start | bytes 1048576 | tf_op jit(solution)/shard_map/all_to_all | solution.py:34
  195.1 3.9 %collective-permute-done.12.refs_1_ = f32[256,128]{1,0:T(8,128)S(1)} collective-permute-done((f32[256,128]{1,0:T(8,128)S(1)}, f32[256,128]{1,0:T(8,128)S(1)}, u32[]{:S(2)}, u32[]{:S(2)}) %collective-permute-start.12) | collective-permute-done | bytes 131104 | tf_op jit(solution)/shard_map/ppermute | solution.py:378
  (50 shorter events, 28.6 us)
Async XLA Ops:
  3.8 14.5 %collective-permute-start.1 = (f32[512,256]{1,0:T(8,128)}, f32[512,256]{1,0:T(8,128)S(1)}, u32[]{:S(2)}, u32[]{:S(2)}) collective-permute-start(f32[512,256]{1,0:T(8,128)} %get-tuple-element.32), channel_id=1, source_target_pairs={{0,192},{64,0},{128,64},{192,128},{1,193},{65,1},{129,65},{193,129... | collective-permute-start | bytes 1572872 | tf_op jit(solution)/shard_map/ppermute | solution.py:589
  7.3 14.3 %collective-permute-start = (f32[512,256]{1,0:T(8,128)}, f32[512,256]{1,0:T(8,128)S(1)}, u32[]{:S(2)}, u32[]{:S(2)}) collective-permute-start(f32[512,256]{1,0:T(8,128)} %get-tuple-element.32), channel_id=1, source_target_pairs={{0,64},{64,128},{128,192},{192,0},{1,65},{65,129},{129,193},{193,1... | collective-permute-start | bytes 1572872 | tf_op jit(solution)/shard_map/ppermute | solution.py:589
  18.2 7.4 %collective-permute-start.3 = (f32[256,256]{1,0:T(8,128)S(1)}, f32[256,256]{1,0:T(8,128)S(1)}, u32[]{:S(2)}, u32[]{:S(2)}) collective-permute-start(f32[256,256]{1,0:T(8,128)S(1)} %slice.73), channel_id=1, source_target_pairs={{0,192},{64,0},{128,64},{192,128},{1,193},{65,1},{129,65},{193,129... | collective-permute-start | bytes 786440 | tf_op jit(solution)/shard_map/ppermute | solution.py:589
  21.6 7.3 %collective-permute-start.2 = (f32[256,256]{1,0:T(8,128)S(1)}, f32[256,256]{1,0:T(8,128)S(1)}, u32[]{:S(2)}, u32[]{:S(2)}) collective-permute-start(f32[256,256]{1,0:T(8,128)S(1)} %slice.72), channel_id=1, source_target_pairs={{0,64},{64,128},{128,192},{192,0},{1,65},{65,129},{129,193},{193,1... | collective-permute-start | bytes 786440 | tf_op jit(solution)/shard_map/ppermute | solution.py:589
  21.7 16.0 %collective-permute-start.5 = (f32[512,256]{1,0:T(8,128)S(1)}, f32[512,256]{1,0:T(8,128)S(1)}, u32[]{:S(2)}, u32[]{:S(2)}) collective-permute-start(f32[512,256]{1,0:T(8,128)S(1)} %collective-permute-done.1.refs_1_), channel_id=1, source_target_pairs={{0,1},{1,0},{2,3},{3,2},{4,5},{5,4},{6,7},{7,6},{8,9},{9,8},{10,11... | collective-permute-start | bytes 1572872 | tf_op jit(solution)/shard_map/ppermute | solution.py:592
  23.7 14.1 %collective-permute-start.4 = (f32[512,256]{1,0:T(8,128)S(1)}, f32[512,256]{1,0:T(8,128)S(1)}, u32[]{:S(2)}, u32[]{:S(2)}) collective-permute-start(f32[512,256]{1,0:T(8,128)S(1)} %collective-permute-done.refs_0_), channel_id=1, source_target_pairs={{0,1},{1,0},{2,3},{3,2},{4,5},{5,4},{6,7},{7,6},{8,9},{9,8},{10,11... | collective-permute-start | bytes 1572872 | tf_op jit(solution)/shard_map/ppermute | solution.py:592
  25.7 12.1 %collective-permute-start.7 = (f32[256,256]{1,0:T(8,128)S(1)}, f32[256,256]{1,0:T(8,128)S(1)}, u32[]{:S(2)}, u32[]{:S(2)}) collective-permute-start(f32[256,256]{1,0:T(8,128)S(1)} %collective-permute-done.3.refs_3_), channel_id=1, source_target_pairs={{0,1},{1,0},{2,3},{3,2},{4,5},{5,4},{6,7},{7,6},{8,9},{9,8},{10,11... | collective-permute-start | bytes 786440 | tf_op jit(solution)/shard_map/ppermute | solution.py:592
  28.9 8.9 %collective-permute-start.6 = (f32[256,256]{1,0:T(8,128)S(1)}, f32[256,256]{1,0:T(8,128)S(1)}, u32[]{:S(2)}, u32[]{:S(2)}) collective-permute-start(f32[256,256]{1,0:T(8,128)S(1)} %collective-permute-done.2.refs_2_), channel_id=1, source_target_pairs={{0,1},{1,0},{2,3},{3,2},{4,5},{5,4},{6,7},{7,6},{8,9},{9,8},{10,11... | collective-permute-start | bytes 786440 | tf_op jit(solution)/shard_map/ppermute | solution.py:592
  45.3 71.3 %copy-start = (bf16[16,2048,128]{2,1,0:T(8,128)(2,1)}, bf16[16,2048,128]{2,1,0:T(8,128)(2,1)S(1)}, u32[]{:S(2)}) copy-start(bf16[16,2048,128]{2,1,0:T(8,128)(2,1)S(1)} %get-tuple-element.42.energy_ref) | copy-start | bytes 25165828
  116.6 8.0 %copy-start.5 = (s32[1,8]{1,0:T(1,128)S(1)}, s32[1,8]{1,0:T(1,128)}, u32[]{:S(2)}) copy-start(s32[1,8]{1,0:T(1,128)} %constant.86) | copy-start | bytes 100
  116.6 8.0 %copy-start.6 = (s32[1,8]{1,0:T(1,128)S(1)}, s32[1,8]{1,0:T(1,128)}, u32[]{:S(2)}) copy-start(s32[1,8]{1,0:T(1,128)} %constant.85) | copy-start | bytes 100
  119.5 15.4 %all-to-all-start.5 = ((f32[32,24,128]{2,1,0:T(8,128)}), f32[32,24,128]{2,1,0:T(8,128)S(1)}, u32[]{:S(2)}, u32[]{:S(2)}) async-start(f32[32,24,128]{2,1,0:T(8,128)} %get-tuple-element.47), calls=%async_computation.5 | async-start | bytes 786432 | tf_op jit(solution)/shard_map/all_to_all | solution.py:34
  134.8 3.4 %copy-start.1 = (bf16[16,2048,128]{2,1,0:T(8,128)(2,1)S(1)}, bf16[16,2048,128]{2,1,0:T(8,128)(2,1)}, u32[]{:S(2)}) copy-start(bf16[16,2048,128]{2,1,0:T(8,128)(2,1)} %copy-done) | copy-start | bytes 25165828
  149.8 1.3 copy-start.2
  151.2 0.8 copy-start.3
  152.0 0.8 copy-start.4
  152.8 32.1 %all-to-all-start.6 = ((f32[32,64,256]{2,1,0:T(8,128)}), f32[32,64,256]{2,1,0:T(8,128)S(1)}, u32[]{:S(2)}, u32[]{:S(2)}) async-start(f32[32,64,256]{2,1,0:T(8,128)} %bitcast.19), calls=%async_computation.6 | async-start | bytes 4194304 | tf_op jit(solution)/shard_map/all_to_all | solution.py:34
  156.8 13.5 %collective-permute-start.8 = (f32[4,256,128]{2,1,0:T(8,128)}, f32[4,256,128]{2,1,0:T(8,128)S(1)}, u32[]{:S(2)}, u32[]{:S(2)}) collective-permute-start(f32[4,256,128]{2,1,0:T(8,128)} %copy-done.4), channel_id=1, source_target_pairs={{0,8},{8,0},{16,24},{24,16},{32,40},{40,32},{48,56},{56,48},{1,9},... | collective-permute-start | bytes 1572872 | tf_op jit(solution)/shard_map/ppermute | solution.py:362
  157.1 14.3 %collective-permute-start.10 = (f32[4,256,128]{2,1,0:T(8,128)}, f32[4,256,128]{2,1,0:T(8,128)S(1)}, u32[]{:S(2)}, u32[]{:S(2)}) collective-permute-start(f32[4,256,128]{2,1,0:T(8,128)} %copy-done.3), channel_id=1, source_target_pairs={{0,56},{8,16},{16,8},{24,32},{32,24},{40,48},{48,40},{56,0},{1,57}... | collective-permute-start | bytes 1572872 | tf_op jit(solution)/shard_map/ppermute | solution.py:362
  170.3 8.1 %collective-permute-start.9 = (f32[2,256,128]{2,1,0:T(8,128)S(1)}, f32[2,256,128]{2,1,0:T(8,128)S(1)}, u32[]{:S(2)}, u32[]{:S(2)}) collective-permute-start(f32[2,256,128]{2,1,0:T(8,128)S(1)} %slice_add_fusion.1), channel_id=1, source_target_pairs={{0,48},{8,24},{16,0},{24,40},{32,16},{40,56},{48,32},{56,8},{1,49}... | collective-permute-start | bytes 786440 | tf_op jit(solution)/shard_map/ppermute | solution.py:370
  171.4 13.4 %collective-permute-start.11 = (f32[2,256,128]{2,1,0:T(8,128)S(1)}, f32[2,256,128]{2,1,0:T(8,128)S(1)}, u32[]{:S(2)}, u32[]{:S(2)}) collective-permute-start(f32[2,256,128]{2,1,0:T(8,128)S(1)} %slice_add_fusion), channel_id=1, source_target_pairs={{0,16},{8,56},{16,32},{24,8},{32,48},{40,24},{48,0},{56,40},{1,17}... | collective-permute-start | bytes 786440 | tf_op jit(solution)/shard_map/ppermute | solution.py:370
  187.3 15.1 %all-to-all-start.7 = ((f32[8,64,256]{2,1,0:T(8,128)}), f32[8,64,256]{2,1,0:T(8,128)S(1)}, u32[]{:S(2)}, u32[]{:S(2)}) async-start(f32[8,64,256]{2,1,0:T(8,128)} %student_end.1), calls=%async_computation.7 | async-start | bytes 1048576 | tf_op jit(solution)/shard_map/all_to_all | solution.py:34
  192.9 6.1 %collective-permute-start.12 = (f32[256,128]{1,0:T(8,128)S(1)}, f32[256,128]{1,0:T(8,128)S(1)}, u32[]{:S(2)}, u32[]{:S(2)}) collective-permute-start(f32[256,128]{1,0:T(8,128)S(1)} %get-tuple-element.57), channel_id=1, source_target_pairs={{0,56},{8,16},{16,8},{24,32},{32,24},{40,48},{48,40},{56,0},{1,57}... | collective-permute-start | bytes 393224 | tf_op jit(solution)/shard_map/ppermute | solution.py:378
  195.1 4.8 %collective-permute-start.13 = (f32[256,128]{1,0:T(8,128)S(1)}, f32[256,128]{1,0:T(8,128)S(1)}, u32[]{:S(2)}, u32[]{:S(2)}) collective-permute-start(f32[256,128]{1,0:T(8,128)S(1)} %get-tuple-element.59), channel_id=1, source_target_pairs={{0,8},{8,0},{16,24},{24,16},{32,40},{40,32},{48,56},{56,48},{1,9},... | collective-permute-start | bytes 393224 | tf_op jit(solution)/shard_map/ppermute | solution.py:378

commit v4 on v3

--- a/solution.py
+++ b/solution.py
@@ -390,10 +390,14 @@
     send_right_ref,
     keep_left_ref,
     keep_right_ref,
-    feature_ref,
+    feature_out_ref,
     r_ref,
     n_ref,
     total_ref,
+    feature_ref,
+    stage_ref,
+    sems,
+    feature_sems,
 ):
     step = pl.program_id(0)
     tiles = energy_ref.shape[0]
@@ -429,6 +433,13 @@
         return nt_dot(sw, units_ref[part, D:])
 
     parts = [slice(c, c + WIDE) for c in range(0, units_ref.shape[0], WIDE)]
+
+    def feature_copy(i):
+        rows = pl.ds(i * WIDE, WIDE)
+        return pltpu.make_async_copy(
+            feature_ref.at[rows, :], feature_out_ref.at[rows, :], feature_sems.at[i]
+        )
+
     logits = logits_of(parts[0])
     for i, part in enumerate(parts):
         following = logits_of(parts[i + 1]) if i + 1 < len(parts) else None
@@ -445,40 +456,58 @@
         feature_ref[part, :] += lax.dot_general(
             logit_grad, sw, (((0,), (0,)), ((), ())), preferred_element_type=f32
         )
+        pl.when(step == pl.num_programs(0) - 1)(feature_copy(i).start)
         logits = following
+
+    def copies(which, at):
+        found = []
+        for half, (sent_ref, kept_ref) in enumerate(
+            ((send_left_ref, keep_left_ref), (send_right_ref, keep_right_ref))
+        ):
+            block_at = 2 * at + which
+            place = table_ref[1 + half, block_at]
+            source, sem = stage_ref.at[half, block_at], sems.at[half, block_at]
+            sent = pltpu.make_async_copy(source, sent_ref.at[jnp.minimum(place, 3)], sem)
+            kept = pltpu.make_async_copy(source, kept_ref.at[jnp.maximum(place - 4, 0)], sem)
+            found += [(place < 4, sent), (place >= 4, kept)]
+        return found
 
     for which in range(2):
         rows_here = slice(which * block, (which + 1) * block)
-        for row, columns_here, sent_ref, kept_ref in (
-            (1, slice(0, D // 2), send_left_ref, keep_left_ref),
-            (2, slice(D // 2, D), send_right_ref, keep_right_ref),
-        ):
-            place = table_ref[row, 2 * step + which]
-
-            @pl.when(place < 4)
-            def _():
-                sent_ref[jnp.minimum(place, 3)] = total_ref[rows_here, columns_here]
-
-            @pl.when(place >= 4)
-            def _():
-                kept_ref[jnp.maximum(place - 4, 0)] = total_ref[rows_here, columns_here]
-
-
-def gradients(y, z, units_all, energy, pieces, student_protos, scale):
+        for half in range(2):
+            columns_here = slice(half * (D // 2), (half + 1) * (D // 2))
+            stage_ref[half, 2 * step + which] = total_ref[rows_here, columns_here]
+        for wanted, copy in copies(which, step):
+            pl.when(wanted)(copy.start)
+
+    @pl.when(step == pl.num_programs(0) - 1)
+    def _():
+        for i in range(len(parts)):
+            feature_copy(i).wait()
+        for at in range(stage_ref.shape[1] // 2):
+            for which in range(2):
+                for wanted, copy in copies(which, at):
+                    pl.when(wanted)(copy.wait)
+
+
+def block_table(y, z):
+    blocks = len(LEFT_PLACE)
+    way = jnp.where(z % 2 == 1, 1, -1)
+    local = (z + way * jnp.arange(blocks) + blocks) % blocks
+    table = [y * blocks + local, jnp.array(LEFT_PLACE), jnp.array(RIGHT_PLACE), local]
+    return jnp.stack(table).astype(jnp.int32)
+
+
+def gradients(table, units_all, energy, pieces, student_protos, scale):
     tiles, share, _ = energy.shape
     tokens = units_all.shape[0]
     block = 256
     blocks = share // block
-    way = jnp.where(z % 2 == 1, 1, -1)
-    local = (z + way * jnp.arange(blocks) + blocks) % blocks
-    table = jnp.stack(
-        [y * blocks + local, jnp.array(LEFT_PLACE), jnp.array(RIGHT_PLACE), local]
-    ).astype(jnp.int32)
     whole = lambda *shape: pl.BlockSpec(shape, lambda i, p: (0,) * len(shape))
     first = pl.BlockSpec((block, D), lambda i, p: (p[0, 2 * i], 0))
     second = pl.BlockSpec((block, D), lambda i, p: (p[0, 2 * i + 1], 0))
     direct = pl.BlockSpec(memory_space=pltpu.VMEM)
-    half = pltpu.VMEM((blocks // 2, block, D // 2), f32)
+    half = pltpu.HBM((blocks // 2, block, D // 2), f32)
     return pl.pallas_call(
         gradient_body,
         grid_spec=pltpu.PrefetchScalarGridSpec(
@@ -492,14 +521,18 @@
                 second,
                 whole(*scale.shape),
             ],
-            out_specs=[direct] * 5,
+            out_specs=[pl.BlockSpec(memory_space=pl.ANY)] * 5,
             scratch_shapes=[
                 pltpu.VMEM((1, tokens), f32),
                 pltpu.VMEM((1, tokens), f32),
                 pltpu.VMEM((2 * block, D), f32),
+                pltpu.VMEM((tokens, D), f32),
+                pltpu.VMEM((2, blocks, block, D // 2), f32),
+                pltpu.SemaphoreType.DMA((2, blocks)),
+                pltpu.SemaphoreType.DMA((tokens // WIDE,)),
             ],
         ),
-        out_shape=[half, half, half, half, pltpu.VMEM((tokens, D), f32)],
+        out_shape=[half, half, half, half, pltpu.HBM((tokens, D), f32)],
         compiler_params=params(24),
         cost_estimate=work(8 * tokens * share * D, 8 * 2**20, tokens * share),
         name="gradients",
@@ -592,11 +625,12 @@
     from_core = lambda value: lax.ppermute(value, "core", [(0, 1), (1, 0)])
     half = mine.shape[0] // 2
     first, third = from_y(mine, 1), from_y(mine, 3)
+    norm_part = student_sums(units, student_protos)
+    norm_part, first, third = lax.optimization_barrier((norm_part, first, third))
     got = [first, third, from_y(first[:half], 1), from_y(third[half:], 3)]
     got = got + [from_core(piece) for piece in got]
-    norm_part = student_sums(units, student_protos)
-    norm_part, got = lax.optimization_barrier((norm_part, got))
-
+
+    table = block_table(y, z)
     rows = ("y",) + PROTOS
     peers = y_size * proto_size
     energy, sums, units_all = energy_of(place, units, got, teacher_protos, share, z_size)
@@ -605,11 +639,12 @@
             sums = column_sums(energy, pieces, z_size)
         norms = (norm_part,) if sweep == ITERS - 1 else ()
         col_scale, row_part = row_sums(energy, spread(sums, "z"), peers, norms)
+        row_part, place, table = lax.optimization_barrier((row_part, place, table))
         pieces = spread(row_part, rows)
     pieces = pieces.reshape((y_size, proto_size) + pieces.shape[1:])
 
     send_left, send_right, keep_left, keep_right, feature_part = gradients(
-        y, z, units_all, energy, pieces, student_protos, col_scale
+        table, units_all, energy, pieces, student_protos, col_scale
     )
     left = pass_on(collect(send_left, keep_left, 0), 0)
     right_half = pass_on(collect(send_right, keep_right, 1), 1)

time: 204 us -> 200 us (0.980)
  waiting for transfers between devices: 54.4 us -> 48.7 us
    ppermute x4, waiting for transfers between devices: 13.6 us -> 9.71 us  [on_device(): lax.ppermute(value, 'y', [(i, (i + step) % y_size) for i in range(y_size)])]
    all_to_all x3, starting transfers between devices: 14.7 us -> 18 us  [spread(): return lax.all_to_all(value, axes, 0, 0, tiled=True)]
    all_to_all x3, waiting for transfers between devices: 10.3 us -> 7.19 us  [spread(): return lax.all_to_all(value, axes, 0, 0, tiled=True)]
    unnamed x15 -> x17, local copies, waits for them, and re-layouts: 7.13 us -> 7.47 us
where the time goes in v4:
time: 200 us; the launch traced here: 199 us
  blocking collectives  62.7 us (31%)
  waiting for transfers between devices  48.7 us (24%)
  Pallas kernels  44.4 us (22%)
  starting transfers between devices  34.5 us (17%)
  local copies, waits for them, and re-layouts  7.59 us (4%)
    all_to_all x5, blocking collectives, spread(): return lax.all_to_all(value, axes, 0, 0, tiled=True)  62.7 us
    all_to_all x3, starting transfers between devices, spread(): return lax.all_to_all(value, axes, 0, 0, tiled=True)  18 us
    ppermute x2, waiting for transfers between devices, collect(): got = lax.ppermute(send, 'z', [(z, (z - way[z]) % n) for z in range(n)])  13.8 us
    pallas_call x1, Pallas kernels, gradients(): pl.pallas_call(gradient_body, grid_spec=pltpu.PrefetchScalarGridSpec(num_...  12.4 us
    ppermute x2, waiting for transfers between devices, pass_on(): got = lax.ppermute(far, 'z', [(z, (z + 2 * way[z]) % n) for z in range(n)])  11.9 us
    ppermute x4, waiting for transfers between devices, on_device(): lax.ppermute(value, 'y', [(i, (i + step) % y_size) for i in range(y_size)])  9.71 us
    pallas_call x1, Pallas kernels, energy_of(): pl.pallas_call(energy_body, grid_spec=pltpu.PrefetchScalarGridSpec(num_sc...  7.52 us
    unnamed x17, local copies, waits for them, and re-layouts  7.47 us
  transfers between devices with their start and end apart: 17, of which 11 were waited for; matrix products, arithmetic and copies ran while one was open for 0% of the time, Pallas kernels for 4%

profile of v4, /device:TPU:1, one launch (start us, length us, event | category | flops | bytes accessed | tf_op | source)
XLA Modules:
  0.0 198.9 jit_solution(18370900937895658521)
XLA Ops:
  0.8 3.0 %select.31 = (f32[512,512]{1,0:T(8,128)}, f32[512,1]{1,0:T(8,128)}, f32[512,256]{1,0:T(8,128)}) custom-call(s32[8]{0:T(128)S(1)} %stack.46.place_ref, bf16[4,256,256]{2,1,0:T(8,128)(2,1)} %teacher_ref.1, bf16[4,256,256]{2,1,0:T(8,128)(2,1)} %student_ref.1, s32[4,256]{1,0:T(4,128)} %order_ref.1), custom_call_target="tpu_custom_call" | custom-call | tf_op jit(solution)/shard_map/select/pallas_call | solution.py:98
  3.8 3.6 %collective-permute-start.1 = (f32[512,256]{1,0:T(8,128)}, f32[512,256]{1,0:T(8,128)S(1)}, u32[]{:S(2)}, u32[]{:S(2)}) collective-permute-start(f32[512,256]{1,0:T(8,128)} %get-tuple-element.35), channel_id=1, source_target_pairs={{0,192},{64,0},{128,64},{192,128},{1,193},{65,1},{129,65},{193,129... | collective-permute-start | bytes 1572872 | tf_op jit(solution)/shard_map/ppermute | solution.py:622
  7.3 6.1 %student.1.refs_0_ = f32[4,128]{1,0:T(4,128)S(1)} custom-call(f32[512,512]{1,0:T(8,128)} %get-tuple-element.34.units_ref.unit_ref, bf16[8192,256]{1,0:T(8,128)(2,1)} %refs_4_.1), custom_call_target="tpu_custom_call" | custom-call | flops 4294967296 | bytes 8388608 | tf_op jit(solution)/shard_map/student/pallas_call | solution.py:261
  13.4 4.8 %collective-permute-done.1.refs_1_ = f32[512,256]{1,0:T(8,128)S(1)} collective-permute-done((f32[512,256]{1,0:T(8,128)}, f32[512,256]{1,0:T(8,128)S(1)}, u32[]{:S(2)}, u32[]{:S(2)}) %collective-permute-start.1) | collective-permute-done | bytes 524320 | tf_op jit(solution)/shard_map/ppermute | solution.py:622
  18.2 3.0 %collective-permute-done.refs_0_ = f32[512,256]{1,0:T(8,128)S(1)} collective-permute-done((f32[512,256]{1,0:T(8,128)}, f32[512,256]{1,0:T(8,128)S(1)}, u32[]{:S(2)}, u32[]{:S(2)}) %collective-permute-start) | collective-permute-done | bytes 524320 | tf_op jit(solution)/shard_map/ppermute | solution.py:622
  22.9 2.4 %collective-permute-start.4 = (f32[512,256]{1,0:T(8,128)S(1)}, f32[512,256]{1,0:T(8,128)S(1)}, u32[]{:S(2)}, u32[]{:S(2)}) collective-permute-start(f32[512,256]{1,0:T(8,128)S(1)} %collective-permute-done.refs_0_), channel_id=1, source_target_pairs={{0,1},{1,0},{2,3},{3,2},{4,5},{5,4},{6,7},{7,6},{8,9},{9,8},{10,11... | collective-permute-start | bytes 1572872 | tf_op jit(solution)/shard_map/ppermute | solution.py:625
  27.2 2.8 %collective-permute-start.7 = (f32[256,256]{1,0:T(8,128)S(1)}, f32[256,256]{1,0:T(8,128)S(1)}, u32[]{:S(2)}, u32[]{:S(2)}) collective-permute-start(f32[256,256]{1,0:T(8,128)S(1)} %collective-permute-done.3.refs_3_), channel_id=1, source_target_pairs={{0,1},{1,0},{2,3},{3,2},{4,5},{5,4},{6,7},{7,6},{8,9},{9,8},{10,11... | collective-permute-start | bytes 786440 | tf_op jit(solution)/shard_map/ppermute | solution.py:625
  32.8 7.5 %energy.1 = (bf16[16,2048,128]{2,1,0:T(8,128)(2,1)S(1)}, f32[8,16,128]{2,1,0:T(8,128)}, bf16[2048,512]{1,0:T(8,128)(2,1)}) custom-call(s32[8]{0:T(128)S(1)} %stack.46.place_ref, f32[512,512]{1,0:T(8,128)} %get-tuple-element.34.units_ref.unit_ref, f32[512,256]{1,0:T(8,128)S(1)} %collective-permute-done.refs_0_, ...), custom_call_target="tpu_custom_call" | custom-call | flops 4294967296 | bytes 8388608 | tf_op jit(solution)/shard_map/energy/pallas_call | solution.py:204
  40.4 3.3 %copy-done = bf16[16,2048,128]{2,1,0:T(8,128)(2,1)} copy-done((bf16[16,2048,128]{2,1,0:T(8,128)(2,1)}, bf16[16,2048,128]{2,1,0:T(8,128)(2,1)S(1)}, u32[]{:S(2)}) %copy-start) | copy-done | bytes 8388632
  43.6 8.2 %all-to-all-start = ((f32[8,16,128]{2,1,0:T(8,128)}), f32[8,16,128]{2,1,0:T(8,128)S(1)}, u32[]{:S(2)}, u32[]{:S(2)}) async-start(f32[8,16,128]{2,1,0:T(8,128)} %get-tuple-element.39), calls=%async_computation | async-start | bytes 131072 | tf_op jit(solution)/shard_map/all_to_all | solution.py:34
  51.8 7.2 %all-to-all-done.pieces_ref = f32[8,16,128]{2,1,0:T(8,128)S(1)} async-done(((f32[8,16,128]{2,1,0:T(8,128)}), f32[8,16,128]{2,1,0:T(8,128)S(1)}, u32[]{:S(2)}, u32[]{:S(2)}) %all-to-all-start) | async-done | bytes 65568 | tf_op jit(solution)/shard_map/all_to_all | solution.py:34
  59.0 3.4 %copy-done.1 = bf16[16,2048,128]{2,1,0:T(8,128)(2,1)S(1)} copy-done((bf16[16,2048,128]{2,1,0:T(8,128)(2,1)S(1)}, bf16[16,2048,128]{2,1,0:T(8,128)(2,1)}, u32[]{:S(2)}) %copy-start.1) | copy-done | bytes 8388632
  64.6 15.0 %all_to_all.40.pieces_ref = f32[32,16,128]{2,1,0:T(8,128)S(1)} all-to-all(f32[32,16,128]{2,1,0:T(8,128)S(1)} %get-tuple-element.41), channel_id=1, replica_groups=mesh['y'=4,'z'=8,'x'=4,'core'=2] {'y','x','core'}, dimensions={0} | all-to-all | bytes 524288 | tf_op jit(solution)/shard_map/all_to_all | solution.py:34
  81.7 9.5 %all_to_all.41.pieces_ref = f32[8,16,128]{2,1,0:T(8,128)S(1)} all-to-all(f32[8,16,128]{2,1,0:T(8,128)S(1)} %column_sums.2), channel_id=1, replica_groups=mesh['y'=4,'z'=8,'x'=4,'core'=2] {'z'}, dimensions={0} | all-to-all | bytes 131072 | tf_op jit(solution)/shard_map/all_to_all | solution.py:34
  93.4 13.7 %all_to_all.42.pieces_ref = f32[32,16,128]{2,1,0:T(8,128)S(1)} all-to-all(f32[32,16,128]{2,1,0:T(8,128)S(1)} %get-tuple-element.45), channel_id=1, replica_groups=mesh['y'=4,'z'=8,'x'=4,'core'=2] {'y','x','core'}, dimensions={0} | all-to-all | bytes 524288 | tf_op jit(solution)/shard_map/all_to_all | solution.py:34
  109.2 9.5 %all_to_all.43.pieces_ref = f32[8,16,128]{2,1,0:T(8,128)S(1)} all-to-all(f32[8,16,128]{2,1,0:T(8,128)S(1)} %column_sums.3), channel_id=1, replica_groups=mesh['y'=4,'z'=8,'x'=4,'core'=2] {'z'}, dimensions={0} | all-to-all | bytes 131072 | tf_op jit(solution)/shard_map/all_to_all | solution.py:34
  120.8 15.0 %all_to_all.44 = f32[32,24,128]{2,1,0:T(8,128)S(1)} all-to-all(f32[32,24,128]{2,1,0:T(8,128)S(1)} %get-tuple-element.53), channel_id=1, replica_groups=mesh['y'=4,'z'=8,'x'=4,'core'=2] {'y','x','core'}, dimensions={0} | all-to-all | bytes 786432 | tf_op jit(solution)/shard_map/all_to_all | solution.py:34
  135.7 12.4 %gradients.1 = (f32[4,256,128]{2,1,0:T(8,128)}, f32[4,256,128]{2,1,0:T(8,128)}, f32[4,256,128]{2,1,0:T(8,128)}, f32[4,256,128]{2,1,0:T(8,128)}, f32[2048,256]{1,0:T(8,128)}) custom-call(s32[4,8]{1,0:T(4,128)S(1)} %pad_add_fusion.table_ref, bf16[2048,512]{1,0:T(8,128)(2,1)} %get-tuple-element.52.units_ref, bf16[16,2048,128]{2,1,0:T(8,128)(2,1)S(1)} %bitcast.20, ...), custom_call_target="tpu_custom_call" | custom-call | flops 8589934592 | bytes 8388608 | tf_op jit(solution)/shard_map/gradients/pallas_call | solution.py:511
  148.2 4.2 %all-to-all-start.6 = ((f32[32,64,256]{2,1,0:T(8,128)}), f32[32,64,256]{2,1,0:T(8,128)S(1)}, u32[]{:S(2)}, u32[]{:S(2)}) async-start(f32[32,64,256]{2,1,0:T(8,128)} %bitcast.22), calls=%async_computation.6 | async-start | bytes 4194304 | tf_op jit(solution)/shard_map/all_to_all | solution.py:34
  152.9 13.0 %collective-permute-done.8 = f32[4,256,128]{2,1,0:T(8,128)S(1)} collective-permute-done((f32[4,256,128]{2,1,0:T(8,128)}, f32[4,256,128]{2,1,0:T(8,128)S(1)}, u32[]{:S(2)}, u32[]{:S(2)}) %collective-permute-start.8) | collective-permute-done | bytes 524320 | tf_op jit(solution)/shard_map/ppermute | solution.py:362
  168.4 5.8 %collective-permute-done.9 = f32[2,256,128]{2,1,0:T(8,128)S(1)} collective-permute-done((f32[2,256,128]{2,1,0:T(8,128)S(1)}, f32[2,256,128]{2,1,0:T(8,128)S(1)}, u32[]{:S(2)}, u32[]{:S(2)}) %collective-permute-start.9) | collective-permute-done | bytes 262176 | tf_op jit(solution)/shard_map/ppermute | solution.py:370
  174.3 6.1 %collective-permute-done.11 = f32[2,256,128]{2,1,0:T(8,128)S(1)} collective-permute-done((f32[2,256,128]{2,1,0:T(8,128)S(1)}, f32[2,256,128]{2,1,0:T(8,128)S(1)}, u32[]{:S(2)}, u32[]{:S(2)}) %collective-permute-start.11) | collective-permute-done | bytes 262176 | tf_op jit(solution)/shard_map/ppermute | solution.py:370
  182.9 5.6 %all-to-all-start.7 = ((f32[8,64,256]{2,1,0:T(8,128)}), f32[8,64,256]{2,1,0:T(8,128)S(1)}, u32[]{:S(2)}, u32[]{:S(2)}) async-start(f32[8,64,256]{2,1,0:T(8,128)} %student_end.1), calls=%async_computation.7 | async-start | bytes 1048576 | tf_op jit(solution)/shard_map/all_to_all | solution.py:34
  190.9 3.8 %collective-permute-done.12.refs_1_ = f32[256,128]{1,0:T(8,128)S(1)} collective-permute-done((f32[256,128]{1,0:T(8,128)S(1)}, f32[256,128]{1,0:T(8,128)S(1)}, u32[]{:S(2)}, u32[]{:S(2)}) %collective-permute-start.12) | collective-permute-done | bytes 131104 | tf_op jit(solution)/shard_map/ppermute | solution.py:378
  (53 shorter events, 29.4 us)
Async XLA Ops:
  3.8 14.5 %collective-permute-start.1 = (f32[512,256]{1,0:T(8,128)}, f32[512,256]{1,0:T(8,128)S(1)}, u32[]{:S(2)}, u32[]{:S(2)}) collective-permute-start(f32[512,256]{1,0:T(8,128)} %get-tuple-element.35), channel_id=1, source_target_pairs={{0,192},{64,0},{128,64},{192,128},{1,193},{65,1},{129,65},{193,129... | collective-permute-start | bytes 1572872 | tf_op jit(solution)/shard_map/ppermute | solution.py:622
  7.3 13.9 %collective-permute-start = (f32[512,256]{1,0:T(8,128)}, f32[512,256]{1,0:T(8,128)S(1)}, u32[]{:S(2)}, u32[]{:S(2)}) collective-permute-start(f32[512,256]{1,0:T(8,128)} %get-tuple-element.35), channel_id=1, source_target_pairs={{0,64},{64,128},{128,192},{192,0},{1,65},{65,129},{129,193},{193,1... | collective-permute-start | bytes 1572872 | tf_op jit(solution)/shard_map/ppermute | solution.py:622
  21.2 6.0 %collective-permute-start.3 = (f32[256,256]{1,0:T(8,128)S(1)}, f32[256,256]{1,0:T(8,128)S(1)}, u32[]{:S(2)}, u32[]{:S(2)}) collective-permute-start(f32[256,256]{1,0:T(8,128)S(1)} %slice.55), channel_id=1, source_target_pairs={{0,192},{64,0},{128,64},{192,128},{1,193},{65,1},{129,65},{193,129... | collective-permute-start | bytes 786440 | tf_op jit(solution)/shard_map/ppermute | solution.py:622
  21.6 8.4 %collective-permute-start.2 = (f32[256,256]{1,0:T(8,128)S(1)}, f32[256,256]{1,0:T(8,128)S(1)}, u32[]{:S(2)}, u32[]{:S(2)}) collective-permute-start(f32[256,256]{1,0:T(8,128)S(1)} %slice.54), channel_id=1, source_target_pairs={{0,64},{64,128},{128,192},{192,0},{1,65},{65,129},{129,193},{193,1... | collective-permute-start | bytes 786440 | tf_op jit(solution)/shard_map/ppermute | solution.py:622
  22.9 10.0 %collective-permute-start.4 = (f32[512,256]{1,0:T(8,128)S(1)}, f32[512,256]{1,0:T(8,128)S(1)}, u32[]{:S(2)}, u32[]{:S(2)}) collective-permute-start(f32[512,256]{1,0:T(8,128)S(1)} %collective-permute-done.refs_0_), channel_id=1, source_target_pairs={{0,1},{1,0},{2,3},{3,2},{4,5},{5,4},{6,7},{7,6},{8,9},{9,8},{10,11... | collective-permute-start | bytes 1572872 | tf_op jit(solution)/shard_map/ppermute | solution.py:625
  25.3 7.5 %collective-permute-start.5 = (f32[512,256]{1,0:T(8,128)S(1)}, f32[512,256]{1,0:T(8,128)S(1)}, u32[]{:S(2)}, u32[]{:S(2)}) collective-permute-start(f32[512,256]{1,0:T(8,128)S(1)} %collective-permute-done.1.refs_1_), channel_id=1, source_target_pairs={{0,1},{1,0},{2,3},{3,2},{4,5},{5,4},{6,7},{7,6},{8,9},{9,8},{10,11... | collective-permute-start | bytes 1572872 | tf_op jit(solution)/shard_map/ppermute | solution.py:625
  27.2 4.4 %collective-permute-start.7 = (f32[256,256]{1,0:T(8,128)S(1)}, f32[256,256]{1,0:T(8,128)S(1)}, u32[]{:S(2)}, u32[]{:S(2)}) collective-permute-start(f32[256,256]{1,0:T(8,128)S(1)} %collective-permute-done.3.refs_3_), channel_id=1, source_target_pairs={{0,1},{1,0},{2,3},{3,2},{4,5},{5,4},{6,7},{7,6},{8,9},{9,8},{10,11... | collective-permute-start | bytes 786440 | tf_op jit(solution)/shard_map/ppermute | solution.py:625
  30.0 2.8 %collective-permute-start.6 = (f32[256,256]{1,0:T(8,128)S(1)}, f32[256,256]{1,0:T(8,128)S(1)}, u32[]{:S(2)}, u32[]{:S(2)}) collective-permute-start(f32[256,256]{1,0:T(8,128)S(1)} %collective-permute-done.2.refs_2_), channel_id=1, source_target_pairs={{0,1},{1,0},{2,3},{3,2},{4,5},{5,4},{6,7},{7,6},{8,9},{9,8},{10,11... | collective-permute-start | bytes 786440 | tf_op jit(solution)/shard_map/ppermute | solution.py:625
  31.7 20.2 %copy-start.4 = (s32[1,8]{1,0:T(1,128)S(1)}, s32[1,8]{1,0:T(1,128)}, u32[]{:S(2)}) copy-start(s32[1,8]{1,0:T(1,128)} %constant.86) | copy-start | bytes 100
  31.7 20.2 %copy-start.5 = (s32[1,8]{1,0:T(1,128)S(1)}, s32[1,8]{1,0:T(1,128)}, u32[]{:S(2)}) copy-start(s32[1,8]{1,0:T(1,128)} %constant.85) | copy-start | bytes 100
  43.6 15.4 %all-to-all-start = ((f32[8,16,128]{2,1,0:T(8,128)}), f32[8,16,128]{2,1,0:T(8,128)S(1)}, u32[]{:S(2)}, u32[]{:S(2)}) async-start(f32[8,16,128]{2,1,0:T(8,128)} %get-tuple-element.39), calls=%async_computation | async-start | bytes 131072 | tf_op jit(solution)/shard_map/all_to_all | solution.py:34
  59.0 3.4 %copy-start.1 = (bf16[16,2048,128]{2,1,0:T(8,128)(2,1)S(1)}, bf16[16,2048,128]{2,1,0:T(8,128)(2,1)}, u32[]{:S(2)}) copy-start(bf16[16,2048,128]{2,1,0:T(8,128)(2,1)} %copy-done) | copy-start | bytes 25165828
  107.1 28.7 %slice-start = ((s8[8388608]{0:T(1024)(128)(4,1)}), s8[4194304]{0:T(1024)(128)(4,1)S(1)}, s32[]{:S(2)}) async-start(s8[8388608]{0:T(1024)(128)(4,1)} %bitcast.19), calls=%async_computation.8 | async-start | bytes 8388608
  118.8 17.0 %slice-start.1 = ((s8[8388608]{0:T(1024)(128)(4,1)}), s8[4194304]{0:T(1024)(128)(4,1)S(1)}, s32[]{:S(2)}) async-start(s8[8388608]{0:T(1024)(128)(4,1)} %bitcast.19), calls=%async_computation.9 | async-start | bytes 8388608
  148.1 17.7 %copy-start.3 = (f32[4,256,128]{2,1,0:T(8,128)S(1)}, f32[4,256,128]{2,1,0:T(8,128)}, u32[]{:S(2)}) copy-start(f32[4,256,128]{2,1,0:T(8,128)} %get-tuple-element.56) | copy-start | bytes 1572868
  148.2 18.8 %copy-start.2 = (f32[4,256,128]{2,1,0:T(8,128)S(1)}, f32[4,256,128]{2,1,0:T(8,128)}, u32[]{:S(2)}) copy-start(f32[4,256,128]{2,1,0:T(8,128)} %get-tuple-element.58) | copy-start | bytes 1572868
  148.2 32.4 %all-to-all-start.6 = ((f32[32,64,256]{2,1,0:T(8,128)}), f32[32,64,256]{2,1,0:T(8,128)S(1)}, u32[]{:S(2)}, u32[]{:S(2)}) async-start(f32[32,64,256]{2,1,0:T(8,128)} %bitcast.22), calls=%async_computation.6 | async-start | bytes 4194304 | tf_op jit(solution)/shard_map/all_to_all | solution.py:34
  152.4 13.5 %collective-permute-start.8 = (f32[4,256,128]{2,1,0:T(8,128)}, f32[4,256,128]{2,1,0:T(8,128)S(1)}, u32[]{:S(2)}, u32[]{:S(2)}) collective-permute-start(f32[4,256,128]{2,1,0:T(8,128)} %get-tuple-element.57), channel_id=1, source_target_pairs={{0,8},{8,0},{16,24},{24,16},{32,40},{40,32},{48,56},{56,48},{1,9},... | collective-permute-start | bytes 1572872 | tf_op jit(solution)/shard_map/ppermute | solution.py:362
  152.7 14.3 %collective-permute-start.10 = (f32[4,256,128]{2,1,0:T(8,128)}, f32[4,256,128]{2,1,0:T(8,128)S(1)}, u32[]{:S(2)}, u32[]{:S(2)}) collective-permute-start(f32[4,256,128]{2,1,0:T(8,128)} %get-tuple-element.59), channel_id=1, source_target_pairs={{0,56},{8,16},{16,8},{24,32},{32,24},{40,48},{48,40},{56,0},{1,57}... | collective-permute-start | bytes 1572872 | tf_op jit(solution)/shard_map/ppermute | solution.py:362
  165.9 8.4 %collective-permute-start.9 = (f32[2,256,128]{2,1,0:T(8,128)S(1)}, f32[2,256,128]{2,1,0:T(8,128)S(1)}, u32[]{:S(2)}, u32[]{:S(2)}) collective-permute-start(f32[2,256,128]{2,1,0:T(8,128)S(1)} %slice_add_fusion.1), channel_id=1, source_target_pairs={{0,48},{8,24},{16,0},{24,40},{32,16},{40,56},{48,32},{56,8},{1,49}... | collective-permute-start | bytes 786440 | tf_op jit(solution)/shard_map/ppermute | solution.py:370
  167.0 13.4 %collective-permute-start.11 = (f32[2,256,128]{2,1,0:T(8,128)S(1)}, f32[2,256,128]{2,1,0:T(8,128)S(1)}, u32[]{:S(2)}, u32[]{:S(2)}) collective-permute-start(f32[2,256,128]{2,1,0:T(8,128)S(1)} %slice_add_fusion), channel_id=1, source_target_pairs={{0,16},{8,56},{16,32},{24,8},{32,48},{40,24},{48,0},{56,40},{1,17}... | collective-permute-start | bytes 786440 | tf_op jit(solution)/shard_map/ppermute | solution.py:370
  182.9 15.2 %all-to-all-start.7 = ((f32[8,64,256]{2,1,0:T(8,128)}), f32[8,64,256]{2,1,0:T(8,128)S(1)}, u32[]{:S(2)}, u32[]{:S(2)}) async-start(f32[8,64,256]{2,1,0:T(8,128)} %student_end.1), calls=%async_computation.7 | async-start | bytes 1048576 | tf_op jit(solution)/shard_map/all_to_all | solution.py:34
  188.5 6.1 %collective-permute-start.12 = (f32[256,128]{1,0:T(8,128)S(1)}, f32[256,128]{1,0:T(8,128)S(1)}, u32[]{:S(2)}, u32[]{:S(2)}) collective-permute-start(f32[256,128]{1,0:T(8,128)S(1)} %get-tuple-element.63), channel_id=1, source_target_pairs={{0,56},{8,16},{16,8},{24,32},{32,24},{40,48},{48,40},{56,0},{1,57}... | collective-permute-start | bytes 393224 | tf_op jit(solution)/shard_map/ppermute | solution.py:378
  190.9 4.8 %collective-permute-start.13 = (f32[256,128]{1,0:T(8,128)S(1)}, f32[256,128]{1,0:T(8,128)S(1)}, u32[]{:S(2)}, u32[]{:S(2)}) collective-permute-start(f32[256,128]{1,0:T(8,128)S(1)} %get-tuple-element.65), channel_id=1, source_target_pairs={{0,8},{8,0},{16,24},{24,16},{32,40},{40,32},{48,56},{56,48},{1,9},... | collective-permute-start | bytes 393224 | tf_op jit(solution)/shard_map/ppermute | solution.py:378
  (1 other events, 3.3 us)

commit v5 on v4

--- a/solution.py
+++ b/solution.py
@@ -390,7 +390,8 @@
     send_right_ref,
     keep_left_ref,
     keep_right_ref,
-    feature_out_ref,
+    feature_send_ref,
+    feature_keep_ref,
     r_ref,
     n_ref,
     total_ref,
@@ -434,11 +435,15 @@
 
     parts = [slice(c, c + WIDE) for c in range(0, units_ref.shape[0], WIDE)]
 
-    def feature_copy(i):
-        rows = pl.ds(i * WIDE, WIDE)
-        return pltpu.make_async_copy(
-            feature_ref.at[rows, :], feature_out_ref.at[rows, :], feature_sems.at[i]
-        )
+    def feature_copies(i):
+        size = feature_send_ref.shape[1]
+        found = []
+        for at in range(i * WIDE // size, (i + 1) * WIDE // size):
+            source, sem = feature_ref.at[pl.ds(at * size, size), :], feature_sems.at[at]
+            kept = pltpu.make_async_copy(source, feature_keep_ref.at[at // 2], sem)
+            sent = pltpu.make_async_copy(source, feature_send_ref.at[at // 2], sem)
+            found += [(table_ref[4, 0] == at % 2, kept), (table_ref[4, 0] != at % 2, sent)]
+        return found
 
     logits = logits_of(parts[0])
     for i, part in enumerate(parts):
@@ -456,7 +461,8 @@
         feature_ref[part, :] += lax.dot_general(
             logit_grad, sw, (((0,), (0,)), ((), ())), preferred_element_type=f32
         )
-        pl.when(step == pl.num_programs(0) - 1)(feature_copy(i).start)
+        for wanted, copy in feature_copies(i):
+            pl.when(jnp.logical_and(step == pl.num_programs(0) - 1, wanted))(copy.start)
         logits = following
 
     def copies(which, at):
@@ -483,22 +489,24 @@
     @pl.when(step == pl.num_programs(0) - 1)
     def _():
         for i in range(len(parts)):
-            feature_copy(i).wait()
+            for wanted, copy in feature_copies(i):
+                pl.when(wanted)(copy.wait)
         for at in range(stage_ref.shape[1] // 2):
             for which in range(2):
                 for wanted, copy in copies(which, at):
                     pl.when(wanted)(copy.wait)
 
 
-def block_table(y, z):
+def block_table(y, z, core):
     blocks = len(LEFT_PLACE)
     way = jnp.where(z % 2 == 1, 1, -1)
     local = (z + way * jnp.arange(blocks) + blocks) % blocks
-    table = [y * blocks + local, jnp.array(LEFT_PLACE), jnp.array(RIGHT_PLACE), local]
+    cores = jnp.full((blocks,), core)
+    table = [y * blocks + local, jnp.array(LEFT_PLACE), jnp.array(RIGHT_PLACE), local, cores]
     return jnp.stack(table).astype(jnp.int32)
 
 
-def gradients(table, units_all, energy, pieces, student_protos, scale):
+def gradients(table, units_all, energy, pieces, student_protos, scale, shares):
     tiles, share, _ = energy.shape
     tokens = units_all.shape[0]
     block = 256
@@ -521,7 +529,7 @@
                 second,
                 whole(*scale.shape),
             ],
-            out_specs=[pl.BlockSpec(memory_space=pl.ANY)] * 5,
+            out_specs=[pl.BlockSpec(memory_space=pl.ANY)] * 6,
             scratch_shapes=[
                 pltpu.VMEM((1, tokens), f32),
                 pltpu.VMEM((1, tokens), f32),
@@ -529,10 +537,10 @@
                 pltpu.VMEM((tokens, D), f32),
                 pltpu.VMEM((2, blocks, block, D // 2), f32),
                 pltpu.SemaphoreType.DMA((2, blocks)),
-                pltpu.SemaphoreType.DMA((tokens // WIDE,)),
+                pltpu.SemaphoreType.DMA((shares,)),
             ],
         ),
-        out_shape=[half, half, half, half, pltpu.HBM((tokens, D), f32)],
+        out_shape=[half] * 4 + [pltpu.HBM((shares // 2, tokens // shares, D), f32)] * 2,
         compiler_params=params(24),
         cost_estimate=work(8 * tokens * share * D, 8 * 2**20, tokens * share),
         name="gradients",
@@ -613,7 +621,9 @@
     y, z = lax.axis_index("y"), lax.axis_index("z")
     others = [(y - step + y_size) % y_size for step in range(y_size)]
     place = [y, y * z_size + z, lax.axis_index(PROTOS), lax.axis_index("core")] + others
-    place = jnp.stack(place).astype(jnp.int32)
+    place, table = lax.optimization_barrier(
+        (jnp.stack(place).astype(jnp.int32), block_table(y, z, lax.axis_index("core")))
+    )
     share = teacher_protos.shape[0] // y_size
 
     units, student_length, mine = select_tokens(
@@ -630,7 +640,6 @@
     got = [first, third, from_y(first[:half], 1), from_y(third[half:], 3)]
     got = got + [from_core(piece) for piece in got]
 
-    table = block_table(y, z)
     rows = ("y",) + PROTOS
     peers = y_size * proto_size
     energy, sums, units_all = energy_of(place, units, got, teacher_protos, share, z_size)
@@ -639,16 +648,19 @@
             sums = column_sums(energy, pieces, z_size)
         norms = (norm_part,) if sweep == ITERS - 1 else ()
         col_scale, row_part = row_sums(energy, spread(sums, "z"), peers, norms)
-        row_part, place, table = lax.optimization_barrier((row_part, place, table))
         pieces = spread(row_part, rows)
     pieces = pieces.reshape((y_size, proto_size) + pieces.shape[1:])
 
-    send_left, send_right, keep_left, keep_right, feature_part = gradients(
-        table, units_all, energy, pieces, student_protos, col_scale
+    send_left, send_right, keep_left, keep_right, feature_send, feature_keep = gradients(
+        table, units_all, energy, pieces, student_protos, col_scale, peers
+    )
+    feature_part = feature_keep + from_core(feature_send)
+    feature_part, keep_left, keep_right = lax.optimization_barrier(
+        (feature_part, keep_left, keep_right)
     )
     left = pass_on(collect(send_left, keep_left, 0), 0)
     right_half = pass_on(collect(send_right, keep_right, 1), 1)
-    feature_pieces = spread(feature_part.reshape(peers, -1, D), rows)
+    feature_pieces = spread(feature_part, ("y", "x"))
     feature_pieces, left, right_half = lax.optimization_barrier((feature_pieces, left, right_half))
     left, right_half = deliver(left, 0), deliver(right_half, 1)
     result = student_end(place, feature_pieces, units, student_length, proto_size)

time: 200 us -> 191 us (0.955)
  blocking collectives: 62.7 us -> 77.9 us
  waiting for transfers between devices: 48.7 us -> 37.1 us
  starting transfers between devices: 34.5 us -> 25.7 us
  local copies, waits for them, and re-layouts: 7.59 us -> 1.62 us
  other arithmetic: 0.23 us -> 2.5 us
    all_to_all x5 -> x6, blocking collectives: 62.7 us -> 77.9 us  [spread(): return lax.all_to_all(value, axes, 0, 0, tiled=True)]
    all_to_all x3 -> x2, starting transfers between devices: 18 us -> 8.9 us  [spread(): return lax.all_to_all(value, axes, 0, 0, tiled=True)]
    ppermute x2, waiting for transfers between devices: 13.8 us -> 6.3 us  [collect(): got = lax.ppermute(send, 'z', [(z, (z - way[z]) % n) for z in range(n)])]
    unnamed x17 -> x5, local copies, waits for them, and re-layouts: 7.47 us -> 0.8 us
    all_to_all x3 -> x2, waiting for transfers between devices: 7.19 us -> 0.98 us  [spread(): return lax.all_to_all(value, axes, 0, 0, tiled=True)]
    add x0 -> x1, other arithmetic: none -> 2.35 us  [on_device(): feature_part = feature_keep + from_core(feature_send)]
    ppermute x2, starting transfers between devices: 2.37 us -> 0.17 us  [deliver(): lax.ppermute(following, 'z', [(z, (z + way[z]) % n) for z in range(n)])]
    ppermute x2, starting transfers between devices: 1.63 us -> 3.7 us  [pass_on(): got = lax.ppermute(far, 'z', [(z, (z + 2 * way[z]) % n) for z in range(n)])]
  transfers between devices with their start and end apart: 17 -> 17, of which waited for: 11 -> 9; matrix products, arithmetic and copies ran while one was open for 0% -> 1% of each run, Pallas kernels for 4% -> 4%
where the time goes in v5:
time: 191 us; the launch traced here: 190 us
  blocking collectives  77.9 us (41%)
  Pallas kernels  44.3 us (23%)
  waiting for transfers between devices  37.1 us (19%)
  starting transfers between devices  25.7 us (13%)
  other arithmetic  2.5 us (1%)
    all_to_all x6, blocking collectives, spread(): return lax.all_to_all(value, axes, 0, 0, tiled=True)  77.9 us
    pallas_call x1, Pallas kernels, gradients(): pl.pallas_call(gradient_body, grid_spec=pltpu.PrefetchScalarGridSpec(num_...  12.5 us
    ppermute x2, waiting for transfers between devices, pass_on(): got = lax.ppermute(far, 'z', [(z, (z + 2 * way[z]) % n) for z in range(n)])  10.9 us
    ppermute x4, waiting for transfers between devices, on_device(): lax.ppermute(value, 'y', [(i, (i + step) % y_size) for i in range(y_size)])  9.75 us
    all_to_all x2, starting transfers between devices, spread(): return lax.all_to_all(value, axes, 0, 0, tiled=True)  8.9 us
    pallas_call x1, Pallas kernels, energy_of(): pl.pallas_call(energy_body, grid_spec=pltpu.PrefetchScalarGridSpec(num_sc...  7.42 us
    ppermute x5, starting transfers between devices, on_device(): from_core = lambda value: lax.ppermute(value, 'core', [(0, 1), (1, 0)])  7.3 us
    ppermute x2, waiting for transfers between devices, collect(): got = lax.ppermute(send, 'z', [(z, (z - way[z]) % n) for z in range(n)])  6.3 us
  transfers between devices with their start and end apart: 17, of which 9 were waited for; matrix products, arithmetic and copies ran while one was open for 1% of the time, Pallas kernels for 4%

profile of v5, /device:TPU:1, one launch (start us, length us, event | category | flops | bytes accessed | tf_op | source)
XLA Modules:
  0.0 190.0 jit_solution(14283212162713830751)
XLA Ops:
  1.5 3.0 %select.31 = (f32[512,512]{1,0:T(8,128)}, f32[512,1]{1,0:T(8,128)}, f32[512,256]{1,0:T(8,128)}) custom-call(s32[8]{0:T(128)S(1)} %stack.46.place_ref, bf16[4,256,256]{2,1,0:T(8,128)(2,1)} %teacher_ref.1, bf16[4,256,256]{2,1,0:T(8,128)(2,1)} %student_ref.1, s32[4,256]{1,0:T(4,128)} %order_ref.1), custom_call_target="tpu_custom_call" | custom-call | tf_op jit(solution)/shard_map/select/pallas_call | solution.py:98
  4.5 3.6 %collective-permute-start.1 = (f32[512,256]{1,0:T(8,128)}, f32[512,256]{1,0:T(8,128)S(1)}, u32[]{:S(2)}, u32[]{:S(2)}) collective-permute-start(f32[512,256]{1,0:T(8,128)} %get-tuple-element.34), channel_id=1, source_target_pairs={{0,192},{64,0},{128,64},{192,128},{1,193},{65,1},{129,65},{193,129... | collective-permute-start | bytes 1572872 | tf_op jit(solution)/shard_map/ppermute | solution.py:632
  8.1 6.1 %student.1.refs_0_ = f32[4,128]{1,0:T(4,128)S(1)} custom-call(f32[512,512]{1,0:T(8,128)} %get-tuple-element.33.units_ref.unit_ref, bf16[8192,256]{1,0:T(8,128)(2,1)} %refs_4_.1), custom_call_target="tpu_custom_call" | custom-call | flops 4294967296 | bytes 8388608 | tf_op jit(solution)/shard_map/student/pallas_call | solution.py:261
  14.2 4.8 %collective-permute-done.1.refs_1_ = f32[512,256]{1,0:T(8,128)S(1)} collective-permute-done((f32[512,256]{1,0:T(8,128)}, f32[512,256]{1,0:T(8,128)S(1)}, u32[]{:S(2)}, u32[]{:S(2)}) %collective-permute-start.1) | collective-permute-done | bytes 524320 | tf_op jit(solution)/shard_map/ppermute | solution.py:632
  19.0 3.0 %collective-permute-done.refs_0_ = f32[512,256]{1,0:T(8,128)S(1)} collective-permute-done((f32[512,256]{1,0:T(8,128)}, f32[512,256]{1,0:T(8,128)S(1)}, u32[]{:S(2)}, u32[]{:S(2)}) %collective-permute-start) | collective-permute-done | bytes 524320 | tf_op jit(solution)/shard_map/ppermute | solution.py:632
  23.6 2.4 %collective-permute-start.4 = (f32[512,256]{1,0:T(8,128)S(1)}, f32[512,256]{1,0:T(8,128)S(1)}, u32[]{:S(2)}, u32[]{:S(2)}) collective-permute-start(f32[512,256]{1,0:T(8,128)S(1)} %collective-permute-done.refs_0_), channel_id=1, source_target_pairs={{0,1},{1,0},{2,3},{3,2},{4,5},{5,4},{6,7},{7,6},{8,9},{9,8},{10,11... | collective-permute-start | bytes 1572872 | tf_op jit(solution)/shard_map/ppermute | solution.py:635
  28.0 2.8 %collective-permute-start.7 = (f32[256,256]{1,0:T(8,128)S(1)}, f32[256,256]{1,0:T(8,128)S(1)}, u32[]{:S(2)}, u32[]{:S(2)}) collective-permute-start(f32[256,256]{1,0:T(8,128)S(1)} %collective-permute-done.3.refs_3_), channel_id=1, source_target_pairs={{0,1},{1,0},{2,3},{3,2},{4,5},{5,4},{6,7},{7,6},{8,9},{9,8},{10,11... | collective-permute-start | bytes 786440 | tf_op jit(solution)/shard_map/ppermute | solution.py:635
  33.6 7.4 %energy.1 = (bf16[16,2048,128]{2,1,0:T(8,128)(2,1)S(1)}, f32[8,16,128]{2,1,0:T(8,128)S(1)}, bf16[2048,512]{1,0:T(8,128)(2,1)}) custom-call(s32[8]{0:T(128)S(1)} %stack.46.place_ref, f32[512,512]{1,0:T(8,128)} %get-tuple-element.33.units_ref.unit_ref, f32[512,256]{1,0:T(8,128)S(1)} %collective-permute-done.refs_0_, ...), custom_call_target="tpu_custom_call" | custom-call | flops 4294967296 | bytes 8388608 | tf_op jit(solution)/shard_map/energy/pallas_call | solution.py:204
  41.0 15.2 %all_to_all.40.pieces_ref = f32[8,16,128]{2,1,0:T(8,128)S(1)} all-to-all(f32[8,16,128]{2,1,0:T(8,128)S(1)} %get-tuple-element.39), channel_id=1, replica_groups=mesh['y'=4,'z'=8,'x'=4,'core'=2] {'z'}, dimensions={0} | all-to-all | bytes 131072 | tf_op jit(solution)/shard_map/all_to_all | solution.py:34
  58.4 14.9 %all_to_all.41.pieces_ref = f32[32,16,128]{2,1,0:T(8,128)S(1)} all-to-all(f32[32,16,128]{2,1,0:T(8,128)S(1)} %get-tuple-element.40), channel_id=1, replica_groups=mesh['y'=4,'z'=8,'x'=4,'core'=2] {'y','x','core'}, dimensions={0} | all-to-all | bytes 524288 | tf_op jit(solution)/shard_map/all_to_all | solution.py:34
  75.5 9.5 %all_to_all.42.pieces_ref = f32[8,16,128]{2,1,0:T(8,128)S(1)} all-to-all(f32[8,16,128]{2,1,0:T(8,128)S(1)} %column_sums.2), channel_id=1, replica_groups=mesh['y'=4,'z'=8,'x'=4,'core'=2] {'z'}, dimensions={0} | all-to-all | bytes 131072 | tf_op jit(solution)/shard_map/all_to_all | solution.py:34
  87.2 13.7 %all_to_all.43.pieces_ref = f32[32,16,128]{2,1,0:T(8,128)S(1)} all-to-all(f32[32,16,128]{2,1,0:T(8,128)S(1)} %get-tuple-element.41), channel_id=1, replica_groups=mesh['y'=4,'z'=8,'x'=4,'core'=2] {'y','x','core'}, dimensions={0} | all-to-all | bytes 524288 | tf_op jit(solution)/shard_map/all_to_all | solution.py:34
  103.1 9.5 %all_to_all.44.pieces_ref = f32[8,16,128]{2,1,0:T(8,128)S(1)} all-to-all(f32[8,16,128]{2,1,0:T(8,128)S(1)} %column_sums.3), channel_id=1, replica_groups=mesh['y'=4,'z'=8,'x'=4,'core'=2] {'z'}, dimensions={0} | all-to-all | bytes 131072 | tf_op jit(solution)/shard_map/all_to_all | solution.py:34
  114.6 15.0 %all_to_all.45 = f32[32,24,128]{2,1,0:T(8,128)S(1)} all-to-all(f32[32,24,128]{2,1,0:T(8,128)S(1)} %get-tuple-element.43), channel_id=1, replica_groups=mesh['y'=4,'z'=8,'x'=4,'core'=2] {'y','x','core'}, dimensions={0} | all-to-all | bytes 786432 | tf_op jit(solution)/shard_map/all_to_all | solution.py:34
  129.5 12.5 %gradients.1 = (f32[4,256,128]{2,1,0:T(8,128)}, f32[4,256,128]{2,1,0:T(8,128)}, f32[4,256,128]{2,1,0:T(8,128)}, f32[4,256,128]{2,1,0:T(8,128)}, f32[16,64,256]{2,1,0:T(8,128)}, /*index=5*/f32[16,64,256]{2,1,0:T(8,128)}) custom-call(s32[5,8]{1,0:T(8,128)S(1)} %stack.49.table_ref, bf16[2048,512]{1,0:T(8,128)(2,1)} %get-tuple-element.37.units_ref, ...), custom_call_target="tpu_custom_call" | custom-call | flops 8589934592 | bytes 8388608 | tf_op jit(solution)/shard_map/gradients/pallas_call | solution.py:519
  145.0 2.4 %add.170 = f32[16,64,256]{2,1,0:T(8,128)} add(f32[16,64,256]{2,1,0:T(8,128)} %get-tuple-element.45, f32[16,64,256]{2,1,0:T(8,128)S(1)} %collective-permute-done.8) | non-fusion elementwise | flops 262144 | bytes 3145728 | tf_op jit(solution)/shard_map/add | solution.py:657
  147.4 3.7 %all-to-all-start.6 = ((f32[16,64,256]{2,1,0:T(8,128)}), f32[16,64,256]{2,1,0:T(8,128)S(1)}, u32[]{:S(2)}, u32[]{:S(2)}) async-start(f32[16,64,256]{2,1,0:T(8,128)} %add.170), calls=%async_computation.6 | async-start | bytes 2097152 | tf_op jit(solution)/shard_map/all_to_all | solution.py:34
  151.0 6.3 %collective-permute-done.11 = f32[4,256,128]{2,1,0:T(8,128)S(1)} collective-permute-done((f32[4,256,128]{2,1,0:T(8,128)}, f32[4,256,128]{2,1,0:T(8,128)S(1)}, u32[]{:S(2)}, u32[]{:S(2)}) %collective-permute-start.11) | collective-permute-done | bytes 524320 | tf_op jit(solution)/shard_map/ppermute | solution.py:362
  157.5 3.6 %collective-permute-start.10 = (f32[2,256,128]{2,1,0:T(8,128)S(1)}, f32[2,256,128]{2,1,0:T(8,128)S(1)}, u32[]{:S(2)}, u32[]{:S(2)}) collective-permute-start(f32[2,256,128]{2,1,0:T(8,128)S(1)} %slice_add_fusion.1), channel_id=1, source_target_pairs={{0,48},{8,24},{16,0},{24,40},{32,16},{40,56},{48,32},{56,8},{1,49}... | collective-permute-start | bytes 786440 | tf_op jit(solution)/shard_map/ppermute | solution.py:370
  161.1 10.9 %collective-permute-done.12 = f32[2,256,128]{2,1,0:T(8,128)S(1)} collective-permute-done((f32[2,256,128]{2,1,0:T(8,128)S(1)}, f32[2,256,128]{2,1,0:T(8,128)S(1)}, u32[]{:S(2)}, u32[]{:S(2)}) %collective-permute-start.12) | collective-permute-done | bytes 262176 | tf_op jit(solution)/shard_map/ppermute | solution.py:370
  172.2 2.3 %student_end.1 = f32[8,64,256]{2,1,0:T(8,128)} custom-call(s32[8]{0:T(128)S(1)} %stack.46.place_ref, f32[16,64,256]{2,1,0:T(8,128)S(1)} %all-to-all-done.6.pieces_ref, f32[512,512]{1,0:T(8,128)} %get-tuple-element.33.units_ref.unit_ref, f32[512,1]{1,0:T(8,128)} %get-tuple-element.55.length_ref), custom_call_target="tpu_custom_call" | custom-call | tf_op jit(solution)/shard_map/student_end/pallas_call | solution.py:570
  174.5 5.2 %all-to-all-start.7 = ((f32[8,64,256]{2,1,0:T(8,128)}), f32[8,64,256]{2,1,0:T(8,128)S(1)}, u32[]{:S(2)}, u32[]{:S(2)}) async-start(f32[8,64,256]{2,1,0:T(8,128)} %student_end.1), calls=%async_computation.7 | async-start | bytes 1048576 | tf_op jit(solution)/shard_map/all_to_all | solution.py:34
  179.9 5.9 %collective-permute-done.13.refs_1_ = f32[256,128]{1,0:T(8,128)S(1)} collective-permute-done((f32[256,128]{1,0:T(8,128)S(1)}, f32[256,128]{1,0:T(8,128)S(1)}, u32[]{:S(2)}, u32[]{:S(2)}) %collective-permute-start.13) | collective-permute-done | bytes 131104 | tf_op jit(solution)/shard_map/ppermute | solution.py:378
  185.9 2.4 %proto_end.1 = f32[256,256]{1,0:T(8,128)} custom-call(s32[8]{0:T(128)S(1)} %stack.46.place_ref, f32[256,128]{1,0:T(8,128)S(1)} %get-tuple-element.56.refs_0_, f32[256,128]{1,0:T(8,128)S(1)} %collective-permute-done.13.refs_1_, f32[256,128]{1,0:T(8,128)S(1)} %get-tuple-element.58.refs_2_, f32[256,128]{1,0:T(8,128)S(1)} %collective-permute-done.14.refs_3_, ...), custom_call_target="tpu_custom_call" | custom-call | tf_op jit(solution)/shard_map/proto_end/pallas_call | solution.py:603
  (43 shorter events, 23.0 us)
Async XLA Ops:
  4.5 14.5 %collective-permute-start.1 = (f32[512,256]{1,0:T(8,128)}, f32[512,256]{1,0:T(8,128)S(1)}, u32[]{:S(2)}, u32[]{:S(2)}) collective-permute-start(f32[512,256]{1,0:T(8,128)} %get-tuple-element.34), channel_id=1, source_target_pairs={{0,192},{64,0},{128,64},{192,128},{1,193},{65,1},{129,65},{193,129... | collective-permute-start | bytes 1572872 | tf_op jit(solution)/shard_map/ppermute | solution.py:632
  8.1 13.9 %collective-permute-start = (f32[512,256]{1,0:T(8,128)}, f32[512,256]{1,0:T(8,128)S(1)}, u32[]{:S(2)}, u32[]{:S(2)}) collective-permute-start(f32[512,256]{1,0:T(8,128)} %get-tuple-element.34), channel_id=1, source_target_pairs={{0,64},{64,128},{128,192},{192,0},{1,65},{65,129},{129,193},{193,1... | collective-permute-start | bytes 1572872 | tf_op jit(solution)/shard_map/ppermute | solution.py:632
  22.0 6.0 %collective-permute-start.3 = (f32[256,256]{1,0:T(8,128)S(1)}, f32[256,256]{1,0:T(8,128)S(1)}, u32[]{:S(2)}, u32[]{:S(2)}) collective-permute-start(f32[256,256]{1,0:T(8,128)S(1)} %slice.55), channel_id=1, source_target_pairs={{0,192},{64,0},{128,64},{192,128},{1,193},{65,1},{129,65},{193,129... | collective-permute-start | bytes 786440 | tf_op jit(solution)/shard_map/ppermute | solution.py:632
  22.4 8.4 %collective-permute-start.2 = (f32[256,256]{1,0:T(8,128)S(1)}, f32[256,256]{1,0:T(8,128)S(1)}, u32[]{:S(2)}, u32[]{:S(2)}) collective-permute-start(f32[256,256]{1,0:T(8,128)S(1)} %slice.54), channel_id=1, source_target_pairs={{0,64},{64,128},{128,192},{192,0},{1,65},{65,129},{129,193},{193,1... | collective-permute-start | bytes 786440 | tf_op jit(solution)/shard_map/ppermute | solution.py:632
  23.6 10.0 %collective-permute-start.4 = (f32[512,256]{1,0:T(8,128)S(1)}, f32[512,256]{1,0:T(8,128)S(1)}, u32[]{:S(2)}, u32[]{:S(2)}) collective-permute-start(f32[512,256]{1,0:T(8,128)S(1)} %collective-permute-done.refs_0_), channel_id=1, source_target_pairs={{0,1},{1,0},{2,3},{3,2},{4,5},{5,4},{6,7},{7,6},{8,9},{9,8},{10,11... | collective-permute-start | bytes 1572872 | tf_op jit(solution)/shard_map/ppermute | solution.py:635
  26.1 7.5 %collective-permute-start.5 = (f32[512,256]{1,0:T(8,128)S(1)}, f32[512,256]{1,0:T(8,128)S(1)}, u32[]{:S(2)}, u32[]{:S(2)}) collective-permute-start(f32[512,256]{1,0:T(8,128)S(1)} %collective-permute-done.1.refs_1_), channel_id=1, source_target_pairs={{0,1},{1,0},{2,3},{3,2},{4,5},{5,4},{6,7},{7,6},{8,9},{9,8},{10,11... | collective-permute-start | bytes 1572872 | tf_op jit(solution)/shard_map/ppermute | solution.py:635
  28.0 4.4 %collective-permute-start.7 = (f32[256,256]{1,0:T(8,128)S(1)}, f32[256,256]{1,0:T(8,128)S(1)}, u32[]{:S(2)}, u32[]{:S(2)}) collective-permute-start(f32[256,256]{1,0:T(8,128)S(1)} %collective-permute-done.3.refs_3_), channel_id=1, source_target_pairs={{0,1},{1,0},{2,3},{3,2},{4,5},{5,4},{6,7},{7,6},{8,9},{9,8},{10,11... | collective-permute-start | bytes 786440 | tf_op jit(solution)/shard_map/ppermute | solution.py:635
  30.8 2.8 %collective-permute-start.6 = (f32[256,256]{1,0:T(8,128)S(1)}, f32[256,256]{1,0:T(8,128)S(1)}, u32[]{:S(2)}, u32[]{:S(2)}) collective-permute-start(f32[256,256]{1,0:T(8,128)S(1)} %collective-permute-done.2.refs_2_), channel_id=1, source_target_pairs={{0,1},{1,0},{2,3},{3,2},{4,5},{5,4},{6,7},{7,6},{8,9},{9,8},{10,11... | collective-permute-start | bytes 786440 | tf_op jit(solution)/shard_map/ppermute | solution.py:635
  142.0 15.3 %copy-start.1 = (f32[4,256,128]{2,1,0:T(8,128)S(1)}, f32[4,256,128]{2,1,0:T(8,128)}, u32[]{:S(2)}) copy-start(f32[4,256,128]{2,1,0:T(8,128)} %get-tuple-element.52) | copy-start | bytes 1572868
  142.0 15.4 %copy-start = (f32[4,256,128]{2,1,0:T(8,128)S(1)}, f32[4,256,128]{2,1,0:T(8,128)}, u32[]{:S(2)}) copy-start(f32[4,256,128]{2,1,0:T(8,128)} %get-tuple-element.50) | copy-start | bytes 1572868
  142.0 3.0 %collective-permute-start.8 = (f32[16,64,256]{2,1,0:T(8,128)}, f32[16,64,256]{2,1,0:T(8,128)S(1)}, u32[]{:S(2)}, u32[]{:S(2)}) collective-permute-start(f32[16,64,256]{2,1,0:T(8,128)} %get-tuple-element.46), channel_id=1, source_target_pairs={{0,1},{1,0},{2,3},{3,2},{4,5},{5,4},{6,7},{7,6},{8,9},{9,8},{10,11... | collective-permute-start | bytes 3145736 | tf_op jit(solution)/shard_map/ppermute | solution.py:635
  142.5 14.8 %collective-permute-start.11 = (f32[4,256,128]{2,1,0:T(8,128)}, f32[4,256,128]{2,1,0:T(8,128)S(1)}, u32[]{:S(2)}, u32[]{:S(2)}) collective-permute-start(f32[4,256,128]{2,1,0:T(8,128)} %get-tuple-element.53), channel_id=1, source_target_pairs={{0,56},{8,16},{16,8},{24,32},{32,24},{40,48},{48,40},{56,0},{1,57}... | collective-permute-start | bytes 1572872 | tf_op jit(solution)/shard_map/ppermute | solution.py:362
  142.5 14.9 %collective-permute-start.9 = (f32[4,256,128]{2,1,0:T(8,128)}, f32[4,256,128]{2,1,0:T(8,128)S(1)}, u32[]{:S(2)}, u32[]{:S(2)}) collective-permute-start(f32[4,256,128]{2,1,0:T(8,128)} %get-tuple-element.51), channel_id=1, source_target_pairs={{0,8},{8,0},{16,24},{24,16},{32,40},{40,32},{48,56},{56,48},{1,9},... | collective-permute-start | bytes 1572872 | tf_op jit(solution)/shard_map/ppermute | solution.py:362
  147.4 24.8 %all-to-all-start.6 = ((f32[16,64,256]{2,1,0:T(8,128)}), f32[16,64,256]{2,1,0:T(8,128)S(1)}, u32[]{:S(2)}, u32[]{:S(2)}) async-start(f32[16,64,256]{2,1,0:T(8,128)} %add.170), calls=%async_computation.6 | async-start | bytes 2097152 | tf_op jit(solution)/shard_map/all_to_all | solution.py:34
  157.3 14.7 %collective-permute-start.12 = (f32[2,256,128]{2,1,0:T(8,128)S(1)}, f32[2,256,128]{2,1,0:T(8,128)S(1)}, u32[]{:S(2)}, u32[]{:S(2)}) collective-permute-start(f32[2,256,128]{2,1,0:T(8,128)S(1)} %slice_add_fusion), channel_id=1, source_target_pairs={{0,16},{8,56},{16,32},{24,8},{32,48},{40,24},{48,0},{56,40},{1,17}... | collective-permute-start | bytes 786440 | tf_op jit(solution)/shard_map/ppermute | solution.py:370
  157.5 14.6 %collective-permute-start.10 = (f32[2,256,128]{2,1,0:T(8,128)S(1)}, f32[2,256,128]{2,1,0:T(8,128)S(1)}, u32[]{:S(2)}, u32[]{:S(2)}) collective-permute-start(f32[2,256,128]{2,1,0:T(8,128)S(1)} %slice_add_fusion.1), channel_id=1, source_target_pairs={{0,48},{8,24},{16,0},{24,40},{32,16},{40,56},{48,32},{56,8},{1,49}... | collective-permute-start | bytes 786440 | tf_op jit(solution)/shard_map/ppermute | solution.py:370
  174.5 14.7 %all-to-all-start.7 = ((f32[8,64,256]{2,1,0:T(8,128)}), f32[8,64,256]{2,1,0:T(8,128)S(1)}, u32[]{:S(2)}, u32[]{:S(2)}) async-start(f32[8,64,256]{2,1,0:T(8,128)} %student_end.1), calls=%async_computation.7 | async-start | bytes 1048576 | tf_op jit(solution)/shard_map/all_to_all | solution.py:34
  179.7 6.1 %collective-permute-start.13 = (f32[256,128]{1,0:T(8,128)S(1)}, f32[256,128]{1,0:T(8,128)S(1)}, u32[]{:S(2)}, u32[]{:S(2)}) collective-permute-start(f32[256,128]{1,0:T(8,128)S(1)} %get-tuple-element.57), channel_id=1, source_target_pairs={{0,56},{8,16},{16,8},{24,32},{32,24},{40,48},{48,40},{56,0},{1,57}... | collective-permute-start | bytes 393224 | tf_op jit(solution)/shard_map/ppermute | solution.py:378
  179.9 6.0 %collective-permute-start.14 = (f32[256,128]{1,0:T(8,128)S(1)}, f32[256,128]{1,0:T(8,128)S(1)}, u32[]{:S(2)}, u32[]{:S(2)}) collective-permute-start(f32[256,128]{1,0:T(8,128)S(1)} %get-tuple-element.59), channel_id=1, source_target_pairs={{0,8},{8,0},{16,24},{24,16},{32,40},{40,32},{48,56},{56,48},{1,9},... | collective-permute-start | bytes 393224 | tf_op jit(solution)/shard_map/ppermute | solution.py:378

commit v6 on v5

--- a/solution.py
+++ b/solution.py
@@ -1,3 +1,4 @@
+import functools
 import math
 
 import jax
@@ -73,7 +74,7 @@
     return jnp.concatenate(parts, axis=0)
 
 
-def select_body(place_ref, teacher_ref, student_ref, order_ref, units_ref, length_ref, mine_ref):
+def select_body(core_ref, teacher_ref, student_ref, order_ref, units_ref, length_ref, mine_ref):
     images, patches, _ = teacher_ref.shape
     for image in range(images):
         chosen = order_ref[image : image + 1, :MASKED]
@@ -90,10 +91,10 @@
         student, length_ref[rows, :] = unit_rows(pick(student_ref))
         units_ref[rows, :D] = teacher
         units_ref[rows, D:] = student
-        mine_ref[rows, :] = jnp.where(place_ref[3] == 0, teacher, student)
-
-
-def select_tokens(place, teacher_patches, student_patches, mask_order):
+        mine_ref[rows, :] = jnp.where(core_ref[0] == 0, teacher, student)
+
+
+def select_tokens(core, teacher_patches, student_patches, mask_order):
     tokens = teacher_patches.shape[0] * MASKED
     return pl.pallas_call(
         select_body,
@@ -107,7 +108,7 @@
         ],
         compiler_params=params(8),
         name="select",
-    )(place, in_hbm(teacher_patches), in_hbm(student_patches), in_hbm(mask_order))
+    )(core, in_hbm(teacher_patches), in_hbm(student_patches), in_hbm(mask_order))
 
 
 def lane_rows(row):
@@ -139,25 +140,25 @@
     units.wait()
 
 
-def energy_body(
-    place_ref, units_ref, *refs
-):
-    piece_refs, (protos_ref, energy_ref, sums_ref, cast_ref, weights_ref, total_ref) = refs[:8], refs[8:]
-    own = units_ref.shape[0]
-    tokens = cast_ref.shape[0]
-
-    def rows_of(slot, start, size):
-        return pl.ds(pl.multiple_of(place_ref[4 + slot] * own + start, size), size)
-
-    cast_ref[rows_of(0, 0, own), :] = units_ref[...].astype(bf16)
-    places = [(1, 0, own), (3, 0, own), (2, 0, own // 2), (2, own // 2, own // 2)]
+STEPS = [0, 1, 3, 2]
+
+
+def energy_body(layout, before, place_ref, *refs):
+    piece_refs, refs = refs[: len(layout)], refs[len(layout) :]
+    protos_ref, refs = refs[0], refs[1:]
+    before_refs, refs = refs[:before], refs[before:]
+    energy_ref, sums_ref, cast_ref, weights_ref, total_ref = refs
+    for ref, (rows, kind) in zip(piece_refs, layout):
+        if kind is None:
+            cast_ref[rows, :] = ref[...].astype(bf16)
     for core in range(2):
 
         @pl.when(place_ref[3] == core)
         def _(core=core):
-            for i, ref in enumerate(piece_refs):
-                kind = core if i < 4 else 1 - core
-                cast_ref[rows_of(*places[i % 4]), kind * D : (kind + 1) * D] = ref[...].astype(bf16)
+            for ref, (rows, kind) in zip(piece_refs, layout):
+                if kind is not None:
+                    half = core if kind == 0 else 1 - core
+                    cast_ref[rows, half * D : (half + 1) * D] = ref[...].astype(bf16)
 
     weights_ref[...] = directions(protos_ref[...])
     total_ref[...] = jnp.zeros_like(total_ref)
@@ -179,8 +180,10 @@
             logits = following
         return carry
 
-    lax.fori_loop(0, tokens // WIDE, step, 0)
+    lax.fori_loop(0, cast_ref.shape[0] // WIDE, step, 0)
     totals = lane_totals(total_ref[...])
+    for ref in before_refs:
+        totals = totals + ref[0]
     for copy in range(sums_ref.shape[0]):
         sums_ref[copy] = totals
 
@@ -197,18 +200,17 @@
     return pl.BlockSpec((tokens, D), lambda *i: (0, 1))
 
 
-def energy_of(place, units, pieces, protos, share, copies):
-    own = units.shape[0]
-    tokens = own * 4
+def energy_of(place, pieces, layout, tokens, protos, share, copies, before=()):
     direct = pl.BlockSpec(memory_space=pltpu.VMEM)
+    whole = lambda value: pl.BlockSpec(value.shape, lambda i, p: (0,) * value.ndim)
     return pl.pallas_call(
-        energy_body,
+        functools.partial(energy_body, layout, len(before)),
         grid_spec=pltpu.PrefetchScalarGridSpec(
             num_scalar_prefetch=1,
             grid=(1,),
-            in_specs=[pl.BlockSpec(units.shape, lambda i, p: (0, 0))]
-            + [pl.BlockSpec(piece.shape, lambda i, p: (0, 0)) for piece in pieces]
-            + [pl.BlockSpec((share, D), lambda i, p: (p[0], 0))],
+            in_specs=[whole(piece) for piece in pieces]
+            + [pl.BlockSpec((share, D), lambda i, p: (p[0], 0))]
+            + [whole(value) for value in before],
             out_specs=[
                 direct,
                 pl.BlockSpec((copies, share // LANES, LANES), lambda i, p: (0, 0, 0)),
@@ -221,10 +223,10 @@
             jax.ShapeDtypeStruct((copies, share // LANES, LANES), f32),
             pltpu.HBM((tokens, 2 * D), bf16),
         ],
-        compiler_params=params(24),
+        compiler_params=params(20),
         cost_estimate=work(4 * tokens * share * D, 8 * 2**20, tokens * share),
         name="energy",
-    )(place, in_hbm(units), *pieces, in_hbm(protos))
+    )(place, *pieces, in_hbm(protos), *before)
 
 
 def student_body(units_ref, protos_ref, sums_ref, unit_ref, cast_ref, total_ref, buffer_ref, sems):
@@ -280,76 +282,88 @@
     return pl.BlockSpec((tokens, D), lambda *i: (0, 1))
 
 
-def row_body(energy_ref, pieces_ref, *refs):
-    norm_refs, (scale_ref, sums_ref, tile_ref) = refs[:-3], refs[-3:]
+def tiles_of(first_ref, second_ref):
+    return [(ref, j) for ref in (first_ref, second_ref) for j in range(ref.shape[0])]
+
+
+def row_at(place_ref, i, tiles):
+    per_group = tiles // len(STEPS)
+    return place_ref[4 + STEPS[i // per_group]] * per_group + i % per_group
+
+
+def row_body(place_ref, first_ref, second_ref, pieces_ref, *refs):
+    norm_refs, (scale_ref, sums_ref, tile_ref, rows_ref) = refs[:-4], refs[-4:]
     scale_ref[...] = 1.0 / jnp.sum(pieces_ref[...], axis=0)
     fill_columns(scale_ref[...], tile_ref)
-    tiles, protos, _ = energy_ref.shape
+    tiles = tiles_of(first_ref, second_ref)
     size = 512
-    totals = []
-    for j in range(tiles):
+    for i, (ref, j) in enumerate(tiles):
         total = jnp.zeros((1, LANES), f32)
-        for start in range(0, protos, size):
+        for start in range(0, ref.shape[1], size):
             part = slice(start, start + size)
-            energy = energy_ref[j, part, :].astype(f32)
+            energy = ref[j, part, :].astype(f32)
             total = total + jnp.sum(energy * tile_ref[part, :], axis=0, keepdims=True)
-        totals.append(total)
+        rows_ref[pl.ds(row_at(place_ref, i, len(tiles)), 1), :] = total
     for ref in norm_refs:
-        totals += [ref[...], jnp.zeros_like(ref)]
-    totals = jnp.concatenate(totals, axis=0)
+        rows_ref[len(tiles) :, :] = jnp.concatenate([ref[...], jnp.zeros_like(ref)], axis=0)
+    rows = rows_ref[...]
     for copy in range(sums_ref.shape[0]):
-        sums_ref[copy] = totals
-
-
-def row_sums(energy, pieces, copies, norm_part=()):
-    tiles, protos, _ = energy.shape
+        sums_ref[copy] = rows
+
+
+def row_sums(place, energy, pieces, copies, norm_part=()):
+    tiles = sum(part.shape[0] for part in energy)
+    protos = energy[0].shape[1]
     whole = pl.BlockSpec(memory_space=pltpu.VMEM)
     rows = tiles + 2 * sum(part.shape[0] for part in norm_part)
     return pl.pallas_call(
         row_body,
-        in_specs=[whole] * (2 + len(norm_part)),
+        in_specs=[pl.BlockSpec(memory_space=pltpu.SMEM)] + [whole] * (3 + len(norm_part)),
         out_specs=[whole] * 2,
         out_shape=[
             jax.ShapeDtypeStruct((protos // LANES, LANES), f32),
             jax.ShapeDtypeStruct((copies, rows, LANES), f32),
         ],
-        scratch_shapes=[pltpu.VMEM((protos, LANES), f32)],
+        scratch_shapes=[pltpu.VMEM((protos, LANES), f32), pltpu.VMEM((rows, LANES), f32)],
         compiler_params=params(12),
-        cost_estimate=work(2 * energy.size, 0),
+        cost_estimate=work(2 * tiles * LANES * protos, 0),
         name="row_sums",
-    )(energy, pieces, *norm_part)
-
-
-def column_body(energy_ref, pieces_ref, sums_ref, scale_ref):
-    tiles, protos, _ = energy_ref.shape
-    scale_ref[...] = 1.0 / jnp.sum(pieces_ref[...], axis=0)
+    )(place, *energy, pieces, *norm_part)
+
+
+def column_body(place_ref, first_ref, second_ref, pieces_ref, sums_ref, scale_ref, rows_ref):
+    tiles = tiles_of(first_ref, second_ref)
+    rows_ref[...] = 1.0 / jnp.sum(pieces_ref[...], axis=0)
+    for i in range(len(tiles)):
+        scale_ref[i : i + 1, :] = rows_ref[pl.ds(row_at(place_ref, i, len(tiles)), 1), :]
 
     def step(k, carry):
         rows = pl.ds(pl.multiple_of(k * LANES, LANES), LANES)
         total = jnp.zeros((LANES, LANES), f32)
-        for j in range(tiles):
-            total = total + energy_ref[j, rows, :].astype(f32) * scale_ref[j : j + 1, :]
+        for i, (ref, j) in enumerate(tiles):
+            total = total + ref[j, rows, :].astype(f32) * scale_ref[i : i + 1, :]
         sums_ref[0, pl.ds(k, 1), :] = lane_totals(total)
         return carry
 
-    lax.fori_loop(0, protos // LANES, step, 0, unroll=4)
+    lax.fori_loop(0, first_ref.shape[1] // LANES, step, 0, unroll=4)
     for copy in range(1, sums_ref.shape[0]):
         sums_ref[copy] = sums_ref[0]
 
 
-def column_sums(energy, pieces, copies):
-    tiles, protos, _ = energy.shape
+def column_sums(place, energy, pieces, copies):
+    tiles = sum(part.shape[0] for part in energy)
+    protos = energy[0].shape[1]
     whole = pl.BlockSpec(memory_space=pltpu.VMEM)
     return pl.pallas_call(
         column_body,
-        in_specs=[whole] * 2,
+        in_specs=[pl.BlockSpec(memory_space=pltpu.SMEM)] + [whole] * 3,
         out_specs=whole,
         out_shape=jax.ShapeDtypeStruct((copies, protos // LANES, LANES), f32),
-        scratch_shapes=[pltpu.VMEM((tiles, LANES), f32)],
+        scratch_shapes=[pltpu.VMEM((tiles, LANES), f32)] * 2,
         compiler_params=params(12),
-        cost_estimate=work(2 * energy.size, 0),
+        cost_estimate=work(2 * tiles * LANES * protos, 0),
         name="column_sums",
-    )(energy, pieces)
+    )(place, *energy, pieces)
 
 
 LEFT_PLACE = [4, 5, 6, 7, 3, 2, 1, 0]
@@ -380,8 +394,10 @@
 
 def gradient_body(
     table_ref,
-    units_ref,
-    energy_ref,
+    units_first_ref,
+    units_second_ref,
+    energy_first_ref,
+    energy_second_ref,
     pieces_ref,
     sw_first_ref,
     sw_second_ref,
@@ -397,24 +413,26 @@
     total_ref,
     feature_ref,
     stage_ref,
+    rows_ref,
     sems,
     feature_sems,
 ):
     step = pl.program_id(0)
-    tiles = energy_ref.shape[0]
+    tiles = tiles_of(energy_first_ref, energy_second_ref)
     groups = pieces_ref.shape[0]
-    own = tiles // groups
+    own = len(tiles) // groups
 
     @pl.when(step == 0)
     def _():
-        scale = (1.0 / student_temp) / jnp.sum(pieces_ref[:, :, :tiles, :], axis=(0, 1))
-        for k in range(tiles):
-            r_ref[:, k * LANES : (k + 1) * LANES] = scale[k : k + 1, :]
+        count = len(tiles)
+        rows_ref[...] = (1.0 / student_temp) / jnp.sum(pieces_ref[:, :, :count, :], axis=(0, 1))
         for group in range(groups):
-            total = jnp.sum(pieces_ref[group, :, tiles : tiles + own, :], axis=0)
+            slot = table_ref[5, group]
+            total = jnp.sum(pieces_ref[slot][:, count : count + own, :], axis=0)
             inverse = (1.0 / student_temp) / total
             for k in range(own):
                 lanes = slice((group * own + k) * LANES, (group * own + k + 1) * LANES)
+                r_ref[:, lanes] = rows_ref[pl.ds(slot * own + k, 1), :]
                 n_ref[:, lanes] = inverse[k : k + 1, :]
         feature_ref[...] = jnp.zeros_like(feature_ref)
 
@@ -430,35 +448,48 @@
             columns.append(to_column(row))
     col_scale = jnp.concatenate(columns, axis=0)
 
-    def logits_of(part):
-        return nt_dot(sw, units_ref[part, D:])
-
-    parts = [slice(c, c + WIDE) for c in range(0, units_ref.shape[0], WIDE)]
+    parts = [
+        (ref, slice(c, c + WIDE))
+        for ref in (units_first_ref, units_second_ref)
+        for c in range(0, ref.shape[0], WIDE)
+    ]
+
+    def tokens_of(i):
+        ref, rows = parts[i]
+        return ref[rows, D:]
+
+    def first_row(i):
+        per_group = len(parts) // groups
+        return (table_ref[5, i // per_group] * per_group + i % per_group) * WIDE
 
     def feature_copies(i):
         size = feature_send_ref.shape[1]
         found = []
-        for at in range(i * WIDE // size, (i + 1) * WIDE // size):
-            source, sem = feature_ref.at[pl.ds(at * size, size), :], feature_sems.at[at]
-            kept = pltpu.make_async_copy(source, feature_keep_ref.at[at // 2], sem)
-            sent = pltpu.make_async_copy(source, feature_send_ref.at[at // 2], sem)
-            found += [(table_ref[4, 0] == at % 2, kept), (table_ref[4, 0] != at % 2, sent)]
+        for k in range(WIDE // size):
+            start = pl.multiple_of(first_row(i) + k * size, size)
+            source, sem = feature_ref.at[pl.ds(start, size), :], feature_sems.at[i * (WIDE // size) + k]
+            at = first_row(i) // (2 * size) + k // 2
+            kept = pltpu.make_async_copy(source, feature_keep_ref.at[at], sem)
+            sent = pltpu.make_async_copy(source, feature_send_ref.at[at], sem)
+            found += [(table_ref[4, 0] == k % 2, kept), (table_ref[4, 0] != k % 2, sent)]
         return found
 
-    logits = logits_of(parts[0])
-    for i, part in enumerate(parts):
-        following = logits_of(parts[i + 1]) if i + 1 < len(parts) else None
+    logits = nt_dot(sw, tokens_of(0))
+    for i in range(len(parts)):
+        following = nt_dot(sw, tokens_of(i + 1)) if i + 1 < len(parts) else None
         grads = []
         for j in range(WIDE // LANES):
             tile = i * (WIDE // LANES) + j
             lanes = slice(tile * LANES, (tile + 1) * LANES)
-            energy = both(energy_ref[tile, here[0], :], energy_ref[tile, here[1], :]).astype(f32)
+            ref, at = tiles[tile]
+            energy = both(ref[at, here[0], :], ref[at, here[1], :]).astype(f32)
             probs = jnp.exp2(logits[:, j * LANES : (j + 1) * LANES] * student_power) * n_ref[:, lanes]
             grads.append((probs - energy * r_ref[:, lanes] * col_scale).astype(bf16))
         logit_grad = jnp.concatenate(grads, axis=1)
-        added = jnp.dot(logit_grad, units_ref[part, D:], preferred_element_type=f32)
+        added = jnp.dot(logit_grad, tokens_of(i), preferred_element_type=f32)
         total_ref[...] = added if i == 0 else total_ref[...] + added
-        feature_ref[part, :] += lax.dot_general(
+        rows = pl.ds(pl.multiple_of(first_row(i), WIDE), WIDE)
+        feature_ref[rows, :] += lax.dot_general(
             logit_grad, sw, (((0,), (0,)), ((), ())), preferred_element_type=f32
         )
         for wanted, copy in feature_copies(i):
@@ -497,18 +528,19 @@
                     pl.when(wanted)(copy.wait)
 
 
-def block_table(y, z, core):
+def block_table(y, z, core, others):
     blocks = len(LEFT_PLACE)
     way = jnp.where(z % 2 == 1, 1, -1)
     local = (z + way * jnp.arange(blocks) + blocks) % blocks
     cores = jnp.full((blocks,), core)
-    table = [y * blocks + local, jnp.array(LEFT_PLACE), jnp.array(RIGHT_PLACE), local, cores]
+    slots = jnp.stack([others[step] for step in STEPS] * 2)
+    table = [y * blocks + local, jnp.array(LEFT_PLACE), jnp.array(RIGHT_PLACE), local, cores, slots]
     return jnp.stack(table).astype(jnp.int32)
 
 
 def gradients(table, units_all, energy, pieces, student_protos, scale, shares):
-    tiles, share, _ = energy.shape
-    tokens = units_all.shape[0]
+    share = energy[0].shape[1]
+    tokens = sum(part.shape[0] for part in units_all)
     block = 256
     blocks = share // block
     whole = lambda *shape: pl.BlockSpec(shape, lambda i, p: (0,) * len(shape))
@@ -522,7 +554,9 @@
             num_scalar_prefetch=1,
             grid=(blocks // 2,),
             in_specs=[
-                whole(tokens, 2 * D),
+                whole(*units_all[0].shape),
+                whole(*units_all[1].shape),
+                direct,
                 direct,
                 whole(*pieces.shape),
                 first,
@@ -536,18 +570,23 @@
                 pltpu.VMEM((2 * block, D), f32),
                 pltpu.VMEM((tokens, D), f32),
                 pltpu.VMEM((2, blocks, block, D // 2), f32),
+                pltpu.VMEM((tokens // LANES, LANES), f32),
                 pltpu.SemaphoreType.DMA((2, blocks)),
                 pltpu.SemaphoreType.DMA((shares,)),
             ],
         ),
-        out_shape=[half] * 4 + [pltpu.HBM((shares // 2, tokens // shares, D), f32)] * 2,
+        out_shape=[half] * 4
+        + [
+            pltpu.HBM((shares // 2, tokens // shares, D), f32),
+            pltpu.VMEM((shares // 2, tokens // shares, D), f32),
+        ],
         compiler_params=params(24),
         cost_estimate=work(8 * tokens * share * D, 8 * 2**20, tokens * share),
         name="gradients",
     )(
         table,
-        in_hbm(units_all),
-        energy,
+        *[in_hbm(part) for part in units_all],
+        *energy,
         pieces,
         in_hbm(student_protos),
         in_hbm(student_protos),
@@ -620,34 +659,54 @@
     proto_size = lax.axis_size("x") * lax.axis_size("core")
     y, z = lax.axis_index("y"), lax.axis_index("z")
     others = [(y - step + y_size) % y_size for step in range(y_size)]
-    place = [y, y * z_size + z, lax.axis_index(PROTOS), lax.axis_index("core")] + others
-    place, table = lax.optimization_barrier(
-        (jnp.stack(place).astype(jnp.int32), block_table(y, z, lax.axis_index("core")))
-    )
+    core = lax.axis_index("core")
+    place = [y, y * z_size + z, lax.axis_index(PROTOS), core] + others
+    place = jnp.stack(place).astype(jnp.int32)
+    table = block_table(y, z, core, others)
     share = teacher_protos.shape[0] // y_size
 
     units, student_length, mine = select_tokens(
-        place, teacher_patches, student_patches, mask_order
+        core.astype(jnp.int32)[None], teacher_patches, student_patches, mask_order
     )
     from_y = lambda value, step: lax.ppermute(
         value, "y", [(i, (i + step) % y_size) for i in range(y_size)]
     )
     from_core = lambda value: lax.ppermute(value, "core", [(0, 1), (1, 0)])
-    half = mine.shape[0] // 2
+    own = mine.shape[0]
+    half = own // 2
     first, third = from_y(mine, 1), from_y(mine, 3)
     norm_part = student_sums(units, student_protos)
-    norm_part, first, third = lax.optimization_barrier((norm_part, first, third))
-    got = [first, third, from_y(first[:half], 1), from_y(third[half:], 3)]
-    got = got + [from_core(piece) for piece in got]
+    norm_part, first, third, place, table = lax.optimization_barrier(
+        (norm_part, first, third, place, table)
+    )
+    second = [from_y(first[:half], 1), from_y(third[half:], 3)]
+    rows = lambda start, size: slice(start, start + size)
+    near = [units, first, third, from_core(first), from_core(third)]
+    layout = [
+        (rows(0, own), None),
+        (rows(own, own), 0),
+        (rows(2 * own, own), 0),
+        (rows(own, own), 1),
+        (rows(2 * own, own), 1),
+    ]
+    energy_near, sums, units_near = energy_of(
+        place, near, layout, 3 * own, teacher_protos, share, 1
+    )
+    sums, second = lax.optimization_barrier((sums, second))
+    far = second + [from_core(piece) for piece in second]
+    layout = [(rows(0, half), 0), (rows(half, half), 0), (rows(0, half), 1), (rows(half, half), 1)]
+    energy_far, sums, units_far = energy_of(
+        place, far, layout, own, teacher_protos, share, z_size, (sums,)
+    )
+    energy, units_all = (energy_near, energy_far), (units_near, units_far)
 
     rows = ("y",) + PROTOS
     peers = y_size * proto_size
-    energy, sums, units_all = energy_of(place, units, got, teacher_protos, share, z_size)
     for sweep in range(ITERS):
         if sweep > 0:
-            sums = column_sums(energy, pieces, z_size)
+            sums = column_sums(place, energy, pieces, z_size)
         norms = (norm_part,) if sweep == ITERS - 1 else ()
-        col_scale, row_part = row_sums(energy, spread(sums, "z"), peers, norms)
+        col_scale, row_part = row_sums(place, energy, spread(sums, "z"), peers, norms)
         pieces = spread(row_part, rows)
     pieces = pieces.reshape((y_size, proto_size) + pieces.shape[1:])
 

time: 191 us -> 200 us (1.047)
  Pallas kernels: 44.3 us -> 56.1 us
  starting transfers between devices: 25.7 us -> 22.5 us
    pallas_call x1, Pallas kernels: 12.5 us -> 19.5 us  [gradients(): pl.pallas_call(gradient_body, grid_spec=pltpu.PrefetchScalarGridSpec(num_...]
    pallas_call x6 -> x7, Pallas kernels: 18.1 us -> 22.7 us  [the longest x2 9.5 us: energy_of(): pl.pallas_call(functools.partial(energy_body, layout, len(before)), grid_...]
    ppermute x5, starting transfers between devices: 7.3 us -> 3.95 us  [on_device(): from_core = lambda value: lax.ppermute(value, 'core', [(0, 1), (1, 0)])]
    ppermute x4, waiting for transfers between devices: 9.75 us -> 7.14 us  [on_device(): lax.ppermute(value, 'y', [(i, (i + step) % y_size) for i in range(y_size)])]
  transfers between devices with their start and end apart: 17 -> 17, of which waited for: 9 -> 11; matrix products, arithmetic and copies ran while one was open for 1% -> 2% of each run, Pallas kernels for 4% -> 7%
where the time goes in v6:
time: 200 us; the launch traced here: 199 us
  blocking collectives  78.1 us (39%)
  Pallas kernels  56.1 us (28%)
  waiting for transfers between devices  36.8 us (18%)
  starting transfers between devices  22.5 us (11%)
  other arithmetic  3.26 us (2%)
    all_to_all x6, blocking collectives, spread(): return lax.all_to_all(value, axes, 0, 0, tiled=True)  78.1 us
    pallas_call x1, Pallas kernels, gradients(): pl.pallas_call(gradient_body, grid_spec=pltpu.PrefetchScalarGridSpec(num_...  19.5 us
    ppermute x2, waiting for transfers between devices, pass_on(): got = lax.ppermute(far, 'z', [(z, (z + 2 * way[z]) % n) for z in range(n)])  10.9 us
    pallas_call x2, Pallas kernels, energy_of(): pl.pallas_call(functools.partial(energy_body, layout, len(before)), grid_...  9.5 us
    all_to_all x2, starting transfers between devices, spread(): return lax.all_to_all(value, axes, 0, 0, tiled=True)  9.09 us
    pallas_call x3, Pallas kernels, row_sums(): pl.pallas_call(row_body, in_specs=[pl.BlockSpec(memory_space=pltpu.SMEM)]...  7.82 us
    ppermute x2, waiting for transfers between devices, collect(): got = lax.ppermute(send, 'z', [(z, (z - way[z]) % n) for z in range(n)])  7.52 us
    ppermute x4, waiting for transfers between devices, on_device(): lax.ppermute(value, 'y', [(i, (i + step) % y_size) for i in range(y_size)])  7.14 us
  transfers between devices with their start and end apart: 17, of which 11 were waited for; matrix products, arithmetic and copies ran while one was open for 2% of the time, Pallas kernels for 7%

profile of v6, /device:TPU:1, one launch (start us, length us, event | category | flops | bytes accessed | tf_op | source)
XLA Modules:
  0.0 199.2 jit_solution(5326438305834463048)
XLA Ops:
  0.6 3.0 %select.31 = (f32[512,512]{1,0:T(8,128)}, f32[512,1]{1,0:T(8,128)}, f32[512,256]{1,0:T(8,128)}) custom-call(s32[1]{0:T(128)} %bitcast.core_ref, bf16[4,256,256]{2,1,0:T(8,128)(2,1)} %teacher_ref.1, bf16[4,256,256]{2,1,0:T(8,128)(2,1)} %student_ref.1, s32[4,256]{1,0:T(4,128)} %order_ref.1), custom_call_target="tpu_custom_call" | custom-call | tf_op jit(solution)/shard_map/select/pallas_call | solution.py:99
  3.6 3.6 %collective-permute-start.1 = (f32[512,256]{1,0:T(8,128)}, f32[512,256]{1,0:T(8,128)S(1)}, u32[]{:S(2)}, u32[]{:S(2)}) collective-permute-start(f32[512,256]{1,0:T(8,128)} %get-tuple-element.38), channel_id=1, source_target_pairs={{0,192},{64,0},{128,64},{192,128},{1,193},{65,1},{129,65},{193,129... | collective-permute-start | bytes 1572872 | tf_op jit(solution)/shard_map/ppermute | solution.py:671
  8.1 6.2 %student.1.refs_0_ = f32[4,128]{1,0:T(4,128)S(1)} custom-call(f32[512,512]{1,0:T(8,128)} %get-tuple-element.37.units_ref.refs_0_.unit_ref, bf16[8192,256]{1,0:T(8,128)(2,1)} %refs_4_.3), custom_call_target="tpu_custom_call" | custom-call | flops 4294967296 | bytes 8388608 | tf_op jit(solution)/shard_map/student/pallas_call | solution.py:263
  14.2 3.8 %collective-permute-done.1.refs_2_ = f32[512,256]{1,0:T(8,128)S(1)} collective-permute-done((f32[512,256]{1,0:T(8,128)}, f32[512,256]{1,0:T(8,128)S(1)}, u32[]{:S(2)}, u32[]{:S(2)}) %collective-permute-start.1) | collective-permute-done | bytes 524320 | tf_op jit(solution)/shard_map/ppermute | solution.py:671
  18.1 3.0 %collective-permute-done.refs_1_ = f32[512,256]{1,0:T(8,128)S(1)} collective-permute-done((f32[512,256]{1,0:T(8,128)}, f32[512,256]{1,0:T(8,128)S(1)}, u32[]{:S(2)}, u32[]{:S(2)}) %collective-permute-start) | collective-permute-done | bytes 524320 | tf_op jit(solution)/shard_map/ppermute | solution.py:671
  25.2 6.0 %energy.2 = (bf16[12,2048,128]{2,1,0:T(8,128)(2,1)S(1)}, f32[1,16,128]{2,1,0:T(8,128)S(1)}, bf16[1536,512]{1,0:T(8,128)(2,1)}) custom-call(s32[8]{0:T(128)S(1)} %stack.57.place_ref, f32[512,512]{1,0:T(8,128)S(1)} %copy-done, f32[512,256]{1,0:T(8,128)S(1)} %collective-permute-done.refs_1_, f32[512,256]{1,0:T(8,128)S(1)} %collective-permute-done.1.refs_2_, ...), custom_call_target="tpu_custom_call" | custom-call | flops 3221225472 | bytes 8388608 | tf_op jit(solution)/shard_map/energy/pallas_call | solution.py:206
  34.6 3.5 %energy.3 = (bf16[4,2048,128]{2,1,0:T(8,128)(2,1)S(1)}, f32[8,16,128]{2,1,0:T(8,128)S(1)}, bf16[512,512]{1,0:T(8,128)(2,1)}) custom-call(s32[8]{0:T(128)S(1)} %stack.57.place_ref, f32[256,256]{1,0:T(8,128)S(1)} %collective-permute-done.4.refs_0_, f32[256,256]{1,0:T(8,128)S(1)} %collective-permute-done.5.refs_1_, ...), custom_call_target="tpu_custom_call" | custom-call | flops 1073741824 | bytes 8388608 | tf_op jit(solution)/shard_map/energy/pallas_call | solution.py:206
  38.2 15.2 %all_to_all.40.pieces_ref = f32[8,16,128]{2,1,0:T(8,128)S(1)} all-to-all(f32[8,16,128]{2,1,0:T(8,128)S(1)} %get-tuple-element.51), channel_id=1, replica_groups=mesh['y'=4,'z'=8,'x'=4,'core'=2] {'z'}, dimensions={0} | all-to-all | bytes 131072 | tf_op jit(solution)/shard_map/all_to_all | solution.py:35
  53.4 2.6 %row_sums.3 = (f32[16,128]{1,0:T(8,128)}, f32[32,16,128]{2,1,0:T(8,128)S(1)}) custom-call(s32[8]{0:T(128)S(1)} %stack.57.place_ref, bf16[12,2048,128]{2,1,0:T(8,128)(2,1)S(1)} %get-tuple-element.49.first_ref.energy_first_ref, bf16[4,2048,128]{2,1,0:T(8,128)(2,1)S(1)} %get-tuple-element.50.second_ref.energy_second_ref, f32[8,16,128]{2,1,0:T(8,128)S(1)} %all_to_all.40.pieces_ref), custom_call_target="tpu_custom_call" | custom-call | flops 8388608 | tf_op jit(solution)/shard_map/row_sums/pallas_call | solution.py:319
  56.0 15.1 %all_to_all.41.pieces_ref = f32[32,16,128]{2,1,0:T(8,128)S(1)} all-to-all(f32[32,16,128]{2,1,0:T(8,128)S(1)} %get-tuple-element.52), channel_id=1, replica_groups=mesh['y'=4,'z'=8,'x'=4,'core'=2] {'y','x','core'}, dimensions={0} | all-to-all | bytes 524288 | tf_op jit(solution)/shard_map/all_to_all | solution.py:35
  71.2 2.7 %column_sums.2 = f32[8,16,128]{2,1,0:T(8,128)S(1)} custom-call(s32[8]{0:T(128)S(1)} %stack.57.place_ref, bf16[12,2048,128]{2,1,0:T(8,128)(2,1)S(1)} %get-tuple-element.49.first_ref.energy_first_ref, bf16[4,2048,128]{2,1,0:T(8,128)(2,1)S(1)} %get-tuple-element.50.second_ref.energy_second_ref, f32[32,16,128]{2,1,0:T(8,128)S(1)} %all_to_all.41.pieces_ref), custom_call_target="tpu_custom_call" | custom-call | flops 8388608 | tf_op jit(solution)/shard_map/column_sums/pallas_call | solution.py:357
  73.9 9.5 %all_to_all.42.pieces_ref = f32[8,16,128]{2,1,0:T(8,128)S(1)} all-to-all(f32[8,16,128]{2,1,0:T(8,128)S(1)} %column_sums.2), channel_id=1, replica_groups=mesh['y'=4,'z'=8,'x'=4,'core'=2] {'z'}, dimensions={0} | all-to-all | bytes 131072 | tf_op jit(solution)/shard_map/all_to_all | solution.py:35
  83.4 2.6 %row_sums.4 = (f32[16,128]{1,0:T(8,128)}, f32[32,16,128]{2,1,0:T(8,128)S(1)}) custom-call(s32[8]{0:T(128)S(1)} %stack.57.place_ref, bf16[12,2048,128]{2,1,0:T(8,128)(2,1)S(1)} %get-tuple-element.49.first_ref.energy_first_ref, bf16[4,2048,128]{2,1,0:T(8,128)(2,1)S(1)} %get-tuple-element.50.second_ref.energy_second_ref, f32[8,16,128]{2,1,0:T(8,128)S(1)} %all_to_all.42.pieces_ref), custom_call_target="tpu_custom_call" | custom-call | flops 8388608 | tf_op jit(solution)/shard_map/row_sums/pallas_call | solution.py:319
  86.0 13.7 %all_to_all.43.pieces_ref = f32[32,16,128]{2,1,0:T(8,128)S(1)} all-to-all(f32[32,16,128]{2,1,0:T(8,128)S(1)} %get-tuple-element.53), channel_id=1, replica_groups=mesh['y'=4,'z'=8,'x'=4,'core'=2] {'y','x','core'}, dimensions={0} | all-to-all | bytes 524288 | tf_op jit(solution)/shard_map/all_to_all | solution.py:35
  99.7 2.7 %column_sums.3 = f32[8,16,128]{2,1,0:T(8,128)S(1)} custom-call(s32[8]{0:T(128)S(1)} %stack.57.place_ref, bf16[12,2048,128]{2,1,0:T(8,128)(2,1)S(1)} %get-tuple-element.49.first_ref.energy_first_ref, bf16[4,2048,128]{2,1,0:T(8,128)(2,1)S(1)} %get-tuple-element.50.second_ref.energy_second_ref, f32[32,16,128]{2,1,0:T(8,128)S(1)} %all_to_all.43.pieces_ref), custom_call_target="tpu_custom_call" | custom-call | flops 8388608 | tf_op jit(solution)/shard_map/column_sums/pallas_call | solution.py:357
  102.4 9.5 %all_to_all.44.pieces_ref = f32[8,16,128]{2,1,0:T(8,128)S(1)} all-to-all(f32[8,16,128]{2,1,0:T(8,128)S(1)} %column_sums.3), channel_id=1, replica_groups=mesh['y'=4,'z'=8,'x'=4,'core'=2] {'z'}, dimensions={0} | all-to-all | bytes 131072 | tf_op jit(solution)/shard_map/all_to_all | solution.py:35
  114.5 15.0 %all_to_all.45 = f32[32,24,128]{2,1,0:T(8,128)S(1)} all-to-all(f32[32,24,128]{2,1,0:T(8,128)S(1)} %get-tuple-element.55), channel_id=1, replica_groups=mesh['y'=4,'z'=8,'x'=4,'core'=2] {'y','x','core'}, dimensions={0} | all-to-all | bytes 786432 | tf_op jit(solution)/shard_map/all_to_all | solution.py:35
  129.5 19.5 %gradients.1 = (f32[4,256,128]{2,1,0:T(8,128)}, f32[4,256,128]{2,1,0:T(8,128)}, f32[4,256,128]{2,1,0:T(8,128)}, f32[4,256,128]{2,1,0:T(8,128)}, f32[16,64,256]{2,1,0:T(8,128)}, /*index=5*/f32[16,64,256]{2,1,0:T(8,128)S(1)}) custom-call(s32[6,8]{1,0:T(8,128)S(1)} %stack.62.table_ref, bf16[1536,512]{1,0:T(8,128)(2,1)} %get-tuple-element.43.units_first_ref, ...), custom_call_target="tpu_custom_call" | custom-call | flops 8589934592 | bytes 8388608 | tf_op jit(solution)/shard_map/gradients/pallas_call | solution.py:551
  153.2 3.9 %all-to-all-start.6 = ((f32[16,64,256]{2,1,0:T(8,128)}), f32[16,64,256]{2,1,0:T(8,128)S(1)}, u32[]{:S(2)}, u32[]{:S(2)}) async-start(f32[16,64,256]{2,1,0:T(8,128)} %add.170), calls=%async_computation.6 | async-start | bytes 2097152 | tf_op jit(solution)/shard_map/all_to_all | solution.py:35
  157.0 7.5 %collective-permute-done.11 = f32[4,256,128]{2,1,0:T(8,128)} collective-permute-done((f32[4,256,128]{2,1,0:T(8,128)}, f32[4,256,128]{2,1,0:T(8,128)}, u32[]{:S(2)}, u32[]{:S(2)}) %collective-permute-start.11) | collective-permute-done | bytes 524320 | tf_op jit(solution)/shard_map/ppermute | solution.py:376
  165.7 3.6 %collective-permute-start.10 = (f32[2,256,128]{2,1,0:T(8,128)S(1)}, f32[2,256,128]{2,1,0:T(8,128)S(1)}, u32[]{:S(2)}, u32[]{:S(2)}) collective-permute-start(f32[2,256,128]{2,1,0:T(8,128)S(1)} %slice_add_fusion.1), channel_id=1, source_target_pairs={{0,48},{8,24},{16,0},{24,40},{32,16},{40,56},{48,32},{56,8},{1,49}... | collective-permute-start | bytes 786440 | tf_op jit(solution)/shard_map/ppermute | solution.py:384
  169.3 10.9 %collective-permute-done.12 = f32[2,256,128]{2,1,0:T(8,128)S(1)} collective-permute-done((f32[2,256,128]{2,1,0:T(8,128)S(1)}, f32[2,256,128]{2,1,0:T(8,128)S(1)}, u32[]{:S(2)}, u32[]{:S(2)}) %collective-permute-start.12) | collective-permute-done | bytes 262176 | tf_op jit(solution)/shard_map/ppermute | solution.py:384
  183.7 5.2 %all-to-all-start.7 = ((f32[8,64,256]{2,1,0:T(8,128)}), f32[8,64,256]{2,1,0:T(8,128)S(1)}, u32[]{:S(2)}, u32[]{:S(2)}) async-start(f32[8,64,256]{2,1,0:T(8,128)} %student_end.1), calls=%async_computation.7 | async-start | bytes 1048576 | tf_op jit(solution)/shard_map/all_to_all | solution.py:35
  189.1 6.0 %collective-permute-done.13.refs_1_ = f32[256,128]{1,0:T(8,128)S(1)} collective-permute-done((f32[256,128]{1,0:T(8,128)S(1)}, f32[256,128]{1,0:T(8,128)S(1)}, u32[]{:S(2)}, u32[]{:S(2)}) %collective-permute-start.13) | collective-permute-done | bytes 131104 | tf_op jit(solution)/shard_map/ppermute | solution.py:392
  (47 shorter events, 24.0 us)
Async XLA Ops:
  3.6 14.5 %collective-permute-start.1 = (f32[512,256]{1,0:T(8,128)}, f32[512,256]{1,0:T(8,128)S(1)}, u32[]{:S(2)}, u32[]{:S(2)}) collective-permute-start(f32[512,256]{1,0:T(8,128)} %get-tuple-element.38), channel_id=1, source_target_pairs={{0,192},{64,0},{128,64},{192,128},{1,193},{65,1},{129,65},{193,129... | collective-permute-start | bytes 1572872 | tf_op jit(solution)/shard_map/ppermute | solution.py:671
  7.2 13.9 %collective-permute-start = (f32[512,256]{1,0:T(8,128)}, f32[512,256]{1,0:T(8,128)S(1)}, u32[]{:S(2)}, u32[]{:S(2)}) collective-permute-start(f32[512,256]{1,0:T(8,128)} %get-tuple-element.38), channel_id=1, source_target_pairs={{0,64},{64,128},{128,192},{192,0},{1,65},{65,129},{129,193},{193,1... | collective-permute-start | bytes 1572872 | tf_op jit(solution)/shard_map/ppermute | solution.py:671
  8.1 17.2 %copy-start = (f32[512,512]{1,0:T(8,128)S(1)}, f32[512,512]{1,0:T(8,128)}, u32[]{:S(2)}) copy-start(f32[512,512]{1,0:T(8,128)} %get-tuple-element.37.units_ref.refs_0_.unit_ref) | copy-start | bytes 3145732
  21.1 3.5 %collective-permute-start.2 = (f32[512,256]{1,0:T(8,128)S(1)}, f32[512,256]{1,0:T(8,128)S(1)}, u32[]{:S(2)}, u32[]{:S(2)}) collective-permute-start(f32[512,256]{1,0:T(8,128)S(1)} %collective-permute-done.refs_1_), channel_id=1, source_target_pairs={{0,1},{1,0},{2,3},{3,2},{4,5},{5,4},{6,7},{7,6},{8,9},{9,8},{10,11... | collective-permute-start | bytes 1572872 | tf_op jit(solution)/shard_map/ppermute | solution.py:674
  22.9 2.3 %collective-permute-start.3 = (f32[512,256]{1,0:T(8,128)S(1)}, f32[512,256]{1,0:T(8,128)S(1)}, u32[]{:S(2)}, u32[]{:S(2)}) collective-permute-start(f32[512,256]{1,0:T(8,128)S(1)} %collective-permute-done.1.refs_2_), channel_id=1, source_target_pairs={{0,1},{1,0},{2,3},{3,2},{4,5},{5,4},{6,7},{7,6},{8,9},{9,8},{10,11... | collective-permute-start | bytes 1572872 | tf_op jit(solution)/shard_map/ppermute | solution.py:674
  23.0 8.2 %collective-permute-start.5 = (f32[256,256]{1,0:T(8,128)S(1)}, f32[256,256]{1,0:T(8,128)S(1)}, u32[]{:S(2)}, u32[]{:S(2)}) collective-permute-start(f32[256,256]{1,0:T(8,128)S(1)} %slice.55), channel_id=1, source_target_pairs={{0,192},{64,0},{128,64},{192,128},{1,193},{65,1},{129,65},{193,129... | collective-permute-start | bytes 786440 | tf_op jit(solution)/shard_map/ppermute | solution.py:671
  23.1 8.4 %collective-permute-start.4 = (f32[256,256]{1,0:T(8,128)S(1)}, f32[256,256]{1,0:T(8,128)S(1)}, u32[]{:S(2)}, u32[]{:S(2)}) collective-permute-start(f32[256,256]{1,0:T(8,128)S(1)} %slice.54), channel_id=1, source_target_pairs={{0,64},{64,128},{128,192},{192,0},{1,65},{65,129},{129,193},{193,1... | collective-permute-start | bytes 786440 | tf_op jit(solution)/shard_map/ppermute | solution.py:671
  31.5 2.7 %collective-permute-start.6 = (f32[256,256]{1,0:T(8,128)S(1)}, f32[256,256]{1,0:T(8,128)S(1)}, u32[]{:S(2)}, u32[]{:S(2)}) collective-permute-start(f32[256,256]{1,0:T(8,128)S(1)} %collective-permute-done.4.refs_0_), channel_id=1, source_target_pairs={{0,1},{1,0},{2,3},{3,2},{4,5},{5,4},{6,7},{7,6},{8,9},{9,8},{10,11... | collective-permute-start | bytes 786440 | tf_op jit(solution)/shard_map/ppermute | solution.py:674
  33.1 1.5 collective-permute-start.7
  149.0 15.5 %copy-start.2 = (f32[4,256,128]{2,1,0:T(8,128)S(1)}, f32[4,256,128]{2,1,0:T(8,128)}, u32[]{:S(2)}) copy-start(f32[4,256,128]{2,1,0:T(8,128)} %get-tuple-element.64) | copy-start | bytes 1572868
  149.0 16.6 %copy-start.1 = (f32[4,256,128]{2,1,0:T(8,128)S(1)}, f32[4,256,128]{2,1,0:T(8,128)}, u32[]{:S(2)}) copy-start(f32[4,256,128]{2,1,0:T(8,128)} %get-tuple-element.62) | copy-start | bytes 1572868
  149.1 3.0 %collective-permute-start.8 = (f32[16,64,256]{2,1,0:T(8,128)}, f32[16,64,256]{2,1,0:T(8,128)S(1)}, u32[]{:S(2)}, u32[]{:S(2)}) collective-permute-start(f32[16,64,256]{2,1,0:T(8,128)} %get-tuple-element.58), channel_id=1, source_target_pairs={{0,1},{1,0},{2,3},{3,2},{4,5},{5,4},{6,7},{7,6},{8,9},{9,8},{10,11... | collective-permute-start | bytes 3145736 | tf_op jit(solution)/shard_map/ppermute | solution.py:674
  149.5 15.0 %collective-permute-start.11 = (f32[4,256,128]{2,1,0:T(8,128)}, f32[4,256,128]{2,1,0:T(8,128)}, u32[]{:S(2)}, u32[]{:S(2)}) collective-permute-start(f32[4,256,128]{2,1,0:T(8,128)} %get-tuple-element.65), channel_id=1, source_target_pairs={{0,56},{8,16},{16,8},{24,32},{32,24},{40,48},{48,40},{56,0},{1,57}... | collective-permute-start | bytes 1572872 | tf_op jit(solution)/shard_map/ppermute | solution.py:376
  149.5 16.1 %collective-permute-start.9 = (f32[4,256,128]{2,1,0:T(8,128)}, f32[4,256,128]{2,1,0:T(8,128)S(1)}, u32[]{:S(2)}, u32[]{:S(2)}) collective-permute-start(f32[4,256,128]{2,1,0:T(8,128)} %get-tuple-element.63), channel_id=1, source_target_pairs={{0,8},{8,0},{16,24},{24,16},{32,40},{40,32},{48,56},{56,48},{1,9},... | collective-permute-start | bytes 1572872 | tf_op jit(solution)/shard_map/ppermute | solution.py:376
  153.2 28.2 %all-to-all-start.6 = ((f32[16,64,256]{2,1,0:T(8,128)}), f32[16,64,256]{2,1,0:T(8,128)S(1)}, u32[]{:S(2)}, u32[]{:S(2)}) async-start(f32[16,64,256]{2,1,0:T(8,128)} %add.170), calls=%async_computation.6 | async-start | bytes 2097152 | tf_op jit(solution)/shard_map/all_to_all | solution.py:35
  165.6 14.7 %collective-permute-start.12 = (f32[2,256,128]{2,1,0:T(8,128)S(1)}, f32[2,256,128]{2,1,0:T(8,128)S(1)}, u32[]{:S(2)}, u32[]{:S(2)}) collective-permute-start(f32[2,256,128]{2,1,0:T(8,128)S(1)} %slice_add_fusion), channel_id=1, source_target_pairs={{0,16},{8,56},{16,32},{24,8},{32,48},{40,24},{48,0},{56,40},{1,17}... | collective-permute-start | bytes 786440 | tf_op jit(solution)/shard_map/ppermute | solution.py:384
  165.7 15.6 %collective-permute-start.10 = (f32[2,256,128]{2,1,0:T(8,128)S(1)}, f32[2,256,128]{2,1,0:T(8,128)S(1)}, u32[]{:S(2)}, u32[]{:S(2)}) collective-permute-start(f32[2,256,128]{2,1,0:T(8,128)S(1)} %slice_add_fusion.1), channel_id=1, source_target_pairs={{0,48},{8,24},{16,0},{24,40},{32,16},{40,56},{48,32},{56,8},{1,49}... | collective-permute-start | bytes 786440 | tf_op jit(solution)/shard_map/ppermute | solution.py:384
  183.7 14.7 %all-to-all-start.7 = ((f32[8,64,256]{2,1,0:T(8,128)}), f32[8,64,256]{2,1,0:T(8,128)S(1)}, u32[]{:S(2)}, u32[]{:S(2)}) async-start(f32[8,64,256]{2,1,0:T(8,128)} %student_end.1), calls=%async_computation.7 | async-start | bytes 1048576 | tf_op jit(solution)/shard_map/all_to_all | solution.py:35
  188.9 6.1 %collective-permute-start.13 = (f32[256,128]{1,0:T(8,128)S(1)}, f32[256,128]{1,0:T(8,128)S(1)}, u32[]{:S(2)}, u32[]{:S(2)}) collective-permute-start(f32[256,128]{1,0:T(8,128)S(1)} %get-tuple-element.69), channel_id=1, source_target_pairs={{0,56},{8,16},{16,8},{24,32},{32,24},{40,48},{48,40},{56,0},{1,57}... | collective-permute-start | bytes 393224 | tf_op jit(solution)/shard_map/ppermute | solution.py:392
  189.1 6.0 %collective-permute-start.14 = (f32[256,128]{1,0:T(8,128)S(1)}, f32[256,128]{1,0:T(8,128)S(1)}, u32[]{:S(2)}, u32[]{:S(2)}) collective-permute-start(f32[256,128]{1,0:T(8,128)S(1)} %get-tuple-element.71), channel_id=1, source_target_pairs={{0,8},{8,0},{16,24},{24,16},{32,40},{40,32},{48,56},{56,48},{1,9},... | collective-permute-start | bytes 393224 | tf_op jit(solution)/shard_map/ppermute | solution.py:392

commit v7 on v6

--- a/solution.py
+++ b/solution.py
@@ -286,45 +286,44 @@
     return [(ref, j) for ref in (first_ref, second_ref) for j in range(ref.shape[0])]
 
 
-def row_at(place_ref, i, tiles):
-    per_group = tiles // len(STEPS)
-    return place_ref[4 + STEPS[i // per_group]] * per_group + i % per_group
-
-
 def row_body(place_ref, first_ref, second_ref, pieces_ref, *refs):
-    norm_refs, (scale_ref, sums_ref, tile_ref, rows_ref) = refs[:-4], refs[-4:]
+    norm_refs, (scale_ref, sums_ref, tile_ref) = refs[:-3], refs[-3:]
     scale_ref[...] = 1.0 / jnp.sum(pieces_ref[...], axis=0)
     fill_columns(scale_ref[...], tile_ref)
     tiles = tiles_of(first_ref, second_ref)
     size = 512
-    for i, (ref, j) in enumerate(tiles):
+    totals = []
+    for ref, j in tiles:
         total = jnp.zeros((1, LANES), f32)
         for start in range(0, ref.shape[1], size):
             part = slice(start, start + size)
             energy = ref[j, part, :].astype(f32)
             total = total + jnp.sum(energy * tile_ref[part, :], axis=0, keepdims=True)
-        rows_ref[pl.ds(row_at(place_ref, i, len(tiles)), 1), :] = total
+        totals.append(total)
+    rows = sums_ref.shape[2]
+    for group, step in enumerate(STEPS):
+        value = jnp.concatenate(totals[group * rows : (group + 1) * rows], axis=0)
+        for copy in range(sums_ref.shape[0]):
+            sums_ref[copy, place_ref[4 + step]] = value
     for ref in norm_refs:
-        rows_ref[len(tiles) :, :] = jnp.concatenate([ref[...], jnp.zeros_like(ref)], axis=0)
-    rows = rows_ref[...]
-    for copy in range(sums_ref.shape[0]):
-        sums_ref[copy] = rows
+        for copy in range(sums_ref.shape[0]):
+            sums_ref[copy, len(STEPS)] = ref[...]
 
 
 def row_sums(place, energy, pieces, copies, norm_part=()):
     tiles = sum(part.shape[0] for part in energy)
     protos = energy[0].shape[1]
     whole = pl.BlockSpec(memory_space=pltpu.VMEM)
-    rows = tiles + 2 * sum(part.shape[0] for part in norm_part)
+    groups = len(STEPS)
     return pl.pallas_call(
         row_body,
         in_specs=[pl.BlockSpec(memory_space=pltpu.SMEM)] + [whole] * (3 + len(norm_part)),
         out_specs=[whole] * 2,
         out_shape=[
             jax.ShapeDtypeStruct((protos // LANES, LANES), f32),
-            jax.ShapeDtypeStruct((copies, rows, LANES), f32),
+            jax.ShapeDtypeStruct((copies, groups + len(norm_part), tiles // groups, LANES), f32),
         ],
-        scratch_shapes=[pltpu.VMEM((protos, LANES), f32), pltpu.VMEM((rows, LANES), f32)],
+        scratch_shapes=[pltpu.VMEM((protos, LANES), f32)],
         compiler_params=params(12),
         cost_estimate=work(2 * tiles * LANES * protos, 0),
         name="row_sums",
@@ -334,14 +333,16 @@
 def column_body(place_ref, first_ref, second_ref, pieces_ref, sums_ref, scale_ref, rows_ref):
     tiles = tiles_of(first_ref, second_ref)
     rows_ref[...] = 1.0 / jnp.sum(pieces_ref[...], axis=0)
-    for i in range(len(tiles)):
-        scale_ref[i : i + 1, :] = rows_ref[pl.ds(row_at(place_ref, i, len(tiles)), 1), :]
+    for group, step in enumerate(STEPS):
+        scale_ref[group] = rows_ref[place_ref[4 + step]]
+    rows = rows_ref.shape[1]
 
     def step(k, carry):
-        rows = pl.ds(pl.multiple_of(k * LANES, LANES), LANES)
+        part = pl.ds(pl.multiple_of(k * LANES, LANES), LANES)
         total = jnp.zeros((LANES, LANES), f32)
         for i, (ref, j) in enumerate(tiles):
-            total = total + ref[j, rows, :].astype(f32) * scale_ref[i : i + 1, :]
+            scale = scale_ref[i // rows, i % rows : i % rows + 1, :]
+            total = total + ref[j, part, :].astype(f32) * scale
         sums_ref[0, pl.ds(k, 1), :] = lane_totals(total)
         return carry
 
@@ -359,7 +360,7 @@
         in_specs=[pl.BlockSpec(memory_space=pltpu.SMEM)] + [whole] * 3,
         out_specs=whole,
         out_shape=jax.ShapeDtypeStruct((copies, protos // LANES, LANES), f32),
-        scratch_shapes=[pltpu.VMEM((tiles, LANES), f32)] * 2,
+        scratch_shapes=[pltpu.VMEM(pieces.shape[1:], f32)] * 2,
         compiler_params=params(12),
         cost_estimate=work(2 * tiles * LANES * protos, 0),
         name="column_sums",
@@ -424,15 +425,15 @@
 
     @pl.when(step == 0)
     def _():
-        count = len(tiles)
-        rows_ref[...] = (1.0 / student_temp) / jnp.sum(pieces_ref[:, :, :count, :], axis=(0, 1))
+        total = jnp.sum(pieces_ref[:, :, :groups], axis=(0, 1))
+        rows_ref[...] = (1.0 / student_temp) / total
         for group in range(groups):
             slot = table_ref[5, group]
-            total = jnp.sum(pieces_ref[slot][:, count : count + own, :], axis=0)
-            inverse = (1.0 / student_temp) / total
+            row_scale = rows_ref[slot]
+            inverse = (1.0 / student_temp) / jnp.sum(pieces_ref[slot][:, groups], axis=0)
             for k in range(own):
                 lanes = slice((group * own + k) * LANES, (group * own + k + 1) * LANES)
-                r_ref[:, lanes] = rows_ref[pl.ds(slot * own + k, 1), :]
+                r_ref[:, lanes] = row_scale[k : k + 1, :]
                 n_ref[:, lanes] = inverse[k : k + 1, :]
         feature_ref[...] = jnp.zeros_like(feature_ref)
 
@@ -466,8 +467,8 @@
         size = feature_send_ref.shape[1]
         found = []
         for k in range(WIDE // size):
-            start = pl.multiple_of(first_row(i) + k * size, size)
-            source, sem = feature_ref.at[pl.ds(start, size), :], feature_sems.at[i * (WIDE // size) + k]
+            source = feature_ref.at[pl.ds(i * WIDE + k * size, size), :]
+            sem = feature_sems.at[i * (WIDE // size) + k]
             at = first_row(i) // (2 * size) + k // 2
             kept = pltpu.make_async_copy(source, feature_keep_ref.at[at], sem)
             sent = pltpu.make_async_copy(source, feature_send_ref.at[at], sem)
@@ -488,13 +489,18 @@
         logit_grad = jnp.concatenate(grads, axis=1)
         added = jnp.dot(logit_grad, tokens_of(i), preferred_element_type=f32)
         total_ref[...] = added if i == 0 else total_ref[...] + added
-        rows = pl.ds(pl.multiple_of(first_row(i), WIDE), WIDE)
-        feature_ref[rows, :] += lax.dot_general(
+        feature_ref[i * WIDE : (i + 1) * WIDE, :] += lax.dot_general(
             logit_grad, sw, (((0,), (0,)), ((), ())), preferred_element_type=f32
         )
-        for wanted, copy in feature_copies(i):
-            pl.when(jnp.logical_and(step == pl.num_programs(0) - 1, wanted))(copy.start)
         logits = following
+        if (i + 1) % (len(parts) // 2) == 0:
+
+            @pl.when(step == pl.num_programs(0) - 1)
+            def _(done=i + 1):
+                for chunk in range(done - len(parts) // 2, done):
+                    for wanted, copy in feature_copies(chunk):
+                        pl.when(wanted)(copy.start)
+
 
     def copies(which, at):
         found = []
@@ -570,7 +576,7 @@
                 pltpu.VMEM((2 * block, D), f32),
                 pltpu.VMEM((tokens, D), f32),
                 pltpu.VMEM((2, blocks, block, D // 2), f32),
-                pltpu.VMEM((tokens // LANES, LANES), f32),
+                pltpu.VMEM((len(STEPS), tokens // LANES // len(STEPS), LANES), f32),
                 pltpu.SemaphoreType.DMA((2, blocks)),
                 pltpu.SemaphoreType.DMA((shares,)),
             ],
@@ -612,7 +618,7 @@
             num_scalar_prefetch=1,
             grid=(1,),
             in_specs=[
-                pl.BlockSpec(pieces.shape, lambda i, p: (0, 0, 0)),
+                pl.BlockSpec(memory_space=pltpu.VMEM),
                 pl.BlockSpec((rows, D), lambda i, p: (p[2], 1)),
                 pl.BlockSpec((rows, 1), lambda i, p: (p[2], 0)),
             ],
@@ -644,7 +650,7 @@
         grid_spec=pltpu.PrefetchScalarGridSpec(
             num_scalar_prefetch=1,
             grid=(1,),
-            in_specs=[pl.BlockSpec((rows, width), lambda i, p: (0, 0))] * len(pieces)
+            in_specs=[pl.BlockSpec(memory_space=pltpu.VMEM)] * len(pieces)
             + [pl.BlockSpec((rows, D), lambda i, p: (p[1], 0))],
             out_specs=pl.BlockSpec((rows, D), lambda i, p: (0, 0)),
         ),

time: 200 us -> 194 us (0.970)
  Pallas kernels: 56.1 us -> 51.1 us
    pallas_call x1, Pallas kernels: 19.5 us -> 14.8 us  [gradients(): pl.pallas_call(gradient_body, grid_spec=pltpu.PrefetchScalarGridSpec(num_...]
  transfers between devices with their start and end apart: 17 -> 17, of which waited for: 11 -> 11; matrix products, arithmetic and copies ran while one was open for 2% -> 2% of each run, Pallas kernels for 7% -> 8%
where the time goes in v7:
time: 194 us
  blocking collectives  77.4 us (40%)
  Pallas kernels  51.1 us (26%)
  waiting for transfers between devices  36.7 us (19%)
  starting transfers between devices  22.6 us (12%)
  other arithmetic  3.26 us (2%)
    all_to_all x6, blocking collectives, spread(): return lax.all_to_all(value, axes, 0, 0, tiled=True)  77.4 us
    pallas_call x1, Pallas kernels, gradients(): pl.pallas_call(gradient_body, grid_spec=pltpu.PrefetchScalarGridSpec(num_...  14.8 us
    ppermute x2, waiting for transfers between devices, pass_on(): got = lax.ppermute(far, 'z', [(z, (z + 2 * way[z]) % n) for z in range(n)])  10.8 us
    pallas_call x2, Pallas kernels, energy_of(): pl.pallas_call(functools.partial(energy_body, layout, len(before)), grid_...  9.5 us
    all_to_all x2, starting transfers between devices, spread(): return lax.all_to_all(value, axes, 0, 0, tiled=True)  9.01 us
    pallas_call x3, Pallas kernels, row_sums(): pl.pallas_call(row_body, in_specs=[pl.BlockSpec(memory_space=pltpu.SMEM)]...  7.56 us
    ppermute x2, waiting for transfers between devices, collect(): got = lax.ppermute(send, 'z', [(z, (z - way[z]) % n) for z in range(n)])  7.53 us
    ppermute x4, waiting for transfers between devices, on_device(): lax.ppermute(value, 'y', [(i, (i + step) % y_size) for i in range(y_size)])  7.14 us
  transfers between devices with their start and end apart: 17, of which 11 were waited for; matrix products, arithmetic and copies ran while one was open for 2% of the time, Pallas kernels for 8%

profile of v7, /device:TPU:1, one launch (start us, length us, event | category | flops | bytes accessed | tf_op | source)
XLA Modules:
  0.0 193.6 jit_solution(12673188070424891432)
XLA Ops:
  0.6 3.0 %select.31 = (f32[512,512]{1,0:T(8,128)}, f32[512,1]{1,0:T(8,128)}, f32[512,256]{1,0:T(8,128)}) custom-call(s32[1]{0:T(128)} %bitcast.core_ref, bf16[4,256,256]{2,1,0:T(8,128)(2,1)} %teacher_ref.1, bf16[4,256,256]{2,1,0:T(8,128)(2,1)} %student_ref.1, s32[4,256]{1,0:T(4,128)} %order_ref.1), custom_call_target="tpu_custom_call" | custom-call | tf_op jit(solution)/shard_map/select/pallas_call | solution.py:99
  3.6 3.6 %collective-permute-start.1 = (f32[512,256]{1,0:T(8,128)}, f32[512,256]{1,0:T(8,128)S(1)}, u32[]{:S(2)}, u32[]{:S(2)}) collective-permute-start(f32[512,256]{1,0:T(8,128)} %get-tuple-element.38), channel_id=1, source_target_pairs={{0,192},{64,0},{128,64},{192,128},{1,193},{65,1},{129,65},{193,129... | collective-permute-start | bytes 1572872 | tf_op jit(solution)/shard_map/ppermute | solution.py:677
  8.1 6.2 %student.1.refs_0_ = f32[4,128]{1,0:T(4,128)S(1)} custom-call(f32[512,512]{1,0:T(8,128)} %get-tuple-element.37.units_ref.refs_0_.unit_ref, bf16[8192,256]{1,0:T(8,128)(2,1)} %refs_4_.3), custom_call_target="tpu_custom_call" | custom-call | flops 4294967296 | bytes 8388608 | tf_op jit(solution)/shard_map/student/pallas_call | solution.py:263
  14.2 3.8 %collective-permute-done.1.refs_2_ = f32[512,256]{1,0:T(8,128)S(1)} collective-permute-done((f32[512,256]{1,0:T(8,128)}, f32[512,256]{1,0:T(8,128)S(1)}, u32[]{:S(2)}, u32[]{:S(2)}) %collective-permute-start.1) | collective-permute-done | bytes 524320 | tf_op jit(solution)/shard_map/ppermute | solution.py:677
  18.1 3.0 %collective-permute-done.refs_1_ = f32[512,256]{1,0:T(8,128)S(1)} collective-permute-done((f32[512,256]{1,0:T(8,128)}, f32[512,256]{1,0:T(8,128)S(1)}, u32[]{:S(2)}, u32[]{:S(2)}) %collective-permute-start) | collective-permute-done | bytes 524320 | tf_op jit(solution)/shard_map/ppermute | solution.py:677
  25.2 6.0 %energy.2 = (bf16[12,2048,128]{2,1,0:T(8,128)(2,1)S(1)}, f32[1,16,128]{2,1,0:T(8,128)S(1)}, bf16[1536,512]{1,0:T(8,128)(2,1)}) custom-call(s32[8]{0:T(128)S(1)} %stack.57.place_ref, f32[512,512]{1,0:T(8,128)S(1)} %copy-done, f32[512,256]{1,0:T(8,128)S(1)} %collective-permute-done.refs_1_, f32[512,256]{1,0:T(8,128)S(1)} %collective-permute-done.1.refs_2_, ...), custom_call_target="tpu_custom_call" | custom-call | flops 3221225472 | bytes 8388608 | tf_op jit(solution)/shard_map/energy/pallas_call | solution.py:206
  34.6 3.5 %energy.3 = (bf16[4,2048,128]{2,1,0:T(8,128)(2,1)S(1)}, f32[8,16,128]{2,1,0:T(8,128)S(1)}, bf16[512,512]{1,0:T(8,128)(2,1)}) custom-call(s32[8]{0:T(128)S(1)} %stack.57.place_ref, f32[256,256]{1,0:T(8,128)S(1)} %collective-permute-done.4.refs_0_, f32[256,256]{1,0:T(8,128)S(1)} %collective-permute-done.5.refs_1_, ...), custom_call_target="tpu_custom_call" | custom-call | flops 1073741824 | bytes 8388608 | tf_op jit(solution)/shard_map/energy/pallas_call | solution.py:206
  38.2 15.2 %all_to_all.40.pieces_ref = f32[8,16,128]{2,1,0:T(8,128)S(1)} all-to-all(f32[8,16,128]{2,1,0:T(8,128)S(1)} %get-tuple-element.51), channel_id=1, replica_groups=mesh['y'=4,'z'=8,'x'=4,'core'=2] {'z'}, dimensions={0} | all-to-all | bytes 131072 | tf_op jit(solution)/shard_map/all_to_all | solution.py:35
  53.4 2.5 %row_sums.3 = (f32[16,128]{1,0:T(8,128)}, f32[32,4,4,128]{3,2,1,0:T(4,128)S(1)}) custom-call(s32[8]{0:T(128)S(1)} %stack.57.place_ref, bf16[12,2048,128]{2,1,0:T(8,128)(2,1)S(1)} %get-tuple-element.49.first_ref.energy_first_ref, bf16[4,2048,128]{2,1,0:T(8,128)(2,1)S(1)} %get-tuple-element.50.second_ref.energy_second_ref, f32[8,16,128]{2,1,0:T(8,128)S(1)} %all_to_all.40.pieces_ref), custom_call_target="tpu_custom_call" | custom-call | flops 8388608 | tf_op jit(solution)/shard_map/row_sums/pallas_call | solution.py:318
  55.9 15.1 %all_to_all.41.pieces_ref = f32[32,4,4,128]{3,2,1,0:T(4,128)S(1)} all-to-all(f32[32,4,4,128]{3,2,1,0:T(4,128)S(1)} %get-tuple-element.52), channel_id=1, replica_groups=mesh['y'=4,'z'=8,'x'=4,'core'=2] {'y','x','core'}, dimensions={0} | all-to-all | bytes 524288 | tf_op jit(solution)/shard_map/all_to_all | solution.py:35
  71.1 2.7 %column_sums.2 = f32[8,16,128]{2,1,0:T(8,128)S(1)} custom-call(s32[8]{0:T(128)S(1)} %stack.57.place_ref, bf16[12,2048,128]{2,1,0:T(8,128)(2,1)S(1)} %get-tuple-element.49.first_ref.energy_first_ref, bf16[4,2048,128]{2,1,0:T(8,128)(2,1)S(1)} %get-tuple-element.50.second_ref.energy_second_ref, f32[32,4,4,128]{3,2,1,0:T(4,128)S(1)} %all_to_all.41.pieces_ref), custom_call_target="tpu_custom_call" | custom-call | flops 8388608 | tf_op jit(solution)/shard_map/column_sums/pallas_call | solution.py:358
  73.8 9.5 %all_to_all.42.pieces_ref = f32[8,16,128]{2,1,0:T(8,128)S(1)} all-to-all(f32[8,16,128]{2,1,0:T(8,128)S(1)} %column_sums.2), channel_id=1, replica_groups=mesh['y'=4,'z'=8,'x'=4,'core'=2] {'z'}, dimensions={0} | all-to-all | bytes 131072 | tf_op jit(solution)/shard_map/all_to_all | solution.py:35
  85.8 13.7 %all_to_all.43.pieces_ref = f32[32,4,4,128]{3,2,1,0:T(4,128)S(1)} all-to-all(f32[32,4,4,128]{3,2,1,0:T(4,128)S(1)} %get-tuple-element.53), channel_id=1, replica_groups=mesh['y'=4,'z'=8,'x'=4,'core'=2] {'y','x','core'}, dimensions={0} | all-to-all | bytes 524288 | tf_op jit(solution)/shard_map/all_to_all | solution.py:35
  99.5 2.7 %column_sums.3 = f32[8,16,128]{2,1,0:T(8,128)S(1)} custom-call(s32[8]{0:T(128)S(1)} %stack.57.place_ref, bf16[12,2048,128]{2,1,0:T(8,128)(2,1)S(1)} %get-tuple-element.49.first_ref.energy_first_ref, bf16[4,2048,128]{2,1,0:T(8,128)(2,1)S(1)} %get-tuple-element.50.second_ref.energy_second_ref, f32[32,4,4,128]{3,2,1,0:T(4,128)S(1)} %all_to_all.43.pieces_ref), custom_call_target="tpu_custom_call" | custom-call | flops 8388608 | tf_op jit(solution)/shard_map/column_sums/pallas_call | solution.py:358
  102.2 9.5 %all_to_all.44.pieces_ref = f32[8,16,128]{2,1,0:T(8,128)S(1)} all-to-all(f32[8,16,128]{2,1,0:T(8,128)S(1)} %column_sums.3), channel_id=1, replica_groups=mesh['y'=4,'z'=8,'x'=4,'core'=2] {'z'}, dimensions={0} | all-to-all | bytes 131072 | tf_op jit(solution)/shard_map/all_to_all | solution.py:35
  111.7 2.5 %row_sums.5 = (f32[16,128]{1,0:T(8,128)S(1)}, f32[32,5,4,128]{3,2,1,0:T(4,128)S(1)}) custom-call(s32[8]{0:T(128)S(1)} %stack.57.place_ref, bf16[12,2048,128]{2,1,0:T(8,128)(2,1)S(1)} %get-tuple-element.49.first_ref.energy_first_ref, bf16[4,2048,128]{2,1,0:T(8,128)(2,1)S(1)} %get-tuple-element.50.second_ref.energy_second_ref, ...), custom_call_target="tpu_custom_call" | custom-call | flops 8388608 | tf_op jit(solution)/shard_map/row_sums/pallas_call | solution.py:318
  114.3 14.3 %all_to_all.45 = f32[32,5,4,128]{3,2,1,0:T(4,128)S(1)} all-to-all(f32[32,5,4,128]{3,2,1,0:T(4,128)S(1)} %get-tuple-element.55), channel_id=1, replica_groups=mesh['y'=4,'z'=8,'x'=4,'core'=2] {'y','x','core'}, dimensions={0} | all-to-all | bytes 655360 | tf_op jit(solution)/shard_map/all_to_all | solution.py:35
  128.6 14.8 %gradients.1 = (f32[4,256,128]{2,1,0:T(8,128)}, f32[4,256,128]{2,1,0:T(8,128)}, f32[4,256,128]{2,1,0:T(8,128)}, f32[4,256,128]{2,1,0:T(8,128)}, f32[16,64,256]{2,1,0:T(8,128)}, /*index=5*/f32[16,64,256]{2,1,0:T(8,128)S(1)}) custom-call(s32[6,8]{1,0:T(8,128)S(1)} %stack.62.table_ref, bf16[1536,512]{1,0:T(8,128)(2,1)} %get-tuple-element.43.units_first_ref, ...), custom_call_target="tpu_custom_call" | custom-call | flops 8589934592 | bytes 8388608 | tf_op jit(solution)/shard_map/gradients/pallas_call | solution.py:557
  147.5 3.7 %all-to-all-start.6 = ((f32[16,64,256]{2,1,0:T(8,128)}), f32[16,64,256]{2,1,0:T(8,128)S(1)}, u32[]{:S(2)}, u32[]{:S(2)}) async-start(f32[16,64,256]{2,1,0:T(8,128)} %add.170), calls=%async_computation.6 | async-start | bytes 2097152 | tf_op jit(solution)/shard_map/all_to_all | solution.py:35
  151.2 7.5 %collective-permute-done.11 = f32[4,256,128]{2,1,0:T(8,128)} collective-permute-done((f32[4,256,128]{2,1,0:T(8,128)}, f32[4,256,128]{2,1,0:T(8,128)}, u32[]{:S(2)}, u32[]{:S(2)}) %collective-permute-start.11) | collective-permute-done | bytes 524320 | tf_op jit(solution)/shard_map/ppermute | solution.py:377
  160.1 3.6 %collective-permute-start.10 = (f32[2,256,128]{2,1,0:T(8,128)S(1)}, f32[2,256,128]{2,1,0:T(8,128)S(1)}, u32[]{:S(2)}, u32[]{:S(2)}) collective-permute-start(f32[2,256,128]{2,1,0:T(8,128)S(1)} %slice_add_fusion.1), channel_id=1, source_target_pairs={{0,48},{8,24},{16,0},{24,40},{32,16},{40,56},{48,32},{56,8},{1,49}... | collective-permute-start | bytes 786440 | tf_op jit(solution)/shard_map/ppermute | solution.py:385
  163.7 10.8 %collective-permute-done.12 = f32[2,256,128]{2,1,0:T(8,128)S(1)} collective-permute-done((f32[2,256,128]{2,1,0:T(8,128)S(1)}, f32[2,256,128]{2,1,0:T(8,128)S(1)}, u32[]{:S(2)}, u32[]{:S(2)}) %collective-permute-start.12) | collective-permute-done | bytes 262176 | tf_op jit(solution)/shard_map/ppermute | solution.py:385
  177.9 5.4 %all-to-all-start.7 = ((f32[8,64,256]{2,1,0:T(8,128)}), f32[8,64,256]{2,1,0:T(8,128)S(1)}, u32[]{:S(2)}, u32[]{:S(2)}) async-start(f32[8,64,256]{2,1,0:T(8,128)} %student_end.1), calls=%async_computation.7 | async-start | bytes 1048576 | tf_op jit(solution)/shard_map/all_to_all | solution.py:35
  183.5 5.9 %collective-permute-done.13.refs_1_ = f32[256,128]{1,0:T(8,128)S(1)} collective-permute-done((f32[256,128]{1,0:T(8,128)S(1)}, f32[256,128]{1,0:T(8,128)S(1)}, u32[]{:S(2)}, u32[]{:S(2)}) %collective-permute-start.13) | collective-permute-done | bytes 131104 | tf_op jit(solution)/shard_map/ppermute | solution.py:393
  (47 shorter events, 24.2 us)
Async XLA Ops:
  3.6 14.5 %collective-permute-start.1 = (f32[512,256]{1,0:T(8,128)}, f32[512,256]{1,0:T(8,128)S(1)}, u32[]{:S(2)}, u32[]{:S(2)}) collective-permute-start(f32[512,256]{1,0:T(8,128)} %get-tuple-element.38), channel_id=1, source_target_pairs={{0,192},{64,0},{128,64},{192,128},{1,193},{65,1},{129,65},{193,129... | collective-permute-start | bytes 1572872 | tf_op jit(solution)/shard_map/ppermute | solution.py:677
  7.2 13.9 %collective-permute-start = (f32[512,256]{1,0:T(8,128)}, f32[512,256]{1,0:T(8,128)S(1)}, u32[]{:S(2)}, u32[]{:S(2)}) collective-permute-start(f32[512,256]{1,0:T(8,128)} %get-tuple-element.38), channel_id=1, source_target_pairs={{0,64},{64,128},{128,192},{192,0},{1,65},{65,129},{129,193},{193,1... | collective-permute-start | bytes 1572872 | tf_op jit(solution)/shard_map/ppermute | solution.py:677
  8.1 17.2 %copy-start = (f32[512,512]{1,0:T(8,128)S(1)}, f32[512,512]{1,0:T(8,128)}, u32[]{:S(2)}) copy-start(f32[512,512]{1,0:T(8,128)} %get-tuple-element.37.units_ref.refs_0_.unit_ref) | copy-start | bytes 3145732
  21.1 3.5 %collective-permute-start.2 = (f32[512,256]{1,0:T(8,128)S(1)}, f32[512,256]{1,0:T(8,128)S(1)}, u32[]{:S(2)}, u32[]{:S(2)}) collective-permute-start(f32[512,256]{1,0:T(8,128)S(1)} %collective-permute-done.refs_1_), channel_id=1, source_target_pairs={{0,1},{1,0},{2,3},{3,2},{4,5},{5,4},{6,7},{7,6},{8,9},{9,8},{10,11... | collective-permute-start | bytes 1572872 | tf_op jit(solution)/shard_map/ppermute | solution.py:680
  22.9 2.3 %collective-permute-start.3 = (f32[512,256]{1,0:T(8,128)S(1)}, f32[512,256]{1,0:T(8,128)S(1)}, u32[]{:S(2)}, u32[]{:S(2)}) collective-permute-start(f32[512,256]{1,0:T(8,128)S(1)} %collective-permute-done.1.refs_2_), channel_id=1, source_target_pairs={{0,1},{1,0},{2,3},{3,2},{4,5},{5,4},{6,7},{7,6},{8,9},{9,8},{10,11... | collective-permute-start | bytes 1572872 | tf_op jit(solution)/shard_map/ppermute | solution.py:680
  23.0 8.2 %collective-permute-start.5 = (f32[256,256]{1,0:T(8,128)S(1)}, f32[256,256]{1,0:T(8,128)S(1)}, u32[]{:S(2)}, u32[]{:S(2)}) collective-permute-start(f32[256,256]{1,0:T(8,128)S(1)} %slice.55), channel_id=1, source_target_pairs={{0,192},{64,0},{128,64},{192,128},{1,193},{65,1},{129,65},{193,129... | collective-permute-start | bytes 786440 | tf_op jit(solution)/shard_map/ppermute | solution.py:677
  23.1 8.4 %collective-permute-start.4 = (f32[256,256]{1,0:T(8,128)S(1)}, f32[256,256]{1,0:T(8,128)S(1)}, u32[]{:S(2)}, u32[]{:S(2)}) collective-permute-start(f32[256,256]{1,0:T(8,128)S(1)} %slice.54), channel_id=1, source_target_pairs={{0,64},{64,128},{128,192},{192,0},{1,65},{65,129},{129,193},{193,1... | collective-permute-start | bytes 786440 | tf_op jit(solution)/shard_map/ppermute | solution.py:677
  31.5 2.7 %collective-permute-start.6 = (f32[256,256]{1,0:T(8,128)S(1)}, f32[256,256]{1,0:T(8,128)S(1)}, u32[]{:S(2)}, u32[]{:S(2)}) collective-permute-start(f32[256,256]{1,0:T(8,128)S(1)} %collective-permute-done.4.refs_0_), channel_id=1, source_target_pairs={{0,1},{1,0},{2,3},{3,2},{4,5},{5,4},{6,7},{7,6},{8,9},{9,8},{10,11... | collective-permute-start | bytes 786440 | tf_op jit(solution)/shard_map/ppermute | solution.py:680
  33.1 1.5 collective-permute-start.7
  143.4 15.3 %copy-start.2 = (f32[4,256,128]{2,1,0:T(8,128)S(1)}, f32[4,256,128]{2,1,0:T(8,128)}, u32[]{:S(2)}) copy-start(f32[4,256,128]{2,1,0:T(8,128)} %get-tuple-element.64) | copy-start | bytes 1572868
  143.4 16.6 %copy-start.1 = (f32[4,256,128]{2,1,0:T(8,128)S(1)}, f32[4,256,128]{2,1,0:T(8,128)}, u32[]{:S(2)}) copy-start(f32[4,256,128]{2,1,0:T(8,128)} %get-tuple-element.62) | copy-start | bytes 1572868
  143.4 3.0 %collective-permute-start.8 = (f32[16,64,256]{2,1,0:T(8,128)}, f32[16,64,256]{2,1,0:T(8,128)S(1)}, u32[]{:S(2)}, u32[]{:S(2)}) collective-permute-start(f32[16,64,256]{2,1,0:T(8,128)} %get-tuple-element.58), channel_id=1, source_target_pairs={{0,1},{1,0},{2,3},{3,2},{4,5},{5,4},{6,7},{7,6},{8,9},{9,8},{10,11... | collective-permute-start | bytes 3145736 | tf_op jit(solution)/shard_map/ppermute | solution.py:680
  143.8 14.9 %collective-permute-start.11 = (f32[4,256,128]{2,1,0:T(8,128)}, f32[4,256,128]{2,1,0:T(8,128)}, u32[]{:S(2)}, u32[]{:S(2)}) collective-permute-start(f32[4,256,128]{2,1,0:T(8,128)} %get-tuple-element.65), channel_id=1, source_target_pairs={{0,56},{8,16},{16,8},{24,32},{32,24},{40,48},{48,40},{56,0},{1,57}... | collective-permute-start | bytes 1572872 | tf_op jit(solution)/shard_map/ppermute | solution.py:377
  143.8 16.2 %collective-permute-start.9 = (f32[4,256,128]{2,1,0:T(8,128)}, f32[4,256,128]{2,1,0:T(8,128)S(1)}, u32[]{:S(2)}, u32[]{:S(2)}) collective-permute-start(f32[4,256,128]{2,1,0:T(8,128)} %get-tuple-element.63), channel_id=1, source_target_pairs={{0,8},{8,0},{16,24},{24,16},{32,40},{40,32},{48,56},{56,48},{1,9},... | collective-permute-start | bytes 1572872 | tf_op jit(solution)/shard_map/ppermute | solution.py:377
  147.5 28.1 %all-to-all-start.6 = ((f32[16,64,256]{2,1,0:T(8,128)}), f32[16,64,256]{2,1,0:T(8,128)S(1)}, u32[]{:S(2)}, u32[]{:S(2)}) async-start(f32[16,64,256]{2,1,0:T(8,128)} %add.170), calls=%async_computation.6 | async-start | bytes 2097152 | tf_op jit(solution)/shard_map/all_to_all | solution.py:35
  159.7 14.8 %collective-permute-start.12 = (f32[2,256,128]{2,1,0:T(8,128)S(1)}, f32[2,256,128]{2,1,0:T(8,128)S(1)}, u32[]{:S(2)}, u32[]{:S(2)}) collective-permute-start(f32[2,256,128]{2,1,0:T(8,128)S(1)} %slice_add_fusion), channel_id=1, source_target_pairs={{0,16},{8,56},{16,32},{24,8},{32,48},{40,24},{48,0},{56,40},{1,17}... | collective-permute-start | bytes 786440 | tf_op jit(solution)/shard_map/ppermute | solution.py:385
  160.1 15.5 %collective-permute-start.10 = (f32[2,256,128]{2,1,0:T(8,128)S(1)}, f32[2,256,128]{2,1,0:T(8,128)S(1)}, u32[]{:S(2)}, u32[]{:S(2)}) collective-permute-start(f32[2,256,128]{2,1,0:T(8,128)S(1)} %slice_add_fusion.1), channel_id=1, source_target_pairs={{0,48},{8,24},{16,0},{24,40},{32,16},{40,56},{48,32},{56,8},{1,49}... | collective-permute-start | bytes 786440 | tf_op jit(solution)/shard_map/ppermute | solution.py:385
  177.9 14.9 %all-to-all-start.7 = ((f32[8,64,256]{2,1,0:T(8,128)}), f32[8,64,256]{2,1,0:T(8,128)S(1)}, u32[]{:S(2)}, u32[]{:S(2)}) async-start(f32[8,64,256]{2,1,0:T(8,128)} %student_end.1), calls=%async_computation.7 | async-start | bytes 1048576 | tf_op jit(solution)/shard_map/all_to_all | solution.py:35
  183.3 6.1 %collective-permute-start.13 = (f32[256,128]{1,0:T(8,128)S(1)}, f32[256,128]{1,0:T(8,128)S(1)}, u32[]{:S(2)}, u32[]{:S(2)}) collective-permute-start(f32[256,128]{1,0:T(8,128)S(1)} %get-tuple-element.69), channel_id=1, source_target_pairs={{0,56},{8,16},{16,8},{24,32},{32,24},{40,48},{48,40},{56,0},{1,57}... | collective-permute-start | bytes 393224 | tf_op jit(solution)/shard_map/ppermute | solution.py:393
  183.5 5.9 %collective-permute-start.14 = (f32[256,128]{1,0:T(8,128)S(1)}, f32[256,128]{1,0:T(8,128)S(1)}, u32[]{:S(2)}, u32[]{:S(2)}) collective-permute-start(f32[256,128]{1,0:T(8,128)S(1)} %get-tuple-element.71), channel_id=1, source_target_pairs={{0,8},{8,0},{16,24},{24,16},{32,40},{40,32},{48,56},{56,48},{1,9},... | collective-permute-start | bytes 393224 | tf_op jit(solution)/shard_map/ppermute | solution.py:393

commit v8 on v5

--- a/solution.py
+++ b/solution.py
@@ -73,7 +73,7 @@
     return jnp.concatenate(parts, axis=0)
 
 
-def select_body(place_ref, teacher_ref, student_ref, order_ref, units_ref, length_ref, mine_ref):
+def select_body(core_ref, teacher_ref, student_ref, order_ref, units_ref, length_ref, mine_ref):
     images, patches, _ = teacher_ref.shape
     for image in range(images):
         chosen = order_ref[image : image + 1, :MASKED]
@@ -90,10 +90,10 @@
         student, length_ref[rows, :] = unit_rows(pick(student_ref))
         units_ref[rows, :D] = teacher
         units_ref[rows, D:] = student
-        mine_ref[rows, :] = jnp.where(place_ref[3] == 0, teacher, student)
-
-
-def select_tokens(place, teacher_patches, student_patches, mask_order):
+        mine_ref[rows, :] = jnp.where(core_ref[0] == 0, teacher, student)
+
+
+def select_tokens(core, teacher_patches, student_patches, mask_order):
     tokens = teacher_patches.shape[0] * MASKED
     return pl.pallas_call(
         select_body,
@@ -107,7 +107,7 @@
         ],
         compiler_params=params(8),
         name="select",
-    )(place, in_hbm(teacher_patches), in_hbm(student_patches), in_hbm(mask_order))
+    )(core, in_hbm(teacher_patches), in_hbm(student_patches), in_hbm(mask_order))
 
 
 def lane_rows(row):
@@ -207,7 +207,7 @@
             num_scalar_prefetch=1,
             grid=(1,),
             in_specs=[pl.BlockSpec(units.shape, lambda i, p: (0, 0))]
-            + [pl.BlockSpec(piece.shape, lambda i, p: (0, 0)) for piece in pieces]
+            + [direct] * len(pieces)
             + [pl.BlockSpec((share, D), lambda i, p: (p[0], 0))],
             out_specs=[
                 direct,
@@ -398,7 +398,6 @@
     feature_ref,
     stage_ref,
     sems,
-    feature_sems,
 ):
     step = pl.program_id(0)
     tiles = energy_ref.shape[0]
@@ -434,16 +433,6 @@
         return nt_dot(sw, units_ref[part, D:])
 
     parts = [slice(c, c + WIDE) for c in range(0, units_ref.shape[0], WIDE)]
-
-    def feature_copies(i):
-        size = feature_send_ref.shape[1]
-        found = []
-        for at in range(i * WIDE // size, (i + 1) * WIDE // size):
-            source, sem = feature_ref.at[pl.ds(at * size, size), :], feature_sems.at[at]
-            kept = pltpu.make_async_copy(source, feature_keep_ref.at[at // 2], sem)
-            sent = pltpu.make_async_copy(source, feature_send_ref.at[at // 2], sem)
-            found += [(table_ref[4, 0] == at % 2, kept), (table_ref[4, 0] != at % 2, sent)]
-        return found
 
     logits = logits_of(parts[0])
     for i, part in enumerate(parts):
@@ -461,8 +450,6 @@
         feature_ref[part, :] += lax.dot_general(
             logit_grad, sw, (((0,), (0,)), ((), ())), preferred_element_type=f32
         )
-        for wanted, copy in feature_copies(i):
-            pl.when(jnp.logical_and(step == pl.num_programs(0) - 1, wanted))(copy.start)
         logits = following
 
     def copies(which, at):
@@ -488,9 +475,15 @@
 
     @pl.when(step == pl.num_programs(0) - 1)
     def _():
-        for i in range(len(parts)):
-            for wanted, copy in feature_copies(i):
-                pl.when(wanted)(copy.wait)
+        size = feature_send_ref.shape[1]
+        for core in range(2):
+
+            @pl.when(table_ref[4, 0] == core)
+            def _(core=core):
+                for at in range(feature_ref.shape[0] // size):
+                    out_ref = feature_keep_ref if at % 2 == core else feature_send_ref
+                    out_ref[at // 2] = feature_ref[at * size : (at + 1) * size, :]
+
         for at in range(stage_ref.shape[1] // 2):
             for which in range(2):
                 for wanted, copy in copies(which, at):
@@ -529,7 +522,7 @@
                 second,
                 whole(*scale.shape),
             ],
-            out_specs=[pl.BlockSpec(memory_space=pl.ANY)] * 6,
+            out_specs=[pl.BlockSpec(memory_space=pl.ANY)] * 4 + [direct] * 2,
             scratch_shapes=[
                 pltpu.VMEM((1, tokens), f32),
                 pltpu.VMEM((1, tokens), f32),
@@ -537,10 +530,9 @@
                 pltpu.VMEM((tokens, D), f32),
                 pltpu.VMEM((2, blocks, block, D // 2), f32),
                 pltpu.SemaphoreType.DMA((2, blocks)),
-                pltpu.SemaphoreType.DMA((shares,)),
             ],
         ),
-        out_shape=[half] * 4 + [pltpu.HBM((shares // 2, tokens // shares, D), f32)] * 2,
+        out_shape=[half] * 4 + [pltpu.VMEM((shares // 2, tokens // shares, D), f32)] * 2,
         compiler_params=params(24),
         cost_estimate=work(8 * tokens * share * D, 8 * 2**20, tokens * share),
         name="gradients",
@@ -573,7 +565,7 @@
             num_scalar_prefetch=1,
             grid=(1,),
             in_specs=[
-                pl.BlockSpec(pieces.shape, lambda i, p: (0, 0, 0)),
+                pl.BlockSpec(memory_space=pltpu.VMEM),
                 pl.BlockSpec((rows, D), lambda i, p: (p[2], 1)),
                 pl.BlockSpec((rows, 1), lambda i, p: (p[2], 0)),
             ],
@@ -605,7 +597,7 @@
         grid_spec=pltpu.PrefetchScalarGridSpec(
             num_scalar_prefetch=1,
             grid=(1,),
-            in_specs=[pl.BlockSpec((rows, width), lambda i, p: (0, 0))] * len(pieces)
+            in_specs=[pl.BlockSpec(memory_space=pltpu.VMEM)] * len(pieces)
             + [pl.BlockSpec((rows, D), lambda i, p: (p[1], 0))],
             out_specs=pl.BlockSpec((rows, D), lambda i, p: (0, 0)),
         ),
@@ -620,14 +612,14 @@
     proto_size = lax.axis_size("x") * lax.axis_size("core")
     y, z = lax.axis_index("y"), lax.axis_index("z")
     others = [(y - step + y_size) % y_size for step in range(y_size)]
-    place = [y, y * z_size + z, lax.axis_index(PROTOS), lax.axis_index("core")] + others
-    place, table = lax.optimization_barrier(
-        (jnp.stack(place).astype(jnp.int32), block_table(y, z, lax.axis_index("core")))
-    )
+    core = lax.axis_index("core")
+    place = [y, y * z_size + z, lax.axis_index(PROTOS), core] + others
+    place = jnp.stack(place).astype(jnp.int32)
+    table = block_table(y, z, core)
     share = teacher_protos.shape[0] // y_size
 
     units, student_length, mine = select_tokens(
-        place, teacher_patches, student_patches, mask_order
+        core.astype(jnp.int32)[None], teacher_patches, student_patches, mask_order
     )
     from_y = lambda value, step: lax.ppermute(
         value, "y", [(i, (i + step) % y_size) for i in range(y_size)]
@@ -636,7 +628,9 @@
     half = mine.shape[0] // 2
     first, third = from_y(mine, 1), from_y(mine, 3)
     norm_part = student_sums(units, student_protos)
-    norm_part, first, third = lax.optimization_barrier((norm_part, first, third))
+    norm_part, first, third, place, table = lax.optimization_barrier(
+        (norm_part, first, third, place, table)
+    )
     got = [first, third, from_y(first[:half], 1), from_y(third[half:], 3)]
     got = got + [from_core(piece) for piece in got]
 

time: 191 us -> 189 us (0.990)
  no operation moved by 1% of the time
where the time goes in v8:
time: 189 us
  blocking collectives  77.9 us (41%)
  Pallas kernels  43.8 us (23%)
  waiting for transfers between devices  37.5 us (20%)
  starting transfers between devices  25.8 us (14%)
    all_to_all x6, blocking collectives, spread(): return lax.all_to_all(value, axes, 0, 0, tiled=True)  77.9 us
    pallas_call x1, Pallas kernels, gradients(): pl.pallas_call(gradient_body, grid_spec=pltpu.PrefetchScalarGridSpec(num_...  12 us
    ppermute x2, waiting for transfers between devices, pass_on(): got = lax.ppermute(far, 'z', [(z, (z + 2 * way[z]) % n) for z in range(n)])  10.9 us
    ppermute x4, waiting for transfers between devices, on_device(): lax.ppermute(value, 'y', [(i, (i + step) % y_size) for i in range(y_size)])  8.93 us
    all_to_all x2, starting transfers between devices, spread(): return lax.all_to_all(value, axes, 0, 0, tiled=True)  8.9 us
    ppermute x2, waiting for transfers between devices, collect(): got = lax.ppermute(send, 'z', [(z, (z - way[z]) % n) for z in range(n)])  7.72 us
    pallas_call x1, Pallas kernels, energy_of(): pl.pallas_call(energy_body, grid_spec=pltpu.PrefetchScalarGridSpec(num_sc...  7.42 us
    ppermute x5, starting transfers between devices, on_device(): from_core = lambda value: lax.ppermute(value, 'core', [(0, 1), (1, 0)])  7.31 us
  transfers between devices with their start and end apart: 17, of which 9 were waited for; matrix products, arithmetic and copies ran while one was open for 1% of the time, Pallas kernels for 4%

profile of v8, /device:TPU:1, one launch (start us, length us, event | category | flops | bytes accessed | tf_op | source)
XLA Modules:
  0.0 188.6 jit_solution(17436790194412438331)
XLA Ops:
  0.6 3.0 %select.31 = (f32[512,512]{1,0:T(8,128)}, f32[512,1]{1,0:T(8,128)}, f32[512,256]{1,0:T(8,128)}) custom-call(s32[1]{0:T(128)} %bitcast.core_ref, bf16[4,256,256]{2,1,0:T(8,128)(2,1)} %teacher_ref.1, bf16[4,256,256]{2,1,0:T(8,128)(2,1)} %student_ref.1, s32[4,256]{1,0:T(4,128)} %order_ref.1), custom_call_target="tpu_custom_call" | custom-call | tf_op jit(solution)/shard_map/select/pallas_call | solution.py:98
  3.6 3.6 %collective-permute-start.1 = (f32[512,256]{1,0:T(8,128)}, f32[512,256]{1,0:T(8,128)S(1)}, u32[]{:S(2)}, u32[]{:S(2)}) collective-permute-start(f32[512,256]{1,0:T(8,128)} %get-tuple-element.32), channel_id=1, source_target_pairs={{0,192},{64,0},{128,64},{192,128},{1,193},{65,1},{129,65},{193,129... | collective-permute-start | bytes 1572872 | tf_op jit(solution)/shard_map/ppermute | solution.py:624
  8.0 6.1 %student.1.refs_0_ = f32[4,128]{1,0:T(4,128)S(1)} custom-call(f32[512,512]{1,0:T(8,128)} %get-tuple-element.31.units_ref.unit_ref, bf16[8192,256]{1,0:T(8,128)(2,1)} %refs_4_.1), custom_call_target="tpu_custom_call" | custom-call | flops 4294967296 | bytes 8388608 | tf_op jit(solution)/shard_map/student/pallas_call | solution.py:261
  14.1 4.0 %collective-permute-done.1.refs_1_ = f32[512,256]{1,0:T(8,128)S(1)} collective-permute-done((f32[512,256]{1,0:T(8,128)}, f32[512,256]{1,0:T(8,128)S(1)}, u32[]{:S(2)}, u32[]{:S(2)}) %collective-permute-start.1) | collective-permute-done | bytes 524320 | tf_op jit(solution)/shard_map/ppermute | solution.py:624
  18.1 3.0 %collective-permute-done.refs_0_ = f32[512,256]{1,0:T(8,128)S(1)} collective-permute-done((f32[512,256]{1,0:T(8,128)}, f32[512,256]{1,0:T(8,128)S(1)}, u32[]{:S(2)}, u32[]{:S(2)}) %collective-permute-start) | collective-permute-done | bytes 524320 | tf_op jit(solution)/shard_map/ppermute | solution.py:624
  22.7 2.4 %collective-permute-start.4 = (f32[512,256]{1,0:T(8,128)S(1)}, f32[512,256]{1,0:T(8,128)S(1)}, u32[]{:S(2)}, u32[]{:S(2)}) collective-permute-start(f32[512,256]{1,0:T(8,128)S(1)} %collective-permute-done.refs_0_), channel_id=1, source_target_pairs={{0,1},{1,0},{2,3},{3,2},{4,5},{5,4},{6,7},{7,6},{8,9},{9,8},{10,11... | collective-permute-start | bytes 1572872 | tf_op jit(solution)/shard_map/ppermute | solution.py:627
  27.1 2.8 %collective-permute-start.7 = (f32[256,256]{1,0:T(8,128)S(1)}, f32[256,256]{1,0:T(8,128)S(1)}, u32[]{:S(2)}, u32[]{:S(2)}) collective-permute-start(f32[256,256]{1,0:T(8,128)S(1)} %collective-permute-done.3.refs_3_), channel_id=1, source_target_pairs={{0,1},{1,0},{2,3},{3,2},{4,5},{5,4},{6,7},{7,6},{8,9},{9,8},{10,11... | collective-permute-start | bytes 786440 | tf_op jit(solution)/shard_map/ppermute | solution.py:627
  32.7 7.4 %energy.1 = (bf16[16,2048,128]{2,1,0:T(8,128)(2,1)S(1)}, f32[8,16,128]{2,1,0:T(8,128)S(1)}, bf16[2048,512]{1,0:T(8,128)(2,1)}) custom-call(s32[8]{0:T(128)S(1)} %stack.43.place_ref, f32[512,512]{1,0:T(8,128)} %get-tuple-element.31.units_ref.unit_ref, f32[512,256]{1,0:T(8,128)S(1)} %collective-permute-done.refs_0_, ...), custom_call_target="tpu_custom_call" | custom-call | flops 4294967296 | bytes 8388608 | tf_op jit(solution)/shard_map/energy/pallas_call | solution.py:204
  40.1 15.2 %all_to_all.40.pieces_ref = f32[8,16,128]{2,1,0:T(8,128)S(1)} all-to-all(f32[8,16,128]{2,1,0:T(8,128)S(1)} %get-tuple-element.39), channel_id=1, replica_groups=mesh['y'=4,'z'=8,'x'=4,'core'=2] {'z'}, dimensions={0} | all-to-all | bytes 131072 | tf_op jit(solution)/shard_map/all_to_all | solution.py:34
  57.5 15.0 %all_to_all.41.pieces_ref = f32[32,16,128]{2,1,0:T(8,128)S(1)} all-to-all(f32[32,16,128]{2,1,0:T(8,128)S(1)} %get-tuple-element.40), channel_id=1, replica_groups=mesh['y'=4,'z'=8,'x'=4,'core'=2] {'y','x','core'}, dimensions={0} | all-to-all | bytes 524288 | tf_op jit(solution)/shard_map/all_to_all | solution.py:34
  72.4 2.2 %column_sums.2 = f32[8,16,128]{2,1,0:T(8,128)S(1)} custom-call(bf16[16,2048,128]{2,1,0:T(8,128)(2,1)S(1)} %get-tuple-element.38.energy_ref, f32[32,16,128]{2,1,0:T(8,128)S(1)} %all_to_all.41.pieces_ref), custom_call_target="tpu_custom_call" | custom-call | flops 8388608 | tf_op jit(solution)/shard_map/column_sums/pallas_call | solution.py:343
  74.6 9.5 %all_to_all.42.pieces_ref = f32[8,16,128]{2,1,0:T(8,128)S(1)} all-to-all(f32[8,16,128]{2,1,0:T(8,128)S(1)} %column_sums.2), channel_id=1, replica_groups=mesh['y'=4,'z'=8,'x'=4,'core'=2] {'z'}, dimensions={0} | all-to-all | bytes 131072 | tf_op jit(solution)/shard_map/all_to_all | solution.py:34
  86.3 13.7 %all_to_all.43.pieces_ref = f32[32,16,128]{2,1,0:T(8,128)S(1)} all-to-all(f32[32,16,128]{2,1,0:T(8,128)S(1)} %get-tuple-element.41), channel_id=1, replica_groups=mesh['y'=4,'z'=8,'x'=4,'core'=2] {'y','x','core'}, dimensions={0} | all-to-all | bytes 524288 | tf_op jit(solution)/shard_map/all_to_all | solution.py:34
  102.2 9.5 %all_to_all.44.pieces_ref = f32[8,16,128]{2,1,0:T(8,128)S(1)} all-to-all(f32[8,16,128]{2,1,0:T(8,128)S(1)} %column_sums.3), channel_id=1, replica_groups=mesh['y'=4,'z'=8,'x'=4,'core'=2] {'z'}, dimensions={0} | all-to-all | bytes 131072 | tf_op jit(solution)/shard_map/all_to_all | solution.py:34
  113.7 15.0 %all_to_all.45 = f32[32,24,128]{2,1,0:T(8,128)S(1)} all-to-all(f32[32,24,128]{2,1,0:T(8,128)S(1)} %get-tuple-element.43), channel_id=1, replica_groups=mesh['y'=4,'z'=8,'x'=4,'core'=2] {'y','x','core'}, dimensions={0} | all-to-all | bytes 786432 | tf_op jit(solution)/shard_map/all_to_all | solution.py:34
  128.6 12.0 %gradients.1 = (f32[4,256,128]{2,1,0:T(8,128)}, f32[4,256,128]{2,1,0:T(8,128)}, f32[4,256,128]{2,1,0:T(8,128)}, f32[4,256,128]{2,1,0:T(8,128)}, f32[16,64,256]{2,1,0:T(8,128)S(1)}, /*index=5*/f32[16,64,256]{2,1,0:T(8,128)S(1)}) custom-call(s32[5,8]{1,0:T(8,128)S(1)} %stack.46.table_ref, bf16[2048,512]{1,0:T(8,128)(2,1)} %get-tuple-element.37.units_ref, ...), custom_call_target="tpu_custom_call" | custom-call | flops 8589934592 | bytes 8388608 | tf_op jit(solution)/shard_map/gradients/pallas_call | solution.py:512
  144.5 3.7 %all-to-all-start.6 = ((f32[16,64,256]{2,1,0:T(8,128)}), f32[16,64,256]{2,1,0:T(8,128)S(1)}, u32[]{:S(2)}, u32[]{:S(2)}) async-start(f32[16,64,256]{2,1,0:T(8,128)} %add.170), calls=%async_computation.6 | async-start | bytes 2097152 | tf_op jit(solution)/shard_map/all_to_all | solution.py:34
  148.2 7.7 %collective-permute-done.11 = f32[4,256,128]{2,1,0:T(8,128)S(1)} collective-permute-done((f32[4,256,128]{2,1,0:T(8,128)}, f32[4,256,128]{2,1,0:T(8,128)S(1)}, u32[]{:S(2)}, u32[]{:S(2)}) %collective-permute-start.11) | collective-permute-done | bytes 524320 | tf_op jit(solution)/shard_map/ppermute | solution.py:362
  156.1 3.6 %collective-permute-start.10 = (f32[2,256,128]{2,1,0:T(8,128)S(1)}, f32[2,256,128]{2,1,0:T(8,128)S(1)}, u32[]{:S(2)}, u32[]{:S(2)}) collective-permute-start(f32[2,256,128]{2,1,0:T(8,128)S(1)} %slice_add_fusion.1), channel_id=1, source_target_pairs={{0,48},{8,24},{16,0},{24,40},{32,16},{40,56},{48,32},{56,8},{1,49}... | collective-permute-start | bytes 786440 | tf_op jit(solution)/shard_map/ppermute | solution.py:370
  159.7 10.9 %collective-permute-done.12 = f32[2,256,128]{2,1,0:T(8,128)S(1)} collective-permute-done((f32[2,256,128]{2,1,0:T(8,128)S(1)}, f32[2,256,128]{2,1,0:T(8,128)S(1)}, u32[]{:S(2)}, u32[]{:S(2)}) %collective-permute-start.12) | collective-permute-done | bytes 262176 | tf_op jit(solution)/shard_map/ppermute | solution.py:370
  170.7 2.3 %student_end.1 = f32[8,64,256]{2,1,0:T(8,128)} custom-call(s32[8]{0:T(128)S(1)} %stack.43.place_ref, f32[16,64,256]{2,1,0:T(8,128)S(1)} %all-to-all-done.6.pieces_ref, f32[512,512]{1,0:T(8,128)} %get-tuple-element.31.units_ref.unit_ref, f32[512,1]{1,0:T(8,128)} %get-tuple-element.55.length_ref), custom_call_target="tpu_custom_call" | custom-call | tf_op jit(solution)/shard_map/student_end/pallas_call | solution.py:562
  173.1 5.3 %all-to-all-start.7 = ((f32[8,64,256]{2,1,0:T(8,128)}), f32[8,64,256]{2,1,0:T(8,128)S(1)}, u32[]{:S(2)}, u32[]{:S(2)}) async-start(f32[8,64,256]{2,1,0:T(8,128)} %student_end.1), calls=%async_computation.7 | async-start | bytes 1048576 | tf_op jit(solution)/shard_map/all_to_all | solution.py:34
  178.5 5.9 %collective-permute-done.13.refs_1_ = f32[256,128]{1,0:T(8,128)S(1)} collective-permute-done((f32[256,128]{1,0:T(8,128)S(1)}, f32[256,128]{1,0:T(8,128)S(1)}, u32[]{:S(2)}, u32[]{:S(2)}) %collective-permute-start.13) | collective-permute-done | bytes 131104 | tf_op jit(solution)/shard_map/ppermute | solution.py:378
  184.5 2.4 %proto_end.1 = f32[256,256]{1,0:T(8,128)} custom-call(s32[8]{0:T(128)S(1)} %stack.43.place_ref, f32[256,128]{1,0:T(8,128)S(1)} %get-tuple-element.56.refs_0_, f32[256,128]{1,0:T(8,128)S(1)} %collective-permute-done.13.refs_1_, f32[256,128]{1,0:T(8,128)S(1)} %get-tuple-element.58.refs_2_, f32[256,128]{1,0:T(8,128)S(1)} %collective-permute-done.14.refs_3_, ...), custom_call_target="tpu_custom_call" | custom-call | tf_op jit(solution)/shard_map/proto_end/pallas_call | solution.py:595
  (43 shorter events, 21.7 us)
Async XLA Ops:
  3.6 14.5 %collective-permute-start.1 = (f32[512,256]{1,0:T(8,128)}, f32[512,256]{1,0:T(8,128)S(1)}, u32[]{:S(2)}, u32[]{:S(2)}) collective-permute-start(f32[512,256]{1,0:T(8,128)} %get-tuple-element.32), channel_id=1, source_target_pairs={{0,192},{64,0},{128,64},{192,128},{1,193},{65,1},{129,65},{193,129... | collective-permute-start | bytes 1572872 | tf_op jit(solution)/shard_map/ppermute | solution.py:624
  7.2 13.9 %collective-permute-start = (f32[512,256]{1,0:T(8,128)}, f32[512,256]{1,0:T(8,128)S(1)}, u32[]{:S(2)}, u32[]{:S(2)}) collective-permute-start(f32[512,256]{1,0:T(8,128)} %get-tuple-element.32), channel_id=1, source_target_pairs={{0,64},{64,128},{128,192},{192,0},{1,65},{65,129},{129,193},{193,1... | collective-permute-start | bytes 1572872 | tf_op jit(solution)/shard_map/ppermute | solution.py:624
  21.1 6.0 %collective-permute-start.3 = (f32[256,256]{1,0:T(8,128)S(1)}, f32[256,256]{1,0:T(8,128)S(1)}, u32[]{:S(2)}, u32[]{:S(2)}) collective-permute-start(f32[256,256]{1,0:T(8,128)S(1)} %slice.55), channel_id=1, source_target_pairs={{0,192},{64,0},{128,64},{192,128},{1,193},{65,1},{129,65},{193,129... | collective-permute-start | bytes 786440 | tf_op jit(solution)/shard_map/ppermute | solution.py:624
  21.5 8.4 %collective-permute-start.2 = (f32[256,256]{1,0:T(8,128)S(1)}, f32[256,256]{1,0:T(8,128)S(1)}, u32[]{:S(2)}, u32[]{:S(2)}) collective-permute-start(f32[256,256]{1,0:T(8,128)S(1)} %slice.54), channel_id=1, source_target_pairs={{0,64},{64,128},{128,192},{192,0},{1,65},{65,129},{129,193},{193,1... | collective-permute-start | bytes 786440 | tf_op jit(solution)/shard_map/ppermute | solution.py:624
  22.7 10.0 %collective-permute-start.4 = (f32[512,256]{1,0:T(8,128)S(1)}, f32[512,256]{1,0:T(8,128)S(1)}, u32[]{:S(2)}, u32[]{:S(2)}) collective-permute-start(f32[512,256]{1,0:T(8,128)S(1)} %collective-permute-done.refs_0_), channel_id=1, source_target_pairs={{0,1},{1,0},{2,3},{3,2},{4,5},{5,4},{6,7},{7,6},{8,9},{9,8},{10,11... | collective-permute-start | bytes 1572872 | tf_op jit(solution)/shard_map/ppermute | solution.py:627
  25.2 7.5 %collective-permute-start.5 = (f32[512,256]{1,0:T(8,128)S(1)}, f32[512,256]{1,0:T(8,128)S(1)}, u32[]{:S(2)}, u32[]{:S(2)}) collective-permute-start(f32[512,256]{1,0:T(8,128)S(1)} %collective-permute-done.1.refs_1_), channel_id=1, source_target_pairs={{0,1},{1,0},{2,3},{3,2},{4,5},{5,4},{6,7},{7,6},{8,9},{9,8},{10,11... | collective-permute-start | bytes 1572872 | tf_op jit(solution)/shard_map/ppermute | solution.py:627
  27.1 4.4 %collective-permute-start.7 = (f32[256,256]{1,0:T(8,128)S(1)}, f32[256,256]{1,0:T(8,128)S(1)}, u32[]{:S(2)}, u32[]{:S(2)}) collective-permute-start(f32[256,256]{1,0:T(8,128)S(1)} %collective-permute-done.3.refs_3_), channel_id=1, source_target_pairs={{0,1},{1,0},{2,3},{3,2},{4,5},{5,4},{6,7},{7,6},{8,9},{9,8},{10,11... | collective-permute-start | bytes 786440 | tf_op jit(solution)/shard_map/ppermute | solution.py:627
  29.9 2.8 %collective-permute-start.6 = (f32[256,256]{1,0:T(8,128)S(1)}, f32[256,256]{1,0:T(8,128)S(1)}, u32[]{:S(2)}, u32[]{:S(2)}) collective-permute-start(f32[256,256]{1,0:T(8,128)S(1)} %collective-permute-done.2.refs_2_), channel_id=1, source_target_pairs={{0,1},{1,0},{2,3},{3,2},{4,5},{5,4},{6,7},{7,6},{8,9},{9,8},{10,11... | collective-permute-start | bytes 786440 | tf_op jit(solution)/shard_map/ppermute | solution.py:627
  140.6 15.3 %copy-start.1 = (f32[4,256,128]{2,1,0:T(8,128)S(1)}, f32[4,256,128]{2,1,0:T(8,128)}, u32[]{:S(2)}) copy-start(f32[4,256,128]{2,1,0:T(8,128)} %get-tuple-element.52) | copy-start | bytes 1572868
  140.6 15.4 %copy-start = (f32[4,256,128]{2,1,0:T(8,128)S(1)}, f32[4,256,128]{2,1,0:T(8,128)}, u32[]{:S(2)}) copy-start(f32[4,256,128]{2,1,0:T(8,128)} %get-tuple-element.50) | copy-start | bytes 1572868
  140.6 2.7 %collective-permute-start.8 = (f32[16,64,256]{2,1,0:T(8,128)S(1)}, f32[16,64,256]{2,1,0:T(8,128)S(1)}, u32[]{:S(2)}, u32[]{:S(2)}) collective-permute-start(f32[16,64,256]{2,1,0:T(8,128)S(1)} %get-tuple-element.46), channel_id=1, source_target_pairs={{0,1},{1,0},{2,3},{3,2},{4,5},{5,4},{6,7},{7,6},{8,9},{9,8},{10,11... | collective-permute-start | bytes 3145736 | tf_op jit(solution)/shard_map/ppermute | solution.py:627
  141.1 14.8 %collective-permute-start.11 = (f32[4,256,128]{2,1,0:T(8,128)}, f32[4,256,128]{2,1,0:T(8,128)S(1)}, u32[]{:S(2)}, u32[]{:S(2)}) collective-permute-start(f32[4,256,128]{2,1,0:T(8,128)} %get-tuple-element.53), channel_id=1, source_target_pairs={{0,56},{8,16},{16,8},{24,32},{32,24},{40,48},{48,40},{56,0},{1,57}... | collective-permute-start | bytes 1572872 | tf_op jit(solution)/shard_map/ppermute | solution.py:362
  141.1 14.9 %collective-permute-start.9 = (f32[4,256,128]{2,1,0:T(8,128)}, f32[4,256,128]{2,1,0:T(8,128)S(1)}, u32[]{:S(2)}, u32[]{:S(2)}) collective-permute-start(f32[4,256,128]{2,1,0:T(8,128)} %get-tuple-element.51), channel_id=1, source_target_pairs={{0,8},{8,0},{16,24},{24,16},{32,40},{40,32},{48,56},{56,48},{1,9},... | collective-permute-start | bytes 1572872 | tf_op jit(solution)/shard_map/ppermute | solution.py:362
  144.5 26.2 %all-to-all-start.6 = ((f32[16,64,256]{2,1,0:T(8,128)}), f32[16,64,256]{2,1,0:T(8,128)S(1)}, u32[]{:S(2)}, u32[]{:S(2)}) async-start(f32[16,64,256]{2,1,0:T(8,128)} %add.170), calls=%async_computation.6 | async-start | bytes 2097152 | tf_op jit(solution)/shard_map/all_to_all | solution.py:34
  155.9 14.7 %collective-permute-start.12 = (f32[2,256,128]{2,1,0:T(8,128)S(1)}, f32[2,256,128]{2,1,0:T(8,128)S(1)}, u32[]{:S(2)}, u32[]{:S(2)}) collective-permute-start(f32[2,256,128]{2,1,0:T(8,128)S(1)} %slice_add_fusion), channel_id=1, source_target_pairs={{0,16},{8,56},{16,32},{24,8},{32,48},{40,24},{48,0},{56,40},{1,17}... | collective-permute-start | bytes 786440 | tf_op jit(solution)/shard_map/ppermute | solution.py:370
  156.1 14.6 %collective-permute-start.10 = (f32[2,256,128]{2,1,0:T(8,128)S(1)}, f32[2,256,128]{2,1,0:T(8,128)S(1)}, u32[]{:S(2)}, u32[]{:S(2)}) collective-permute-start(f32[2,256,128]{2,1,0:T(8,128)S(1)} %slice_add_fusion.1), channel_id=1, source_target_pairs={{0,48},{8,24},{16,0},{24,40},{32,16},{40,56},{48,32},{56,8},{1,49}... | collective-permute-start | bytes 786440 | tf_op jit(solution)/shard_map/ppermute | solution.py:370
  173.1 14.8 %all-to-all-start.7 = ((f32[8,64,256]{2,1,0:T(8,128)}), f32[8,64,256]{2,1,0:T(8,128)S(1)}, u32[]{:S(2)}, u32[]{:S(2)}) async-start(f32[8,64,256]{2,1,0:T(8,128)} %student_end.1), calls=%async_computation.7 | async-start | bytes 1048576 | tf_op jit(solution)/shard_map/all_to_all | solution.py:34
  178.3 6.1 %collective-permute-start.13 = (f32[256,128]{1,0:T(8,128)S(1)}, f32[256,128]{1,0:T(8,128)S(1)}, u32[]{:S(2)}, u32[]{:S(2)}) collective-permute-start(f32[256,128]{1,0:T(8,128)S(1)} %get-tuple-element.57), channel_id=1, source_target_pairs={{0,56},{8,16},{16,8},{24,32},{32,24},{40,48},{48,40},{56,0},{1,57}... | collective-permute-start | bytes 393224 | tf_op jit(solution)/shard_map/ppermute | solution.py:378
  178.5 6.0 %collective-permute-start.14 = (f32[256,128]{1,0:T(8,128)S(1)}, f32[256,128]{1,0:T(8,128)S(1)}, u32[]{:S(2)}, u32[]{:S(2)}) collective-permute-start(f32[256,128]{1,0:T(8,128)S(1)} %get-tuple-element.59), channel_id=1, source_target_pairs={{0,8},{8,0},{16,24},{24,16},{32,40},{40,32},{48,56},{56,48},{1,9},... | collective-permute-start | bytes 393224 | tf_op jit(solution)/shard_map/ppermute | solution.py:378

commit v9 on v8

--- a/solution.py
+++ b/solution.py
@@ -73,7 +73,7 @@
     return jnp.concatenate(parts, axis=0)
 
 
-def select_body(core_ref, teacher_ref, student_ref, order_ref, units_ref, length_ref, mine_ref):
+def select_body(core_ref, teacher_ref, student_ref, order_ref, units_ref, length_ref, top_ref, bottom_ref):
     images, patches, _ = teacher_ref.shape
     for image in range(images):
         chosen = order_ref[image : image + 1, :MASKED]
@@ -90,7 +90,12 @@
         student, length_ref[rows, :] = unit_rows(pick(student_ref))
         units_ref[rows, :D] = teacher
         units_ref[rows, D:] = student
-        mine_ref[rows, :] = jnp.where(core_ref[0] == 0, teacher, student)
+        mine = jnp.where(core_ref[0] == 0, teacher, student)
+        half = top_ref.shape[0]
+        if image * MASKED < half:
+            top_ref[rows, :] = mine
+        else:
+            bottom_ref[image * MASKED - half : (image + 1) * MASKED - half, :] = mine
 
 
 def select_tokens(core, teacher_patches, student_patches, mask_order):
@@ -99,11 +104,12 @@
         select_body,
         in_specs=[pl.BlockSpec(memory_space=pltpu.SMEM)]
         + [pl.BlockSpec(memory_space=pltpu.VMEM)] * 3,
-        out_specs=[pl.BlockSpec(memory_space=pltpu.VMEM)] * 3,
+        out_specs=[pl.BlockSpec(memory_space=pltpu.VMEM)] * 4,
         out_shape=[
             pltpu.HBM((tokens, 2 * D), f32),
             pltpu.HBM((tokens, 1), f32),
-            pltpu.HBM((tokens, D), f32),
+            pltpu.HBM((tokens // 2, D), f32),
+            pltpu.HBM((tokens // 2, D), f32),
         ],
         compiler_params=params(8),
         name="select",
@@ -142,7 +148,7 @@
 def energy_body(
     place_ref, units_ref, *refs
 ):
-    piece_refs, (protos_ref, energy_ref, sums_ref, cast_ref, weights_ref, total_ref) = refs[:8], refs[8:]
+    piece_refs, (protos_ref, energy_ref, sums_ref, cast_ref, weights_ref, total_ref) = refs[:12], refs[12:]
     own = units_ref.shape[0]
     tokens = cast_ref.shape[0]
 
@@ -150,14 +156,15 @@
         return pl.ds(pl.multiple_of(place_ref[4 + slot] * own + start, size), size)
 
     cast_ref[rows_of(0, 0, own), :] = units_ref[...].astype(bf16)
-    places = [(1, 0, own), (3, 0, own), (2, 0, own // 2), (2, own // 2, own // 2)]
+    places = [(slot, start, own // 2) for slot in (1, 3, 2) for start in (0, own // 2)]
     for core in range(2):
 
         @pl.when(place_ref[3] == core)
         def _(core=core):
             for i, ref in enumerate(piece_refs):
-                kind = core if i < 4 else 1 - core
-                cast_ref[rows_of(*places[i % 4]), kind * D : (kind + 1) * D] = ref[...].astype(bf16)
+                kind = core if i < len(places) else 1 - core
+                rows = rows_of(*places[i % len(places)])
+                cast_ref[rows, kind * D : (kind + 1) * D] = ref[...].astype(bf16)
 
     weights_ref[...] = directions(protos_ref[...])
     total_ref[...] = jnp.zeros_like(total_ref)
@@ -618,20 +625,20 @@
     table = block_table(y, z, core)
     share = teacher_protos.shape[0] // y_size
 
-    units, student_length, mine = select_tokens(
+    units, student_length, top, bottom = select_tokens(
         core.astype(jnp.int32)[None], teacher_patches, student_patches, mask_order
     )
     from_y = lambda value, step: lax.ppermute(
         value, "y", [(i, (i + step) % y_size) for i in range(y_size)]
     )
     from_core = lambda value: lax.ppermute(value, "core", [(0, 1), (1, 0)])
-    half = mine.shape[0] // 2
-    first, third = from_y(mine, 1), from_y(mine, 3)
+    first_top, third_bottom = from_y(top, 1), from_y(bottom, 3)
+    first_bottom, third_top = from_y(bottom, 1), from_y(top, 3)
+    units, first_top, third_bottom = lax.optimization_barrier((units, first_top, third_bottom))
+    second_top, second_bottom = from_y(first_top, 1), from_y(third_bottom, 3)
     norm_part = student_sums(units, student_protos)
-    norm_part, first, third, place, table = lax.optimization_barrier(
-        (norm_part, first, third, place, table)
-    )
-    got = [first, third, from_y(first[:half], 1), from_y(third[half:], 3)]
+    got = [first_top, first_bottom, third_top, third_bottom, second_top, second_bottom]
+    norm_part, got, place, table = lax.optimization_barrier((norm_part, got, place, table))
     got = got + [from_core(piece) for piece in got]
 
     rows = ("y",) + PROTOS
@@ -652,10 +659,10 @@
     feature_part, keep_left, keep_right = lax.optimization_barrier(
         (feature_part, keep_left, keep_right)
     )
-    left = pass_on(collect(send_left, keep_left, 0), 0)
-    right_half = pass_on(collect(send_right, keep_right, 1), 1)
+    left, right_half = collect(send_left, keep_left, 0), collect(send_right, keep_right, 1)
     feature_pieces = spread(feature_part, ("y", "x"))
-    feature_pieces, left, right_half = lax.optimization_barrier((feature_pieces, left, right_half))
+    feature_pieces, _, _ = lax.optimization_barrier((feature_pieces, left, right_half))
+    left, right_half = pass_on(left, 0), pass_on(right_half, 1)
     left, right_half = deliver(left, 0), deliver(right_half, 1)
     result = student_end(place, feature_pieces, units, student_length, proto_size)
     result = spread(result, PROTOS)

time: 189 us -> 188 us (level)
  waiting for transfers between devices: 37.5 us -> 33.2 us
    ppermute x4 -> x6, waiting for transfers between devices: 8.93 us -> 5.64 us  [on_device(): lax.ppermute(value, 'y', [(i, (i + step) % y_size) for i in range(y_size)])]
    ppermute x4 -> x6, starting transfers between devices: 5.19 us -> 7.71 us  [on_device(): lax.ppermute(value, 'y', [(i, (i + step) % y_size) for i in range(y_size)])]
    ppermute x5 -> x7, starting transfers between devices: 7.31 us -> 4.95 us  [on_device(): from_core = lambda value: lax.ppermute(value, 'core', [(0, 1), (1, 0)])]
  transfers between devices with their start and end apart: 17 -> 21, of which waited for: 9 -> 15; matrix products, arithmetic and copies ran while one was open for 1% -> 1% of each run, Pallas kernels for 4% -> 5%
where the time goes in v9:
time: 188 us; the launch traced here: 187 us
  blocking collectives  79.2 us (42%)
  Pallas kernels  43.8 us (23%)
  waiting for transfers between devices  33.2 us (18%)
  starting transfers between devices  27.2 us (14%)
    all_to_all x6, blocking collectives, spread(): return lax.all_to_all(value, axes, 0, 0, tiled=True)  79.2 us
    pallas_call x1, Pallas kernels, gradients(): pl.pallas_call(gradient_body, grid_spec=pltpu.PrefetchScalarGridSpec(num_...  12 us
    ppermute x2, waiting for transfers between devices, pass_on(): got = lax.ppermute(far, 'z', [(z, (z + 2 * way[z]) % n) for z in range(n)])  10.7 us
    all_to_all x2, starting transfers between devices, spread(): return lax.all_to_all(value, axes, 0, 0, tiled=True)  9.1 us
    ppermute x6, starting transfers between devices, on_device(): lax.ppermute(value, 'y', [(i, (i + step) % y_size) for i in range(y_size)])  7.71 us
    ppermute x2, waiting for transfers between devices, collect(): got = lax.ppermute(send, 'z', [(z, (z - way[z]) % n) for z in range(n)])  7.55 us
    pallas_call x1, Pallas kernels, energy_of(): pl.pallas_call(energy_body, grid_spec=pltpu.PrefetchScalarGridSpec(num_sc...  7.45 us
    pallas_call x3, Pallas kernels, row_sums(): pl.pallas_call(row_body, in_specs=[whole] * (2 + len(norm_part)), out_spe...  6.24 us
  transfers between devices with their start and end apart: 21, of which 15 were waited for; matrix products, arithmetic and copies ran while one was open for 1% of the time, Pallas kernels for 5%

profile of v9, /device:TPU:1, one launch (start us, length us, event | category | flops | bytes accessed | tf_op | source)
XLA Modules:
  0.0 187.1 jit_solution(13896870286211390724)
XLA Ops:
  0.6 3.0 %select.31 = (f32[512,512]{1,0:T(8,128)}, f32[512,1]{1,0:T(8,128)}, f32[256,256]{1,0:T(8,128)}, f32[256,256]{1,0:T(8,128)}) custom-call(s32[1]{0:T(128)} %bitcast.core_ref, bf16[4,256,256]{2,1,0:T(8,128)(2,1)} %teacher_ref.1, bf16[4,256,256]{2,1,0:T(8,128)(2,1)} %student_ref.1, s32[4,256]{1,0:T(4,128)} %order_ref.1), custom_call_target="tpu_custom_call" | custom-call | tf_op jit(solution)/shard_map/select/pallas_call | solution.py:103
  3.6 2.1 %collective-permute-start = (f32[256,256]{1,0:T(8,128)}, f32[256,256]{1,0:T(8,128)S(1)}, u32[]{:S(2)}, u32[]{:S(2)}) collective-permute-start(f32[256,256]{1,0:T(8,128)} %get-tuple-element.36), channel_id=1, source_target_pairs={{0,64},{64,128},{128,192},{192,0},{1,65},{65,129},{129,193},{193,1... | collective-permute-start | bytes 786440 | tf_op jit(solution)/shard_map/ppermute | solution.py:631
  15.3 6.1 %student.1.refs_0_ = f32[4,128]{1,0:T(4,128)S(1)} custom-call(f32[512,512]{1,0:T(8,128)} %get-tuple-element.38.units_ref.unit_ref, bf16[8192,256]{1,0:T(8,128)(2,1)} %refs_4_.1), custom_call_target="tpu_custom_call" | custom-call | flops 4294967296 | bytes 8388608 | tf_op jit(solution)/shard_map/student/pallas_call | solution.py:268
  23.9 3.1 %collective-permute-start.6 = (f32[256,256]{1,0:T(8,128)S(1)}, f32[256,256]{1,0:T(8,128)S(1)}, u32[]{:S(2)}, u32[]{:S(2)}) collective-permute-start(f32[256,256]{1,0:T(8,128)S(1)} %collective-permute-done.refs_0_), channel_id=1, source_target_pairs={{0,1},{1,0},{2,3},{3,2},{4,5},{5,4},{6,7},{7,6},{8,9},{9,8},{10,11... | collective-permute-start | bytes 786440 | tf_op jit(solution)/shard_map/ppermute | solution.py:634
  30.0 7.4 %energy.1 = (bf16[16,2048,128]{2,1,0:T(8,128)(2,1)S(1)}, f32[8,16,128]{2,1,0:T(8,128)S(1)}, bf16[2048,512]{1,0:T(8,128)(2,1)}) custom-call(s32[8]{0:T(128)S(1)} %stack.43.place_ref, f32[512,512]{1,0:T(8,128)} %get-tuple-element.38.units_ref.unit_ref, f32[256,256]{1,0:T(8,128)S(1)} %collective-permute-done.refs_0_, ...), custom_call_target="tpu_custom_call" | custom-call | flops 4294967296 | bytes 8388608 | tf_op jit(solution)/shard_map/energy/pallas_call | solution.py:211
  37.4 14.1 %all_to_all.40.pieces_ref = f32[8,16,128]{2,1,0:T(8,128)S(1)} all-to-all(f32[8,16,128]{2,1,0:T(8,128)S(1)} %get-tuple-element.51), channel_id=1, replica_groups=mesh['y'=4,'z'=8,'x'=4,'core'=2] {'z'}, dimensions={0} | all-to-all | bytes 131072 | tf_op jit(solution)/shard_map/all_to_all | solution.py:34
  51.6 2.1 %row_sums.3 = (f32[16,128]{1,0:T(8,128)}, f32[32,16,128]{2,1,0:T(8,128)S(1)}) custom-call(bf16[16,2048,128]{2,1,0:T(8,128)(2,1)S(1)} %get-tuple-element.50.energy_ref, f32[8,16,128]{2,1,0:T(8,128)S(1)} %all_to_all.40.pieces_ref), custom_call_target="tpu_custom_call" | custom-call | flops 8388608 | tf_op jit(solution)/shard_map/row_sums/pallas_call | solution.py:315
  53.7 17.3 %all_to_all.41.pieces_ref = f32[32,16,128]{2,1,0:T(8,128)S(1)} all-to-all(f32[32,16,128]{2,1,0:T(8,128)S(1)} %get-tuple-element.52), channel_id=1, replica_groups=mesh['y'=4,'z'=8,'x'=4,'core'=2] {'y','x','core'}, dimensions={0} | all-to-all | bytes 524288 | tf_op jit(solution)/shard_map/all_to_all | solution.py:34
  71.0 2.2 %column_sums.2 = f32[8,16,128]{2,1,0:T(8,128)S(1)} custom-call(bf16[16,2048,128]{2,1,0:T(8,128)(2,1)S(1)} %get-tuple-element.50.energy_ref, f32[32,16,128]{2,1,0:T(8,128)S(1)} %all_to_all.41.pieces_ref), custom_call_target="tpu_custom_call" | custom-call | flops 8388608 | tf_op jit(solution)/shard_map/column_sums/pallas_call | solution.py:350
  73.2 9.5 %all_to_all.42.pieces_ref = f32[8,16,128]{2,1,0:T(8,128)S(1)} all-to-all(f32[8,16,128]{2,1,0:T(8,128)S(1)} %column_sums.2), channel_id=1, replica_groups=mesh['y'=4,'z'=8,'x'=4,'core'=2] {'z'}, dimensions={0} | all-to-all | bytes 131072 | tf_op jit(solution)/shard_map/all_to_all | solution.py:34
  82.8 2.1 %row_sums.4 = (f32[16,128]{1,0:T(8,128)}, f32[32,16,128]{2,1,0:T(8,128)S(1)}) custom-call(bf16[16,2048,128]{2,1,0:T(8,128)(2,1)S(1)} %get-tuple-element.50.energy_ref, f32[8,16,128]{2,1,0:T(8,128)S(1)} %all_to_all.42.pieces_ref), custom_call_target="tpu_custom_call" | custom-call | flops 8388608 | tf_op jit(solution)/shard_map/row_sums/pallas_call | solution.py:315
  84.9 13.7 %all_to_all.43.pieces_ref = f32[32,16,128]{2,1,0:T(8,128)S(1)} all-to-all(f32[32,16,128]{2,1,0:T(8,128)S(1)} %get-tuple-element.53), channel_id=1, replica_groups=mesh['y'=4,'z'=8,'x'=4,'core'=2] {'y','x','core'}, dimensions={0} | all-to-all | bytes 524288 | tf_op jit(solution)/shard_map/all_to_all | solution.py:34
  98.6 2.2 %column_sums.3 = f32[8,16,128]{2,1,0:T(8,128)S(1)} custom-call(bf16[16,2048,128]{2,1,0:T(8,128)(2,1)S(1)} %get-tuple-element.50.energy_ref, f32[32,16,128]{2,1,0:T(8,128)S(1)} %all_to_all.43.pieces_ref), custom_call_target="tpu_custom_call" | custom-call | flops 8388608 | tf_op jit(solution)/shard_map/column_sums/pallas_call | solution.py:350
  100.8 9.5 %all_to_all.44.pieces_ref = f32[8,16,128]{2,1,0:T(8,128)S(1)} all-to-all(f32[8,16,128]{2,1,0:T(8,128)S(1)} %column_sums.3), channel_id=1, replica_groups=mesh['y'=4,'z'=8,'x'=4,'core'=2] {'z'}, dimensions={0} | all-to-all | bytes 131072 | tf_op jit(solution)/shard_map/all_to_all | solution.py:34
  112.3 15.0 %all_to_all.45 = f32[32,24,128]{2,1,0:T(8,128)S(1)} all-to-all(f32[32,24,128]{2,1,0:T(8,128)S(1)} %get-tuple-element.55), channel_id=1, replica_groups=mesh['y'=4,'z'=8,'x'=4,'core'=2] {'y','x','core'}, dimensions={0} | all-to-all | bytes 786432 | tf_op jit(solution)/shard_map/all_to_all | solution.py:34
  127.3 12.0 %gradients.1 = (f32[4,256,128]{2,1,0:T(8,128)}, f32[4,256,128]{2,1,0:T(8,128)}, f32[4,256,128]{2,1,0:T(8,128)}, f32[4,256,128]{2,1,0:T(8,128)}, f32[16,64,256]{2,1,0:T(8,128)S(1)}, /*index=5*/f32[16,64,256]{2,1,0:T(8,128)S(1)}) custom-call(s32[5,8]{1,0:T(8,128)S(1)} %stack.46.table_ref, bf16[2048,512]{1,0:T(8,128)(2,1)} %get-tuple-element.49.units_ref, ...), custom_call_target="tpu_custom_call" | custom-call | flops 8589934592 | bytes 8388608 | tf_op jit(solution)/shard_map/gradients/pallas_call | solution.py:519
  143.1 3.7 %all-to-all-start.6 = ((f32[16,64,256]{2,1,0:T(8,128)}), f32[16,64,256]{2,1,0:T(8,128)S(1)}, u32[]{:S(2)}, u32[]{:S(2)}) async-start(f32[16,64,256]{2,1,0:T(8,128)} %add.166), calls=%async_computation.6 | async-start | bytes 2097152 | tf_op jit(solution)/shard_map/all_to_all | solution.py:34
  146.8 7.5 %collective-permute-done.14 = f32[4,256,128]{2,1,0:T(8,128)S(1)} collective-permute-done((f32[4,256,128]{2,1,0:T(8,128)}, f32[4,256,128]{2,1,0:T(8,128)S(1)}, u32[]{:S(2)}, u32[]{:S(2)}) %collective-permute-start.14) | collective-permute-done | bytes 524320 | tf_op jit(solution)/shard_map/ppermute | solution.py:369
  154.5 3.6 %collective-permute-start.15 = (f32[2,256,128]{2,1,0:T(8,128)S(1)}, f32[2,256,128]{2,1,0:T(8,128)S(1)}, u32[]{:S(2)}, u32[]{:S(2)}) collective-permute-start(f32[2,256,128]{2,1,0:T(8,128)S(1)} %slice_add_fusion.1), channel_id=1, source_target_pairs={{0,48},{8,24},{16,0},{24,40},{32,16},{40,56},{48,32},{56,8},{1,49}... | collective-permute-start | bytes 786440 | tf_op jit(solution)/shard_map/ppermute | solution.py:377
  158.1 10.7 %collective-permute-done.17 = f32[2,256,128]{2,1,0:T(8,128)S(1)} collective-permute-done((f32[2,256,128]{2,1,0:T(8,128)S(1)}, f32[2,256,128]{2,1,0:T(8,128)S(1)}, u32[]{:S(2)}, u32[]{:S(2)}) %collective-permute-start.17) | collective-permute-done | bytes 262176 | tf_op jit(solution)/shard_map/ppermute | solution.py:377
  169.0 2.3 %student_end.1 = f32[8,64,256]{2,1,0:T(8,128)} custom-call(s32[8]{0:T(128)S(1)} %stack.43.place_ref, f32[16,64,256]{2,1,0:T(8,128)S(1)} %all-to-all-done.6.pieces_ref, f32[512,512]{1,0:T(8,128)} %get-tuple-element.38.units_ref.unit_ref, f32[512,1]{1,0:T(8,128)} %get-tuple-element.67.length_ref), custom_call_target="tpu_custom_call" | custom-call | tf_op jit(solution)/shard_map/student_end/pallas_call | solution.py:569
  171.3 5.4 %all-to-all-start.7 = ((f32[8,64,256]{2,1,0:T(8,128)}), f32[8,64,256]{2,1,0:T(8,128)S(1)}, u32[]{:S(2)}, u32[]{:S(2)}) async-start(f32[8,64,256]{2,1,0:T(8,128)} %student_end.1), calls=%async_computation.7 | async-start | bytes 1048576 | tf_op jit(solution)/shard_map/all_to_all | solution.py:34
  178.0 3.7 %collective-permute-done.18.refs_3_ = f32[256,128]{1,0:T(8,128)S(1)} collective-permute-done((f32[256,128]{1,0:T(8,128)S(1)}, f32[256,128]{1,0:T(8,128)S(1)}, u32[]{:S(2)}, u32[]{:S(2)}) %collective-permute-start.18) | collective-permute-done | bytes 131104 | tf_op jit(solution)/shard_map/ppermute | solution.py:385
  182.8 2.4 %proto_end.1 = f32[256,256]{1,0:T(8,128)} custom-call(s32[8]{0:T(128)S(1)} %stack.43.place_ref, f32[256,128]{1,0:T(8,128)S(1)} %get-tuple-element.80.refs_0_, f32[256,128]{1,0:T(8,128)S(1)} %collective-permute-done.16.refs_1_, f32[256,128]{1,0:T(8,128)S(1)} %get-tuple-element.78.refs_2_, f32[256,128]{1,0:T(8,128)S(1)} %collective-permute-done.18.refs_3_, ...), custom_call_target="tpu_custom_call" | custom-call | tf_op jit(solution)/shard_map/proto_end/pallas_call | solution.py:602
  (49 shorter events, 25.4 us)
Async XLA Ops:
  3.6 7.5 %collective-permute-start = (f32[256,256]{1,0:T(8,128)}, f32[256,256]{1,0:T(8,128)S(1)}, u32[]{:S(2)}, u32[]{:S(2)}) collective-permute-start(f32[256,256]{1,0:T(8,128)} %get-tuple-element.36), channel_id=1, source_target_pairs={{0,64},{64,128},{128,192},{192,0},{1,65},{65,129},{129,193},{193,1... | collective-permute-start | bytes 786440 | tf_op jit(solution)/shard_map/ppermute | solution.py:631
  5.7 6.9 %collective-permute-start.1 = (f32[256,256]{1,0:T(8,128)}, f32[256,256]{1,0:T(8,128)S(1)}, u32[]{:S(2)}, u32[]{:S(2)}) collective-permute-start(f32[256,256]{1,0:T(8,128)} %get-tuple-element.37), channel_id=1, source_target_pairs={{0,192},{64,0},{128,64},{192,128},{1,193},{65,1},{129,65},{193,129... | collective-permute-start | bytes 786440 | tf_op jit(solution)/shard_map/ppermute | solution.py:631
  7.2 14.2 %collective-permute-start.3 = (f32[256,256]{1,0:T(8,128)}, f32[256,256]{1,0:T(8,128)S(1)}, u32[]{:S(2)}, u32[]{:S(2)}) collective-permute-start(f32[256,256]{1,0:T(8,128)} %get-tuple-element.36), channel_id=1, source_target_pairs={{0,192},{64,0},{128,64},{192,128},{1,193},{65,1},{129,65},{193,129... | collective-permute-start | bytes 786440 | tf_op jit(solution)/shard_map/ppermute | solution.py:631
  8.6 12.8 %collective-permute-start.2 = (f32[256,256]{1,0:T(8,128)}, f32[256,256]{1,0:T(8,128)S(1)}, u32[]{:S(2)}, u32[]{:S(2)}) collective-permute-start(f32[256,256]{1,0:T(8,128)} %get-tuple-element.37), channel_id=1, source_target_pairs={{0,64},{64,128},{128,192},{192,0},{1,65},{65,129},{129,193},{193,1... | collective-permute-start | bytes 786440 | tf_op jit(solution)/shard_map/ppermute | solution.py:631
  12.6 10.8 %collective-permute-start.4 = (f32[256,256]{1,0:T(8,128)S(1)}, f32[256,256]{1,0:T(8,128)S(1)}, u32[]{:S(2)}, u32[]{:S(2)}) collective-permute-start(f32[256,256]{1,0:T(8,128)S(1)} %collective-permute-done.refs_0_), channel_id=1, source_target_pairs={{0,64},{64,128},{128,192},{192,0},{1,65},{65,129},{129,193},{193,1... | collective-permute-start | bytes 786440 | tf_op jit(solution)/shard_map/ppermute | solution.py:631
  14.1 9.8 %collective-permute-start.5 = (f32[256,256]{1,0:T(8,128)S(1)}, f32[256,256]{1,0:T(8,128)S(1)}, u32[]{:S(2)}, u32[]{:S(2)}) collective-permute-start(f32[256,256]{1,0:T(8,128)S(1)} %collective-permute-done.1.refs_3_), channel_id=1, source_target_pairs={{0,192},{64,0},{128,64},{192,128},{1,193},{65,1},{129,65},{193,129... | collective-permute-start | bytes 786440 | tf_op jit(solution)/shard_map/ppermute | solution.py:631
  23.9 4.3 %collective-permute-start.6 = (f32[256,256]{1,0:T(8,128)S(1)}, f32[256,256]{1,0:T(8,128)S(1)}, u32[]{:S(2)}, u32[]{:S(2)}) collective-permute-start(f32[256,256]{1,0:T(8,128)S(1)} %collective-permute-done.refs_0_), channel_id=1, source_target_pairs={{0,1},{1,0},{2,3},{3,2},{4,5},{5,4},{6,7},{7,6},{8,9},{9,8},{10,11... | collective-permute-start | bytes 786440 | tf_op jit(solution)/shard_map/ppermute | solution.py:634
  27.0 1.5 collective-permute-start.7
  27.1 1.8 collective-permute-start.8
  27.5 1.8 collective-permute-start.9
  27.6 2.0 %collective-permute-start.10 = (f32[256,256]{1,0:T(8,128)S(1)}, f32[256,256]{1,0:T(8,128)S(1)}, u32[]{:S(2)}, u32[]{:S(2)}) collective-permute-start(f32[256,256]{1,0:T(8,128)S(1)} %collective-permute-done.4.refs_4_), channel_id=1, source_target_pairs={{0,1},{1,0},{2,3},{3,2},{4,5},{5,4},{6,7},{7,6},{8,9},{9,8},{10,11... | collective-permute-start | bytes 786440 | tf_op jit(solution)/shard_map/ppermute | solution.py:634
  28.1 1.9 %collective-permute-start.11 = (f32[256,256]{1,0:T(8,128)S(1)}, f32[256,256]{1,0:T(8,128)S(1)}, u32[]{:S(2)}, u32[]{:S(2)}) collective-permute-start(f32[256,256]{1,0:T(8,128)S(1)} %collective-permute-done.5.refs_5_), channel_id=1, source_target_pairs={{0,1},{1,0},{2,3},{3,2},{4,5},{5,4},{6,7},{7,6},{8,9},{9,8},{10,11... | collective-permute-start | bytes 786440 | tf_op jit(solution)/shard_map/ppermute | solution.py:634
  139.3 15.1 %copy-start.1 = (f32[4,256,128]{2,1,0:T(8,128)S(1)}, f32[4,256,128]{2,1,0:T(8,128)}, u32[]{:S(2)}) copy-start(f32[4,256,128]{2,1,0:T(8,128)} %get-tuple-element.64) | copy-start | bytes 1572868
  139.3 15.2 %copy-start = (f32[4,256,128]{2,1,0:T(8,128)S(1)}, f32[4,256,128]{2,1,0:T(8,128)}, u32[]{:S(2)}) copy-start(f32[4,256,128]{2,1,0:T(8,128)} %get-tuple-element.62) | copy-start | bytes 1572868
  139.3 2.7 %collective-permute-start.12 = (f32[16,64,256]{2,1,0:T(8,128)S(1)}, f32[16,64,256]{2,1,0:T(8,128)S(1)}, u32[]{:S(2)}, u32[]{:S(2)}) collective-permute-start(f32[16,64,256]{2,1,0:T(8,128)S(1)} %get-tuple-element.58), channel_id=1, source_target_pairs={{0,1},{1,0},{2,3},{3,2},{4,5},{5,4},{6,7},{7,6},{8,9},{9,8},{10,11... | collective-permute-start | bytes 3145736 | tf_op jit(solution)/shard_map/ppermute | solution.py:634
  139.7 14.6 %collective-permute-start.14 = (f32[4,256,128]{2,1,0:T(8,128)}, f32[4,256,128]{2,1,0:T(8,128)S(1)}, u32[]{:S(2)}, u32[]{:S(2)}) collective-permute-start(f32[4,256,128]{2,1,0:T(8,128)} %get-tuple-element.65), channel_id=1, source_target_pairs={{0,56},{8,16},{16,8},{24,32},{32,24},{40,48},{48,40},{56,0},{1,57}... | collective-permute-start | bytes 1572872 | tf_op jit(solution)/shard_map/ppermute | solution.py:369
  139.7 14.7 %collective-permute-start.13 = (f32[4,256,128]{2,1,0:T(8,128)}, f32[4,256,128]{2,1,0:T(8,128)S(1)}, u32[]{:S(2)}, u32[]{:S(2)}) collective-permute-start(f32[4,256,128]{2,1,0:T(8,128)} %get-tuple-element.63), channel_id=1, source_target_pairs={{0,8},{8,0},{16,24},{24,16},{32,40},{40,32},{48,56},{56,48},{1,9},... | collective-permute-start | bytes 1572872 | tf_op jit(solution)/shard_map/ppermute | solution.py:369
  143.1 25.8 %all-to-all-start.6 = ((f32[16,64,256]{2,1,0:T(8,128)}), f32[16,64,256]{2,1,0:T(8,128)S(1)}, u32[]{:S(2)}, u32[]{:S(2)}) async-start(f32[16,64,256]{2,1,0:T(8,128)} %add.166), calls=%async_computation.6 | async-start | bytes 2097152 | tf_op jit(solution)/shard_map/all_to_all | solution.py:34
  154.4 14.5 %collective-permute-start.17 = (f32[2,256,128]{2,1,0:T(8,128)S(1)}, f32[2,256,128]{2,1,0:T(8,128)S(1)}, u32[]{:S(2)}, u32[]{:S(2)}) collective-permute-start(f32[2,256,128]{2,1,0:T(8,128)S(1)} %slice_add_fusion), channel_id=1, source_target_pairs={{0,16},{8,56},{16,32},{24,8},{32,48},{40,24},{48,0},{56,40},{1,17}... | collective-permute-start | bytes 786440 | tf_op jit(solution)/shard_map/ppermute | solution.py:377
  154.5 14.4 %collective-permute-start.15 = (f32[2,256,128]{2,1,0:T(8,128)S(1)}, f32[2,256,128]{2,1,0:T(8,128)S(1)}, u32[]{:S(2)}, u32[]{:S(2)}) collective-permute-start(f32[2,256,128]{2,1,0:T(8,128)S(1)} %slice_add_fusion.1), channel_id=1, source_target_pairs={{0,48},{8,24},{16,0},{24,40},{32,16},{40,56},{48,32},{56,8},{1,49}... | collective-permute-start | bytes 786440 | tf_op jit(solution)/shard_map/ppermute | solution.py:377
  171.3 14.9 %all-to-all-start.7 = ((f32[8,64,256]{2,1,0:T(8,128)}), f32[8,64,256]{2,1,0:T(8,128)S(1)}, u32[]{:S(2)}, u32[]{:S(2)}) async-start(f32[8,64,256]{2,1,0:T(8,128)} %student_end.1), calls=%async_computation.7 | async-start | bytes 1048576 | tf_op jit(solution)/shard_map/all_to_all | solution.py:34
  176.8 4.9 %collective-permute-start.18 = (f32[256,128]{1,0:T(8,128)S(1)}, f32[256,128]{1,0:T(8,128)S(1)}, u32[]{:S(2)}, u32[]{:S(2)}) collective-permute-start(f32[256,128]{1,0:T(8,128)S(1)} %get-tuple-element.68), channel_id=1, source_target_pairs={{0,8},{8,0},{16,24},{24,16},{32,40},{40,32},{48,56},{56,48},{1,9},... | collective-permute-start | bytes 393224 | tf_op jit(solution)/shard_map/ppermute | solution.py:385
  176.8 6.0 %collective-permute-start.16 = (f32[256,128]{1,0:T(8,128)S(1)}, f32[256,128]{1,0:T(8,128)S(1)}, u32[]{:S(2)}, u32[]{:S(2)}) collective-permute-start(f32[256,128]{1,0:T(8,128)S(1)} %get-tuple-element.72), channel_id=1, source_target_pairs={{0,56},{8,16},{16,8},{24,32},{32,24},{40,48},{48,40},{56,0},{1,57}... | collective-permute-start | bytes 393224 | tf_op jit(solution)/shard_map/ppermute | solution.py:385

commit v10 on v9

--- a/solution.py
+++ b/solution.py
@@ -219,14 +219,14 @@
             out_specs=[
                 direct,
                 pl.BlockSpec((copies, share // LANES, LANES), lambda i, p: (0, 0, 0)),
-                pl.BlockSpec((tokens, 2 * D), lambda i, p: (0, 0)),
+                direct,
             ],
             scratch_shapes=[pltpu.VMEM((share, D), bf16), pltpu.VMEM((share, LANES), f32)],
         ),
         out_shape=[
             pltpu.VMEM((tokens // LANES, share, LANES), bf16),
             jax.ShapeDtypeStruct((copies, share // LANES, LANES), f32),
-            pltpu.HBM((tokens, 2 * D), bf16),
+            pltpu.VMEM((tokens, 2 * D), bf16),
         ],
         compiler_params=params(24),
         cost_estimate=work(4 * tokens * share * D, 8 * 2**20, tokens * share),
@@ -370,11 +370,12 @@
     return keep[0] + got[0], keep[1] + got[1], keep[2:] + got[2:]
 
 
-def pass_on(sums, offset):
+def pass_on(sums, offset, after):
     n = lax.axis_size("z")
     way = [1 if (z + offset) % 2 else -1 for z in range(n)]
     own, following, far = sums
     got = lax.ppermute(far, "z", [(z, (z + 2 * way[z]) % n) for z in range(n)])
+    own, following, _ = lax.optimization_barrier((own, following, after))
     return own + got[0], following + got[1]
 
 
@@ -522,7 +523,7 @@
             num_scalar_prefetch=1,
             grid=(blocks // 2,),
             in_specs=[
-                whole(tokens, 2 * D),
+                direct,
                 direct,
                 whole(*pieces.shape),
                 first,
@@ -545,7 +546,7 @@
         name="gradients",
     )(
         table,
-        in_hbm(units_all),
+        units_all,
         energy,
         pieces,
         in_hbm(student_protos),
@@ -662,9 +663,9 @@
     left, right_half = collect(send_left, keep_left, 0), collect(send_right, keep_right, 1)
     feature_pieces = spread(feature_part, ("y", "x"))
     feature_pieces, _, _ = lax.optimization_barrier((feature_pieces, left, right_half))
-    left, right_half = pass_on(left, 0), pass_on(right_half, 1)
+    result = student_end(place, feature_pieces, units, student_length, proto_size)
+    left, right_half = pass_on(left, 0, result), pass_on(right_half, 1, result)
     left, right_half = deliver(left, 0), deliver(right_half, 1)
-    result = student_end(place, feature_pieces, units, student_length, proto_size)
     result = spread(result, PROTOS)
     grad_protos = proto_end(place, left + right_half, student_protos)
     return (result.reshape(-1, MASKED, D), grad_protos)

time: 188 us -> 182 us (0.968)
  waiting for transfers between devices: 33.2 us -> 25.7 us
  other arithmetic: 1.27 us -> 4.65 us
    ppermute x2, waiting for transfers between devices: 10.7 us -> 0.01 us  [pass_on(): got = lax.ppermute(far, 'z', [(z, (z + 2 * way[z]) % n) for z in range(n)])]
    all_to_all x2, waiting for transfers between devices: 1.09 us -> 4.43 us  [spread(): return lax.all_to_all(value, axes, 0, 0, tiled=True)]
    add x2, other arithmetic: 0.08 us -> 2.02 us  [pass_on(): return (own + got[0], following + got[1])]
  transfers between devices with their start and end apart: 21 -> 21, of which waited for: 15 -> 14; matrix products, arithmetic and copies ran while one was open for 1% -> 3% of each run, Pallas kernels for 5% -> 6%
where the time goes in v10:
time: 182 us
  blocking collectives  79.2 us (44%)
  Pallas kernels  42.7 us (23%)
  starting transfers between devices  27.3 us (15%)
  waiting for transfers between devices  25.7 us (14%)
  other arithmetic  4.65 us (3%)
    all_to_all x6, blocking collectives, spread(): return lax.all_to_all(value, axes, 0, 0, tiled=True)  79.2 us
    pallas_call x1, Pallas kernels, gradients(): pl.pallas_call(gradient_body, grid_spec=pltpu.PrefetchScalarGridSpec(num_...  11.4 us
    all_to_all x2, starting transfers between devices, spread(): return lax.all_to_all(value, axes, 0, 0, tiled=True)  8.73 us
    ppermute x6, starting transfers between devices, on_device(): lax.ppermute(value, 'y', [(i, (i + step) % y_size) for i in range(y_size)])  7.71 us
    ppermute x2, waiting for transfers between devices, collect(): got = lax.ppermute(send, 'z', [(z, (z - way[z]) % n) for z in range(n)])  7.55 us
    pallas_call x1, Pallas kernels, energy_of(): pl.pallas_call(energy_body, grid_spec=pltpu.PrefetchScalarGridSpec(num_sc...  6.87 us
    pallas_call x3, Pallas kernels, row_sums(): pl.pallas_call(row_body, in_specs=[whole] * (2 + len(norm_part)), out_spe...  6.24 us
    pallas_call x1, Pallas kernels, student_sums(): pl.pallas_call(student_body, in_specs=[pl.BlockSpec(memory_space=pl.ANY)]...  6.07 us
  transfers between devices with their start and end apart: 21, of which 14 were waited for; matrix products, arithmetic and copies ran while one was open for 3% of the time, Pallas kernels for 6%

profile of v10, /device:TPU:1, one launch (start us, length us, event | category | flops | bytes accessed | tf_op | source)
XLA Modules:
  0.0 181.8 jit_solution(525051140345136876)
XLA Ops:
  0.6 3.0 %select.31 = (f32[512,512]{1,0:T(8,128)}, f32[512,1]{1,0:T(8,128)}, f32[256,256]{1,0:T(8,128)}, f32[256,256]{1,0:T(8,128)}) custom-call(s32[1]{0:T(128)} %bitcast.core_ref, bf16[4,256,256]{2,1,0:T(8,128)(2,1)} %teacher_ref.1, bf16[4,256,256]{2,1,0:T(8,128)(2,1)} %student_ref.1, s32[4,256]{1,0:T(4,128)} %order_ref.1), custom_call_target="tpu_custom_call" | custom-call | tf_op jit(solution)/shard_map/select/pallas_call | solution.py:103
  3.6 2.1 %collective-permute-start = (f32[256,256]{1,0:T(8,128)}, f32[256,256]{1,0:T(8,128)S(1)}, u32[]{:S(2)}, u32[]{:S(2)}) collective-permute-start(f32[256,256]{1,0:T(8,128)} %get-tuple-element.40), channel_id=1, source_target_pairs={{0,64},{64,128},{128,192},{192,0},{1,65},{65,129},{129,193},{193,1... | collective-permute-start | bytes 786440 | tf_op jit(solution)/shard_map/ppermute | solution.py:632
  15.3 6.1 %student.1.refs_0_ = f32[4,128]{1,0:T(4,128)S(1)} custom-call(f32[512,512]{1,0:T(8,128)} %get-tuple-element.42.units_ref.unit_ref, bf16[8192,256]{1,0:T(8,128)(2,1)} %refs_4_.1), custom_call_target="tpu_custom_call" | custom-call | flops 4294967296 | bytes 8388608 | tf_op jit(solution)/shard_map/student/pallas_call | solution.py:268
  23.9 3.1 %collective-permute-start.6 = (f32[256,256]{1,0:T(8,128)S(1)}, f32[256,256]{1,0:T(8,128)S(1)}, u32[]{:S(2)}, u32[]{:S(2)}) collective-permute-start(f32[256,256]{1,0:T(8,128)S(1)} %collective-permute-done.refs_0_), channel_id=1, source_target_pairs={{0,1},{1,0},{2,3},{3,2},{4,5},{5,4},{6,7},{7,6},{8,9},{9,8},{10,11... | collective-permute-start | bytes 786440 | tf_op jit(solution)/shard_map/ppermute | solution.py:635
  30.0 6.9 %energy.1 = (bf16[16,2048,128]{2,1,0:T(8,128)(2,1)S(1)}, f32[8,16,128]{2,1,0:T(8,128)S(1)}, bf16[2048,512]{1,0:T(8,128)(2,1)S(1)}) custom-call(s32[8]{0:T(128)S(1)} %stack.43.place_ref, f32[512,512]{1,0:T(8,128)} %get-tuple-element.42.units_ref.unit_ref, f32[256,256]{1,0:T(8,128)S(1)} %collective-permute-done.refs_0_, ...), custom_call_target="tpu_custom_call" | custom-call | flops 4294967296 | bytes 8388608 | tf_op jit(solution)/shard_map/energy/pallas_call | solution.py:211
  36.9 14.2 %all_to_all.40.pieces_ref = f32[8,16,128]{2,1,0:T(8,128)S(1)} all-to-all(f32[8,16,128]{2,1,0:T(8,128)S(1)} %get-tuple-element.55), channel_id=1, replica_groups=mesh['y'=4,'z'=8,'x'=4,'core'=2] {'z'}, dimensions={0} | all-to-all | bytes 131072 | tf_op jit(solution)/shard_map/all_to_all | solution.py:34
  51.1 2.1 %row_sums.3 = (f32[16,128]{1,0:T(8,128)}, f32[32,16,128]{2,1,0:T(8,128)S(1)}) custom-call(bf16[16,2048,128]{2,1,0:T(8,128)(2,1)S(1)} %get-tuple-element.54.energy_ref, f32[8,16,128]{2,1,0:T(8,128)S(1)} %all_to_all.40.pieces_ref), custom_call_target="tpu_custom_call" | custom-call | flops 8388608 | tf_op jit(solution)/shard_map/row_sums/pallas_call | solution.py:315
  53.2 17.3 %all_to_all.41.pieces_ref = f32[32,16,128]{2,1,0:T(8,128)S(1)} all-to-all(f32[32,16,128]{2,1,0:T(8,128)S(1)} %get-tuple-element.56), channel_id=1, replica_groups=mesh['y'=4,'z'=8,'x'=4,'core'=2] {'y','x','core'}, dimensions={0} | all-to-all | bytes 524288 | tf_op jit(solution)/shard_map/all_to_all | solution.py:34
  70.5 2.2 %column_sums.2 = f32[8,16,128]{2,1,0:T(8,128)S(1)} custom-call(bf16[16,2048,128]{2,1,0:T(8,128)(2,1)S(1)} %get-tuple-element.54.energy_ref, f32[32,16,128]{2,1,0:T(8,128)S(1)} %all_to_all.41.pieces_ref), custom_call_target="tpu_custom_call" | custom-call | flops 8388608 | tf_op jit(solution)/shard_map/column_sums/pallas_call | solution.py:350
  72.7 9.5 %all_to_all.42.pieces_ref = f32[8,16,128]{2,1,0:T(8,128)S(1)} all-to-all(f32[8,16,128]{2,1,0:T(8,128)S(1)} %column_sums.2), channel_id=1, replica_groups=mesh['y'=4,'z'=8,'x'=4,'core'=2] {'z'}, dimensions={0} | all-to-all | bytes 131072 | tf_op jit(solution)/shard_map/all_to_all | solution.py:34
  82.2 2.1 %row_sums.4 = (f32[16,128]{1,0:T(8,128)}, f32[32,16,128]{2,1,0:T(8,128)S(1)}) custom-call(bf16[16,2048,128]{2,1,0:T(8,128)(2,1)S(1)} %get-tuple-element.54.energy_ref, f32[8,16,128]{2,1,0:T(8,128)S(1)} %all_to_all.42.pieces_ref), custom_call_target="tpu_custom_call" | custom-call | flops 8388608 | tf_op jit(solution)/shard_map/row_sums/pallas_call | solution.py:315
  84.4 13.7 %all_to_all.43.pieces_ref = f32[32,16,128]{2,1,0:T(8,128)S(1)} all-to-all(f32[32,16,128]{2,1,0:T(8,128)S(1)} %get-tuple-element.57), channel_id=1, replica_groups=mesh['y'=4,'z'=8,'x'=4,'core'=2] {'y','x','core'}, dimensions={0} | all-to-all | bytes 524288 | tf_op jit(solution)/shard_map/all_to_all | solution.py:34
  98.1 2.2 %column_sums.3 = f32[8,16,128]{2,1,0:T(8,128)S(1)} custom-call(bf16[16,2048,128]{2,1,0:T(8,128)(2,1)S(1)} %get-tuple-element.54.energy_ref, f32[32,16,128]{2,1,0:T(8,128)S(1)} %all_to_all.43.pieces_ref), custom_call_target="tpu_custom_call" | custom-call | flops 8388608 | tf_op jit(solution)/shard_map/column_sums/pallas_call | solution.py:350
  100.3 9.5 %all_to_all.44.pieces_ref = f32[8,16,128]{2,1,0:T(8,128)S(1)} all-to-all(f32[8,16,128]{2,1,0:T(8,128)S(1)} %column_sums.3), channel_id=1, replica_groups=mesh['y'=4,'z'=8,'x'=4,'core'=2] {'z'}, dimensions={0} | all-to-all | bytes 131072 | tf_op jit(solution)/shard_map/all_to_all | solution.py:34
  111.8 15.0 %all_to_all.45 = f32[32,24,128]{2,1,0:T(8,128)S(1)} all-to-all(f32[32,24,128]{2,1,0:T(8,128)S(1)} %get-tuple-element.59), channel_id=1, replica_groups=mesh['y'=4,'z'=8,'x'=4,'core'=2] {'y','x','core'}, dimensions={0} | all-to-all | bytes 786432 | tf_op jit(solution)/shard_map/all_to_all | solution.py:34
  126.8 11.4 %gradients.1 = (f32[4,256,128]{2,1,0:T(8,128)}, f32[4,256,128]{2,1,0:T(8,128)}, f32[4,256,128]{2,1,0:T(8,128)}, f32[4,256,128]{2,1,0:T(8,128)}, f32[16,64,256]{2,1,0:T(8,128)S(1)}, /*index=5*/f32[16,64,256]{2,1,0:T(8,128)S(1)}) custom-call(s32[5,8]{1,0:T(8,128)S(1)} %stack.46.table_ref, bf16[2048,512]{1,0:T(8,128)(2,1)S(1)} %get-tuple-element.53.units_ref, ...), custom_call_target="tpu_custom_call" | custom-call | flops 8589934592 | bytes 8388608 | tf_op jit(solution)/shard_map/gradients/pallas_call | solution.py:520
  142.0 3.7 %all-to-all-start.6 = ((f32[16,64,256]{2,1,0:T(8,128)}), f32[16,64,256]{2,1,0:T(8,128)S(1)}, u32[]{:S(2)}, u32[]{:S(2)}) async-start(f32[16,64,256]{2,1,0:T(8,128)} %add.166), calls=%async_computation.6 | async-start | bytes 2097152 | tf_op jit(solution)/shard_map/all_to_all | solution.py:34
  145.7 7.5 %collective-permute-done.14 = f32[4,256,128]{2,1,0:T(8,128)S(1)} collective-permute-done((f32[4,256,128]{2,1,0:T(8,128)}, f32[4,256,128]{2,1,0:T(8,128)S(1)}, u32[]{:S(2)}, u32[]{:S(2)}) %collective-permute-start.14) | collective-permute-done | bytes 524320 | tf_op jit(solution)/shard_map/ppermute | solution.py:369
  154.7 3.6 %collective-permute-start.15 = (f32[2,256,128]{2,1,0:T(8,128)}, f32[2,256,128]{2,1,0:T(8,128)}, u32[]{:S(2)}, u32[]{:S(2)}) collective-permute-start(f32[2,256,128]{2,1,0:T(8,128)} %slice_add_fusion.1), channel_id=1, source_target_pairs={{0,48},{8,24},{16,0},{24,40},{32,16},{40,56},{48,32},{56,8},{1,49}... | collective-permute-start | bytes 786440 | tf_op jit(solution)/shard_map/ppermute | solution.py:377
  158.3 4.4 %all-to-all-done.6.pieces_ref = f32[16,64,256]{2,1,0:T(8,128)S(1)} async-done(((f32[16,64,256]{2,1,0:T(8,128)}), f32[16,64,256]{2,1,0:T(8,128)S(1)}, u32[]{:S(2)}, u32[]{:S(2)}) %all-to-all-start.6) | async-done | bytes 1048608 | tf_op jit(solution)/shard_map/all_to_all | solution.py:34
  162.8 2.3 %student_end.1 = f32[8,64,256]{2,1,0:T(8,128)} custom-call(s32[8]{0:T(128)S(1)} %stack.43.place_ref, f32[16,64,256]{2,1,0:T(8,128)S(1)} %all-to-all-done.6.pieces_ref, f32[512,512]{1,0:T(8,128)} %get-tuple-element.42.units_ref.unit_ref, f32[512,1]{1,0:T(8,128)} %get-tuple-element.71.length_ref), custom_call_target="tpu_custom_call" | custom-call | tf_op jit(solution)/shard_map/student_end/pallas_call | solution.py:570
  165.1 5.1 %all-to-all-start.7 = ((f32[8,64,256]{2,1,0:T(8,128)}), f32[8,64,256]{2,1,0:T(8,128)S(1)}, u32[]{:S(2)}, u32[]{:S(2)}) async-start(f32[8,64,256]{2,1,0:T(8,128)} %student_end.1), calls=%async_computation.7 | async-start | bytes 1048576 | tf_op jit(solution)/shard_map/all_to_all | solution.py:34
  175.7 2.9 %collective-permute-done.16.refs_1_ = f32[256,128]{1,0:T(8,128)S(1)} collective-permute-done((f32[256,128]{1,0:T(8,128)S(1)}, f32[256,128]{1,0:T(8,128)S(1)}, u32[]{:S(2)}, u32[]{:S(2)}) %collective-permute-start.16) | collective-permute-done | bytes 131104 | tf_op jit(solution)/shard_map/ppermute | solution.py:386
  178.6 2.4 %proto_end.1 = f32[256,256]{1,0:T(8,128)} custom-call(s32[8]{0:T(128)S(1)} %stack.43.place_ref, f32[256,128]{1,0:T(8,128)S(1)} %get-tuple-element.85.refs_0_, f32[256,128]{1,0:T(8,128)S(1)} %collective-permute-done.16.refs_1_, f32[256,128]{1,0:T(8,128)S(1)} %get-tuple-element.83.refs_2_, f32[256,128]{1,0:T(8,128)S(1)} %collective-permute-done.18.refs_3_, ...), custom_call_target="tpu_custom_call" | custom-call | tf_op jit(solution)/shard_map/proto_end/pallas_call | solution.py:603
  (51 shorter events, 28.7 us)
Async XLA Ops:
  3.6 7.5 %collective-permute-start = (f32[256,256]{1,0:T(8,128)}, f32[256,256]{1,0:T(8,128)S(1)}, u32[]{:S(2)}, u32[]{:S(2)}) collective-permute-start(f32[256,256]{1,0:T(8,128)} %get-tuple-element.40), channel_id=1, source_target_pairs={{0,64},{64,128},{128,192},{192,0},{1,65},{65,129},{129,193},{193,1... | collective-permute-start | bytes 786440 | tf_op jit(solution)/shard_map/ppermute | solution.py:632
  5.7 6.9 %collective-permute-start.1 = (f32[256,256]{1,0:T(8,128)}, f32[256,256]{1,0:T(8,128)S(1)}, u32[]{:S(2)}, u32[]{:S(2)}) collective-permute-start(f32[256,256]{1,0:T(8,128)} %get-tuple-element.41), channel_id=1, source_target_pairs={{0,192},{64,0},{128,64},{192,128},{1,193},{65,1},{129,65},{193,129... | collective-permute-start | bytes 786440 | tf_op jit(solution)/shard_map/ppermute | solution.py:632
  7.2 14.2 %collective-permute-start.3 = (f32[256,256]{1,0:T(8,128)}, f32[256,256]{1,0:T(8,128)S(1)}, u32[]{:S(2)}, u32[]{:S(2)}) collective-permute-start(f32[256,256]{1,0:T(8,128)} %get-tuple-element.40), channel_id=1, source_target_pairs={{0,192},{64,0},{128,64},{192,128},{1,193},{65,1},{129,65},{193,129... | collective-permute-start | bytes 786440 | tf_op jit(solution)/shard_map/ppermute | solution.py:632
  8.6 12.8 %collective-permute-start.2 = (f32[256,256]{1,0:T(8,128)}, f32[256,256]{1,0:T(8,128)S(1)}, u32[]{:S(2)}, u32[]{:S(2)}) collective-permute-start(f32[256,256]{1,0:T(8,128)} %get-tuple-element.41), channel_id=1, source_target_pairs={{0,64},{64,128},{128,192},{192,0},{1,65},{65,129},{129,193},{193,1... | collective-permute-start | bytes 786440 | tf_op jit(solution)/shard_map/ppermute | solution.py:632
  12.6 10.8 %collective-permute-start.4 = (f32[256,256]{1,0:T(8,128)S(1)}, f32[256,256]{1,0:T(8,128)S(1)}, u32[]{:S(2)}, u32[]{:S(2)}) collective-permute-start(f32[256,256]{1,0:T(8,128)S(1)} %collective-permute-done.refs_0_), channel_id=1, source_target_pairs={{0,64},{64,128},{128,192},{192,0},{1,65},{65,129},{129,193},{193,1... | collective-permute-start | bytes 786440 | tf_op jit(solution)/shard_map/ppermute | solution.py:632
  14.1 9.8 %collective-permute-start.5 = (f32[256,256]{1,0:T(8,128)S(1)}, f32[256,256]{1,0:T(8,128)S(1)}, u32[]{:S(2)}, u32[]{:S(2)}) collective-permute-start(f32[256,256]{1,0:T(8,128)S(1)} %collective-permute-done.1.refs_3_), channel_id=1, source_target_pairs={{0,192},{64,0},{128,64},{192,128},{1,193},{65,1},{129,65},{193,129... | collective-permute-start | bytes 786440 | tf_op jit(solution)/shard_map/ppermute | solution.py:632
  23.9 4.3 %collective-permute-start.6 = (f32[256,256]{1,0:T(8,128)S(1)}, f32[256,256]{1,0:T(8,128)S(1)}, u32[]{:S(2)}, u32[]{:S(2)}) collective-permute-start(f32[256,256]{1,0:T(8,128)S(1)} %collective-permute-done.refs_0_), channel_id=1, source_target_pairs={{0,1},{1,0},{2,3},{3,2},{4,5},{5,4},{6,7},{7,6},{8,9},{9,8},{10,11... | collective-permute-start | bytes 786440 | tf_op jit(solution)/shard_map/ppermute | solution.py:635
  27.0 1.5 collective-permute-start.7
  27.1 1.8 collective-permute-start.8
  27.5 1.8 collective-permute-start.9
  27.6 2.0 %collective-permute-start.10 = (f32[256,256]{1,0:T(8,128)S(1)}, f32[256,256]{1,0:T(8,128)S(1)}, u32[]{:S(2)}, u32[]{:S(2)}) collective-permute-start(f32[256,256]{1,0:T(8,128)S(1)} %collective-permute-done.4.refs_4_), channel_id=1, source_target_pairs={{0,1},{1,0},{2,3},{3,2},{4,5},{5,4},{6,7},{7,6},{8,9},{9,8},{10,11... | collective-permute-start | bytes 786440 | tf_op jit(solution)/shard_map/ppermute | solution.py:635
  28.1 1.9 %collective-permute-start.11 = (f32[256,256]{1,0:T(8,128)S(1)}, f32[256,256]{1,0:T(8,128)S(1)}, u32[]{:S(2)}, u32[]{:S(2)}) collective-permute-start(f32[256,256]{1,0:T(8,128)S(1)} %collective-permute-done.5.refs_5_), channel_id=1, source_target_pairs={{0,1},{1,0},{2,3},{3,2},{4,5},{5,4},{6,7},{7,6},{8,9},{9,8},{10,11... | collective-permute-start | bytes 786440 | tf_op jit(solution)/shard_map/ppermute | solution.py:635
  138.2 15.1 %copy-start = (f32[4,256,128]{2,1,0:T(8,128)S(1)}, f32[4,256,128]{2,1,0:T(8,128)}, u32[]{:S(2)}) copy-start(f32[4,256,128]{2,1,0:T(8,128)} %get-tuple-element.68) | copy-start | bytes 1572868
  138.2 15.8 %copy-start.1 = (f32[4,256,128]{2,1,0:T(8,128)S(1)}, f32[4,256,128]{2,1,0:T(8,128)}, u32[]{:S(2)}) copy-start(f32[4,256,128]{2,1,0:T(8,128)} %get-tuple-element.66) | copy-start | bytes 1572868
  138.2 2.7 %collective-permute-start.12 = (f32[16,64,256]{2,1,0:T(8,128)S(1)}, f32[16,64,256]{2,1,0:T(8,128)S(1)}, u32[]{:S(2)}, u32[]{:S(2)}) collective-permute-start(f32[16,64,256]{2,1,0:T(8,128)S(1)} %get-tuple-element.62), channel_id=1, source_target_pairs={{0,1},{1,0},{2,3},{3,2},{4,5},{5,4},{6,7},{7,6},{8,9},{9,8},{10,11... | collective-permute-start | bytes 3145736 | tf_op jit(solution)/shard_map/ppermute | solution.py:635
  138.6 14.6 %collective-permute-start.14 = (f32[4,256,128]{2,1,0:T(8,128)}, f32[4,256,128]{2,1,0:T(8,128)S(1)}, u32[]{:S(2)}, u32[]{:S(2)}) collective-permute-start(f32[4,256,128]{2,1,0:T(8,128)} %get-tuple-element.69), channel_id=1, source_target_pairs={{0,56},{8,16},{16,8},{24,32},{32,24},{40,48},{48,40},{56,0},{1,57}... | collective-permute-start | bytes 1572872 | tf_op jit(solution)/shard_map/ppermute | solution.py:369
  138.6 15.3 %collective-permute-start.13 = (f32[4,256,128]{2,1,0:T(8,128)}, f32[4,256,128]{2,1,0:T(8,128)S(1)}, u32[]{:S(2)}, u32[]{:S(2)}) collective-permute-start(f32[4,256,128]{2,1,0:T(8,128)} %get-tuple-element.67), channel_id=1, source_target_pairs={{0,8},{8,0},{16,24},{24,16},{32,40},{40,32},{48,56},{56,48},{1,9},... | collective-permute-start | bytes 1572872 | tf_op jit(solution)/shard_map/ppermute | solution.py:369
  142.0 20.7 %all-to-all-start.6 = ((f32[16,64,256]{2,1,0:T(8,128)}), f32[16,64,256]{2,1,0:T(8,128)S(1)}, u32[]{:S(2)}, u32[]{:S(2)}) async-start(f32[16,64,256]{2,1,0:T(8,128)} %add.166), calls=%async_computation.6 | async-start | bytes 2097152 | tf_op jit(solution)/shard_map/all_to_all | solution.py:34
  154.0 16.2 %collective-permute-start.17 = (f32[2,256,128]{2,1,0:T(8,128)}, f32[2,256,128]{2,1,0:T(8,128)}, u32[]{:S(2)}, u32[]{:S(2)}) collective-permute-start(f32[2,256,128]{2,1,0:T(8,128)} %slice_add_fusion), channel_id=1, source_target_pairs={{0,16},{8,56},{16,32},{24,8},{32,48},{40,24},{48,0},{56,40},{1,17}... | collective-permute-start | bytes 786440 | tf_op jit(solution)/shard_map/ppermute | solution.py:377
  154.7 17.0 %collective-permute-start.15 = (f32[2,256,128]{2,1,0:T(8,128)}, f32[2,256,128]{2,1,0:T(8,128)}, u32[]{:S(2)}, u32[]{:S(2)}) collective-permute-start(f32[2,256,128]{2,1,0:T(8,128)} %slice_add_fusion.1), channel_id=1, source_target_pairs={{0,48},{8,24},{16,0},{24,40},{32,16},{40,56},{48,32},{56,8},{1,49}... | collective-permute-start | bytes 786440 | tf_op jit(solution)/shard_map/ppermute | solution.py:377
  165.1 15.9 %all-to-all-start.7 = ((f32[8,64,256]{2,1,0:T(8,128)}), f32[8,64,256]{2,1,0:T(8,128)S(1)}, u32[]{:S(2)}, u32[]{:S(2)}) async-start(f32[8,64,256]{2,1,0:T(8,128)} %student_end.1), calls=%async_computation.7 | async-start | bytes 1048576 | tf_op jit(solution)/shard_map/all_to_all | solution.py:34
  171.2 4.5 %collective-permute-start.18 = (f32[256,128]{1,0:T(8,128)S(1)}, f32[256,128]{1,0:T(8,128)S(1)}, u32[]{:S(2)}, u32[]{:S(2)}) collective-permute-start(f32[256,128]{1,0:T(8,128)S(1)} %get-tuple-element.82), channel_id=1, source_target_pairs={{0,8},{8,0},{16,24},{24,16},{32,40},{40,32},{48,56},{56,48},{1,9},... | collective-permute-start | bytes 393224 | tf_op jit(solution)/shard_map/ppermute | solution.py:386
  172.7 5.9 %collective-permute-start.16 = (f32[256,128]{1,0:T(8,128)S(1)}, f32[256,128]{1,0:T(8,128)S(1)}, u32[]{:S(2)}, u32[]{:S(2)}) collective-permute-start(f32[256,128]{1,0:T(8,128)S(1)} %get-tuple-element.84), channel_id=1, source_target_pairs={{0,56},{8,16},{16,8},{24,32},{32,24},{40,48},{48,40},{56,0},{1,57}... | collective-permute-start | bytes 393224 | tf_op jit(solution)/shard_map/ppermute | solution.py:386

commit v11 on v10

--- a/solution.py
+++ b/solution.py
@@ -375,15 +375,15 @@
     way = [1 if (z + offset) % 2 else -1 for z in range(n)]
     own, following, far = sums
     got = lax.ppermute(far, "z", [(z, (z + 2 * way[z]) % n) for z in range(n)])
-    own, following, _ = lax.optimization_barrier((own, following, after))
-    return own + got[0], following + got[1]
+    following, _ = lax.optimization_barrier((following, after))
+    return [own, got], following + got[1]
 
 
 def deliver(sums, offset):
     n = lax.axis_size("z")
     way = [1 if (z + offset) % 2 else -1 for z in range(n)]
     own, following = sums
-    return [own, lax.ppermute(following, "z", [(z, (z + way[z]) % n) for z in range(n)])]
+    return own + [lax.ppermute(following, "z", [(z, (z + way[z]) % n) for z in range(n)])]
 
 
 def gradient_body(
@@ -593,7 +593,7 @@
     for group in (piece_refs[:half], piece_refs[half:]):
         total = group[0][...]
         for ref in group[1:]:
-            total = total + ref[...]
+            total = total + (ref[0] if len(ref.shape) == 3 else ref[...])
         sums.append(total)
     out_ref[...] = project(jnp.concatenate(sums, axis=1), unit, length)
 
@@ -642,19 +642,19 @@
     norm_part, got, place, table = lax.optimization_barrier((norm_part, got, place, table))
     got = got + [from_core(piece) for piece in got]
 
-    rows = ("y",) + PROTOS
-    peers = y_size * proto_size
     energy, sums, units_all = energy_of(place, units, got, teacher_protos, share, z_size)
+    peers = y_size * lax.axis_size("x")
     for sweep in range(ITERS):
         if sweep > 0:
             sums = column_sums(energy, pieces, z_size)
         norms = (norm_part,) if sweep == ITERS - 1 else ()
-        col_scale, row_part = row_sums(energy, spread(sums, "z"), peers, norms)
-        pieces = spread(row_part, rows)
-    pieces = pieces.reshape((y_size, proto_size) + pieces.shape[1:])
+        col_scale, row_part = row_sums(energy, spread(sums, "z"), 1, norms)
+        row_part = row_part + from_core(row_part)
+        pieces = spread(jnp.broadcast_to(row_part, (peers,) + row_part.shape[1:]), ("y", "x"))
+    pieces = pieces.reshape((y_size, peers // y_size) + pieces.shape[1:])
 
     send_left, send_right, keep_left, keep_right, feature_send, feature_keep = gradients(
-        table, units_all, energy, pieces, student_protos, col_scale, peers
+        table, units_all, energy, pieces, student_protos, col_scale, y_size * proto_size
     )
     feature_part = feature_keep + from_core(feature_send)
     feature_part, keep_left, keep_right = lax.optimization_barrier(

time: 182 us -> 180 us (0.989)
  blocking collectives: 79.2 us -> 66.3 us
  starting transfers between devices: 27.3 us -> 36.3 us
    all_to_all x6, blocking collectives: 79.2 us -> 66.3 us  [spread(): return lax.all_to_all(value, axes, 0, 0, tiled=True)]
    ppermute x7 -> x10, starting transfers between devices: 4.94 us -> 14.1 us  [on_device(): from_core = lambda value: lax.ppermute(value, 'core', [(0, 1), (1, 0)])]
    ppermute x7 -> x10, waiting for transfers between devices: 3.45 us -> 5.91 us  [on_device(): from_core = lambda value: lax.ppermute(value, 'core', [(0, 1), (1, 0)])]
    add x2, other arithmetic: 2.02 us -> 0.04 us  [pass_on(): return ([own, got], following + got[1])]
    add x4, other arithmetic: 1.5 us -> 3.47 us  [collect(): return (keep[0] + got[0], keep[1] + got[1], keep[2:] + got[2:])]
  transfers between devices with their start and end apart: 21 -> 24, of which waited for: 14 -> 18; matrix products, arithmetic and copies ran while one was open for 3% -> 3% of each run, Pallas kernels for 6% -> 6%
where the time goes in v11:
time: 180 us; the launch traced here: 179 us
  blocking collectives  66.3 us (37%)
  Pallas kernels  42.6 us (24%)
  starting transfers between devices  36.3 us (20%)
  waiting for transfers between devices  26.9 us (15%)
  other arithmetic  4.63 us (3%)
    all_to_all x6, blocking collectives, spread(): return lax.all_to_all(value, axes, 0, 0, tiled=True)  66.3 us
    ppermute x10, starting transfers between devices, on_device(): from_core = lambda value: lax.ppermute(value, 'core', [(0, 1), (1, 0)])  14.1 us
    pallas_call x1, Pallas kernels, gradients(): pl.pallas_call(gradient_body, grid_spec=pltpu.PrefetchScalarGridSpec(num_...  11.4 us
    all_to_all x2, starting transfers between devices, spread(): return lax.all_to_all(value, axes, 0, 0, tiled=True)  8.76 us
    ppermute x2, waiting for transfers between devices, collect(): got = lax.ppermute(send, 'z', [(z, (z - way[z]) % n) for z in range(n)])  7.87 us
    ppermute x6, starting transfers between devices, on_device(): lax.ppermute(value, 'y', [(i, (i + step) % y_size) for i in range(y_size)])  7.71 us
    pallas_call x1, Pallas kernels, energy_of(): pl.pallas_call(energy_body, grid_spec=pltpu.PrefetchScalarGridSpec(num_sc...  6.89 us
    pallas_call x3, Pallas kernels, row_sums(): pl.pallas_call(row_body, in_specs=[whole] * (2 + len(norm_part)), out_spe...  6.22 us
  transfers between devices with their start and end apart: 24, of which 18 were waited for; matrix products, arithmetic and copies ran while one was open for 3% of the time, Pallas kernels for 6%

profile of v11, /device:TPU:1, one launch (start us, length us, event | category | flops | bytes accessed | tf_op | source)
XLA Modules:
  0.0 179.2 jit_solution(15782907213420056690)
XLA Ops:
  0.6 3.0 %select.31 = (f32[512,512]{1,0:T(8,128)}, f32[512,1]{1,0:T(8,128)}, f32[256,256]{1,0:T(8,128)}, f32[256,256]{1,0:T(8,128)}) custom-call(s32[1]{0:T(128)} %bitcast.core_ref, bf16[4,256,256]{2,1,0:T(8,128)(2,1)} %teacher_ref.1, bf16[4,256,256]{2,1,0:T(8,128)(2,1)} %student_ref.1, s32[4,256]{1,0:T(4,128)} %order_ref.1), custom_call_target="tpu_custom_call" | custom-call | tf_op jit(solution)/shard_map/select/pallas_call | solution.py:103
  15.3 6.1 %student.1.refs_0_ = f32[4,128]{1,0:T(4,128)S(1)} custom-call(f32[512,512]{1,0:T(8,128)} %get-tuple-element.40.units_ref.unit_ref, bf16[8192,256]{1,0:T(8,128)(2,1)} %refs_6_.1), custom_call_target="tpu_custom_call" | custom-call | flops 4294967296 | bytes 8388608 | tf_op jit(solution)/shard_map/student/pallas_call | solution.py:268
  23.9 3.1 %collective-permute-start.6 = (f32[256,256]{1,0:T(8,128)S(1)}, f32[256,256]{1,0:T(8,128)S(1)}, u32[]{:S(2)}, u32[]{:S(2)}) collective-permute-start(f32[256,256]{1,0:T(8,128)S(1)} %collective-permute-done.refs_0_), channel_id=1, source_target_pairs={{0,1},{1,0},{2,3},{3,2},{4,5},{5,4},{6,7},{7,6},{8,9},{9,8},{10,11... | collective-permute-start | bytes 786440 | tf_op jit(solution)/shard_map/ppermute | solution.py:635
  30.0 6.9 %energy.1 = (bf16[16,2048,128]{2,1,0:T(8,128)(2,1)S(1)}, f32[8,16,128]{2,1,0:T(8,128)S(1)}, bf16[2048,512]{1,0:T(8,128)(2,1)S(1)}) custom-call(s32[8]{0:T(128)S(1)} %stack.43.place_ref, f32[512,512]{1,0:T(8,128)} %get-tuple-element.40.units_ref.unit_ref, f32[256,256]{1,0:T(8,128)S(1)} %collective-permute-done.refs_0_, ...), custom_call_target="tpu_custom_call" | custom-call | flops 4294967296 | bytes 8388608 | tf_op jit(solution)/shard_map/energy/pallas_call | solution.py:211
  36.9 14.1 %all_to_all.40.pieces_ref = f32[8,16,128]{2,1,0:T(8,128)S(1)} all-to-all(f32[8,16,128]{2,1,0:T(8,128)S(1)} %get-tuple-element.53), channel_id=1, replica_groups=mesh['y'=4,'z'=8,'x'=4,'core'=2] {'z'}, dimensions={0} | all-to-all | bytes 131072 | tf_op jit(solution)/shard_map/all_to_all | solution.py:34
  51.0 2.1 %row_sums.3 = (f32[16,128]{1,0:T(8,128)}, f32[1,16,128]{2,1,0:T(8,128)S(1)}) custom-call(bf16[16,2048,128]{2,1,0:T(8,128)(2,1)S(1)} %get-tuple-element.52.energy_ref, f32[8,16,128]{2,1,0:T(8,128)S(1)} %all_to_all.40.pieces_ref), custom_call_target="tpu_custom_call" | custom-call | flops 8388608 | tf_op jit(solution)/shard_map/row_sums/pallas_call | solution.py:315
  55.9 13.1 %all_to_all.41.pieces_ref = f32[16,16,128]{2,1,0:T(8,128)S(1)} all-to-all(f32[16,16,128]{2,1,0:T(8,128)S(1)} %broadcast_in_dim.26), channel_id=1, replica_groups=mesh['y'=4,'z'=8,'x'=4,'core'=2] {'y','x'}, dimensions={0} | all-to-all | bytes 262144 | tf_op jit(solution)/shard_map/all_to_all | solution.py:34
  69.0 2.2 %column_sums.2 = f32[8,16,128]{2,1,0:T(8,128)S(1)} custom-call(bf16[16,2048,128]{2,1,0:T(8,128)(2,1)S(1)} %get-tuple-element.52.energy_ref, f32[16,16,128]{2,1,0:T(8,128)S(1)} %all_to_all.41.pieces_ref), custom_call_target="tpu_custom_call" | custom-call | flops 8388608 | tf_op jit(solution)/shard_map/column_sums/pallas_call | solution.py:350
  71.2 9.7 %all_to_all.42.pieces_ref = f32[8,16,128]{2,1,0:T(8,128)S(1)} all-to-all(f32[8,16,128]{2,1,0:T(8,128)S(1)} %column_sums.2), channel_id=1, replica_groups=mesh['y'=4,'z'=8,'x'=4,'core'=2] {'z'}, dimensions={0} | all-to-all | bytes 131072 | tf_op jit(solution)/shard_map/all_to_all | solution.py:34
  80.9 2.1 %row_sums.4 = (f32[16,128]{1,0:T(8,128)}, f32[1,16,128]{2,1,0:T(8,128)S(1)}) custom-call(bf16[16,2048,128]{2,1,0:T(8,128)(2,1)S(1)} %get-tuple-element.52.energy_ref, f32[8,16,128]{2,1,0:T(8,128)S(1)} %all_to_all.42.pieces_ref), custom_call_target="tpu_custom_call" | custom-call | flops 8388608 | tf_op jit(solution)/shard_map/row_sums/pallas_call | solution.py:315
  83.1 2.9 %collective-permute-start.13 = (f32[1,16,128]{2,1,0:T(8,128)S(1)}, f32[1,16,128]{2,1,0:T(8,128)S(1)}, u32[]{:S(2)}, u32[]{:S(2)}) collective-permute-start(f32[1,16,128]{2,1,0:T(8,128)S(1)} %get-tuple-element.55), channel_id=1, source_target_pairs={{0,1},{1,0},{2,3},{3,2},{4,5},{5,4},{6,7},{7,6},{8,9},{9,8},{10,11... | collective-permute-start | bytes 24584 | tf_op jit(solution)/shard_map/ppermute | solution.py:635
  86.8 9.6 %all_to_all.43.pieces_ref = f32[16,16,128]{2,1,0:T(8,128)S(1)} all-to-all(f32[16,16,128]{2,1,0:T(8,128)S(1)} %broadcast_in_dim.28), channel_id=1, replica_groups=mesh['y'=4,'z'=8,'x'=4,'core'=2] {'y','x'}, dimensions={0} | all-to-all | bytes 262144 | tf_op jit(solution)/shard_map/all_to_all | solution.py:34
  96.4 2.2 %column_sums.3 = f32[8,16,128]{2,1,0:T(8,128)S(1)} custom-call(bf16[16,2048,128]{2,1,0:T(8,128)(2,1)S(1)} %get-tuple-element.52.energy_ref, f32[16,16,128]{2,1,0:T(8,128)S(1)} %all_to_all.43.pieces_ref), custom_call_target="tpu_custom_call" | custom-call | flops 8388608 | tf_op jit(solution)/shard_map/column_sums/pallas_call | solution.py:350
  98.6 9.7 %all_to_all.44.pieces_ref = f32[8,16,128]{2,1,0:T(8,128)S(1)} all-to-all(f32[8,16,128]{2,1,0:T(8,128)S(1)} %column_sums.3), channel_id=1, replica_groups=mesh['y'=4,'z'=8,'x'=4,'core'=2] {'z'}, dimensions={0} | all-to-all | bytes 131072 | tf_op jit(solution)/shard_map/all_to_all | solution.py:34
  110.3 2.9 %collective-permute-start.14 = (f32[1,24,128]{2,1,0:T(8,128)S(1)}, f32[1,24,128]{2,1,0:T(8,128)S(1)}, u32[]{:S(2)}, u32[]{:S(2)}) collective-permute-start(f32[1,24,128]{2,1,0:T(8,128)S(1)} %get-tuple-element.57), channel_id=1, source_target_pairs={{0,1},{1,0},{2,3},{3,2},{4,5},{5,4},{6,7},{7,6},{8,9},{9,8},{10,11... | collective-permute-start | bytes 36872 | tf_op jit(solution)/shard_map/ppermute | solution.py:635
  114.1 10.0 %all_to_all.45 = f32[16,24,128]{2,1,0:T(8,128)S(1)} all-to-all(f32[16,24,128]{2,1,0:T(8,128)S(1)} %broadcast_in_dim.30), channel_id=1, replica_groups=mesh['y'=4,'z'=8,'x'=4,'core'=2] {'y','x'}, dimensions={0} | all-to-all | bytes 393216 | tf_op jit(solution)/shard_map/all_to_all | solution.py:34
  124.1 11.4 %gradients.1 = (f32[4,256,128]{2,1,0:T(8,128)}, f32[4,256,128]{2,1,0:T(8,128)}, f32[4,256,128]{2,1,0:T(8,128)}, f32[4,256,128]{2,1,0:T(8,128)}, f32[16,64,256]{2,1,0:T(8,128)S(1)}, /*index=5*/f32[16,64,256]{2,1,0:T(8,128)S(1)}) custom-call(s32[5,8]{1,0:T(8,128)S(1)} %stack.46.table_ref, bf16[2048,512]{1,0:T(8,128)(2,1)S(1)} %get-tuple-element.51.units_ref, ...), custom_call_target="tpu_custom_call" | custom-call | flops 8589934592 | bytes 8388608 | tf_op jit(solution)/shard_map/gradients/pallas_call | solution.py:520
  140.7 3.7 %all-to-all-start.6 = ((f32[16,64,256]{2,1,0:T(8,128)}), f32[16,64,256]{2,1,0:T(8,128)S(1)}, u32[]{:S(2)}, u32[]{:S(2)}) async-start(f32[16,64,256]{2,1,0:T(8,128)} %add.170), calls=%async_computation.6 | async-start | bytes 2097152 | tf_op jit(solution)/shard_map/all_to_all | solution.py:34
  144.4 7.9 %collective-permute-done.17 = f32[4,256,128]{2,1,0:T(8,128)S(1)} collective-permute-done((f32[4,256,128]{2,1,0:T(8,128)}, f32[4,256,128]{2,1,0:T(8,128)S(1)}, u32[]{:S(2)}, u32[]{:S(2)}) %collective-permute-start.17) | collective-permute-done | bytes 524320 | tf_op jit(solution)/shard_map/ppermute | solution.py:369
  154.7 3.6 %collective-permute-start.18 = (f32[2,256,128]{2,1,0:T(8,128)}, f32[2,256,128]{2,1,0:T(8,128)S(1)}, u32[]{:S(2)}, u32[]{:S(2)}) collective-permute-start(f32[2,256,128]{2,1,0:T(8,128)} %slice_add_fusion.1), channel_id=1, source_target_pairs={{0,48},{8,24},{16,0},{24,40},{32,16},{40,56},{48,32},{56,8},{1,49}... | collective-permute-start | bytes 786440 | tf_op jit(solution)/shard_map/ppermute | solution.py:377
  161.4 2.3 %student_end.1 = f32[8,64,256]{2,1,0:T(8,128)} custom-call(s32[8]{0:T(128)S(1)} %stack.43.place_ref, f32[16,64,256]{2,1,0:T(8,128)S(1)} %all-to-all-done.6.pieces_ref, f32[512,512]{1,0:T(8,128)} %get-tuple-element.40.units_ref.unit_ref, f32[512,1]{1,0:T(8,128)} %get-tuple-element.69.length_ref), custom_call_target="tpu_custom_call" | custom-call | tf_op jit(solution)/shard_map/student_end/pallas_call | solution.py:570
  163.8 5.1 %all-to-all-start.7 = ((f32[8,64,256]{2,1,0:T(8,128)}), f32[8,64,256]{2,1,0:T(8,128)S(1)}, u32[]{:S(2)}, u32[]{:S(2)}) async-start(f32[8,64,256]{2,1,0:T(8,128)} %student_end.1), calls=%async_computation.7 | async-start | bytes 1048576 | tf_op jit(solution)/shard_map/all_to_all | solution.py:34
  170.6 2.5 %collective-permute-done.21.refs_5_ = f32[256,128]{1,0:T(8,128)S(1)} collective-permute-done((f32[256,128]{1,0:T(8,128)S(1)}, f32[256,128]{1,0:T(8,128)S(1)}, u32[]{:S(2)}, u32[]{:S(2)}) %collective-permute-start.21) | collective-permute-done | bytes 131104 | tf_op jit(solution)/shard_map/ppermute | solution.py:386
  175.0 2.4 %proto_end.1 = f32[256,256]{1,0:T(8,128)} custom-call(s32[8]{0:T(128)S(1)} %stack.43.place_ref, f32[256,128]{1,0:T(8,128)S(1)} %get-tuple-element.77.refs_0_, f32[2,256,128]{2,1,0:T(8,128)S(1)} %collective-permute-done.18.refs_1_, f32[256,128]{1,0:T(8,128)S(1)} %collective-permute-done.19.refs_2_, f32[256,128]{1,0:T(8,128)S(1)} %get-tuple-element.75.refs_3_, ...), custom_call_target="tpu_custom_call" | custom-call | tf_op jit(solution)/shard_map/proto_end/pallas_call | solution.py:603
  (63 shorter events, 39.8 us)
Async XLA Ops:
  3.6 7.5 %collective-permute-start = (f32[256,256]{1,0:T(8,128)}, f32[256,256]{1,0:T(8,128)S(1)}, u32[]{:S(2)}, u32[]{:S(2)}) collective-permute-start(f32[256,256]{1,0:T(8,128)} %get-tuple-element.38), channel_id=1, source_target_pairs={{0,64},{64,128},{128,192},{192,0},{1,65},{65,129},{129,193},{193,1... | collective-permute-start | bytes 786440 | tf_op jit(solution)/shard_map/ppermute | solution.py:632
  5.7 6.9 %collective-permute-start.1 = (f32[256,256]{1,0:T(8,128)}, f32[256,256]{1,0:T(8,128)S(1)}, u32[]{:S(2)}, u32[]{:S(2)}) collective-permute-start(f32[256,256]{1,0:T(8,128)} %get-tuple-element.39), channel_id=1, source_target_pairs={{0,192},{64,0},{128,64},{192,128},{1,193},{65,1},{129,65},{193,129... | collective-permute-start | bytes 786440 | tf_op jit(solution)/shard_map/ppermute | solution.py:632
  7.2 14.2 %collective-permute-start.3 = (f32[256,256]{1,0:T(8,128)}, f32[256,256]{1,0:T(8,128)S(1)}, u32[]{:S(2)}, u32[]{:S(2)}) collective-permute-start(f32[256,256]{1,0:T(8,128)} %get-tuple-element.38), channel_id=1, source_target_pairs={{0,192},{64,0},{128,64},{192,128},{1,193},{65,1},{129,65},{193,129... | collective-permute-start | bytes 786440 | tf_op jit(solution)/shard_map/ppermute | solution.py:632
  8.6 12.8 %collective-permute-start.2 = (f32[256,256]{1,0:T(8,128)}, f32[256,256]{1,0:T(8,128)S(1)}, u32[]{:S(2)}, u32[]{:S(2)}) collective-permute-start(f32[256,256]{1,0:T(8,128)} %get-tuple-element.39), channel_id=1, source_target_pairs={{0,64},{64,128},{128,192},{192,0},{1,65},{65,129},{129,193},{193,1... | collective-permute-start | bytes 786440 | tf_op jit(solution)/shard_map/ppermute | solution.py:632
  12.6 10.8 %collective-permute-start.4 = (f32[256,256]{1,0:T(8,128)S(1)}, f32[256,256]{1,0:T(8,128)S(1)}, u32[]{:S(2)}, u32[]{:S(2)}) collective-permute-start(f32[256,256]{1,0:T(8,128)S(1)} %collective-permute-done.refs_0_), channel_id=1, source_target_pairs={{0,64},{64,128},{128,192},{192,0},{1,65},{65,129},{129,193},{193,1... | collective-permute-start | bytes 786440 | tf_op jit(solution)/shard_map/ppermute | solution.py:632
  14.1 9.8 %collective-permute-start.5 = (f32[256,256]{1,0:T(8,128)S(1)}, f32[256,256]{1,0:T(8,128)S(1)}, u32[]{:S(2)}, u32[]{:S(2)}) collective-permute-start(f32[256,256]{1,0:T(8,128)S(1)} %collective-permute-done.1.refs_3_), channel_id=1, source_target_pairs={{0,192},{64,0},{128,64},{192,128},{1,193},{65,1},{129,65},{193,129... | collective-permute-start | bytes 786440 | tf_op jit(solution)/shard_map/ppermute | solution.py:632
  23.9 4.3 %collective-permute-start.6 = (f32[256,256]{1,0:T(8,128)S(1)}, f32[256,256]{1,0:T(8,128)S(1)}, u32[]{:S(2)}, u32[]{:S(2)}) collective-permute-start(f32[256,256]{1,0:T(8,128)S(1)} %collective-permute-done.refs_0_), channel_id=1, source_target_pairs={{0,1},{1,0},{2,3},{3,2},{4,5},{5,4},{6,7},{7,6},{8,9},{9,8},{10,11... | collective-permute-start | bytes 786440 | tf_op jit(solution)/shard_map/ppermute | solution.py:635
  27.0 1.5 collective-permute-start.7
  27.1 1.8 %collective-permute-start.8 = (f32[256,256]{1,0:T(8,128)S(1)}, f32[256,256]{1,0:T(8,128)S(1)}, u32[]{:S(2)}, u32[]{:S(2)}) collective-permute-start(f32[256,256]{1,0:T(8,128)S(1)} %collective-permute-done.3.refs_2_), channel_id=1, source_target_pairs={{0,1},{1,0},{2,3},{3,2},{4,5},{5,4},{6,7},{7,6},{8,9},{9,8},{10,11... | collective-permute-start | bytes 786440 | tf_op jit(solution)/shard_map/ppermute | solution.py:635
  27.5 1.8 collective-permute-start.9
  27.6 2.0 %collective-permute-start.10 = (f32[256,256]{1,0:T(8,128)S(1)}, f32[256,256]{1,0:T(8,128)S(1)}, u32[]{:S(2)}, u32[]{:S(2)}) collective-permute-start(f32[256,256]{1,0:T(8,128)S(1)} %collective-permute-done.4.refs_4_), channel_id=1, source_target_pairs={{0,1},{1,0},{2,3},{3,2},{4,5},{5,4},{6,7},{7,6},{8,9},{9,8},{10,11... | collective-permute-start | bytes 786440 | tf_op jit(solution)/shard_map/ppermute | solution.py:635
  28.1 1.9 %collective-permute-start.11 = (f32[256,256]{1,0:T(8,128)S(1)}, f32[256,256]{1,0:T(8,128)S(1)}, u32[]{:S(2)}, u32[]{:S(2)}) collective-permute-start(f32[256,256]{1,0:T(8,128)S(1)} %collective-permute-done.5.refs_5_), channel_id=1, source_target_pairs={{0,1},{1,0},{2,3},{3,2},{4,5},{5,4},{6,7},{7,6},{8,9},{9,8},{10,11... | collective-permute-start | bytes 786440 | tf_op jit(solution)/shard_map/ppermute | solution.py:635
  53.2 2.7 %collective-permute-start.12 = (f32[1,16,128]{2,1,0:T(8,128)S(1)}, f32[1,16,128]{2,1,0:T(8,128)S(1)}, u32[]{:S(2)}, u32[]{:S(2)}) collective-permute-start(f32[1,16,128]{2,1,0:T(8,128)S(1)} %get-tuple-element.54), channel_id=1, source_target_pairs={{0,1},{1,0},{2,3},{3,2},{4,5},{5,4},{6,7},{7,6},{8,9},{9,8},{10,11... | collective-permute-start | bytes 24584 | tf_op jit(solution)/shard_map/ppermute | solution.py:635
  83.1 3.7 %collective-permute-start.13 = (f32[1,16,128]{2,1,0:T(8,128)S(1)}, f32[1,16,128]{2,1,0:T(8,128)S(1)}, u32[]{:S(2)}, u32[]{:S(2)}) collective-permute-start(f32[1,16,128]{2,1,0:T(8,128)S(1)} %get-tuple-element.55), channel_id=1, source_target_pairs={{0,1},{1,0},{2,3},{3,2},{4,5},{5,4},{6,7},{7,6},{8,9},{9,8},{10,11... | collective-permute-start | bytes 24584 | tf_op jit(solution)/shard_map/ppermute | solution.py:635
  110.3 3.7 %collective-permute-start.14 = (f32[1,24,128]{2,1,0:T(8,128)S(1)}, f32[1,24,128]{2,1,0:T(8,128)S(1)}, u32[]{:S(2)}, u32[]{:S(2)}) collective-permute-start(f32[1,24,128]{2,1,0:T(8,128)S(1)} %get-tuple-element.57), channel_id=1, source_target_pairs={{0,1},{1,0},{2,3},{3,2},{4,5},{5,4},{6,7},{7,6},{8,9},{9,8},{10,11... | collective-permute-start | bytes 36872 | tf_op jit(solution)/shard_map/ppermute | solution.py:635
  135.5 4.1 %collective-permute-start.15 = (f32[16,64,256]{2,1,0:T(8,128)S(1)}, f32[16,64,256]{2,1,0:T(8,128)S(1)}, u32[]{:S(2)}, u32[]{:S(2)}) collective-permute-start(f32[16,64,256]{2,1,0:T(8,128)S(1)} %get-tuple-element.60), channel_id=1, source_target_pairs={{0,1},{1,0},{2,3},{3,2},{4,5},{5,4},{6,7},{7,6},{8,9},{9,8},{10,11... | collective-permute-start | bytes 3145736 | tf_op jit(solution)/shard_map/ppermute | solution.py:635
  137.3 14.9 %collective-permute-start.17 = (f32[4,256,128]{2,1,0:T(8,128)}, f32[4,256,128]{2,1,0:T(8,128)S(1)}, u32[]{:S(2)}, u32[]{:S(2)}) collective-permute-start(f32[4,256,128]{2,1,0:T(8,128)} %get-tuple-element.67), channel_id=1, source_target_pairs={{0,56},{8,16},{16,8},{24,32},{32,24},{40,48},{48,40},{56,0},{1,57}... | collective-permute-start | bytes 1572872 | tf_op jit(solution)/shard_map/ppermute | solution.py:369
  137.4 15.6 %collective-permute-start.16 = (f32[4,256,128]{2,1,0:T(8,128)}, f32[4,256,128]{2,1,0:T(8,128)}, u32[]{:S(2)}, u32[]{:S(2)}) collective-permute-start(f32[4,256,128]{2,1,0:T(8,128)} %get-tuple-element.65), channel_id=1, source_target_pairs={{0,8},{8,0},{16,24},{24,16},{32,40},{40,32},{48,56},{56,48},{1,9},... | collective-permute-start | bytes 1572872 | tf_op jit(solution)/shard_map/ppermute | solution.py:369
  140.7 20.7 %all-to-all-start.6 = ((f32[16,64,256]{2,1,0:T(8,128)}), f32[16,64,256]{2,1,0:T(8,128)S(1)}, u32[]{:S(2)}, u32[]{:S(2)}) async-start(f32[16,64,256]{2,1,0:T(8,128)} %add.170), calls=%async_computation.6 | async-start | bytes 2097152 | tf_op jit(solution)/shard_map/all_to_all | solution.py:34
  153.0 15.9 %collective-permute-start.20 = (f32[2,256,128]{2,1,0:T(8,128)}, f32[2,256,128]{2,1,0:T(8,128)S(1)}, u32[]{:S(2)}, u32[]{:S(2)}) collective-permute-start(f32[2,256,128]{2,1,0:T(8,128)} %slice_add_fusion), channel_id=1, source_target_pairs={{0,16},{8,56},{16,32},{24,8},{32,48},{40,24},{48,0},{56,40},{1,17}... | collective-permute-start | bytes 786440 | tf_op jit(solution)/shard_map/ppermute | solution.py:377
  154.7 14.6 %collective-permute-start.18 = (f32[2,256,128]{2,1,0:T(8,128)}, f32[2,256,128]{2,1,0:T(8,128)S(1)}, u32[]{:S(2)}, u32[]{:S(2)}) collective-permute-start(f32[2,256,128]{2,1,0:T(8,128)} %slice_add_fusion.1), channel_id=1, source_target_pairs={{0,48},{8,24},{16,0},{24,40},{32,16},{40,56},{48,32},{56,8},{1,49}... | collective-permute-start | bytes 786440 | tf_op jit(solution)/shard_map/ppermute | solution.py:377
  163.8 14.6 %all-to-all-start.7 = ((f32[8,64,256]{2,1,0:T(8,128)}), f32[8,64,256]{2,1,0:T(8,128)S(1)}, u32[]{:S(2)}, u32[]{:S(2)}) async-start(f32[8,64,256]{2,1,0:T(8,128)} %student_end.1), calls=%async_computation.7 | async-start | bytes 1048576 | tf_op jit(solution)/shard_map/all_to_all | solution.py:34
  168.9 4.2 %collective-permute-start.21 = (f32[256,128]{1,0:T(8,128)S(1)}, f32[256,128]{1,0:T(8,128)S(1)}, u32[]{:S(2)}, u32[]{:S(2)}) collective-permute-start(f32[256,128]{1,0:T(8,128)S(1)} %fusion), channel_id=1, source_target_pairs={{0,8},{8,0},{16,24},{24,16},{32,40},{40,32},{48,56},{56,48},{1,9},... | collective-permute-start | bytes 393224 | tf_op jit(solution)/shard_map/ppermute | solution.py:386
  169.3 5.7 %collective-permute-start.19 = (f32[256,128]{1,0:T(8,128)S(1)}, f32[256,128]{1,0:T(8,128)S(1)}, u32[]{:S(2)}, u32[]{:S(2)}) collective-permute-start(f32[256,128]{1,0:T(8,128)S(1)} %fusion.1), channel_id=1, source_target_pairs={{0,56},{8,16},{16,8},{24,32},{32,24},{40,48},{48,40},{56,0},{1,57}... | collective-permute-start | bytes 393224 | tf_op jit(solution)/shard_map/ppermute | solution.py:386
  (2 other events, 34.3 us)

commit v12 on v11

--- a/solution.py
+++ b/solution.py
@@ -172,21 +172,21 @@
     parts = [slice(c, c + size) for c in range(0, weights_ref.shape[0], size)]
 
     def step(i, carry):
-        chunk = cast_ref[pl.ds(pl.multiple_of(i * WIDE, WIDE), WIDE), :][:, :D]
+        chunk = cast_ref[pl.ds(pl.multiple_of(i * size, size), size), :][:, :D]
         logits = nt_dot(weights_ref[parts[0], :], chunk)
         for k, part in enumerate(parts):
             following = nt_dot(weights_ref[parts[k + 1], :], chunk) if k + 1 < len(parts) else None
             energy = jnp.exp2(logits * teacher_power)
             total = total_ref[part, :]
-            for j in range(WIDE // LANES):
+            for j in range(size // LANES):
                 tile = energy[:, j * LANES : (j + 1) * LANES]
-                energy_ref[i * (WIDE // LANES) + j, part, :] = tile.astype(bf16)
+                energy_ref[i * (size // LANES) + j, part, :] = tile.astype(bf16)
                 total = total + tile
             total_ref[part, :] = total
             logits = following
         return carry
 
-    lax.fori_loop(0, tokens // WIDE, step, 0)
+    lax.fori_loop(0, tokens // size, step, 0)
     totals = lane_totals(total_ref[...])
     for copy in range(sums_ref.shape[0]):
         sums_ref[copy] = totals
@@ -453,8 +453,13 @@
             probs = jnp.exp2(logits[:, j * LANES : (j + 1) * LANES] * student_power) * n_ref[:, lanes]
             grads.append((probs - energy * r_ref[:, lanes] * col_scale).astype(bf16))
         logit_grad = jnp.concatenate(grads, axis=1)
-        added = jnp.dot(logit_grad, units_ref[part, D:], preferred_element_type=f32)
-        total_ref[...] = added if i == 0 else total_ref[...] + added
+        if i % 2 == 0:
+            before = logit_grad
+        else:
+            pair = jnp.concatenate([before, logit_grad], axis=1)
+            rows = slice(part.start - WIDE, part.stop)
+            added = jnp.dot(pair, units_ref[rows, D:], preferred_element_type=f32)
+            total_ref[...] = added if i == 1 else total_ref[...] + added
         feature_ref[part, :] += lax.dot_general(
             logit_grad, sw, (((0,), (0,)), ((), ())), preferred_element_type=f32
         )

time: 180 us -> 180 us (level)
  no operation moved by 1% of the time
where the time goes in v12:
time: 180 us; the launch traced here: 179 us
  blocking collectives  66.3 us (37%)
  Pallas kernels  42.5 us (24%)
  starting transfers between devices  36.3 us (20%)
  waiting for transfers between devices  26.9 us (15%)
  other arithmetic  4.63 us (3%)
    all_to_all x6, blocking collectives, spread(): return lax.all_to_all(value, axes, 0, 0, tiled=True)  66.3 us
    ppermute x10, starting transfers between devices, on_device(): from_core = lambda value: lax.ppermute(value, 'core', [(0, 1), (1, 0)])  14 us
    pallas_call x1, Pallas kernels, gradients(): pl.pallas_call(gradient_body, grid_spec=pltpu.PrefetchScalarGridSpec(num_...  12.1 us
    all_to_all x2, starting transfers between devices, spread(): return lax.all_to_all(value, axes, 0, 0, tiled=True)  8.76 us
    ppermute x2, waiting for transfers between devices, collect(): got = lax.ppermute(send, 'z', [(z, (z - way[z]) % n) for z in range(n)])  7.87 us
    ppermute x6, starting transfers between devices, on_device(): lax.ppermute(value, 'y', [(i, (i + step) % y_size) for i in range(y_size)])  7.71 us
    pallas_call x3, Pallas kernels, row_sums(): pl.pallas_call(row_body, in_specs=[whole] * (2 + len(norm_part)), out_spe...  6.22 us
    pallas_call x1, Pallas kernels, student_sums(): pl.pallas_call(student_body, in_specs=[pl.BlockSpec(memory_space=pl.ANY)]...  6.08 us
  transfers between devices with their start and end apart: 24, of which 18 were waited for; matrix products, arithmetic and copies ran while one was open for 3% of the time, Pallas kernels for 6%

profile of v12, /device:TPU:1, one launch (start us, length us, event | category | flops | bytes accessed | tf_op | source)
XLA Modules:
  0.0 179.0 jit_solution(15494516255627122141)
XLA Ops:
  0.6 3.0 %select.31 = (f32[512,512]{1,0:T(8,128)}, f32[512,1]{1,0:T(8,128)}, f32[256,256]{1,0:T(8,128)}, f32[256,256]{1,0:T(8,128)}) custom-call(s32[1]{0:T(128)} %bitcast.core_ref, bf16[4,256,256]{2,1,0:T(8,128)(2,1)} %teacher_ref.1, bf16[4,256,256]{2,1,0:T(8,128)(2,1)} %student_ref.1, s32[4,256]{1,0:T(4,128)} %order_ref.1), custom_call_target="tpu_custom_call" | custom-call | tf_op jit(solution)/shard_map/select/pallas_call | solution.py:103
  15.3 6.1 %student.1.refs_0_ = f32[4,128]{1,0:T(4,128)S(1)} custom-call(f32[512,512]{1,0:T(8,128)} %get-tuple-element.40.units_ref.unit_ref, bf16[8192,256]{1,0:T(8,128)(2,1)} %refs_6_.1), custom_call_target="tpu_custom_call" | custom-call | flops 4294967296 | bytes 8388608 | tf_op jit(solution)/shard_map/student/pallas_call | solution.py:268
  23.9 3.1 %collective-permute-start.6 = (f32[256,256]{1,0:T(8,128)S(1)}, f32[256,256]{1,0:T(8,128)S(1)}, u32[]{:S(2)}, u32[]{:S(2)}) collective-permute-start(f32[256,256]{1,0:T(8,128)S(1)} %collective-permute-done.refs_0_), channel_id=1, source_target_pairs={{0,1},{1,0},{2,3},{3,2},{4,5},{5,4},{6,7},{7,6},{8,9},{9,8},{10,11... | collective-permute-start | bytes 786440 | tf_op jit(solution)/shard_map/ppermute | solution.py:640
  30.0 6.1 %energy.1 = (bf16[16,2048,128]{2,1,0:T(8,128)(2,1)S(1)}, f32[8,16,128]{2,1,0:T(8,128)S(1)}, bf16[2048,512]{1,0:T(8,128)(2,1)S(1)}) custom-call(s32[8]{0:T(128)S(1)} %stack.43.place_ref, f32[512,512]{1,0:T(8,128)} %get-tuple-element.40.units_ref.unit_ref, f32[256,256]{1,0:T(8,128)S(1)} %collective-permute-done.refs_0_, ...), custom_call_target="tpu_custom_call" | custom-call | flops 4294967296 | bytes 8388608 | tf_op jit(solution)/shard_map/energy/pallas_call | solution.py:211
  36.1 14.2 %all_to_all.40.pieces_ref = f32[8,16,128]{2,1,0:T(8,128)S(1)} all-to-all(f32[8,16,128]{2,1,0:T(8,128)S(1)} %get-tuple-element.53), channel_id=1, replica_groups=mesh['y'=4,'z'=8,'x'=4,'core'=2] {'z'}, dimensions={0} | all-to-all | bytes 131072 | tf_op jit(solution)/shard_map/all_to_all | solution.py:34
  50.2 2.1 %row_sums.3 = (f32[16,128]{1,0:T(8,128)}, f32[1,16,128]{2,1,0:T(8,128)S(1)}) custom-call(bf16[16,2048,128]{2,1,0:T(8,128)(2,1)S(1)} %get-tuple-element.52.energy_ref, f32[8,16,128]{2,1,0:T(8,128)S(1)} %all_to_all.40.pieces_ref), custom_call_target="tpu_custom_call" | custom-call | flops 8388608 | tf_op jit(solution)/shard_map/row_sums/pallas_call | solution.py:315
  55.1 13.1 %all_to_all.41.pieces_ref = f32[16,16,128]{2,1,0:T(8,128)S(1)} all-to-all(f32[16,16,128]{2,1,0:T(8,128)S(1)} %broadcast_in_dim.26), channel_id=1, replica_groups=mesh['y'=4,'z'=8,'x'=4,'core'=2] {'y','x'}, dimensions={0} | all-to-all | bytes 262144 | tf_op jit(solution)/shard_map/all_to_all | solution.py:34
  68.2 2.2 %column_sums.2 = f32[8,16,128]{2,1,0:T(8,128)S(1)} custom-call(bf16[16,2048,128]{2,1,0:T(8,128)(2,1)S(1)} %get-tuple-element.52.energy_ref, f32[16,16,128]{2,1,0:T(8,128)S(1)} %all_to_all.41.pieces_ref), custom_call_target="tpu_custom_call" | custom-call | flops 8388608 | tf_op jit(solution)/shard_map/column_sums/pallas_call | solution.py:350
  70.4 9.7 %all_to_all.42.pieces_ref = f32[8,16,128]{2,1,0:T(8,128)S(1)} all-to-all(f32[8,16,128]{2,1,0:T(8,128)S(1)} %column_sums.2), channel_id=1, replica_groups=mesh['y'=4,'z'=8,'x'=4,'core'=2] {'z'}, dimensions={0} | all-to-all | bytes 131072 | tf_op jit(solution)/shard_map/all_to_all | solution.py:34
  80.1 2.1 %row_sums.4 = (f32[16,128]{1,0:T(8,128)}, f32[1,16,128]{2,1,0:T(8,128)S(1)}) custom-call(bf16[16,2048,128]{2,1,0:T(8,128)(2,1)S(1)} %get-tuple-element.52.energy_ref, f32[8,16,128]{2,1,0:T(8,128)S(1)} %all_to_all.42.pieces_ref), custom_call_target="tpu_custom_call" | custom-call | flops 8388608 | tf_op jit(solution)/shard_map/row_sums/pallas_call | solution.py:315
  82.2 2.9 %collective-permute-start.13 = (f32[1,16,128]{2,1,0:T(8,128)S(1)}, f32[1,16,128]{2,1,0:T(8,128)S(1)}, u32[]{:S(2)}, u32[]{:S(2)}) collective-permute-start(f32[1,16,128]{2,1,0:T(8,128)S(1)} %get-tuple-element.55), channel_id=1, source_target_pairs={{0,1},{1,0},{2,3},{3,2},{4,5},{5,4},{6,7},{7,6},{8,9},{9,8},{10,11... | collective-permute-start | bytes 24584 | tf_op jit(solution)/shard_map/ppermute | solution.py:640
  86.0 9.6 %all_to_all.43.pieces_ref = f32[16,16,128]{2,1,0:T(8,128)S(1)} all-to-all(f32[16,16,128]{2,1,0:T(8,128)S(1)} %broadcast_in_dim.28), channel_id=1, replica_groups=mesh['y'=4,'z'=8,'x'=4,'core'=2] {'y','x'}, dimensions={0} | all-to-all | bytes 262144 | tf_op jit(solution)/shard_map/all_to_all | solution.py:34
  95.6 2.2 %column_sums.3 = f32[8,16,128]{2,1,0:T(8,128)S(1)} custom-call(bf16[16,2048,128]{2,1,0:T(8,128)(2,1)S(1)} %get-tuple-element.52.energy_ref, f32[16,16,128]{2,1,0:T(8,128)S(1)} %all_to_all.43.pieces_ref), custom_call_target="tpu_custom_call" | custom-call | flops 8388608 | tf_op jit(solution)/shard_map/column_sums/pallas_call | solution.py:350
  97.8 9.7 %all_to_all.44.pieces_ref = f32[8,16,128]{2,1,0:T(8,128)S(1)} all-to-all(f32[8,16,128]{2,1,0:T(8,128)S(1)} %column_sums.3), channel_id=1, replica_groups=mesh['y'=4,'z'=8,'x'=4,'core'=2] {'z'}, dimensions={0} | all-to-all | bytes 131072 | tf_op jit(solution)/shard_map/all_to_all | solution.py:34
  109.5 2.9 %collective-permute-start.14 = (f32[1,24,128]{2,1,0:T(8,128)S(1)}, f32[1,24,128]{2,1,0:T(8,128)S(1)}, u32[]{:S(2)}, u32[]{:S(2)}) collective-permute-start(f32[1,24,128]{2,1,0:T(8,128)S(1)} %get-tuple-element.57), channel_id=1, source_target_pairs={{0,1},{1,0},{2,3},{3,2},{4,5},{5,4},{6,7},{7,6},{8,9},{9,8},{10,11... | collective-permute-start | bytes 36872 | tf_op jit(solution)/shard_map/ppermute | solution.py:640
  113.3 10.0 %all_to_all.45 = f32[16,24,128]{2,1,0:T(8,128)S(1)} all-to-all(f32[16,24,128]{2,1,0:T(8,128)S(1)} %broadcast_in_dim.30), channel_id=1, replica_groups=mesh['y'=4,'z'=8,'x'=4,'core'=2] {'y','x'}, dimensions={0} | all-to-all | bytes 393216 | tf_op jit(solution)/shard_map/all_to_all | solution.py:34
  123.2 12.1 %gradients.1 = (f32[4,256,128]{2,1,0:T(8,128)}, f32[4,256,128]{2,1,0:T(8,128)}, f32[4,256,128]{2,1,0:T(8,128)}, f32[4,256,128]{2,1,0:T(8,128)}, f32[16,64,256]{2,1,0:T(8,128)S(1)}, /*index=5*/f32[16,64,256]{2,1,0:T(8,128)S(1)}) custom-call(s32[5,8]{1,0:T(8,128)S(1)} %stack.46.table_ref, bf16[2048,512]{1,0:T(8,128)(2,1)S(1)} %get-tuple-element.51.units_ref, ...), custom_call_target="tpu_custom_call" | custom-call | flops 8589934592 | bytes 8388608 | tf_op jit(solution)/shard_map/gradients/pallas_call | solution.py:525
  140.6 3.7 %all-to-all-start.6 = ((f32[16,64,256]{2,1,0:T(8,128)}), f32[16,64,256]{2,1,0:T(8,128)S(1)}, u32[]{:S(2)}, u32[]{:S(2)}) async-start(f32[16,64,256]{2,1,0:T(8,128)} %add.170), calls=%async_computation.6 | async-start | bytes 2097152 | tf_op jit(solution)/shard_map/all_to_all | solution.py:34
  144.2 7.9 %collective-permute-done.17 = f32[4,256,128]{2,1,0:T(8,128)S(1)} collective-permute-done((f32[4,256,128]{2,1,0:T(8,128)}, f32[4,256,128]{2,1,0:T(8,128)S(1)}, u32[]{:S(2)}, u32[]{:S(2)}) %collective-permute-start.17) | collective-permute-done | bytes 524320 | tf_op jit(solution)/shard_map/ppermute | solution.py:369
  154.6 3.6 %collective-permute-start.18 = (f32[2,256,128]{2,1,0:T(8,128)}, f32[2,256,128]{2,1,0:T(8,128)S(1)}, u32[]{:S(2)}, u32[]{:S(2)}) collective-permute-start(f32[2,256,128]{2,1,0:T(8,128)} %slice_add_fusion.1), channel_id=1, source_target_pairs={{0,48},{8,24},{16,0},{24,40},{32,16},{40,56},{48,32},{56,8},{1,49}... | collective-permute-start | bytes 786440 | tf_op jit(solution)/shard_map/ppermute | solution.py:377
  161.3 2.3 %student_end.1 = f32[8,64,256]{2,1,0:T(8,128)} custom-call(s32[8]{0:T(128)S(1)} %stack.43.place_ref, f32[16,64,256]{2,1,0:T(8,128)S(1)} %all-to-all-done.6.pieces_ref, f32[512,512]{1,0:T(8,128)} %get-tuple-element.40.units_ref.unit_ref, f32[512,1]{1,0:T(8,128)} %get-tuple-element.69.length_ref), custom_call_target="tpu_custom_call" | custom-call | tf_op jit(solution)/shard_map/student_end/pallas_call | solution.py:575
  163.6 5.1 %all-to-all-start.7 = ((f32[8,64,256]{2,1,0:T(8,128)}), f32[8,64,256]{2,1,0:T(8,128)S(1)}, u32[]{:S(2)}, u32[]{:S(2)}) async-start(f32[8,64,256]{2,1,0:T(8,128)} %student_end.1), calls=%async_computation.7 | async-start | bytes 1048576 | tf_op jit(solution)/shard_map/all_to_all | solution.py:34
  170.5 2.5 %collective-permute-done.21.refs_5_ = f32[256,128]{1,0:T(8,128)S(1)} collective-permute-done((f32[256,128]{1,0:T(8,128)S(1)}, f32[256,128]{1,0:T(8,128)S(1)}, u32[]{:S(2)}, u32[]{:S(2)}) %collective-permute-start.21) | collective-permute-done | bytes 131104 | tf_op jit(solution)/shard_map/ppermute | solution.py:386
  174.9 2.4 %proto_end.1 = f32[256,256]{1,0:T(8,128)} custom-call(s32[8]{0:T(128)S(1)} %stack.43.place_ref, f32[256,128]{1,0:T(8,128)S(1)} %get-tuple-element.77.refs_0_, f32[2,256,128]{2,1,0:T(8,128)S(1)} %collective-permute-done.18.refs_1_, f32[256,128]{1,0:T(8,128)S(1)} %collective-permute-done.19.refs_2_, f32[256,128]{1,0:T(8,128)S(1)} %get-tuple-element.75.refs_3_, ...), custom_call_target="tpu_custom_call" | custom-call | tf_op jit(solution)/shard_map/proto_end/pallas_call | solution.py:608
  (63 shorter events, 39.8 us)
Async XLA Ops:
  3.6 7.5 %collective-permute-start = (f32[256,256]{1,0:T(8,128)}, f32[256,256]{1,0:T(8,128)S(1)}, u32[]{:S(2)}, u32[]{:S(2)}) collective-permute-start(f32[256,256]{1,0:T(8,128)} %get-tuple-element.38), channel_id=1, source_target_pairs={{0,64},{64,128},{128,192},{192,0},{1,65},{65,129},{129,193},{193,1... | collective-permute-start | bytes 786440 | tf_op jit(solution)/shard_map/ppermute | solution.py:637
  5.7 6.9 %collective-permute-start.1 = (f32[256,256]{1,0:T(8,128)}, f32[256,256]{1,0:T(8,128)S(1)}, u32[]{:S(2)}, u32[]{:S(2)}) collective-permute-start(f32[256,256]{1,0:T(8,128)} %get-tuple-element.39), channel_id=1, source_target_pairs={{0,192},{64,0},{128,64},{192,128},{1,193},{65,1},{129,65},{193,129... | collective-permute-start | bytes 786440 | tf_op jit(solution)/shard_map/ppermute | solution.py:637
  7.2 14.2 %collective-permute-start.3 = (f32[256,256]{1,0:T(8,128)}, f32[256,256]{1,0:T(8,128)S(1)}, u32[]{:S(2)}, u32[]{:S(2)}) collective-permute-start(f32[256,256]{1,0:T(8,128)} %get-tuple-element.38), channel_id=1, source_target_pairs={{0,192},{64,0},{128,64},{192,128},{1,193},{65,1},{129,65},{193,129... | collective-permute-start | bytes 786440 | tf_op jit(solution)/shard_map/ppermute | solution.py:637
  8.6 12.8 %collective-permute-start.2 = (f32[256,256]{1,0:T(8,128)}, f32[256,256]{1,0:T(8,128)S(1)}, u32[]{:S(2)}, u32[]{:S(2)}) collective-permute-start(f32[256,256]{1,0:T(8,128)} %get-tuple-element.39), channel_id=1, source_target_pairs={{0,64},{64,128},{128,192},{192,0},{1,65},{65,129},{129,193},{193,1... | collective-permute-start | bytes 786440 | tf_op jit(solution)/shard_map/ppermute | solution.py:637
  12.6 10.8 %collective-permute-start.4 = (f32[256,256]{1,0:T(8,128)S(1)}, f32[256,256]{1,0:T(8,128)S(1)}, u32[]{:S(2)}, u32[]{:S(2)}) collective-permute-start(f32[256,256]{1,0:T(8,128)S(1)} %collective-permute-done.refs_0_), channel_id=1, source_target_pairs={{0,64},{64,128},{128,192},{192,0},{1,65},{65,129},{129,193},{193,1... | collective-permute-start | bytes 786440 | tf_op jit(solution)/shard_map/ppermute | solution.py:637
  14.1 9.8 %collective-permute-start.5 = (f32[256,256]{1,0:T(8,128)S(1)}, f32[256,256]{1,0:T(8,128)S(1)}, u32[]{:S(2)}, u32[]{:S(2)}) collective-permute-start(f32[256,256]{1,0:T(8,128)S(1)} %collective-permute-done.1.refs_3_), channel_id=1, source_target_pairs={{0,192},{64,0},{128,64},{192,128},{1,193},{65,1},{129,65},{193,129... | collective-permute-start | bytes 786440 | tf_op jit(solution)/shard_map/ppermute | solution.py:637
  23.9 4.3 %collective-permute-start.6 = (f32[256,256]{1,0:T(8,128)S(1)}, f32[256,256]{1,0:T(8,128)S(1)}, u32[]{:S(2)}, u32[]{:S(2)}) collective-permute-start(f32[256,256]{1,0:T(8,128)S(1)} %collective-permute-done.refs_0_), channel_id=1, source_target_pairs={{0,1},{1,0},{2,3},{3,2},{4,5},{5,4},{6,7},{7,6},{8,9},{9,8},{10,11... | collective-permute-start | bytes 786440 | tf_op jit(solution)/shard_map/ppermute | solution.py:640
  27.0 1.5 collective-permute-start.7
  27.1 1.8 %collective-permute-start.8 = (f32[256,256]{1,0:T(8,128)S(1)}, f32[256,256]{1,0:T(8,128)S(1)}, u32[]{:S(2)}, u32[]{:S(2)}) collective-permute-start(f32[256,256]{1,0:T(8,128)S(1)} %collective-permute-done.3.refs_2_), channel_id=1, source_target_pairs={{0,1},{1,0},{2,3},{3,2},{4,5},{5,4},{6,7},{7,6},{8,9},{9,8},{10,11... | collective-permute-start | bytes 786440 | tf_op jit(solution)/shard_map/ppermute | solution.py:640
  27.5 1.8 collective-permute-start.9
  27.6 2.0 %collective-permute-start.10 = (f32[256,256]{1,0:T(8,128)S(1)}, f32[256,256]{1,0:T(8,128)S(1)}, u32[]{:S(2)}, u32[]{:S(2)}) collective-permute-start(f32[256,256]{1,0:T(8,128)S(1)} %collective-permute-done.4.refs_4_), channel_id=1, source_target_pairs={{0,1},{1,0},{2,3},{3,2},{4,5},{5,4},{6,7},{7,6},{8,9},{9,8},{10,11... | collective-permute-start | bytes 786440 | tf_op jit(solution)/shard_map/ppermute | solution.py:640
  28.1 1.9 %collective-permute-start.11 = (f32[256,256]{1,0:T(8,128)S(1)}, f32[256,256]{1,0:T(8,128)S(1)}, u32[]{:S(2)}, u32[]{:S(2)}) collective-permute-start(f32[256,256]{1,0:T(8,128)S(1)} %collective-permute-done.5.refs_5_), channel_id=1, source_target_pairs={{0,1},{1,0},{2,3},{3,2},{4,5},{5,4},{6,7},{7,6},{8,9},{9,8},{10,11... | collective-permute-start | bytes 786440 | tf_op jit(solution)/shard_map/ppermute | solution.py:640
  52.4 2.7 %collective-permute-start.12 = (f32[1,16,128]{2,1,0:T(8,128)S(1)}, f32[1,16,128]{2,1,0:T(8,128)S(1)}, u32[]{:S(2)}, u32[]{:S(2)}) collective-permute-start(f32[1,16,128]{2,1,0:T(8,128)S(1)} %get-tuple-element.54), channel_id=1, source_target_pairs={{0,1},{1,0},{2,3},{3,2},{4,5},{5,4},{6,7},{7,6},{8,9},{9,8},{10,11... | collective-permute-start | bytes 24584 | tf_op jit(solution)/shard_map/ppermute | solution.py:640
  82.2 3.7 %collective-permute-start.13 = (f32[1,16,128]{2,1,0:T(8,128)S(1)}, f32[1,16,128]{2,1,0:T(8,128)S(1)}, u32[]{:S(2)}, u32[]{:S(2)}) collective-permute-start(f32[1,16,128]{2,1,0:T(8,128)S(1)} %get-tuple-element.55), channel_id=1, source_target_pairs={{0,1},{1,0},{2,3},{3,2},{4,5},{5,4},{6,7},{7,6},{8,9},{9,8},{10,11... | collective-permute-start | bytes 24584 | tf_op jit(solution)/shard_map/ppermute | solution.py:640
  109.5 3.7 %collective-permute-start.14 = (f32[1,24,128]{2,1,0:T(8,128)S(1)}, f32[1,24,128]{2,1,0:T(8,128)S(1)}, u32[]{:S(2)}, u32[]{:S(2)}) collective-permute-start(f32[1,24,128]{2,1,0:T(8,128)S(1)} %get-tuple-element.57), channel_id=1, source_target_pairs={{0,1},{1,0},{2,3},{3,2},{4,5},{5,4},{6,7},{7,6},{8,9},{9,8},{10,11... | collective-permute-start | bytes 36872 | tf_op jit(solution)/shard_map/ppermute | solution.py:640
  135.3 4.1 %collective-permute-start.15 = (f32[16,64,256]{2,1,0:T(8,128)S(1)}, f32[16,64,256]{2,1,0:T(8,128)S(1)}, u32[]{:S(2)}, u32[]{:S(2)}) collective-permute-start(f32[16,64,256]{2,1,0:T(8,128)S(1)} %get-tuple-element.60), channel_id=1, source_target_pairs={{0,1},{1,0},{2,3},{3,2},{4,5},{5,4},{6,7},{7,6},{8,9},{9,8},{10,11... | collective-permute-start | bytes 3145736 | tf_op jit(solution)/shard_map/ppermute | solution.py:640
  137.2 14.9 %collective-permute-start.17 = (f32[4,256,128]{2,1,0:T(8,128)}, f32[4,256,128]{2,1,0:T(8,128)S(1)}, u32[]{:S(2)}, u32[]{:S(2)}) collective-permute-start(f32[4,256,128]{2,1,0:T(8,128)} %get-tuple-element.67), channel_id=1, source_target_pairs={{0,56},{8,16},{16,8},{24,32},{32,24},{40,48},{48,40},{56,0},{1,57}... | collective-permute-start | bytes 1572872 | tf_op jit(solution)/shard_map/ppermute | solution.py:369
  137.3 15.6 %collective-permute-start.16 = (f32[4,256,128]{2,1,0:T(8,128)}, f32[4,256,128]{2,1,0:T(8,128)}, u32[]{:S(2)}, u32[]{:S(2)}) collective-permute-start(f32[4,256,128]{2,1,0:T(8,128)} %get-tuple-element.65), channel_id=1, source_target_pairs={{0,8},{8,0},{16,24},{24,16},{32,40},{40,32},{48,56},{56,48},{1,9},... | collective-permute-start | bytes 1572872 | tf_op jit(solution)/shard_map/ppermute | solution.py:369
  140.6 20.7 %all-to-all-start.6 = ((f32[16,64,256]{2,1,0:T(8,128)}), f32[16,64,256]{2,1,0:T(8,128)S(1)}, u32[]{:S(2)}, u32[]{:S(2)}) async-start(f32[16,64,256]{2,1,0:T(8,128)} %add.170), calls=%async_computation.6 | async-start | bytes 2097152 | tf_op jit(solution)/shard_map/all_to_all | solution.py:34
  152.9 15.9 %collective-permute-start.20 = (f32[2,256,128]{2,1,0:T(8,128)}, f32[2,256,128]{2,1,0:T(8,128)S(1)}, u32[]{:S(2)}, u32[]{:S(2)}) collective-permute-start(f32[2,256,128]{2,1,0:T(8,128)} %slice_add_fusion), channel_id=1, source_target_pairs={{0,16},{8,56},{16,32},{24,8},{32,48},{40,24},{48,0},{56,40},{1,17}... | collective-permute-start | bytes 786440 | tf_op jit(solution)/shard_map/ppermute | solution.py:377
  154.6 14.6 %collective-permute-start.18 = (f32[2,256,128]{2,1,0:T(8,128)}, f32[2,256,128]{2,1,0:T(8,128)S(1)}, u32[]{:S(2)}, u32[]{:S(2)}) collective-permute-start(f32[2,256,128]{2,1,0:T(8,128)} %slice_add_fusion.1), channel_id=1, source_target_pairs={{0,48},{8,24},{16,0},{24,40},{32,16},{40,56},{48,32},{56,8},{1,49}... | collective-permute-start | bytes 786440 | tf_op jit(solution)/shard_map/ppermute | solution.py:377
  163.6 14.6 %all-to-all-start.7 = ((f32[8,64,256]{2,1,0:T(8,128)}), f32[8,64,256]{2,1,0:T(8,128)S(1)}, u32[]{:S(2)}, u32[]{:S(2)}) async-start(f32[8,64,256]{2,1,0:T(8,128)} %student_end.1), calls=%async_computation.7 | async-start | bytes 1048576 | tf_op jit(solution)/shard_map/all_to_all | solution.py:34
  168.8 4.2 %collective-permute-start.21 = (f32[256,128]{1,0:T(8,128)S(1)}, f32[256,128]{1,0:T(8,128)S(1)}, u32[]{:S(2)}, u32[]{:S(2)}) collective-permute-start(f32[256,128]{1,0:T(8,128)S(1)} %fusion), channel_id=1, source_target_pairs={{0,8},{8,0},{16,24},{24,16},{32,40},{40,32},{48,56},{56,48},{1,9},... | collective-permute-start | bytes 393224 | tf_op jit(solution)/shard_map/ppermute | solution.py:386
  169.2 5.7 %collective-permute-start.19 = (f32[256,128]{1,0:T(8,128)S(1)}, f32[256,128]{1,0:T(8,128)S(1)}, u32[]{:S(2)}, u32[]{:S(2)}) collective-permute-start(f32[256,128]{1,0:T(8,128)S(1)} %fusion.1), channel_id=1, source_target_pairs={{0,56},{8,16},{16,8},{24,32},{32,24},{40,48},{48,40},{56,0},{1,57}... | collective-permute-start | bytes 393224 | tf_op jit(solution)/shard_map/ppermute | solution.py:386
  (2 other events, 34.3 us)

commit v13 on v11

--- a/solution.py
+++ b/solution.py
@@ -172,21 +172,21 @@
     parts = [slice(c, c + size) for c in range(0, weights_ref.shape[0], size)]
 
     def step(i, carry):
-        chunk = cast_ref[pl.ds(pl.multiple_of(i * WIDE, WIDE), WIDE), :][:, :D]
+        chunk = cast_ref[pl.ds(pl.multiple_of(i * size, size), size), :][:, :D]
         logits = nt_dot(weights_ref[parts[0], :], chunk)
         for k, part in enumerate(parts):
             following = nt_dot(weights_ref[parts[k + 1], :], chunk) if k + 1 < len(parts) else None
             energy = jnp.exp2(logits * teacher_power)
             total = total_ref[part, :]
-            for j in range(WIDE // LANES):
+            for j in range(size // LANES):
                 tile = energy[:, j * LANES : (j + 1) * LANES]
-                energy_ref[i * (WIDE // LANES) + j, part, :] = tile.astype(bf16)
+                energy_ref[i * (size // LANES) + j, part, :] = tile.astype(bf16)
                 total = total + tile
             total_ref[part, :] = total
             logits = following
         return carry
 
-    lax.fori_loop(0, tokens // WIDE, step, 0)
+    lax.fori_loop(0, tokens // size, step, 0)
     totals = lane_totals(total_ref[...])
     for copy in range(sums_ref.shape[0]):
         sums_ref[copy] = totals
@@ -235,7 +235,7 @@
 
 
 def student_body(units_ref, protos_ref, sums_ref, unit_ref, cast_ref, total_ref, buffer_ref, sems):
-    size = buffer_ref.shape[0] // FETCHES
+    size, wide = buffer_ref.shape[0] // FETCHES, 512
     fetch_all(units_ref, D, unit_ref, protos_ref, buffer_ref, sems)
     cast_ref[...] = unit_ref[...].astype(bf16)
     total_ref[...] = jnp.zeros_like(total_ref)
@@ -245,16 +245,16 @@
         total = total_ref[...]
 
         def logits_of(part):
-            rows = pl.ds(pl.multiple_of(i * size + part * WIDE, WIDE), WIDE)
+            rows = pl.ds(pl.multiple_of(i * size + part * wide, wide), wide)
             return nt_dot(cast_ref[...], directions(buffer_ref[rows, :]))
 
-        parts = size // WIDE
+        parts = size // wide
         logits = logits_of(0)
         for part in range(parts):
             following = logits_of(part + 1) if part + 1 < parts else None
             values = jnp.exp2(logits * student_power)
             logits = following
-            for j in range(WIDE // LANES):
+            for j in range(wide // LANES):
                 total = total + values[:, j * LANES : (j + 1) * LANES]
         total_ref[...] = total
         return carry

time: 180 us -> 179 us (level)
  no operation moved by 1% of the time
where the time goes in v13:
time: 179 us; the launch traced here: 178 us
  blocking collectives  66.3 us (37%)
  Pallas kernels  41.8 us (23%)
  starting transfers between devices  36.3 us (20%)
  waiting for transfers between devices  26.9 us (15%)
  other arithmetic  4.63 us (3%)
    all_to_all x6, blocking collectives, spread(): return lax.all_to_all(value, axes, 0, 0, tiled=True)  66.3 us
    ppermute x10, starting transfers between devices, on_device(): from_core = lambda value: lax.ppermute(value, 'core', [(0, 1), (1, 0)])  14 us
    pallas_call x1, Pallas kernels, gradients(): pl.pallas_call(gradient_body, grid_spec=pltpu.PrefetchScalarGridSpec(num_...  11.4 us
    all_to_all x2, starting transfers between devices, spread(): return lax.all_to_all(value, axes, 0, 0, tiled=True)  8.76 us
    ppermute x2, waiting for transfers between devices, collect(): got = lax.ppermute(send, 'z', [(z, (z - way[z]) % n) for z in range(n)])  7.87 us
    ppermute x6, starting transfers between devices, on_device(): lax.ppermute(value, 'y', [(i, (i + step) % y_size) for i in range(y_size)])  7.71 us
    pallas_call x3, Pallas kernels, row_sums(): pl.pallas_call(row_body, in_specs=[whole] * (2 + len(norm_part)), out_spe...  6.22 us
    pallas_call x1, Pallas kernels, student_sums(): pl.pallas_call(student_body, in_specs=[pl.BlockSpec(memory_space=pl.ANY)]...  6.06 us
  transfers between devices with their start and end apart: 24, of which 18 were waited for; matrix products, arithmetic and copies ran while one was open for 3% of the time, Pallas kernels for 6%

profile of v13, /device:TPU:1, one launch (start us, length us, event | category | flops | bytes accessed | tf_op | source)
XLA Modules:
  0.0 178.3 jit_solution(8810521767811540704)
XLA Ops:
  0.6 3.0 %select.31 = (f32[512,512]{1,0:T(8,128)}, f32[512,1]{1,0:T(8,128)}, f32[256,256]{1,0:T(8,128)}, f32[256,256]{1,0:T(8,128)}) custom-call(s32[1]{0:T(128)} %bitcast.core_ref, bf16[4,256,256]{2,1,0:T(8,128)(2,1)} %teacher_ref.1, bf16[4,256,256]{2,1,0:T(8,128)(2,1)} %student_ref.1, s32[4,256]{1,0:T(4,128)} %order_ref.1), custom_call_target="tpu_custom_call" | custom-call | tf_op jit(solution)/shard_map/select/pallas_call | solution.py:103
  15.3 6.1 %student.1.refs_0_ = f32[4,128]{1,0:T(4,128)S(1)} custom-call(f32[512,512]{1,0:T(8,128)} %get-tuple-element.40.units_ref.unit_ref, bf16[8192,256]{1,0:T(8,128)(2,1)} %refs_6_.1), custom_call_target="tpu_custom_call" | custom-call | flops 4294967296 | bytes 8388608 | tf_op jit(solution)/shard_map/student/pallas_call | solution.py:268
  23.9 3.1 %collective-permute-start.6 = (f32[256,256]{1,0:T(8,128)S(1)}, f32[256,256]{1,0:T(8,128)S(1)}, u32[]{:S(2)}, u32[]{:S(2)}) collective-permute-start(f32[256,256]{1,0:T(8,128)S(1)} %collective-permute-done.refs_0_), channel_id=1, source_target_pairs={{0,1},{1,0},{2,3},{3,2},{4,5},{5,4},{6,7},{7,6},{8,9},{9,8},{10,11... | collective-permute-start | bytes 786440 | tf_op jit(solution)/shard_map/ppermute | solution.py:635
  30.0 6.0 %energy.1 = (bf16[16,2048,128]{2,1,0:T(8,128)(2,1)S(1)}, f32[8,16,128]{2,1,0:T(8,128)S(1)}, bf16[2048,512]{1,0:T(8,128)(2,1)S(1)}) custom-call(s32[8]{0:T(128)S(1)} %stack.43.place_ref, f32[512,512]{1,0:T(8,128)} %get-tuple-element.40.units_ref.unit_ref, f32[256,256]{1,0:T(8,128)S(1)} %collective-permute-done.refs_0_, ...), custom_call_target="tpu_custom_call" | custom-call | flops 4294967296 | bytes 8388608 | tf_op jit(solution)/shard_map/energy/pallas_call | solution.py:211
  36.1 14.2 %all_to_all.40.pieces_ref = f32[8,16,128]{2,1,0:T(8,128)S(1)} all-to-all(f32[8,16,128]{2,1,0:T(8,128)S(1)} %get-tuple-element.53), channel_id=1, replica_groups=mesh['y'=4,'z'=8,'x'=4,'core'=2] {'z'}, dimensions={0} | all-to-all | bytes 131072 | tf_op jit(solution)/shard_map/all_to_all | solution.py:34
  50.2 2.1 %row_sums.3 = (f32[16,128]{1,0:T(8,128)}, f32[1,16,128]{2,1,0:T(8,128)S(1)}) custom-call(bf16[16,2048,128]{2,1,0:T(8,128)(2,1)S(1)} %get-tuple-element.52.energy_ref, f32[8,16,128]{2,1,0:T(8,128)S(1)} %all_to_all.40.pieces_ref), custom_call_target="tpu_custom_call" | custom-call | flops 8388608 | tf_op jit(solution)/shard_map/row_sums/pallas_call | solution.py:315
  55.1 13.1 %all_to_all.41.pieces_ref = f32[16,16,128]{2,1,0:T(8,128)S(1)} all-to-all(f32[16,16,128]{2,1,0:T(8,128)S(1)} %broadcast_in_dim.26), channel_id=1, replica_groups=mesh['y'=4,'z'=8,'x'=4,'core'=2] {'y','x'}, dimensions={0} | all-to-all | bytes 262144 | tf_op jit(solution)/shard_map/all_to_all | solution.py:34
  68.2 2.2 %column_sums.2 = f32[8,16,128]{2,1,0:T(8,128)S(1)} custom-call(bf16[16,2048,128]{2,1,0:T(8,128)(2,1)S(1)} %get-tuple-element.52.energy_ref, f32[16,16,128]{2,1,0:T(8,128)S(1)} %all_to_all.41.pieces_ref), custom_call_target="tpu_custom_call" | custom-call | flops 8388608 | tf_op jit(solution)/shard_map/column_sums/pallas_call | solution.py:350
  70.4 9.7 %all_to_all.42.pieces_ref = f32[8,16,128]{2,1,0:T(8,128)S(1)} all-to-all(f32[8,16,128]{2,1,0:T(8,128)S(1)} %column_sums.2), channel_id=1, replica_groups=mesh['y'=4,'z'=8,'x'=4,'core'=2] {'z'}, dimensions={0} | all-to-all | bytes 131072 | tf_op jit(solution)/shard_map/all_to_all | solution.py:34
  80.1 2.1 %row_sums.4 = (f32[16,128]{1,0:T(8,128)}, f32[1,16,128]{2,1,0:T(8,128)S(1)}) custom-call(bf16[16,2048,128]{2,1,0:T(8,128)(2,1)S(1)} %get-tuple-element.52.energy_ref, f32[8,16,128]{2,1,0:T(8,128)S(1)} %all_to_all.42.pieces_ref), custom_call_target="tpu_custom_call" | custom-call | flops 8388608 | tf_op jit(solution)/shard_map/row_sums/pallas_call | solution.py:315
  82.2 2.9 %collective-permute-start.13 = (f32[1,16,128]{2,1,0:T(8,128)S(1)}, f32[1,16,128]{2,1,0:T(8,128)S(1)}, u32[]{:S(2)}, u32[]{:S(2)}) collective-permute-start(f32[1,16,128]{2,1,0:T(8,128)S(1)} %get-tuple-element.55), channel_id=1, source_target_pairs={{0,1},{1,0},{2,3},{3,2},{4,5},{5,4},{6,7},{7,6},{8,9},{9,8},{10,11... | collective-permute-start | bytes 24584 | tf_op jit(solution)/shard_map/ppermute | solution.py:635
  86.0 9.6 %all_to_all.43.pieces_ref = f32[16,16,128]{2,1,0:T(8,128)S(1)} all-to-all(f32[16,16,128]{2,1,0:T(8,128)S(1)} %broadcast_in_dim.28), channel_id=1, replica_groups=mesh['y'=4,'z'=8,'x'=4,'core'=2] {'y','x'}, dimensions={0} | all-to-all | bytes 262144 | tf_op jit(solution)/shard_map/all_to_all | solution.py:34
  95.6 2.2 %column_sums.3 = f32[8,16,128]{2,1,0:T(8,128)S(1)} custom-call(bf16[16,2048,128]{2,1,0:T(8,128)(2,1)S(1)} %get-tuple-element.52.energy_ref, f32[16,16,128]{2,1,0:T(8,128)S(1)} %all_to_all.43.pieces_ref), custom_call_target="tpu_custom_call" | custom-call | flops 8388608 | tf_op jit(solution)/shard_map/column_sums/pallas_call | solution.py:350
  97.8 9.7 %all_to_all.44.pieces_ref = f32[8,16,128]{2,1,0:T(8,128)S(1)} all-to-all(f32[8,16,128]{2,1,0:T(8,128)S(1)} %column_sums.3), channel_id=1, replica_groups=mesh['y'=4,'z'=8,'x'=4,'core'=2] {'z'}, dimensions={0} | all-to-all | bytes 131072 | tf_op jit(solution)/shard_map/all_to_all | solution.py:34
  109.5 2.9 %collective-permute-start.14 = (f32[1,24,128]{2,1,0:T(8,128)S(1)}, f32[1,24,128]{2,1,0:T(8,128)S(1)}, u32[]{:S(2)}, u32[]{:S(2)}) collective-permute-start(f32[1,24,128]{2,1,0:T(8,128)S(1)} %get-tuple-element.57), channel_id=1, source_target_pairs={{0,1},{1,0},{2,3},{3,2},{4,5},{5,4},{6,7},{7,6},{8,9},{9,8},{10,11... | collective-permute-start | bytes 36872 | tf_op jit(solution)/shard_map/ppermute | solution.py:635
  113.3 10.0 %all_to_all.45 = f32[16,24,128]{2,1,0:T(8,128)S(1)} all-to-all(f32[16,24,128]{2,1,0:T(8,128)S(1)} %broadcast_in_dim.30), channel_id=1, replica_groups=mesh['y'=4,'z'=8,'x'=4,'core'=2] {'y','x'}, dimensions={0} | all-to-all | bytes 393216 | tf_op jit(solution)/shard_map/all_to_all | solution.py:34
  123.2 11.4 %gradients.1 = (f32[4,256,128]{2,1,0:T(8,128)}, f32[4,256,128]{2,1,0:T(8,128)}, f32[4,256,128]{2,1,0:T(8,128)}, f32[4,256,128]{2,1,0:T(8,128)}, f32[16,64,256]{2,1,0:T(8,128)S(1)}, /*index=5*/f32[16,64,256]{2,1,0:T(8,128)S(1)}) custom-call(s32[5,8]{1,0:T(8,128)S(1)} %stack.46.table_ref, bf16[2048,512]{1,0:T(8,128)(2,1)S(1)} %get-tuple-element.51.units_ref, ...), custom_call_target="tpu_custom_call" | custom-call | flops 8589934592 | bytes 8388608 | tf_op jit(solution)/shard_map/gradients/pallas_call | solution.py:520
  139.9 3.7 %all-to-all-start.6 = ((f32[16,64,256]{2,1,0:T(8,128)}), f32[16,64,256]{2,1,0:T(8,128)S(1)}, u32[]{:S(2)}, u32[]{:S(2)}) async-start(f32[16,64,256]{2,1,0:T(8,128)} %add.170), calls=%async_computation.6 | async-start | bytes 2097152 | tf_op jit(solution)/shard_map/all_to_all | solution.py:34
  143.5 7.9 %collective-permute-done.17 = f32[4,256,128]{2,1,0:T(8,128)S(1)} collective-permute-done((f32[4,256,128]{2,1,0:T(8,128)}, f32[4,256,128]{2,1,0:T(8,128)S(1)}, u32[]{:S(2)}, u32[]{:S(2)}) %collective-permute-start.17) | collective-permute-done | bytes 524320 | tf_op jit(solution)/shard_map/ppermute | solution.py:369
  153.9 3.6 %collective-permute-start.18 = (f32[2,256,128]{2,1,0:T(8,128)}, f32[2,256,128]{2,1,0:T(8,128)S(1)}, u32[]{:S(2)}, u32[]{:S(2)}) collective-permute-start(f32[2,256,128]{2,1,0:T(8,128)} %slice_add_fusion.1), channel_id=1, source_target_pairs={{0,48},{8,24},{16,0},{24,40},{32,16},{40,56},{48,32},{56,8},{1,49}... | collective-permute-start | bytes 786440 | tf_op jit(solution)/shard_map/ppermute | solution.py:377
  160.6 2.3 %student_end.1 = f32[8,64,256]{2,1,0:T(8,128)} custom-call(s32[8]{0:T(128)S(1)} %stack.43.place_ref, f32[16,64,256]{2,1,0:T(8,128)S(1)} %all-to-all-done.6.pieces_ref, f32[512,512]{1,0:T(8,128)} %get-tuple-element.40.units_ref.unit_ref, f32[512,1]{1,0:T(8,128)} %get-tuple-element.69.length_ref), custom_call_target="tpu_custom_call" | custom-call | tf_op jit(solution)/shard_map/student_end/pallas_call | solution.py:570
  162.9 5.1 %all-to-all-start.7 = ((f32[8,64,256]{2,1,0:T(8,128)}), f32[8,64,256]{2,1,0:T(8,128)S(1)}, u32[]{:S(2)}, u32[]{:S(2)}) async-start(f32[8,64,256]{2,1,0:T(8,128)} %student_end.1), calls=%async_computation.7 | async-start | bytes 1048576 | tf_op jit(solution)/shard_map/all_to_all | solution.py:34
  169.8 2.5 %collective-permute-done.21.refs_5_ = f32[256,128]{1,0:T(8,128)S(1)} collective-permute-done((f32[256,128]{1,0:T(8,128)S(1)}, f32[256,128]{1,0:T(8,128)S(1)}, u32[]{:S(2)}, u32[]{:S(2)}) %collective-permute-start.21) | collective-permute-done | bytes 131104 | tf_op jit(solution)/shard_map/ppermute | solution.py:386
  174.2 2.4 %proto_end.1 = f32[256,256]{1,0:T(8,128)} custom-call(s32[8]{0:T(128)S(1)} %stack.43.place_ref, f32[256,128]{1,0:T(8,128)S(1)} %get-tuple-element.77.refs_0_, f32[2,256,128]{2,1,0:T(8,128)S(1)} %collective-permute-done.18.refs_1_, f32[256,128]{1,0:T(8,128)S(1)} %collective-permute-done.19.refs_2_, f32[256,128]{1,0:T(8,128)S(1)} %get-tuple-element.75.refs_3_, ...), custom_call_target="tpu_custom_call" | custom-call | tf_op jit(solution)/shard_map/proto_end/pallas_call | solution.py:603
  (63 shorter events, 39.8 us)
Async XLA Ops:
  3.6 7.5 %collective-permute-start = (f32[256,256]{1,0:T(8,128)}, f32[256,256]{1,0:T(8,128)S(1)}, u32[]{:S(2)}, u32[]{:S(2)}) collective-permute-start(f32[256,256]{1,0:T(8,128)} %get-tuple-element.38), channel_id=1, source_target_pairs={{0,64},{64,128},{128,192},{192,0},{1,65},{65,129},{129,193},{193,1... | collective-permute-start | bytes 786440 | tf_op jit(solution)/shard_map/ppermute | solution.py:632
  5.7 6.9 %collective-permute-start.1 = (f32[256,256]{1,0:T(8,128)}, f32[256,256]{1,0:T(8,128)S(1)}, u32[]{:S(2)}, u32[]{:S(2)}) collective-permute-start(f32[256,256]{1,0:T(8,128)} %get-tuple-element.39), channel_id=1, source_target_pairs={{0,192},{64,0},{128,64},{192,128},{1,193},{65,1},{129,65},{193,129... | collective-permute-start | bytes 786440 | tf_op jit(solution)/shard_map/ppermute | solution.py:632
  7.2 14.2 %collective-permute-start.3 = (f32[256,256]{1,0:T(8,128)}, f32[256,256]{1,0:T(8,128)S(1)}, u32[]{:S(2)}, u32[]{:S(2)}) collective-permute-start(f32[256,256]{1,0:T(8,128)} %get-tuple-element.38), channel_id=1, source_target_pairs={{0,192},{64,0},{128,64},{192,128},{1,193},{65,1},{129,65},{193,129... | collective-permute-start | bytes 786440 | tf_op jit(solution)/shard_map/ppermute | solution.py:632
  8.6 12.8 %collective-permute-start.2 = (f32[256,256]{1,0:T(8,128)}, f32[256,256]{1,0:T(8,128)S(1)}, u32[]{:S(2)}, u32[]{:S(2)}) collective-permute-start(f32[256,256]{1,0:T(8,128)} %get-tuple-element.39), channel_id=1, source_target_pairs={{0,64},{64,128},{128,192},{192,0},{1,65},{65,129},{129,193},{193,1... | collective-permute-start | bytes 786440 | tf_op jit(solution)/shard_map/ppermute | solution.py:632
  12.6 10.8 %collective-permute-start.4 = (f32[256,256]{1,0:T(8,128)S(1)}, f32[256,256]{1,0:T(8,128)S(1)}, u32[]{:S(2)}, u32[]{:S(2)}) collective-permute-start(f32[256,256]{1,0:T(8,128)S(1)} %collective-permute-done.refs_0_), channel_id=1, source_target_pairs={{0,64},{64,128},{128,192},{192,0},{1,65},{65,129},{129,193},{193,1... | collective-permute-start | bytes 786440 | tf_op jit(solution)/shard_map/ppermute | solution.py:632
  14.1 9.8 %collective-permute-start.5 = (f32[256,256]{1,0:T(8,128)S(1)}, f32[256,256]{1,0:T(8,128)S(1)}, u32[]{:S(2)}, u32[]{:S(2)}) collective-permute-start(f32[256,256]{1,0:T(8,128)S(1)} %collective-permute-done.1.refs_3_), channel_id=1, source_target_pairs={{0,192},{64,0},{128,64},{192,128},{1,193},{65,1},{129,65},{193,129... | collective-permute-start | bytes 786440 | tf_op jit(solution)/shard_map/ppermute | solution.py:632
  23.9 4.2 %collective-permute-start.6 = (f32[256,256]{1,0:T(8,128)S(1)}, f32[256,256]{1,0:T(8,128)S(1)}, u32[]{:S(2)}, u32[]{:S(2)}) collective-permute-start(f32[256,256]{1,0:T(8,128)S(1)} %collective-permute-done.refs_0_), channel_id=1, source_target_pairs={{0,1},{1,0},{2,3},{3,2},{4,5},{5,4},{6,7},{7,6},{8,9},{9,8},{10,11... | collective-permute-start | bytes 786440 | tf_op jit(solution)/shard_map/ppermute | solution.py:635
  27.0 1.5 collective-permute-start.7
  27.1 1.8 %collective-permute-start.8 = (f32[256,256]{1,0:T(8,128)S(1)}, f32[256,256]{1,0:T(8,128)S(1)}, u32[]{:S(2)}, u32[]{:S(2)}) collective-permute-start(f32[256,256]{1,0:T(8,128)S(1)} %collective-permute-done.3.refs_2_), channel_id=1, source_target_pairs={{0,1},{1,0},{2,3},{3,2},{4,5},{5,4},{6,7},{7,6},{8,9},{9,8},{10,11... | collective-permute-start | bytes 786440 | tf_op jit(solution)/shard_map/ppermute | solution.py:635
  27.5 1.8 collective-permute-start.9
  27.6 2.0 %collective-permute-start.10 = (f32[256,256]{1,0:T(8,128)S(1)}, f32[256,256]{1,0:T(8,128)S(1)}, u32[]{:S(2)}, u32[]{:S(2)}) collective-permute-start(f32[256,256]{1,0:T(8,128)S(1)} %collective-permute-done.4.refs_4_), channel_id=1, source_target_pairs={{0,1},{1,0},{2,3},{3,2},{4,5},{5,4},{6,7},{7,6},{8,9},{9,8},{10,11... | collective-permute-start | bytes 786440 | tf_op jit(solution)/shard_map/ppermute | solution.py:635
  28.1 1.9 %collective-permute-start.11 = (f32[256,256]{1,0:T(8,128)S(1)}, f32[256,256]{1,0:T(8,128)S(1)}, u32[]{:S(2)}, u32[]{:S(2)}) collective-permute-start(f32[256,256]{1,0:T(8,128)S(1)} %collective-permute-done.5.refs_5_), channel_id=1, source_target_pairs={{0,1},{1,0},{2,3},{3,2},{4,5},{5,4},{6,7},{7,6},{8,9},{9,8},{10,11... | collective-permute-start | bytes 786440 | tf_op jit(solution)/shard_map/ppermute | solution.py:635
  52.4 2.7 %collective-permute-start.12 = (f32[1,16,128]{2,1,0:T(8,128)S(1)}, f32[1,16,128]{2,1,0:T(8,128)S(1)}, u32[]{:S(2)}, u32[]{:S(2)}) collective-permute-start(f32[1,16,128]{2,1,0:T(8,128)S(1)} %get-tuple-element.54), channel_id=1, source_target_pairs={{0,1},{1,0},{2,3},{3,2},{4,5},{5,4},{6,7},{7,6},{8,9},{9,8},{10,11... | collective-permute-start | bytes 24584 | tf_op jit(solution)/shard_map/ppermute | solution.py:635
  82.2 3.7 %collective-permute-start.13 = (f32[1,16,128]{2,1,0:T(8,128)S(1)}, f32[1,16,128]{2,1,0:T(8,128)S(1)}, u32[]{:S(2)}, u32[]{:S(2)}) collective-permute-start(f32[1,16,128]{2,1,0:T(8,128)S(1)} %get-tuple-element.55), channel_id=1, source_target_pairs={{0,1},{1,0},{2,3},{3,2},{4,5},{5,4},{6,7},{7,6},{8,9},{9,8},{10,11... | collective-permute-start | bytes 24584 | tf_op jit(solution)/shard_map/ppermute | solution.py:635
  109.5 3.7 %collective-permute-start.14 = (f32[1,24,128]{2,1,0:T(8,128)S(1)}, f32[1,24,128]{2,1,0:T(8,128)S(1)}, u32[]{:S(2)}, u32[]{:S(2)}) collective-permute-start(f32[1,24,128]{2,1,0:T(8,128)S(1)} %get-tuple-element.57), channel_id=1, source_target_pairs={{0,1},{1,0},{2,3},{3,2},{4,5},{5,4},{6,7},{7,6},{8,9},{9,8},{10,11... | collective-permute-start | bytes 36872 | tf_op jit(solution)/shard_map/ppermute | solution.py:635
  134.7 4.1 %collective-permute-start.15 = (f32[16,64,256]{2,1,0:T(8,128)S(1)}, f32[16,64,256]{2,1,0:T(8,128)S(1)}, u32[]{:S(2)}, u32[]{:S(2)}) collective-permute-start(f32[16,64,256]{2,1,0:T(8,128)S(1)} %get-tuple-element.60), channel_id=1, source_target_pairs={{0,1},{1,0},{2,3},{3,2},{4,5},{5,4},{6,7},{7,6},{8,9},{9,8},{10,11... | collective-permute-start | bytes 3145736 | tf_op jit(solution)/shard_map/ppermute | solution.py:635
  136.5 14.9 %collective-permute-start.17 = (f32[4,256,128]{2,1,0:T(8,128)}, f32[4,256,128]{2,1,0:T(8,128)S(1)}, u32[]{:S(2)}, u32[]{:S(2)}) collective-permute-start(f32[4,256,128]{2,1,0:T(8,128)} %get-tuple-element.67), channel_id=1, source_target_pairs={{0,56},{8,16},{16,8},{24,32},{32,24},{40,48},{48,40},{56,0},{1,57}... | collective-permute-start | bytes 1572872 | tf_op jit(solution)/shard_map/ppermute | solution.py:369
  136.6 15.6 %collective-permute-start.16 = (f32[4,256,128]{2,1,0:T(8,128)}, f32[4,256,128]{2,1,0:T(8,128)}, u32[]{:S(2)}, u32[]{:S(2)}) collective-permute-start(f32[4,256,128]{2,1,0:T(8,128)} %get-tuple-element.65), channel_id=1, source_target_pairs={{0,8},{8,0},{16,24},{24,16},{32,40},{40,32},{48,56},{56,48},{1,9},... | collective-permute-start | bytes 1572872 | tf_op jit(solution)/shard_map/ppermute | solution.py:369
  139.9 20.7 %all-to-all-start.6 = ((f32[16,64,256]{2,1,0:T(8,128)}), f32[16,64,256]{2,1,0:T(8,128)S(1)}, u32[]{:S(2)}, u32[]{:S(2)}) async-start(f32[16,64,256]{2,1,0:T(8,128)} %add.170), calls=%async_computation.6 | async-start | bytes 2097152 | tf_op jit(solution)/shard_map/all_to_all | solution.py:34
  152.2 15.9 %collective-permute-start.20 = (f32[2,256,128]{2,1,0:T(8,128)}, f32[2,256,128]{2,1,0:T(8,128)S(1)}, u32[]{:S(2)}, u32[]{:S(2)}) collective-permute-start(f32[2,256,128]{2,1,0:T(8,128)} %slice_add_fusion), channel_id=1, source_target_pairs={{0,16},{8,56},{16,32},{24,8},{32,48},{40,24},{48,0},{56,40},{1,17}... | collective-permute-start | bytes 786440 | tf_op jit(solution)/shard_map/ppermute | solution.py:377
  153.9 14.6 %collective-permute-start.18 = (f32[2,256,128]{2,1,0:T(8,128)}, f32[2,256,128]{2,1,0:T(8,128)S(1)}, u32[]{:S(2)}, u32[]{:S(2)}) collective-permute-start(f32[2,256,128]{2,1,0:T(8,128)} %slice_add_fusion.1), channel_id=1, source_target_pairs={{0,48},{8,24},{16,0},{24,40},{32,16},{40,56},{48,32},{56,8},{1,49}... | collective-permute-start | bytes 786440 | tf_op jit(solution)/shard_map/ppermute | solution.py:377
  162.9 14.6 %all-to-all-start.7 = ((f32[8,64,256]{2,1,0:T(8,128)}), f32[8,64,256]{2,1,0:T(8,128)S(1)}, u32[]{:S(2)}, u32[]{:S(2)}) async-start(f32[8,64,256]{2,1,0:T(8,128)} %student_end.1), calls=%async_computation.7 | async-start | bytes 1048576 | tf_op jit(solution)/shard_map/all_to_all | solution.py:34
  168.1 4.2 %collective-permute-start.21 = (f32[256,128]{1,0:T(8,128)S(1)}, f32[256,128]{1,0:T(8,128)S(1)}, u32[]{:S(2)}, u32[]{:S(2)}) collective-permute-start(f32[256,128]{1,0:T(8,128)S(1)} %fusion), channel_id=1, source_target_pairs={{0,8},{8,0},{16,24},{24,16},{32,40},{40,32},{48,56},{56,48},{1,9},... | collective-permute-start | bytes 393224 | tf_op jit(solution)/shard_map/ppermute | solution.py:386
  168.5 5.7 %collective-permute-start.19 = (f32[256,128]{1,0:T(8,128)S(1)}, f32[256,128]{1,0:T(8,128)S(1)}, u32[]{:S(2)}, u32[]{:S(2)}) collective-permute-start(f32[256,128]{1,0:T(8,128)S(1)} %fusion.1), channel_id=1, source_target_pairs={{0,56},{8,16},{16,8},{24,32},{32,24},{40,48},{48,40},{56,0},{1,57}... | collective-permute-start | bytes 393224 | tf_op jit(solution)/shard_map/ppermute | solution.py:386
  (2 other events, 34.3 us)
